TPU v7x, 128 devices: a whole 4x4x4 slice. The times are simulated.
128 devices in a mesh: dp: 8 (over y, z_lo), tensor: 16 (over z_hi, x, core).
Axes of the slice: x: 4, y: 4, z: 4 (z_hi: 2, z_lo: 2; z = z_hi * 2 + z_lo), core: 2. Of those that a mesh axis runs over, the one named last changes fastest.
Arguments:
- token_ids: int32 [512, 4], P(('dp', 'tensor')), may hold values from 0 to 76031
- lengths: int32 [512], P(('dp', 'tensor')), may hold values from 1 to 508, 130048 in all
- embedding: bfloat16 [76032, 8192], P('tensor', 'dp'), may hold values from -6 to 6
- norm_gain: bfloat16 [8192], replicated, may hold values from 0.099609375 to 1.8984375
- q_weight: bfloat16 [8192, 8192], P('dp', 'tensor'), may hold values from -0.0625 to 0.0625
- k_weight: bfloat16 [8192, 1024], P('dp', 'tensor'), may hold values from -0.0625 to 0.0625
- v_weight: bfloat16 [8192, 1024], P('dp', 'tensor'), may hold values from -0.0625 to 0.0625
- q_bias: bfloat16 [8192], P('tensor'), may hold values from -6 to 6
- k_bias: bfloat16 [1024], P('tensor'), may hold values from -6 to 6
- v_bias: bfloat16 [1024], P('tensor'), may hold values from -6 to 6
- o_weight: bfloat16 [8192, 8192], P('tensor', 'dp'), may hold values from -0.0625 to 0.0625
- key_cache: bfloat16 [512, 512, 1024], P(('dp', 'tensor')), may hold values from -400 to 400, as said below
- value_cache: bfloat16 [512, 512, 1024], P(('dp', 'tensor')), may hold values from -6 to 6
Outputs:
- hidden: bfloat16 [512, 4, 8192], P(('dp', 'tensor'))
- new_keys: bfloat16 [512, 4, 1024], P(('dp', 'tensor'))
- new_values: bfloat16 [512, 4, 1024], P(('dp', 'tensor'))
Inputs may be any that keep to these rules, and one draw needn't show every extreme that they name: The next 4 tokens of sequence b take positions lengths[b] to lengths[b] + 3. `key_cache`: keys are stored already rotated; slots at or past a sequence's length are unused.
All inputs are finite; a program needn't handle non-finite values. No bound on the sum of `lengths` on one device may be relied on, other than what follows from the above.
Results may differ from a plain program's by a relative error of at most 0.03.
Values may be sent and summed in bfloat16 or wider, within the bound.
No kernel may reach another device: no remote copies, remote signals or barrier semaphores. Data moves between devices by JAX's collectives and lax.ppermute only.
A program may use at most 128 MiB of HBM per device.

v0:
```python
import jax
import jax.numpy as jnp
from jax import lax
from jax.sharding import PartitionSpec as P

HD = 128


norm_epsilon = 1e-06
rope_base = 1000000.0
masked_low = -1e30


def rotate(features, positions):
    head_width = features.shape[-1]
    half_width = head_width // 2
    frequency = rope_base ** (-(2.0 * jnp.arange(half_width, dtype=jnp.float32)) / head_width)
    angles = positions.astype(jnp.float32)[..., None, None] * frequency
    cosine = jnp.cos(angles)
    sine_part = jnp.sin(angles)
    leading = features[..., :half_width]
    trailing = features[..., half_width:]
    return jnp.concatenate(
        [leading * cosine - trailing * sine_part, trailing * cosine + leading * sine_part], axis=-1
    )


def attend(rotated, fresh_keys, fresh_values, key_cache, value_cache, lengths, first_step):
    seq_here, step_span, heads, head_width = rotated.shape
    kv_heads = fresh_keys.shape[2]
    group_size = heads // kv_heads
    cache_len = key_cache.shape[1]
    cache_keys = key_cache.reshape(seq_here, cache_len, kv_heads, head_width)
    cache_values = value_cache.reshape(seq_here, cache_len, kv_heads, head_width)
    grouped = rotated.reshape(seq_here, step_span, kv_heads, group_size, head_width)
    score_scale = head_width ** (-0.5)
    cached = (
        jnp.einsum("skgrd,sjgd->skgrj", grouped, cache_keys, preferred_element_type=jnp.float32)
        * score_scale
    )
    fresh_scores = (
        jnp.einsum("skgrd,sjgd->skgrj", grouped, fresh_keys, preferred_element_type=jnp.float32)
        * score_scale
    )
    cache_valid = (jnp.arange(cache_len, dtype=jnp.int32)[None, :] < lengths[:, None])[
        :, None, None, None, :
    ]
    fresh_count = fresh_keys.shape[1]
    fresh_valid = (
        jnp.arange(fresh_count, dtype=jnp.int32)[None, :]
        <= first_step + jnp.arange(step_span, dtype=jnp.int32)[:, None]
    )[None, :, None, None, :]
    row_top = jnp.maximum(
        jnp.max(jnp.where(cache_valid, cached, masked_low), axis=-1),
        jnp.max(jnp.where(fresh_valid, fresh_scores, masked_low), axis=-1),
    )[..., None]
    cache_exp = jnp.exp(jnp.where(cache_valid, cached - row_top, masked_low))
    fresh_exp = jnp.exp(jnp.where(fresh_valid, fresh_scores - row_top, masked_low))
    denominator = jnp.sum(cache_exp, axis=-1, keepdims=True) + jnp.sum(
        fresh_exp, axis=-1, keepdims=True
    )
    cache_weights = (cache_exp / denominator).astype(jnp.bfloat16)
    fresh_weights = (fresh_exp / denominator).astype(jnp.bfloat16)
    attended = jnp.einsum(
        "skgrj,sjgd->skgrd", cache_weights, cache_values, preferred_element_type=jnp.float32
    )
    attended = attended + jnp.einsum(
        "skgrj,sjgd->skgrd", fresh_weights, fresh_values, preferred_element_type=jnp.float32
    )
    return attended.reshape(seq_here, step_span, heads * head_width).astype(jnp.bfloat16)


def per_device(
    token_ids,
    lengths,
    embedding,
    norm_gain,
    q_weight,
    k_weight,
    v_weight,
    q_bias,
    k_bias,
    v_bias,
    o_weight,
    key_cache,
    value_cache,
):
    tensor_count = lax.axis_size("tensor")
    replica_count = lax.axis_size("dp")
    seq_here, step_count = token_ids.shape
    model_width = norm_gain.shape[0]
    q_cols = q_weight.shape[1]
    k_cols = k_weight.shape[1]
    every_id = lax.all_gather(token_ids, ("dp", "tensor"), axis=0, tiled=True)
    ordered = (
        every_id.reshape(replica_count, tensor_count, seq_here * step_count)
        .transpose(1, 0, 2)
        .reshape(-1)
    )
    rows_here = embedding.shape[0]
    offset = ordered - lax.axis_index("tensor") * rows_here
    inside = (offset >= 0) & (offset < rows_here)
    picked = jnp.take(embedding, jnp.clip(offset, 0, rows_here - 1), axis=0)
    masked_rows = jnp.where(inside[:, None], picked, jnp.zeros_like(picked))
    own_rows = lax.psum_scatter(
        masked_rows.astype(jnp.float32).astype(jnp.bfloat16),
        "tensor",
        scatter_dimension=0,
        tiled=True,
    )
    inputs = lax.all_to_all(own_rows, "dp", split_axis=0, concat_axis=1, tiled=True).reshape(
        seq_here, step_count, model_width
    )
    widened = inputs.astype(jnp.float32)
    normed = (
        widened
        * lax.rsqrt(jnp.mean(widened * widened, axis=-1, keepdims=True) + norm_epsilon)
        * norm_gain.astype(jnp.float32)
    ).astype(jnp.bfloat16)
    bias_row = jnp.concatenate([q_bias, k_bias, v_bias]).astype(jnp.float32)
    full_q, full_k, full_v, full_o = (
        lax.all_gather(q_weight, "dp", axis=0, tiled=True),
        lax.all_gather(k_weight, "dp", axis=0, tiled=True),
        lax.all_gather(v_weight, "dp", axis=0, tiled=True),
        lax.all_gather(o_weight, "dp", axis=1, tiled=True),
    )
    step_spans = [(first_step, 1) for first_step in range(step_count)]
    key_parts = []
    value_parts = []
    hidden_parts = []
    for first_step, step_span in step_spans:
        row_count = seq_here * step_span
        flat_rows = normed[:, first_step : first_step + step_span].reshape(row_count, model_width)
        row_piece = lax.all_gather(flat_rows, "tensor", axis=0, tiled=True)
        joined = jnp.concatenate(
            [
                jnp.dot(row_piece, full_q, preferred_element_type=jnp.float32),
                jnp.dot(row_piece, full_k, preferred_element_type=jnp.float32),
                jnp.dot(row_piece, full_v, preferred_element_type=jnp.float32),
            ],
            axis=1,
        )
        joined = (joined + bias_row).astype(jnp.bfloat16)
        queries, fresh_keys, fresh_values = (
            lax.all_to_all(joined[:, :q_cols], "tensor", split_axis=0, concat_axis=1, tiled=True),
            lax.all_to_all(
                joined[:, q_cols : q_cols + k_cols],
                "tensor",
                split_axis=0,
                concat_axis=1,
                tiled=True,
            ),
            lax.all_to_all(
                joined[:, q_cols + k_cols :], "tensor", split_axis=0, concat_axis=1, tiled=True
            ),
        )
        positions = lengths[:, None] + first_step + jnp.arange(step_span, dtype=jnp.int32)[None, :]
        rotated = rotate(
            queries.reshape(seq_here, step_span, -1, HD).astype(jnp.float32), positions
        ).astype(jnp.bfloat16)
        rotated_keys = rotate(
            fresh_keys.reshape(seq_here, step_span, -1, HD).astype(jnp.float32), positions
        ).astype(jnp.bfloat16)
        key_parts.append(rotated_keys)
        value_parts.append(fresh_values.reshape(seq_here, step_span, -1, HD))
        attended = attend(
            rotated,
            jnp.concatenate(key_parts, axis=1),
            jnp.concatenate(value_parts, axis=1),
            key_cache,
            value_cache,
            lengths,
            first_step,
        )
        gathered = lax.all_to_all(
            attended.reshape(row_count, -1), "tensor", split_axis=1, concat_axis=0, tiled=True
        )
        branch = lax.psum_scatter(
            jnp.dot(gathered, full_o, preferred_element_type=jnp.float32).astype(jnp.bfloat16),
            "tensor",
            scatter_dimension=0,
            tiled=True,
        ).astype(jnp.float32)
        residual = (
            inputs[:, first_step : first_step + step_span]
            .reshape(row_count, model_width)
            .astype(jnp.float32)
        )
        hidden_parts.append(
            (residual + branch).astype(jnp.bfloat16).reshape(seq_here, step_span, model_width)
        )
    hidden = jnp.concatenate(hidden_parts, axis=1)
    new_keys = jnp.concatenate(key_parts, axis=1).reshape(seq_here, step_count, -1)
    new_values = jnp.concatenate(value_parts, axis=1).reshape(seq_here, step_count, -1)
    return (hidden, new_keys, new_values)


def solution(mesh):
    placed = (
        P(("dp", "tensor"), None),
        P(("dp", "tensor")),
        P("tensor", "dp"),
        P(),
        P("dp", "tensor"),
        P("dp", "tensor"),
        P("dp", "tensor"),
        P("tensor"),
        P("tensor"),
        P("tensor"),
        P("tensor", "dp"),
        P(("dp", "tensor"), None, None),
        P(("dp", "tensor"), None, None),
    )
    return jax.shard_map(
        per_device,
        mesh=mesh,
        in_specs=placed,
        out_specs=(
            P(("dp", "tensor"), None, None),
            P(("dp", "tensor"), None, None),
            P(("dp", "tensor"), None, None),
        ),
        check_vma=False,
    )
```

profile of v0, /device:TPU:0, one launch (start us, length us, event | category | flops | bytes accessed | tf_op | source)
XLA Modules:
  0.0 1145.6 jit_solution(17424322273596815426)
XLA Ops:
  8.0 179.8 %all-gather.4 = s32[128,4,4]{2,1,0:T(4,128)S(1)} all-gather(s32[1,4,4]{2,1,0:T(4,128)} %bitcast.431), channel_id=1, replica_groups=mesh['dp'=8,'tensor'=16] {'dp','tensor'}, dimensions={0}, use_global_device_ids=true | all-gather | bytes 8256 | tf_op jit(solution)/shard_map/all_gather | solution.py:94
  188.8 16.0 %gather_fusion = bf16[2048,1024]{1,0:T(8,128)(2,1)} fusion(bf16[4752,1024]{1,0:T(8,128)(2,1)} %param.15, s32[2048]{0:T(1024)S(1)} %broadcast_clamp_fusion), kind=kCustom, calls=%fused_computation | custom fusion | bytes 8396800 | tf_op jit(solution)/shard_map/jit(_take)/gather | solution.py:103
  204.8 3.9 select_select_fusion
  208.7 74.2 %reduce-scatter.2.cloned.1.call-done = bf16[128,1024]{1,0:T(8,128)(2,1)} async-done(((bf16[2048,1024]{1,0:T(8,128)(2,1)}), bf16[128,1024]{1,0:T(8,128)(2,1)}) %reduce-scatter.2.cloned.1.call-update) | async-done | bytes 262160 | tf_op jit(solution)/shard_map/reduce_scatter | solution.py:105
  282.9 4.4 all-to-all-start
  288.0 6.3 all-to-all-done
  300.7 27.9 %all-gather.18.cloned.1.call-done = bf16[8192,64]{0,1:T(8,128)(2,1)} async-done(((bf16[1024,64]{0,1:T(8,128)(2,1)}), bf16[8192,64]{0,1:T(8,128)(2,1)}) %all-gather.18.cloned.1.call-update) | async-done | bytes 1048592 | tf_op jit(solution)/shard_map/all_gather | solution.py:124
  328.6 51.0 %all-gather.22.cloned.1.call-done = bf16[64,1,8192]{2,1,0:T(2,128)(2,1)} async-done(((bf16[4,1,8192]{2,1,0:T(2,128)(2,1)}), bf16[64,1,8192]{2,1,0:T(2,128)(2,1)}) %all-gather.22.cloned.1.call-update) | async-done | bytes 1048592 | tf_op jit(solution)/shard_map/all_gather | solution.py:134
  379.6 3.2 fusion.117
  382.8 36.3 %all-gather.16.cloned.1.call-done = bf16[8192,64]{0,1:T(8,128)(2,1)} async-done(((bf16[1024,64]{0,1:T(8,128)(2,1)}), bf16[8192,64]{0,1:T(8,128)(2,1)}) %all-gather.16.cloned.1.call-update) | async-done | bytes 1048592 | tf_op jit(solution)/shard_map/all_gather | solution.py:123
  419.1 3.3 fusion.119
  422.4 47.5 %all-gather.24.cloned.1.call-done = bf16[64,1,8192]{2,1,0:T(2,128)(2,1)} async-done(((bf16[4,1,8192]{2,1,0:T(2,128)(2,1)}), bf16[64,1,8192]{2,1,0:T(2,128)(2,1)}) %all-gather.24.cloned.1.call-update) | async-done | bytes 1048592 | tf_op jit(solution)/shard_map/all_gather | solution.py:134
  469.9 2.9 fusion.111
  472.8 2.9 fusion.113
  475.8 44.0 %all-gather.26.cloned.1.call-done = bf16[64,1,8192]{2,1,0:T(2,128)(2,1)} async-done(((bf16[4,1,8192]{2,1,0:T(2,128)(2,1)}), bf16[64,1,8192]{2,1,0:T(2,128)(2,1)}) %all-gather.26.cloned.1.call-update) | async-done | bytes 1048592 | tf_op jit(solution)/shard_map/all_gather | solution.py:134
  519.7 3.2 fusion.105
  522.9 3.2 fusion.107
  526.1 43.5 %all-gather.28.cloned.1.call-done = bf16[64,1,8192]{2,1,0:T(2,128)(2,1)} async-done(((bf16[4,1,8192]{2,1,0:T(2,128)(2,1)}), bf16[64,1,8192]{2,1,0:T(2,128)(2,1)}) %all-gather.28.cloned.1.call-update) | async-done | bytes 1048592 | tf_op jit(solution)/shard_map/all_gather | solution.py:134
  569.6 3.2 fusion.99
  572.8 3.2 fusion.101
  576.0 162.3 %all-gather.14.cloned.1.call-done = bf16[8192,512]{1,0:T(8,128)(2,1)} async-done(((bf16[1024,512]{1,0:T(8,128)(2,1)}), bf16[8192,512]{1,0:T(8,128)(2,1)}) %all-gather.14.cloned.1.call-update) | async-done | bytes 8388624 | tf_op jit(solution)/shard_map/all_gather | solution.py:122
  738.3 5.5 fusion.121
  744.6 1.8 fusion.115
  746.5 1.8 fusion.109
  748.3 1.8 fusion.103
  751.0 6.7 all-to-all-start.15
  758.5 11.1 all-to-all-done.15
  769.6 4.4 all-to-all-start.11
  774.7 6.7 all-to-all-done.11
  781.4 3.5 all-to-all-start.3
  785.6 6.9 all-to-all-done.3
  792.5 3.5 all-to-all-start.14
  801.5 1.9 all-to-all-done.14
  803.4 5.3 all-to-all-start.10
  808.8 7.4 all-to-all-done.10
  816.2 3.5 all-to-all-start.6
  819.7 7.3 all-to-all-done.6
  827.1 3.5 all-to-all-start.7
  830.7 7.5 all-to-all-done.7
  838.1 3.5 all-to-all-start.2
  842.6 6.5 all-to-all-done.2
  849.1 3.5 all-to-all-start.13
  854.0 6.4 all-to-all-done.13
  860.4 3.5 all-to-all-start.5
  863.9 7.6 all-to-all-done.5
  871.5 3.5 all-to-all-start.9
  875.0 7.6 all-to-all-done.9
  882.5 3.9 all-to-all-start.1
  886.7 7.4 all-to-all-done.1
  894.9 3.9 fusion.33
  906.0 4.0 all-to-all-start.16
  910.9 3.3 fusion.90
  917.6 5.4 all-to-all-start.12
  923.8 6.9 all-to-all-done.12
  930.7 3.5 all-to-all-start.8
  934.2 3.1 fusion.84
  938.0 3.7 all-to-all-done.8
  941.8 3.5 all-to-all-start.4
  945.6 7.2 all-to-all-done.4
  952.9 6.1 convolution_convert_fusion
  959.0 2.6 convolution_convert_fusion.1
  961.6 2.6 convolution_convert_fusion.2
  964.2 2.6 convolution_convert_fusion.3
  971.0 163.5 %all-reduce.7.cloned.1.call-done = (bf16[64,8192]{1,0:T(8,128)(2,1)}, bf16[64,8192]{1,0:T(8,128)(2,1)}, bf16[64,8192]{1,0:T(8,128)(2,1)}, bf16[64,8192]{1,0:T(8,128)(2,1)}) async-done(((bf16[64,8192]{1,0:T(8,128)(2,1)}, bf16[64,8192]{1,0:T(8,128)(2,1)}, bf16[64,8192]{1,0:T(8,128)(2,1)}, bf16[64,8192]{1,0:T(8,128)(2,1)}), (bf16[64,8192]{1,0:T(8,128)(2,1)}, bf16[64,8192]{1,0:T(8,128)(2,1)}, ...) | async-done | bytes 4194320
  (216 shorter events, 40.9 us)
Async XLA Ops:
  8.0 274.9 %reduce-scatter.2.cloned.1.call-start = ((), (), s32[]{:S(2)}) async-start(), calls=%async_computation.18 | async-start | bytes 4456448 | tf_op jit(solution)/shard_map/reduce_scatter | solution.py:105
  208.7 79.3 %copy-start.7 = (bf16[8192]{0:T(1024)(128)(2,1)S(1)}, bf16[8192]{0:T(1024)(128)(2,1)}, u32[]{:S(2)}) copy-start(bf16[8192]{0:T(1024)(128)(2,1)} %param.16) | copy-start | bytes 49156
  208.7 91.6 %copy-start.8 = (s32[4]{0:T(128)S(1)}, s32[4]{0:T(128)}, u32[]{:S(2)}) copy-start(s32[4]{0:T(128)} %param.14) | copy-start | bytes 52
  208.7 91.7 %copy-start.9 = (bf16[512]{0:T(512)(128)(2,1)S(1)}, bf16[512]{0:T(512)(128)(2,1)}, u32[]{:S(2)}) copy-start(bf16[512]{0:T(512)(128)(2,1)} %param.20) | copy-start | bytes 3076
  208.7 91.7 %copy-start.10 = (bf16[64]{0:T(256)(128)(2,1)S(1)}, bf16[64]{0:T(256)(128)(2,1)}, u32[]{:S(2)}) copy-start(bf16[64]{0:T(256)(128)(2,1)} %param.22) | copy-start | bytes 388
  208.7 91.7 %copy-start.11 = (bf16[64]{0:T(256)(128)(2,1)S(1)}, bf16[64]{0:T(256)(128)(2,1)}, u32[]{:S(2)}) copy-start(bf16[64]{0:T(256)(128)(2,1)} %param.21) | copy-start | bytes 388
  282.9 11.3 all-to-all-start
  287.3 41.3 %all-gather.18.cloned.1.call-start = ((), (), s32[]{:S(2)}) async-start(), calls=%async_computation.21 | async-start | bytes 1179648 | tf_op jit(solution)/shard_map/all_gather | solution.py:124
  287.9 91.7 %all-gather.22.cloned.1.call-start = ((), (), s32[]{:S(2)}) async-start(), calls=%async_computation.23 | async-start | bytes 2228224 | tf_op jit(solution)/shard_map/all_gather | solution.py:134
  296.3 122.8 %all-gather.16.cloned.1.call-start = ((), (), s32[]{:S(2)}) async-start(), calls=%async_computation.20 | async-start | bytes 1179648 | tf_op jit(solution)/shard_map/all_gather | solution.py:123
  296.9 173.0 %all-gather.24.cloned.1.call-start = ((), (), s32[]{:S(2)}) async-start(), calls=%async_computation.24 | async-start | bytes 2228224 | tf_op jit(solution)/shard_map/all_gather | solution.py:134
  297.6 222.1 %all-gather.26.cloned.1.call-start = ((), (), s32[]{:S(2)}) async-start(), calls=%async_computation.25 | async-start | bytes 2228224 | tf_op jit(solution)/shard_map/all_gather | solution.py:134
  298.4 271.2 %all-gather.28.cloned.1.call-start = ((), (), s32[]{:S(2)}) async-start(), calls=%async_computation.26 | async-start | bytes 2228224 | tf_op jit(solution)/shard_map/all_gather | solution.py:134
  299.1 439.1 %all-gather.14.cloned.1.call-start = ((), (), s32[]{:S(2)}) async-start(), calls=%async_computation.19 | async-start | bytes 9437184 | tf_op jit(solution)/shard_map/all_gather | solution.py:122
  299.7 653.2 %all-gather.20.cloned.1.call-start = ((), (), s32[]{:S(2)}) async-start(), calls=%async_computation.22 | async-start | bytes 9437184 | tf_op jit(solution)/shard_map/all_gather | solution.py:125
  328.6 141.3 %copy-start.14 = (bf16[8192,64]{0,1:T(8,128)(2,1)S(1)}, bf16[8192,64]{0,1:T(8,128)(2,1)}, u32[]{:S(2)}) copy-start(bf16[8192,64]{0,1:T(8,128)(2,1)} %all-gather.18.cloned.1.call-done) | copy-start | bytes 3145732
  419.1 53.7 %copy-start.15 = (bf16[8192,64]{0,1:T(8,128)(2,1)S(1)}, bf16[8192,64]{0,1:T(8,128)(2,1)}, u32[]{:S(2)}) copy-start(bf16[8192,64]{0,1:T(8,128)(2,1)} %all-gather.16.cloned.1.call-done) | copy-start | bytes 3145732
  475.7 262.5 %copy-start.3 = (bf16[64,1,8192]{2,1,0:T(2,128)(2,1)S(1)}, bf16[64,1,8192]{2,1,0:T(2,128)(2,1)}, u32[]{:S(2)}) copy-start(bf16[64,1,8192]{2,1,0:T(2,128)(2,1)} %all-gather.22.cloned.1.call-done) | copy-start | bytes 3145732
  738.3 5.8 copy-start
  738.3 6.4 copy-start.4
  744.6 1.8 copy-start.5
  746.5 1.8 copy-start.6
  751.0 18.6 %all-to-all-start.15 = ((bf16[16,2,128]{2,1,0:T(2,128)(2,1)}), bf16[16,2,128]{2,1,0:T(2,128)(2,1)S(1)}, u32[]{:S(2)}, u32[]{:S(2)}) async-start(bf16[16,2,128]{2,1,0:T(2,128)(2,1)} %reshape.1255), calls=%async_computation.16 | async-start | bytes 16384 | tf_op jit(solution)/shard_map/all_to_all | solution.py:153
  769.6 11.8 %all-to-all-start.11 = ((bf16[16,2,128]{2,1,0:T(2,128)(2,1)}), bf16[16,2,128]{2,1,0:T(2,128)(2,1)S(1)}, u32[]{:S(2)}, u32[]{:S(2)}) async-start(bf16[16,2,128]{2,1,0:T(2,128)(2,1)} %reshape.1257), calls=%async_computation.12 | async-start | bytes 16384 | tf_op jit(solution)/shard_map/all_to_all | solution.py:153
  781.4 11.0 all-to-all-start.3
  792.5 10.9 all-to-all-start.14
  803.4 12.8 %all-to-all-start.10 = ((bf16[16,2,128]{2,1,0:T(2,128)(2,1)}), bf16[16,2,128]{2,1,0:T(2,128)(2,1)S(1)}, u32[]{:S(2)}, u32[]{:S(2)}) async-start(bf16[16,2,128]{2,1,0:T(2,128)(2,1)} %reshape.1265), calls=%async_computation.11 | async-start | bytes 16384 | tf_op jit(solution)/shard_map/all_to_all | solution.py:146
  816.2 10.9 all-to-all-start.6
  827.1 11.0 all-to-all-start.7
  838.1 11.0 all-to-all-start.2
  849.1 11.3 all-to-all-start.13
  860.4 11.1 all-to-all-start.5
  871.5 11.1 all-to-all-start.9
  882.5 11.5 %all-to-all-start.1 = ((bf16[16,4,512]{2,1,0:T(4,128)(2,1)}), bf16[16,4,512]{2,1,0:T(4,128)(2,1)S(1)}, u32[]{:S(2)}, u32[]{:S(2)}) async-start(bf16[16,4,512]{2,1,0:T(4,128)(2,1)} %all_to_all.191), calls=%async_computation.2 | async-start | bytes 131072 | tf_op jit(solution)/shard_map/all_to_all | solution.py:145
  894.1 4.6 copy-start.2
  901.2 3.2 copy-start.12
  906.0 11.6 %all-to-all-start.16 = ((bf16[4,16,512]{2,0,1:T(4,128)(2,1)}), bf16[4,16,512]{2,0,1:T(4,128)(2,1)S(1)}, u32[]{:S(2)}, u32[]{:S(2)}) async-start(bf16[4,16,512]{2,0,1:T(4,128)(2,1)} %copy.227), calls=%async_computation.17 | async-start | bytes 131072 | tf_op jit(solution)/shard_map/all_to_all | solution.py:175
  910.0 4.2 copy-start.13
  917.6 13.0 %all-to-all-start.12 = ((bf16[4,16,512]{2,0,1:T(4,128)(2,1)}), bf16[4,16,512]{2,0,1:T(4,128)(2,1)S(1)}, u32[]{:S(2)}, u32[]{:S(2)}) async-start(bf16[4,16,512]{2,0,1:T(4,128)(2,1)} %copy.217), calls=%async_computation.13 | async-start | bytes 131072 | tf_op jit(solution)/shard_map/all_to_all | solution.py:175
  930.7 11.1 all-to-all-start.8
  941.8 11.1 all-to-all-start.4
  945.3 189.2 %all-reduce.7.cloned.1.call-start = ((), (), s32[]{:S(2)}) async-start(), calls=%async_computation.27 | async-start | bytes 8388608
  952.9 6.1 copy-start.1
  966.8 0.7 copy-start.16
Sparse Core Ops, SparseCore 0:
  208.8 74.0 reduce-scatter.1
  966.9 167.4 all-reduce.6
Sparse Core Ops, SparseCore 1:
  289.5 39.0 all-gather.17
  331.8 47.8 all-gather.21
  381.3 37.8 all-gather.15
  421.9 47.9 all-gather.23
  472.7 47.0 all-gather.25
  522.5 47.0 all-gather.27
  571.2 167.0 all-gather.13
  739.9 177.1 all-gather.19
where the time goes:
time: 1150 us
  waiting for transfers between devices  764 us (66%)
  blocking collectives  180 us (16%)
  starting transfers between devices  70.1 us (6%)
  matrix products  67.7 us (6%)
  local copies, waits for them, and re-layouts  36.2 us (3%)
  between operations  17.4 us (2%)
    all_gather x4, waiting for transfers between devices, per_device(): row_piece = lax.all_gather(flat_rows, 'tensor', axis=0, tiled=True)  186 us
    all_gather x1, blocking collectives, per_device(): every_id = lax.all_gather(token_ids, ('dp', 'tensor'), axis=0, tiled=True)  180 us
    unnamed x11, waiting for transfers between devices  167 us
    all_gather x1, waiting for transfers between devices, per_device(): lax.all_gather(q_weight, 'dp', axis=0, tiled=True)  162 us
    reduce_scatter x1, waiting for transfers between devices, per_device(): lax.psum_scatter(masked_rows.astype(jnp.float32).astype(jnp.bfloat16), 't...  74.2 us
    all_gather x1, waiting for transfers between devices, per_device(): lax.all_gather(k_weight, 'dp', axis=0, tiled=True)  36.3 us
    all_to_all x4, waiting for transfers between devices, per_device(): lax.all_to_all(joined[:, q_cols + k_cols:], 'tensor', split_axis=0, conca...  32.2 us
    all_to_all x4, waiting for transfers between devices, per_device(): lax.all_to_all(joined[:, :q_cols], 'tensor', split_axis=0, concat_axis=1,...  28.9 us
  transfers between devices with their start and end apart: 27, of which 26 were waited for; matrix products, arithmetic and copies ran while one was open for 6% of the time, Pallas kernels for 0%

commit v1 on v0

v1 whole, which is shorter than its diff:
```python
import jax
import jax.numpy as jnp
from jax import lax
from jax.sharding import Mesh
from jax.sharding import PartitionSpec as P

HD = 128
ROUND_ROWS = 128

norm_epsilon = 1e-06
rope_base = 1000000.0
masked_low = -1e30

DP = ("y", "zl")
CHIPS = ("zh", "x")
PLANE = ("y", "zl", "zh", "x")
EVERY = ("y", "zl", "zh", "x", "core")


def rotate(features, positions):
    head_width = features.shape[-1]
    half_width = head_width // 2
    frequency = rope_base ** (-(2.0 * jnp.arange(half_width, dtype=jnp.float32)) / head_width)
    angles = positions.astype(jnp.float32)[..., None, None] * frequency
    cosine = jnp.cos(angles)
    sine_part = jnp.sin(angles)
    leading = features[..., :half_width]
    trailing = features[..., half_width:]
    return jnp.concatenate(
        [leading * cosine - trailing * sine_part, trailing * cosine + leading * sine_part], axis=-1
    )


def attend(rotated, fresh_keys, fresh_values, key_cache, value_cache, lengths):
    seq_here, step_span, heads, head_width = rotated.shape
    kv_heads = fresh_keys.shape[2]
    group_size = heads // kv_heads
    cache_len = key_cache.shape[1]
    cache_keys = key_cache.reshape(seq_here, cache_len, kv_heads, head_width)
    cache_values = value_cache.reshape(seq_here, cache_len, kv_heads, head_width)
    grouped = rotated.reshape(seq_here, step_span, kv_heads, group_size, head_width)
    score_scale = head_width ** (-0.5)
    cached = (
        jnp.einsum("skgrd,sjgd->skgrj", grouped, cache_keys, preferred_element_type=jnp.float32)
        * score_scale
    )
    fresh_scores = (
        jnp.einsum("skgrd,sjgd->skgrj", grouped, fresh_keys, preferred_element_type=jnp.float32)
        * score_scale
    )
    cache_valid = (jnp.arange(cache_len, dtype=jnp.int32)[None, :] < lengths[:, None])[
        :, None, None, None, :
    ]
    fresh_count = fresh_keys.shape[1]
    fresh_valid = (
        jnp.arange(fresh_count, dtype=jnp.int32)[None, :]
        <= jnp.arange(step_span, dtype=jnp.int32)[:, None]
    )[None, :, None, None, :]
    row_top = jnp.maximum(
        jnp.max(jnp.where(cache_valid, cached, masked_low), axis=-1),
        jnp.max(jnp.where(fresh_valid, fresh_scores, masked_low), axis=-1),
    )[..., None]
    cache_exp = jnp.exp(jnp.where(cache_valid, cached - row_top, masked_low))
    fresh_exp = jnp.exp(jnp.where(fresh_valid, fresh_scores - row_top, masked_low))
    denominator = jnp.sum(cache_exp, axis=-1, keepdims=True) + jnp.sum(
        fresh_exp, axis=-1, keepdims=True
    )
    cache_weights = (cache_exp / denominator).astype(jnp.bfloat16)
    fresh_weights = (fresh_exp / denominator).astype(jnp.bfloat16)
    attended = jnp.einsum(
        "skgrj,sjgd->skgrd", cache_weights, cache_values, preferred_element_type=jnp.float32
    )
    attended = attended + jnp.einsum(
        "skgrj,sjgd->skgrd", fresh_weights, fresh_values, preferred_element_type=jnp.float32
    )
    return attended.reshape(seq_here, step_span, heads * head_width).astype(jnp.bfloat16)


def swap_cores(value):
    return lax.ppermute(value, "core", [(0, 1), (1, 0)])


def per_device(
    token_ids,
    lengths,
    embedding,
    norm_gain,
    q_weight,
    k_weight,
    v_weight,
    q_bias,
    k_bias,
    v_bias,
    o_weight,
    key_cache,
    value_cache,
):
    seq_here, step_count = token_ids.shape
    rows_here = seq_here * step_count
    vocab_here, width_here = embedding.shape
    replicas = lax.axis_size(DP)
    chips = lax.axis_size(CHIPS)
    chip = lax.axis_index(CHIPS)
    core = lax.axis_index("core")
    replica = lax.axis_index(DP)
    parties = replicas * chips
    plane_rows = parties * rows_here

    sent_ids = jnp.broadcast_to(token_ids.reshape(1, rows_here), (parties * 2, rows_here))
    every_id = lax.all_to_all(sent_ids, EVERY, split_axis=0, concat_axis=0, tiled=True)
    plane_ids = every_id.reshape(parties, 2, rows_here).transpose(1, 0, 2).reshape(2, plane_rows)
    holder = plane_ids // (2 * vocab_here)
    place = jnp.arange(plane_rows, dtype=jnp.int32)
    same = plane_ids[:, :, None] == plane_ids[:, None, :]
    leader = jnp.min(jnp.where(same, place[None, None, :], plane_rows), axis=2)
    leads = leader == place[None, :]
    before = (
        leads[:, None, :]
        & (holder[:, :, None] == holder[:, None, :])
        & (place[None, None, :] < leader[:, :, None])
    )
    rank = jnp.sum(before.astype(jnp.int32), axis=2)
    rounds = jnp.max(rank) // ROUND_ROWS + 1
    own_holder = jnp.where(core == 0, holder[0], holder[1])
    own_rank = jnp.where(core == 0, rank[0], rank[1])
    listed_here = leads & (holder == chip)

    def exchange(turn):
        first = turn * ROUND_ROWS
        wanted = listed_here[:, None, :] & (
            rank[:, None, :] == first + jnp.arange(ROUND_ROWS, dtype=jnp.int32)[None, :, None]
        )
        listed = jnp.max(jnp.where(wanted, plane_ids[:, None, :], -1), axis=2)
        offset = listed - (2 * chip + core) * vocab_here
        inside = (listed >= 0) & (offset >= 0) & (offset < vocab_here)
        picked = jnp.take(
            embedding, jnp.clip(offset, 0, vocab_here - 1).reshape(-1), axis=0
        ).reshape(2, ROUND_ROWS, width_here)
        picked = jnp.where(inside[:, :, None], picked, jnp.zeros_like(picked))
        mine = jnp.where(core == 0, picked[0], picked[1])
        theirs = jnp.where(core == 0, picked[1], picked[0])
        merged = mine + swap_cores(theirs)
        table = lax.all_to_all(
            jnp.broadcast_to(merged[None], (chips, ROUND_ROWS, width_here)),
            CHIPS,
            split_axis=0,
            concat_axis=0,
            tiled=True,
        ).reshape(chips * ROUND_ROWS, width_here)
        here = (own_rank >= first) & (own_rank < first + ROUND_ROWS)
        slot = jnp.where(here, own_holder * ROUND_ROWS + own_rank - first, -1)
        chosen = (
            slot[:, None] == jnp.arange(chips * ROUND_ROWS, dtype=jnp.int32)[None, :]
        ).astype(jnp.bfloat16)
        return jnp.dot(chosen, table, preferred_element_type=jnp.float32).astype(jnp.bfloat16)

    plane_inputs = lax.fori_loop(
        1, rounds, lambda turn, sofar: sofar + exchange(turn), exchange(0)
    )

    both = jnp.concatenate([q_weight, k_weight, v_weight], axis=1)
    other = swap_cores(both)
    low = jnp.where(core == 0, both, other)
    high = jnp.where(core == 0, other, both)
    q_cols = q_weight.shape[1]
    k_cols = k_weight.shape[1]
    q_end, k_end = q_cols, q_cols + k_cols
    pair_weight = jnp.concatenate(
        [
            low[:, :q_end],
            high[:, :q_end],
            low[:, q_end:k_end],
            high[:, q_end:k_end],
            low[:, k_end:],
            high[:, k_end:],
        ],
        axis=1,
    )
    own_bias = jnp.concatenate([q_bias, k_bias, v_bias])
    every_bias = lax.all_gather(own_bias, CHIPS + ("core",), axis=0, tiled=False)
    every_bias = every_bias.reshape(chips, 2, -1).astype(jnp.float32)
    pair_bias = jnp.concatenate(
        [
            every_bias[:, :, :q_end].reshape(chips, -1),
            every_bias[:, :, q_end:k_end].reshape(chips, -1),
            every_bias[:, :, k_end:].reshape(chips, -1),
        ],
        axis=1,
    )
    own_gain = lax.dynamic_slice_in_dim(norm_gain, replica * width_here, width_here)

    gained = (plane_inputs.astype(jnp.float32) * own_gain.astype(jnp.float32)).astype(jnp.bfloat16)
    partial = jnp.dot(gained, pair_weight, preferred_element_type=jnp.float32).astype(jnp.bfloat16)
    strip = width_here // chips
    shown = lax.dynamic_slice_in_dim(plane_inputs, chip * strip, strip, axis=1)
    payload = jnp.concatenate([partial, shown], axis=1)
    arrived = lax.all_to_all(payload, PLANE, split_axis=0, concat_axis=0, tiled=True)
    pair_cols = pair_weight.shape[1]
    arrived = arrived.reshape(replicas, chips, rows_here, pair_cols + strip)
    inputs = (
        arrived[..., pair_cols:].transpose(2, 0, 1, 3).reshape(rows_here, -1).astype(jnp.float32)
    )
    scale = lax.rsqrt(jnp.mean(inputs * inputs, axis=-1, keepdims=True) + norm_epsilon)
    summed = jnp.sum(arrived[..., :pair_cols].astype(jnp.float32), axis=0)
    joined = (summed * scale[None] + pair_bias[:, None, :]).astype(jnp.bfloat16)
    joined = joined.transpose(1, 0, 2)
    group = 2 * q_cols
    queries = joined[..., :group].reshape(seq_here, step_count, -1, HD)
    fresh_keys = joined[..., group : group + 2 * k_cols].reshape(seq_here, step_count, -1, HD)
    fresh_values = joined[..., group + 2 * k_cols :].reshape(seq_here, step_count, -1, HD)
    positions = lengths[:, None] + jnp.arange(step_count, dtype=jnp.int32)[None, :]
    rotated = rotate(queries.astype(jnp.float32), positions).astype(jnp.bfloat16)
    new_keys = rotate(fresh_keys.astype(jnp.float32), positions).astype(jnp.bfloat16)
    attended = attend(rotated, new_keys, fresh_values, key_cache, value_cache, lengths)

    full_o = lax.all_gather(o_weight, DP, axis=0, tiled=False)
    other_o = swap_cores(full_o)
    gathered = lax.all_to_all(
        attended.reshape(rows_here, chips, 2 * q_cols).transpose(1, 0, 2),
        CHIPS,
        split_axis=0,
        concat_axis=0,
        tiled=True,
    ).reshape(chips * rows_here, 2 * q_cols)
    own_part = jnp.where(core == 0, gathered[:, :q_cols], gathered[:, q_cols:])
    other_part = jnp.where(core == 0, gathered[:, q_cols:], gathered[:, :q_cols])
    branch = jnp.concatenate(
        [
            (
                jnp.dot(own_part, full_o[block], preferred_element_type=jnp.float32)
                + jnp.dot(other_part, other_o[block], preferred_element_type=jnp.float32)
            ).astype(jnp.bfloat16)
            for block in range(replicas)
        ],
        axis=1,
    )
    branches = lax.all_to_all(branch, CHIPS, split_axis=0, concat_axis=0, tiled=True)
    branches = branches.reshape(chips, rows_here, -1).astype(jnp.float32)
    hidden = (inputs + jnp.sum(branches, axis=0)).astype(jnp.bfloat16)
    return (
        hidden.reshape(seq_here, step_count, -1),
        new_keys.reshape(seq_here, step_count, -1),
        fresh_values.reshape(seq_here, step_count, -1),
    )


def solution(mesh):
    fine = Mesh(mesh.devices.reshape(4, 2, 2, 4, 2), EVERY)
    tensor = CHIPS + ("core",)
    placed = (
        P(EVERY, None),
        P(EVERY),
        P(tensor, DP),
        P(),
        P(DP, tensor),
        P(DP, tensor),
        P(DP, tensor),
        P(tensor),
        P(tensor),
        P(tensor),
        P(tensor, DP),
        P(EVERY, None, None),
        P(EVERY, None, None),
    )
    return jax.shard_map(
        per_device,
        mesh=fine,
        in_specs=placed,
        out_specs=(
            P(EVERY, None, None),
            P(EVERY, None, None),
            P(EVERY, None, None),
        ),
        check_vma=False,
    )
```

time: 1150 us -> 371 us (0.32)
  waiting for transfers between devices: 764 us -> 163 us
  blocking collectives: 180 us -> 65.2 us
  starting transfers between devices: 70.1 us -> 29.7 us
  matrix products: 67.7 us -> 42.4 us
    all_gather x8 -> x1, waiting for transfers between devices: 412 us -> 93.7 us  [per_device(): full_o = lax.all_gather(o_weight, DP, axis=0, tiled=False)]
    unnamed x11 -> x1, waiting for transfers between devices: 167 us -> 0.02 us
    all_gather x1, blocking collectives: 180 us -> 49.6 us  [per_device(): lax.all_gather(own_bias, CHIPS + ('core',), axis=0, tiled=False)]
    reduce_scatter x1 -> x0, waiting for transfers between devices: 74.2 us -> none  [per_device(): lax.psum_scatter(masked_rows.astype(jnp.float32).astype(jnp.bfloat16), 't...]
    all_to_all x17 -> x4, waiting for transfers between devices: 110 us -> 68.6 us  [the longest x1 32.5 us: exchange(): lax.all_to_all(jnp.broadcast_to(merged[None], (chips, ROUND_ROWS, width_h...]
    all_to_all x17 -> x4, starting transfers between devices: 68.9 us -> 29.2 us  [the longest x1 11.1 us: per_device(): lax.all_to_all(sent_ids, EVERY, split_axis=0, concat_axis=0, tiled=True)]
    all_to_all x0 -> x1, blocking collectives: none -> 15.6 us  [per_device(): lax.all_to_all(attended.reshape(rows_here, chips, 2 * q_cols).transpose(1...]
    dot_general x16 -> x18, matrix products: 50 us -> 35.2 us  [the longest x8 12.3 us: per_device(): jnp.dot(other_part, other_o[block], preferred_element_type=jnp.float32)]
  transfers between devices with their start and end apart: 27 -> 8, of which waited for: 26 -> 5; matrix products, arithmetic and copies ran while one was open for 6% -> 16% of each run, Pallas kernels for 0% -> 0%
where the time goes in v1:
time: 371 us; the launch traced here: 366 us
  waiting for transfers between devices  163 us (44%)
  blocking collectives  65.2 us (18%)
  matrix products  42.4 us (11%)
  local copies, waits for them, and re-layouts  30.1 us (8%)
  starting transfers between devices  29.7 us (8%)
  other arithmetic  18.1 us (5%)
  between operations  17.3 us (5%)
    all_gather x1, waiting for transfers between devices, per_device(): full_o = lax.all_gather(o_weight, DP, axis=0, tiled=False)  93.7 us
    all_gather x1, blocking collectives, per_device(): lax.all_gather(own_bias, CHIPS + ('core',), axis=0, tiled=False)  49.6 us
    all_to_all x1, waiting for transfers between devices, exchange(): lax.all_to_all(jnp.broadcast_to(merged[None], (chips, ROUND_ROWS, width_h...  32.5 us
    all_to_all x1, waiting for transfers between devices, per_device(): lax.all_to_all(branch, CHIPS, split_axis=0, concat_axis=0, tiled=True)  26.8 us
    all_to_all x1, blocking collectives, per_device(): lax.all_to_all(attended.reshape(rows_here, chips, 2 * q_cols).transpose(1...  15.6 us
    dot_general x8, matrix products, per_device(): jnp.dot(other_part, other_o[block], preferred_element_type=jnp.float32)  12.3 us
    dot_general x8, matrix products, per_device(): jnp.dot(own_part, full_o[block], preferred_element_type=jnp.float32)  12.3 us
    all_to_all x1, starting transfers between devices, per_device(): lax.all_to_all(sent_ids, EVERY, split_axis=0, concat_axis=0, tiled=True)  11.1 us
  transfers between devices with their start and end apart: 8, of which 5 were waited for; matrix products, arithmetic and copies ran while one was open for 16% of the time, Pallas kernels for 0%

profile of v1, /device:TPU:0, one launch (start us, length us, event | category | flops | bytes accessed | tf_op | source)
XLA Modules:
  0.0 365.7 jit_solution(10159250669775926967)
XLA Ops:
  7.2 0.8 broadcast_in_dim.186
  7.9 0.7 broadcast_in_dim.187
  8.6 11.1 %all-to-all-start.1 = ((s32[128,1,16]{2,1,0:T(1,128)}), s32[128,1,16]{2,1,0:T(1,128)S(1)}, u32[]{:S(2)}, u32[]{:S(2)}) async-start(s32[128,1,16]{2,1,0:T(1,128)} %broadcast_in_dim.187), calls=%async_computation.1 | async-start | bytes 131072 | tf_op jit(solution)/shard_map/all_to_all | solution.py:110
  19.8 9.2 %all-to-all-done.1 = s32[128,1,16]{2,1,0:T(1,128)S(1)} async-done(((s32[128,1,16]{2,1,0:T(1,128)}), s32[128,1,16]{2,1,0:T(1,128)S(1)}, u32[]{:S(2)}, u32[]{:S(2)}) %all-to-all-start.1) | async-done | bytes 8224 | tf_op jit(solution)/shard_map/all_to_all | solution.py:110
  29.1 1.6 select_reduce_fusion.1
  30.7 2.7 convert_reduce_fusion
  33.5 0.3 select_reduce_fusion.2
  33.8 6.6 %gather_fusion.1 = bf16[256,1024]{1,0:T(8,128)(2,1)S(1)} fusion(bf16[4752,1024]{1,0:T(8,128)(2,1)} %param.17, s32[1024]{0:T(1024)S(1)} %pad_clamp_fusion.1), kind=kCustom, calls=%fused_computation.1 | custom fusion | bytes 1049600 | tf_op jit(solution)/shard_map/jit(_take)/gather | solution.py:136
  40.6 0.7 select_bitcast_fusion.1
  42.1 0.4 collective-permute-start.2
  42.5 0.7 collective-permute-done.1
  43.2 1.0 bitcast_add_fusion.1
  44.2 1.6 broadcast_in_dim.197
  45.8 4.4 %all-to-all-start.2 = ((bf16[8,128,1024]{2,1,0:T(8,128)(2,1)}), bf16[8,128,1024]{2,1,0:T(8,128)(2,1)}, u32[]{:S(2)}, u32[]{:S(2)}) async-start(bf16[8,128,1024]{2,1,0:T(8,128)(2,1)} %broadcast_in_dim.197), calls=%async_computation.2 | async-start | bytes 4194304 | tf_op jit(solution)/shard_map/all_to_all | solution.py:143
  50.2 0.7 dynamic-slice_convert_fusion
  51.0 0.6 reduce_max.48
  54.2 1.9 broadcast_select_fusion
  56.3 0.3 fusion.75
  56.6 4.0 %concatenate.31 = bf16[1024,1280]{1,0:T(8,128)(2,1)} concatenate(bf16[1024,512]{1,0:T(8,128)(2,1)S(1)} %slice.204, bf16[1024,512]{1,0:T(8,128)(2,1)S(1)} %slice.205, bf16[1024,64]{1,0:T(8,128)(2,1)S(1)} %get-tuple-element.250, bf16[1024,64]{1,0:T(8,128)(2,1)S(1)} %get-tuple-element.226, bf16[1024,64]{1,0:T(8,128)(2,1)S(1)} %get-tuple-element.251, ...), dimensions={1} | concatenate | bytes 5242880 | tf_op jit(solution)/shard_map/concatenate | solution.py:168
  60.5 32.5 %all-to-all-done.2 = bf16[8,128,1024]{2,1,0:T(8,128)(2,1)} async-done(((bf16[8,128,1024]{2,1,0:T(8,128)(2,1)}), bf16[8,128,1024]{2,1,0:T(8,128)(2,1)}, u32[]{:S(2)}, u32[]{:S(2)}) %all-to-all-start.2) | async-done | bytes 2097184 | tf_op jit(solution)/shard_map/all_to_all | solution.py:143
  93.1 5.3 %fusion.13 = bf16[1024,1024]{1,0:T(8,128)(2,1)} fusion(bf16[1024,1024]{1,0:T(8,128)(2,1)} %bitcast.15, s32[1024]{0:T(1024)S(1)} %add_select_fusion), kind=kOutput, calls=%fused_computation.43 | convolution fusion | flops 2149580800 | bytes 4198400 | tf_op jit(solution)/shard_map/dot_general | solution.py:155
  98.4 1.0 constant_dynamic-slice_fusion
  99.3 5.3 %convolution_convert_fusion = bf16[1024,1280]{1,0:T(8,128)(2,1)S(1)} fusion(bf16[1024,1280]{1,0:T(8,128)(2,1)} %concatenate.31, bf16[1024,1024]{1,0:T(8,128)(2,1)} %get-tuple-element.137, f32[1024]{0:T(1024)S(1)} %dynamic-slice_convert_fusion), kind=kOutput, calls=%fused_computation.33 | convolution fusion | flops 2688811008 | bytes 7344128 | tf_op jit(solution)/shard_map/dot_general | solution.py:193
  104.7 1.9 pad_maximum_fusion
  106.6 9.3 %all-to-all-start.3 = ((bf16[64,16,1408]{2,1,0:T(8,128)(2,1)}), bf16[64,16,1408]{2,1,0:T(8,128)(2,1)S(1)}, u32[]{:S(2)}, u32[]{:S(2)}) async-start(bf16[64,16,1408]{2,1,0:T(8,128)(2,1)} %bitcast.166), calls=%async_computation.3 | async-start | bytes 5767168 | tf_op jit(solution)/shard_map/all_to_all | solution.py:197
  116.0 49.6 %all-gather.2 = bf16[16,1,640]{2,1,0:T(2,128)(2,1)S(1)} all-gather(bf16[1,1,640]{2,1,0:T(2,128)(2,1)S(1)} %reshape.451), channel_id=2, replica_groups=mesh['y'=4,'zl'=2,'zh'=2,'x'=4,'core'=2] {'zh','x','core'}, dimensions={0}, use_global_device_ids=true | all-gather | bytes 21760 | tf_op jit(solution)/shard_map/all_gather | solution.py:180
  166.0 93.7 %all-gather.5.cloned.1.call-done = bf16[4096,1024]{1,0:T(8,128)(2,1)} async-done(((bf16[512,1024]{1,0:T(8,128)(2,1)}), bf16[4096,1024]{1,0:T(8,128)(2,1)}) %all-gather.5.cloned.1.call-update) | async-done | bytes 8388624 | tf_op jit(solution)/shard_map/all_gather | solution.py:216
  259.9 3.5 copy.117
  263.4 1.1 copy.118
  264.7 2.2 bitcast_bitcast_fusion.1
  266.9 2.2 bitcast_bitcast_fusion
  269.4 0.4 convert_reduce_fusion.1
  270.0 1.1 copy.87
  271.1 1.1 reshape.413
  272.6 1.4 select_reduce_fusion.3
  274.0 4.0 %fusion.8 = (f32[4,4,8,8]{3,1,2,0:T(4,128)S(1)}, f32[4,8,4,8,512]{4,3,2,1,0:T(8,128)S(1)}) fusion(pred[4,512]{1,0:T(4,128)(4,1)S(1)} %iota_compare_fusion.10, bf16[4,512,8,128,1]{3,2,1,0,4:T(8,128)(2,1)} %bitcast_bitcast_fusion.1, bf16[4,4,8,8,64]{4,3,2,1,0:T(8,128)(2,1)S(1)} %get-tuple-element.230, bf16[4,4,8,8,64]{4,3,2,1,0:T(8,128)(2,1)S(1)} %get-tuple-element.229), kind=kOutput, calls=%fused_computation.37 | convolution fusion | flops 136313856 | bytes 6559744 | tf_op jit(solution)/shard_map/skgrd,sjgd->skgrj/dot_general | solution.py:44
  278.1 0.4 fusion.65
  278.4 0.7 fusion.14
  279.2 1.4 fusion.16
  280.6 0.4 fusion.19
  281.4 15.6 %all_to_all.43 = bf16[8,16,1024]{2,1,0:T(8,128)(2,1)S(1)} all-to-all(bf16[8,16,1024]{2,1,0:T(8,128)(2,1)S(1)} %copy.98), channel_id=1, replica_groups=mesh['y'=4,'zl'=2,'zh'=2,'x'=4,'core'=2] {'zh','x'}, dimensions={0} | all-to-all | bytes 524288 | tf_op jit(solution)/shard_map/all_to_all | solution.py:218
  297.0 1.5 fusion.37
  298.5 1.5 fusion.39
  300.1 1.5 fusion.41
  301.6 1.5 fusion.43
  303.1 1.5 fusion.45
  304.7 1.5 fusion.47
  306.2 1.5 fusion.49
  307.8 1.5 fusion.51
  309.3 1.5 fusion.21
  310.9 1.5 fusion.23
  312.4 1.5 fusion.25
  314.0 1.5 fusion.27
  315.5 1.5 fusion.29
  317.0 1.5 fusion.31
  318.6 1.5 fusion.33
  320.1 1.5 fusion.35
  321.7 1.3 copy-done.3
  323.0 4.3 %all-to-all-start.5 = ((bf16[8,16,8192]{2,1,0:T(8,128)(2,1)}), bf16[8,16,8192]{2,1,0:T(8,128)(2,1)}, u32[]{:S(2)}, u32[]{:S(2)}) async-start(bf16[8,16,8192]{2,1,0:T(8,128)(2,1)} %bitcast.170), calls=%async_computation.5 | async-start | bytes 4194304 | tf_op jit(solution)/shard_map/all_to_all | solution.py:237
  327.8 0.6 reshape_reshape.3
  328.4 0.7 fusion.80
  329.1 26.8 %all-to-all-done.5 = bf16[8,16,8192]{2,1,0:T(8,128)(2,1)} async-done(((bf16[8,16,8192]{2,1,0:T(8,128)(2,1)}), bf16[8,16,8192]{2,1,0:T(8,128)(2,1)}, u32[]{:S(2)}, u32[]{:S(2)}) %all-to-all-start.5) | async-done | bytes 2097184 | tf_op jit(solution)/shard_map/all_to_all | solution.py:237
  355.9 1.9 convert_reduce_fusion.2
  358.0 0.8 add_convert_fusion.1
  (79 shorter events, 3.9 us)
Async XLA Ops:
  8.6 20.4 %all-to-all-start.1 = ((s32[128,1,16]{2,1,0:T(1,128)}), s32[128,1,16]{2,1,0:T(1,128)S(1)}, u32[]{:S(2)}, u32[]{:S(2)}) async-start(s32[128,1,16]{2,1,0:T(1,128)} %broadcast_in_dim.187), calls=%async_computation.1 | async-start | bytes 131072 | tf_op jit(solution)/shard_map/all_to_all | solution.py:110
  19.7 240.0 %all-gather.5.cloned.1.call-start = ((), (), s32[]{:S(2)}) async-start(), calls=%async_computation.6 | async-start | bytes 9437184 | tf_op jit(solution)/shard_map/all_gather | solution.py:216
  29.0 21.9 %copy-start.4 = (s32[2,64,16]{2,1,0:T(8,128)}, s32[2,64,16]{2,1,0:T(8,128)S(1)}, u32[]{:S(2)}) copy-start(s32[2,64,16]{2,1,0:T(8,128)S(1)} %copy.82) | copy-start | bytes 24580
  40.4 0.9 copy-start.5
  40.4 1.1 copy-start.6
  40.5 1.4 copy-start.2
  41.3 1.9 collective-permute-start.1
  42.1 12.1 %collective-permute-start.2 = (bf16[1024,640]{1,0:T(8,128)(2,1)S(1)}, bf16[1024,640]{1,0:T(8,128)(2,1)}, u32[]{:S(2)}, u32[]{:S(2)}) collective-permute-start(bf16[1024,640]{1,0:T(8,128)(2,1)S(1)} %pad_maximum_fusion.1), channel_id=1, source_target_pairs={{0,1},{1,0},{2,3},{3,2},{4,5},{5,4},{6,7},{7,6},{8,9},{9,8},{10,11... | collective-permute-start | bytes 3932168 | tf_op jit(solution)/shard_map/ppermute | solution.py:80
  45.8 47.3 %all-to-all-start.2 = ((bf16[8,128,1024]{2,1,0:T(8,128)(2,1)}), bf16[8,128,1024]{2,1,0:T(8,128)(2,1)}, u32[]{:S(2)}, u32[]{:S(2)}) async-start(bf16[8,128,1024]{2,1,0:T(8,128)(2,1)} %broadcast_in_dim.197), calls=%async_computation.2 | async-start | bytes 4194304 | tf_op jit(solution)/shard_map/all_to_all | solution.py:143
  106.5 9.3 %copy-start.8 = (bf16[512]{0:T(512)(128)(2,1)S(1)}, bf16[512]{0:T(512)(128)(2,1)}, u32[]{:S(2)}) copy-start(bf16[512]{0:T(512)(128)(2,1)} %param.22) | copy-start | bytes 3076
  106.6 9.4 %copy-start.9 = (bf16[64]{0:T(256)(128)(2,1)S(1)}, bf16[64]{0:T(256)(128)(2,1)}, u32[]{:S(2)}) copy-start(bf16[64]{0:T(256)(128)(2,1)} %param.24) | copy-start | bytes 388
  106.6 9.4 %copy-start.10 = (bf16[64]{0:T(256)(128)(2,1)S(1)}, bf16[64]{0:T(256)(128)(2,1)}, u32[]{:S(2)}) copy-start(bf16[64]{0:T(256)(128)(2,1)} %param.23) | copy-start | bytes 388
  106.6 59.2 %copy-start.7 = (s32[4]{0:T(128)S(1)}, s32[4]{0:T(128)}, u32[]{:S(2)}) copy-start(s32[4]{0:T(128)} %param.16) | copy-start | bytes 52
  106.6 162.6 %all-to-all-start.3 = ((bf16[64,16,1408]{2,1,0:T(8,128)(2,1)}), bf16[64,16,1408]{2,1,0:T(8,128)(2,1)S(1)}, u32[]{:S(2)}, u32[]{:S(2)}) async-start(bf16[64,16,1408]{2,1,0:T(8,128)(2,1)} %bitcast.166), calls=%async_computation.3 | async-start | bytes 5767168 | tf_op jit(solution)/shard_map/all_to_all | solution.py:197
  259.7 49.6 %collective-permute-start.3 = (bf16[8,512,1024]{2,1,0:T(8,128)(2,1)}, bf16[8,512,1024]{2,1,0:T(8,128)(2,1)}, u32[]{:S(2)}, u32[]{:S(2)}) collective-permute-start(bf16[8,512,1024]{2,1,0:T(8,128)(2,1)} %bitcast.167), channel_id=1, source_target_pairs={{0,1},{1,0},{2,3},{3,2},{4,5},{5,4},{6,7},{7,6},{8,9},{9,8},{10,11... | collective-permute-start | bytes 25165832 | tf_op jit(solution)/shard_map/ppermute | solution.py:80
  259.9 3.5 copy-start
  274.0 5.2 %copy-start.1 = (bf16[4,512,8,128,1]{3,2,1,0,4:T(8,128)(2,1)S(1)}, bf16[4,512,8,128,1]{3,2,1,0,4:T(8,128)(2,1)}, u32[]{:S(2)}) copy-start(bf16[4,512,8,128,1]{3,2,1,0,4:T(8,128)(2,1)} %bitcast_bitcast_fusion) | copy-start | bytes 12582916
  321.7 1.3 copy-start.3
  323.0 33.0 %all-to-all-start.5 = ((bf16[8,16,8192]{2,1,0:T(8,128)(2,1)}), bf16[8,16,8192]{2,1,0:T(8,128)(2,1)}, u32[]{:S(2)}, u32[]{:S(2)}) async-start(bf16[8,16,8192]{2,1,0:T(8,128)(2,1)} %bitcast.170), calls=%async_computation.5 | async-start | bytes 4194304 | tf_op jit(solution)/shard_map/all_to_all | solution.py:237
Sparse Core Ops, SparseCore 0:
  41.5 218.1 all-gather.4

commit v2 on v1

v2 whole, which is shorter than its diff:
```python
import jax
import jax.numpy as jnp
from jax import lax
from jax.experimental import pallas as pl
from jax.experimental.pallas import tpu as pltpu
from jax.sharding import Mesh
from jax.sharding import PartitionSpec as P

HD = 128
ROUND_ROWS = 72
SENT_ROWS = 80

norm_epsilon = 1e-06
rope_base = 1000000.0
masked_low = -1e30

DP = ("y", "zl")
CHIPS = ("zh", "x")
LAYER = ("zl", "zh", "x")
PLANE = ("y", "zh", "x")
EVERY = ("y", "zl", "zh", "x", "core")


def rotate(features, positions):
    head_width = features.shape[-1]
    half_width = head_width // 2
    frequency = rope_base ** (-(2.0 * jnp.arange(half_width, dtype=jnp.float32)) / head_width)
    angles = positions.astype(jnp.float32)[..., None, None] * frequency
    cosine = jnp.cos(angles)
    sine_part = jnp.sin(angles)
    leading = features[..., :half_width]
    trailing = features[..., half_width:]
    return jnp.concatenate(
        [leading * cosine - trailing * sine_part, trailing * cosine + leading * sine_part], axis=-1
    )


def attend(rotated, fresh_keys, fresh_values, key_cache, value_cache, lengths):
    seq_here, step_span, heads, head_width = rotated.shape
    kv_heads = fresh_keys.shape[2]
    group_size = heads // kv_heads
    cache_len = key_cache.shape[1]
    cache_keys = key_cache.reshape(seq_here, cache_len, kv_heads, head_width)
    cache_values = value_cache.reshape(seq_here, cache_len, kv_heads, head_width)
    grouped = rotated.reshape(seq_here, step_span, kv_heads, group_size, head_width)
    score_scale = head_width ** (-0.5)
    cached = (
        jnp.einsum("skgrd,sjgd->skgrj", grouped, cache_keys, preferred_element_type=jnp.float32)
        * score_scale
    )
    fresh_scores = (
        jnp.einsum("skgrd,sjgd->skgrj", grouped, fresh_keys, preferred_element_type=jnp.float32)
        * score_scale
    )
    cache_valid = (jnp.arange(cache_len, dtype=jnp.int32)[None, :] < lengths[:, None])[
        :, None, None, None, :
    ]
    fresh_count = fresh_keys.shape[1]
    fresh_valid = (
        jnp.arange(fresh_count, dtype=jnp.int32)[None, :]
        <= jnp.arange(step_span, dtype=jnp.int32)[:, None]
    )[None, :, None, None, :]
    row_top = jnp.maximum(
        jnp.max(jnp.where(cache_valid, cached, masked_low), axis=-1),
        jnp.max(jnp.where(fresh_valid, fresh_scores, masked_low), axis=-1),
    )[..., None]
    cache_exp = jnp.exp(jnp.where(cache_valid, cached - row_top, masked_low))
    fresh_exp = jnp.exp(jnp.where(fresh_valid, fresh_scores - row_top, masked_low))
    denominator = jnp.sum(cache_exp, axis=-1, keepdims=True) + jnp.sum(
        fresh_exp, axis=-1, keepdims=True
    )
    cache_weights = (cache_exp / denominator).astype(jnp.bfloat16)
    fresh_weights = (fresh_exp / denominator).astype(jnp.bfloat16)
    attended = jnp.einsum(
        "skgrj,sjgd->skgrd", cache_weights, cache_values, preferred_element_type=jnp.float32
    )
    attended = attended + jnp.einsum(
        "skgrj,sjgd->skgrd", fresh_weights, fresh_values, preferred_element_type=jnp.float32
    )
    return attended.reshape(seq_here, step_span, heads * head_width).astype(jnp.bfloat16)


def swap_cores(value):
    return lax.ppermute(value, "core", [(0, 1), (1, 0)])


def swap_layers(value):
    return lax.ppermute(value, "zl", [(0, 1), (1, 0)])


VMEM = pl.BlockSpec(memory_space=pltpu.VMEM)
SMEM = pl.BlockSpec(memory_space=pltpu.SMEM)


def projection_kernel(place_ref, slot_ref, table_ref, gain_ref, *rest):
    weight_refs, out_ref, wide_ref, total_ref = rest[:4], rest[4], rest[5], rest[6]
    chip, layer, core = place_ref[0], place_ref[1], place_ref[2]
    rows = slot_ref.shape[0]
    width = table_ref.shape[2]
    table_rows = table_ref.shape[1]
    cols = weight_refs[0].shape[1]
    chosen = (
        lax.broadcasted_iota(jnp.int32, (rows, table_rows), 1) == slot_ref[...]
    ).astype(jnp.bfloat16)
    for flip in range(2):
        block = (layer + flip) % 2
        found = jnp.dot(chosen, table_ref[block], preferred_element_type=jnp.float32)
        wide_ref[:, pl.ds(pl.multiple_of(block * width, width), width)] = found.astype(
            jnp.bfloat16
        )
        gained = (found * gain_ref[block]).astype(jnp.bfloat16)
        for side in range(2):
            product = jnp.dot(
                gained, weight_refs[2 * flip + side][...], preferred_element_type=jnp.float32
            )
            if flip == 0:
                total_ref[side] = product
            else:
                where = pl.multiple_of(((core + side) % 2) * cols, cols)
                out_ref[:, pl.ds(where, cols)] = (total_ref[side] + product).astype(jnp.bfloat16)
    strip = out_ref.shape[1] - 2 * cols
    out_ref[:, 2 * cols :] = wide_ref[:, pl.ds(pl.multiple_of(chip * strip, strip), strip)]


def project(place, slot, table, gain, weights, chips):
    rows = slot.shape[0]
    width = table.shape[2]
    cols = weights[0].shape[1]
    return pl.pallas_call(
        projection_kernel,
        out_shape=jax.ShapeDtypeStruct((rows, 2 * cols + 2 * width // chips), jnp.bfloat16),
        in_specs=[SMEM] + [VMEM] * 7,
        out_specs=VMEM,
        scratch_shapes=[
            pltpu.VMEM((rows, 2 * width), jnp.bfloat16),
            pltpu.VMEM((2, rows, cols), jnp.float32),
        ],
        compiler_params=pltpu.CompilerParams(vmem_limit_bytes=48 * 1024 * 1024),
        name="project",
    )(place, slot, table, gain, *weights)


def branch_kernel(place_ref, rows_ref, *rest):
    weight_refs, out_ref = rest[:4], rest[4]
    layer, core = place_ref[1], place_ref[2]
    depth, width = weight_refs[0].shape
    for flip in range(2):
        block = pl.multiple_of(((layer + flip) % 2) * width, width)
        parts = []
        for side in range(2):
            where = pl.multiple_of(((core + side) % 2) * depth, depth)
            parts.append(
                jnp.dot(
                    rows_ref[:, pl.ds(where, depth)],
                    weight_refs[2 * flip + side][...],
                    preferred_element_type=jnp.float32,
                )
            )
        out_ref[:, pl.ds(block, width)] = (parts[0] + parts[1]).astype(jnp.bfloat16)


def branch_out(place, rows, weights):
    return pl.pallas_call(
        branch_kernel,
        out_shape=jax.ShapeDtypeStruct((rows.shape[0], 2 * weights[0].shape[1]), jnp.bfloat16),
        in_specs=[SMEM] + [VMEM] * 5,
        out_specs=VMEM,
        compiler_params=pltpu.CompilerParams(vmem_limit_bytes=48 * 1024 * 1024),
        name="branch",
    )(place, rows, *weights)


def hidden_kernel(branch_ref, strip_ref, out_ref):
    chips = branch_ref.shape[1]
    strip = strip_ref.shape[3]
    for part in range(chips):
        span = slice(part * strip, (part + 1) * strip)
        total = strip_ref[0, part].astype(jnp.float32)
        for chip in range(chips):
            total = total + branch_ref[0, chip, :, span].astype(jnp.float32)
        out_ref[:, span] = total.astype(jnp.bfloat16)


def hidden_sum(branches, arrived):
    groups, chips, rows, width = branches.shape
    strip = width // chips
    last = arrived.shape[3] // strip - 1
    return pl.pallas_call(
        hidden_kernel,
        out_shape=jax.ShapeDtypeStruct((rows, groups * width), jnp.bfloat16),
        grid=(groups,),
        in_specs=[
            pl.BlockSpec((1, chips, rows, width), lambda y: (y, 0, 0, 0)),
            pl.BlockSpec((1, chips, rows, strip), lambda y: (y, 0, 0, last)),
        ],
        out_specs=pl.BlockSpec((rows, width), lambda y: (0, y)),
        compiler_params=pltpu.CompilerParams(vmem_limit_bytes=48 * 1024 * 1024),
        name="hidden_sum",
    )(branches, arrived)


def per_device(
    token_ids,
    lengths,
    embedding,
    norm_gain,
    q_weight,
    k_weight,
    v_weight,
    q_bias,
    k_bias,
    v_bias,
    o_weight,
    key_cache,
    value_cache,
):
    seq_here, step_count = token_ids.shape
    rows_here = seq_here * step_count
    vocab_here, width_here = embedding.shape
    groups = lax.axis_size("y")
    chips = lax.axis_size(CHIPS)
    chip = lax.axis_index(CHIPS)
    core = lax.axis_index("core")
    layer = lax.axis_index("zl")
    parties = groups * chips
    plane_rows = parties * rows_here
    place = jnp.stack([chip, layer, core]).astype(jnp.int32)

    both = jnp.concatenate([q_weight, k_weight, v_weight], axis=1)
    both_layer = swap_layers(both)
    weights = (both, swap_cores(both), both_layer, swap_cores(both_layer))
    o_layer = swap_layers(o_weight)
    o_weights = (o_weight, swap_cores(o_weight), o_layer, swap_cores(o_layer))
    own_bias = jnp.concatenate([q_bias, k_bias, v_bias])
    core_cols = own_bias.shape[0]
    q_cols = q_bias.shape[0]
    k_cols = k_bias.shape[0]

    sent_ids = jnp.broadcast_to(token_ids.reshape(1, rows_here), (parties * 4, rows_here))
    every_id = lax.all_to_all(sent_ids, EVERY, split_axis=0, concat_axis=0, tiled=True)
    plane_ids = (
        every_id.reshape(groups, 2, chips, 2, rows_here)
        .transpose(1, 3, 0, 2, 4)
        .reshape(4, plane_rows)
    )
    holder = plane_ids // (2 * vocab_here)
    spot = jnp.arange(plane_rows, dtype=jnp.int32)
    same = plane_ids[:, :, None] == plane_ids[:, None, :]
    leader = jnp.min(jnp.where(same, spot[None, None, :], plane_rows), axis=2)
    leads = leader == spot[None, :]
    before = (
        leads[:, None, :]
        & (holder[:, :, None] == holder[:, None, :])
        & (spot[None, None, :] < leader[:, :, None])
    )
    rank = jnp.sum(before.astype(jnp.int32), axis=2)
    rounds = jnp.max(rank) // ROUND_ROWS + 1
    own_plane = 2 * layer + core
    own_holder = lax.dynamic_index_in_dim(holder, own_plane, 0, keepdims=False)
    own_rank = lax.dynamic_index_in_dim(rank, own_plane, 0, keepdims=False)
    own_offset = plane_ids - (2 * chip + core) * vocab_here
    listed_here = leads & (own_offset >= 0) & (own_offset < vocab_here)
    row_at = jnp.arange(SENT_ROWS, dtype=jnp.int32)
    bias_rows = jnp.where(
        row_at[:, None] == ROUND_ROWS + core,
        jnp.pad(own_bias, (0, width_here - core_cols))[None, :],
        jnp.zeros((), jnp.bfloat16),
    )

    def exchange(turn):
        first = turn * ROUND_ROWS
        wanted_rank = jnp.where(row_at < ROUND_ROWS, first + row_at, -1)
        wanted = listed_here[:, None, :] & (rank[:, None, :] == wanted_rank[None, :, None])
        listed = jnp.max(jnp.where(wanted, own_offset[:, None, :], -1), axis=2)
        picked = jnp.dot(
            (
                listed.reshape(-1, 1) == jnp.arange(vocab_here, dtype=jnp.int32)[None, :]
            ).astype(jnp.bfloat16),
            embedding,
            preferred_element_type=jnp.float32,
        ).astype(jnp.bfloat16)
        picked = picked.reshape(2, 2, SENT_ROWS, width_here) + bias_rows
        mine = jnp.where(core == 0, picked[:, 0], picked[:, 1])
        theirs = jnp.where(core == 0, picked[:, 1], picked[:, 0])
        merged = mine + swap_cores(theirs)
        table = lax.all_to_all(
            jnp.broadcast_to(merged[:, None], (2, chips, SENT_ROWS, width_here)).reshape(
                2 * chips, SENT_ROWS, width_here
            ),
            LAYER,
            split_axis=0,
            concat_axis=0,
            tiled=True,
        ).reshape(2, chips * SENT_ROWS, width_here)
        here = (own_rank >= first) & (own_rank < first + ROUND_ROWS)
        slot = jnp.where(here, own_holder * SENT_ROWS + own_rank - first, -1)
        return slot.reshape(plane_rows, 1), table

    near_gain = lax.dynamic_slice_in_dim(
        norm_gain, lax.axis_index("y") * 2 * width_here, 2 * width_here
    )
    near_gain = near_gain.reshape(2, 1, width_here).astype(jnp.float32)
    slot, table = exchange(0)
    pair_bias = table[0].reshape(chips, SENT_ROWS, width_here)
    pair_bias = pair_bias[:, ROUND_ROWS : ROUND_ROWS + 2, :core_cols].astype(jnp.float32)
    payload = project(place, slot, table, near_gain, weights, chips)

    def further(turn, sofar):
        turn_slot, turn_table = exchange(turn)
        return sofar + project(place, turn_slot, turn_table, near_gain, weights, chips)

    payload = lax.fori_loop(1, rounds, further, payload)
    arrived = lax.all_to_all(payload, PLANE, split_axis=0, concat_axis=0, tiled=True)
    arrived = arrived.reshape(groups, chips, rows_here, -1)
    pair_cols = 2 * core_cols
    inputs = arrived[..., pair_cols:].astype(jnp.float32)
    square = jnp.sum(inputs * inputs, axis=(0, 1, 3))
    scale = lax.rsqrt(square / norm_gain.shape[0] + norm_epsilon)
    summed = jnp.sum(arrived[..., :pair_cols].astype(jnp.float32), axis=0)
    summed = summed.reshape(chips, rows_here, 2, core_cols)
    joined = (summed * scale[None, :, None, None] + pair_bias[:, None]).astype(jnp.bfloat16)
    joined = joined.transpose(1, 0, 2, 3)
    queries = joined[..., :q_cols].reshape(seq_here, step_count, -1, HD)
    fresh_keys = joined[..., q_cols : q_cols + k_cols].reshape(seq_here, step_count, -1, HD)
    fresh_values = joined[..., q_cols + k_cols :].reshape(seq_here, step_count, -1, HD)
    positions = lengths[:, None] + jnp.arange(step_count, dtype=jnp.int32)[None, :]
    rotated = rotate(queries.astype(jnp.float32), positions).astype(jnp.bfloat16)
    new_keys = rotate(fresh_keys.astype(jnp.float32), positions).astype(jnp.bfloat16)
    attended = attend(rotated, new_keys, fresh_values, key_cache, value_cache, lengths)

    spread = attended.reshape(rows_here, chips, 2 * q_cols).transpose(1, 0, 2)
    spread = jnp.broadcast_to(spread[None], (groups,) + spread.shape)
    gathered = lax.all_to_all(
        spread.reshape(parties, rows_here, 2 * q_cols), PLANE, split_axis=0, concat_axis=0, tiled=True
    ).reshape(plane_rows, 2 * q_cols)
    branch = branch_out(place, gathered, o_weights)
    branches = lax.all_to_all(branch, PLANE, split_axis=0, concat_axis=0, tiled=True)
    hidden = hidden_sum(branches.reshape(groups, chips, rows_here, -1), arrived)
    return (
        hidden.reshape(seq_here, step_count, -1),
        new_keys.reshape(seq_here, step_count, -1),
        fresh_values.reshape(seq_here, step_count, -1),
    )


def solution(mesh):
    fine = Mesh(mesh.devices.reshape(4, 2, 2, 4, 2), EVERY)
    tensor = CHIPS + ("core",)
    placed = (
        P(EVERY, None),
        P(EVERY),
        P(tensor, DP),
        P(),
        P(DP, tensor),
        P(DP, tensor),
        P(DP, tensor),
        P(tensor),
        P(tensor),
        P(tensor),
        P(tensor, DP),
        P(EVERY, None, None),
        P(EVERY, None, None),
    )
    return jax.shard_map(
        per_device,
        mesh=fine,
        in_specs=placed,
        out_specs=(
            P(EVERY, None, None),
            P(EVERY, None, None),
            P(EVERY, None, None),
        ),
        check_vma=False,
    )
```

time: 371 us -> 221 us (0.60); the launches traced: 366 us -> 220 us
  blocking collectives: 65.2 us -> 0 us
  waiting for transfers between devices: 163 us -> 115 us
  matrix products: 42.4 us -> 16.9 us
  Pallas kernels: 0 us -> 17.7 us
  between operations: 17.3 us -> 3.04 us
  other arithmetic: 18.1 us -> 10.5 us
  local copies, waits for them, and re-layouts: 30.1 us -> 25.6 us
    all_gather x1 -> x0, waiting for transfers between devices: 93.7 us -> none  [per_device(): full_o = lax.all_gather(o_weight, DP, axis=0, tiled=False)]
    all_gather x1 -> x0, blocking collectives: 49.6 us -> none  [per_device(): lax.all_gather(own_bias, CHIPS + ('core',), axis=0, tiled=False)]
    ppermute x0 -> x2, waiting for transfers between devices: none -> 46.5 us  [swap_layers(): return lax.ppermute(value, 'zl', [(0, 1), (1, 0)])]
    dot_general x18 -> x1, matrix products: 35.2 us -> 7.18 us  [exchange(): jnp.dot((listed.reshape(-1, 1) == jnp.arange(vocab_here, dtype=jnp.int32)...]
    pallas_call x0 -> x3, Pallas kernels: none -> 17.7 us  [the longest x1 9.72 us: project(): pl.pallas_call(projection_kernel, out_shape=jax.ShapeDtypeStruct((rows, 2...]
    all_to_all x2 -> x3, waiting for transfers between devices: 59.4 us -> 43.2 us  [the longest x1 25.9 us: per_device(): lax.all_to_all(branch, PLANE, split_axis=0, concat_axis=0, tiled=True)]
    all_to_all x1, waiting for transfers between devices: 0.01 us -> 16 us  [per_device(): lax.all_to_all(payload, PLANE, split_axis=0, concat_axis=0, tiled=True)]
    all_to_all x1 -> x0, blocking collectives: 15.6 us -> none  [per_device(): lax.all_to_all(attended.reshape(rows_here, chips, 2 * q_cols).transpose(1...]
  transfers between devices with their start and end apart: 8 -> 12, of which waited for: 5 -> 5; matrix products, arithmetic and copies ran while one was open for 16% -> 17% of each run, Pallas kernels for 0% -> 4%
where the time goes in v2:
time: 221 us; the launch traced here: 220 us
  waiting for transfers between devices  115 us (52%)
  starting transfers between devices  31.4 us (14%)
  local copies, waits for them, and re-layouts  25.6 us (12%)
  Pallas kernels  17.7 us (8%)
  matrix products  16.9 us (8%)
  other arithmetic  10.5 us (5%)
  between operations  3.04 us (1%)
    ppermute x2, waiting for transfers between devices, swap_layers(): return lax.ppermute(value, 'zl', [(0, 1), (1, 0)])  46.5 us
    all_to_all x1, waiting for transfers between devices, per_device(): lax.all_to_all(branch, PLANE, split_axis=0, concat_axis=0, tiled=True)  25.9 us
    all_to_all x1, waiting for transfers between devices, per_device(): lax.all_to_all(spread.reshape(parties, rows_here, 2 * q_cols), PLANE, spl...  17.2 us
    all_to_all x1, waiting for transfers between devices, per_device(): lax.all_to_all(payload, PLANE, split_axis=0, concat_axis=0, tiled=True)  16 us
    all_to_all x1, starting transfers between devices, per_device(): lax.all_to_all(sent_ids, EVERY, split_axis=0, concat_axis=0, tiled=True)  11.1 us
    unnamed x22, local copies, waits for them, and re-layouts  11 us
    pallas_call x1, Pallas kernels, project(): pl.pallas_call(projection_kernel, out_shape=jax.ShapeDtypeStruct((rows, 2...  9.72 us
    all_to_all x1, waiting for transfers between devices, per_device(): lax.all_to_all(sent_ids, EVERY, split_axis=0, concat_axis=0, tiled=True)  9.22 us
  transfers between devices with their start and end apart: 12, of which 5 were waited for; matrix products, arithmetic and copies ran while one was open for 17% of the time, Pallas kernels for 4%

profile of v2, /device:TPU:0, one launch (start us, length us, event | category | flops | bytes accessed | tf_op | source)
XLA Modules:
  0.0 220.1 jit_solution(1328288239990266719)
XLA Ops:
  0.6 0.8 broadcast_in_dim.178
  1.4 0.8 fusion.55
  2.3 0.7 broadcast_in_dim.179
  2.9 11.1 %all-to-all-start.1 = ((s32[128,1,16]{2,1,0:T(1,128)}), s32[128,1,16]{2,1,0:T(1,128)S(1)}, u32[]{:S(2)}, u32[]{:S(2)}) async-start(s32[128,1,16]{2,1,0:T(1,128)} %broadcast_in_dim.179), calls=%async_computation.1 | async-start | bytes 131072 | tf_op jit(solution)/shard_map/all_to_all | solution.py:240
  14.1 9.2 %all-to-all-done.1 = s32[128,1,16]{2,1,0:T(1,128)S(1)} async-done(((s32[128,1,16]{2,1,0:T(1,128)}), s32[128,1,16]{2,1,0:T(1,128)S(1)}, u32[]{:S(2)}, u32[]{:S(2)}) %all-to-all-start.1) | async-done | bytes 8224 | tf_op jit(solution)/shard_map/all_to_all | solution.py:240
  23.4 0.1 eq.129
  23.5 1.0 select_reduce_fusion.1
  24.5 1.5 convert_reduce_fusion
  26.0 0.3 select_reduce_fusion.2
  26.3 0.1 eq.141
  26.4 7.2 %fusion.21 = bf16[320,1024]{1,0:T(8,128)(2,1)S(1)} fusion(bf16[4752,1024]{1,0:T(8,128)(2,1)} %param.17, s32[320]{0:T(512)S(1)} %eq.141), kind=kOutput, calls=%fused_computation.38 | convolution fusion | flops 3116119040 | bytes 10388736 | tf_op jit(solution)/shard_map/dot_general | solution.py:275
  33.7 0.1 collective-permute-start.1
  33.8 0.7 copy-done.8
  34.5 0.2 copy.151
  34.7 0.2 copy.152
  34.8 0.1 copy-done.7
  34.9 1.2 pad_maximum_fusion.rest_0_
  36.2 0.8 collective-permute-start.3
  37.1 1.8 broadcast_in_dim.190
  38.9 3.7 %all-to-all-start.2 = ((bf16[16,80,1024]{2,1,0:T(8,128)(2,1)}), bf16[16,80,1024]{2,1,0:T(8,128)(2,1)S(1)}, u32[]{:S(2)}, u32[]{:S(2)}) async-start(bf16[16,80,1024]{2,1,0:T(8,128)(2,1)} %bitcast.167), calls=%async_computation.2 | async-start | bytes 5242880 | tf_op jit(solution)/shard_map/all_to_all | solution.py:286
  42.6 0.1 collective-permute-start.2
  42.7 46.5 %collective-permute-done.3.rest_2_ = bf16[1024,640]{1,0:T(8,128)(2,1)} collective-permute-done((bf16[1024,640]{1,0:T(8,128)(2,1)}, bf16[1024,640]{1,0:T(8,128)(2,1)}, u32[]{:S(2)}, u32[]{:S(2)}) %collective-permute-start.3) | collective-permute-done | bytes 1310752 | tf_op jit(solution)/shard_map/ppermute | solution.py:88
  89.2 0.8 collective-permute-start.6
  90.1 0.2 collective-permute-start.5
  90.3 5.5 %copy.184 = bf16[256,8,8,128]{3,2,1,0:T(8,128)(2,1)} copy(bf16[256,8,8,128]{3,1,2,0:T(8,128)(2,1)} %bitcast.170) | data formatting | bytes 8388608
  95.8 3.1 %copy.185 = bf16[256,8,8,128]{3,2,1,0:T(8,128)(2,1)} copy(bf16[256,8,8,128]{3,1,2,0:T(8,128)(2,1)S(1)} %bitcast.171) | data formatting | bytes 8388608
  99.0 0.7 dynamic-slice_convert_fusion
  99.8 0.6 reduce_max.48
  102.4 0.1 copy.153.slot_ref
  102.6 9.7 %project.4 = bf16[512,1536]{1,0:T(8,128)(2,1)} custom-call(s32[3]{0:T(128)S(1)} %pad_add_fusion.place_ref, s32[512,1]{1,0:T(8,128)S(1)} %copy.153.slot_ref, bf16[2,640,1024]{2,1,0:T(8,128)(2,1)S(1)} %bitcast.160, f32[2,1,1024]{2,1,0:T(1,128)S(1)} %bitcast.175, bf16[1024,640]{1,0:T(8,128)(2,1)} %pad_maximum_fusion.rest_0_, ...), custom_call_target="tpu_custom_call" | custom-call | tf_op jit(solution)/shard_map/project/pallas_call | solution.py:129
  112.3 4.4 %all-to-all-start.3 = ((bf16[32,16,1536]{2,1,0:T(8,128)(2,1)}), bf16[32,16,1536]{2,1,0:T(8,128)(2,1)S(1)}, u32[]{:S(2)}, u32[]{:S(2)}) async-start(bf16[32,16,1536]{2,1,0:T(8,128)(2,1)} %bitcast.163), calls=%async_computation.3 | async-start | bytes 3145728 | tf_op jit(solution)/shard_map/all_to_all | solution.py:313
  116.8 0.1 multiply_cosine_fusion
  117.0 4.6 %bitcast_bitcast_fusion.1 = bf16[4,512,8,128,1]{3,2,1,0,4:T(8,128)(2,1)} fusion(bf16[4,512,8,128]{3,2,1,0:T(8,128)(2,1)} %bitcast.165), kind=kLoop, calls=%fused_computation.20 | loop fusion | bytes 8388608 | tf_op jit(solution)/shard_map/reshape | solution.py:43
  121.6 2.3 %bitcast_bitcast_fusion = bf16[4,512,8,128,1]{3,2,1,0,4:T(8,128)(2,1)} fusion(bf16[4,512,8,128]{3,2,1,0:T(8,128)(2,1)S(1)} %bitcast.164), kind=kLoop, calls=%fused_computation.19 | loop fusion | bytes 8388608 | tf_op jit(solution)/shard_map/reshape | solution.py:44
  123.8 0.9 slice_convert_fusion.2
  124.7 16.0 %all-to-all-done.3 = bf16[32,16,1536]{2,1,0:T(8,128)(2,1)S(1)} async-done(((bf16[32,16,1536]{2,1,0:T(8,128)(2,1)}), bf16[32,16,1536]{2,1,0:T(8,128)(2,1)S(1)}, u32[]{:S(2)}, u32[]{:S(2)}) %all-to-all-start.3) | async-done | bytes 1572896 | tf_op jit(solution)/shard_map/all_to_all | solution.py:313
  140.8 0.2 convert_reduce_fusion.1
  141.0 0.2 multiply_reduce_fusion
  141.2 0.2 fusion.36
  141.3 0.1 fusion.60
  141.6 0.1 reshape.442
  141.8 0.4 copy.155
  142.2 0.4 reshape.441
  142.6 0.2 fusion.39
  142.9 3.9 %fusion.17 = (f32[4,4,8,8]{3,1,2,0:T(4,128)S(1)}, f32[4,8,4,8,512]{4,3,2,1,0:T(8,128)S(1)}) fusion(pred[4,512]{1,0:T(4,128)(4,1)S(1)} %iota_compare_fusion.10, bf16[4,512,8,128,1]{3,2,1,0,4:T(8,128)(2,1)} %bitcast_bitcast_fusion.1, bf16[4,4,8,8,64]{4,3,2,1,0:T(8,128)(2,1)S(1)} %get-tuple-element.334, bf16[4,4,8,8,64]{4,3,2,1,0:T(8,128)(2,1)S(1)} %get-tuple-element.333), kind=kOutput, calls=%fused_computation.33 | convolution fusion | flops 136313856 | bytes 6559744 | tf_op jit(solution)/shard_map/skgrd,sjgd->skgrj/dot_general | solution.py:48
  146.8 1.4 select_reduce_fusion.3
  148.2 0.4 fusion.43
  148.6 0.7 fusion.20
  149.3 0.1 reshape.432
  149.5 4.1 %fusion.23 = f32[4,4,8,8,128]{4,3,1,2,0:T(8,128)S(1)} fusion(bf16[4,512,8,128,1]{3,2,1,0,4:T(8,128)(2,1)} %bitcast_bitcast_fusion, f32[4,8,4,8,512]{4,3,2,1,0:T(8,128)} %copy-done.5, f32[4,4,8,8]{3,1,2,0:T(4,128)S(1)} %add.187, f32[4,4,8,8]{3,1,2,0:T(4,128)S(1)} %max.7, pred[4,512]{1,0:T(4,128)(4,1)S(1)} %iota_compare_fusion.10), kind=kOutput, calls=%fused_computation.42 | convolution fusion | flops 136839168 | bytes 6825984 | tf_op jit(solution)/shard_map/skgrj,sjgd->skgrd/dot_general | solution.py:74
  153.5 0.4 fusion.26
  154.0 0.1 convert_element_type.91
  154.1 0.2 copy.166
  154.3 1.1 broadcast_in_dim.194
  155.4 5.2 %all-to-all-start.4 = ((bf16[32,16,1024]{2,1,0:T(8,128)(2,1)}), bf16[32,16,1024]{2,1,0:T(8,128)(2,1)S(1)}, u32[]{:S(2)}, u32[]{:S(2)}) async-start(bf16[32,16,1024]{2,1,0:T(8,128)(2,1)} %bitcast.169), calls=%async_computation.4 | async-start | bytes 2097152 | tf_op jit(solution)/shard_map/all_to_all | solution.py:333
  160.6 17.2 %all-to-all-done.4 = bf16[32,16,1024]{2,1,0:T(8,128)(2,1)S(1)} async-done(((bf16[32,16,1024]{2,1,0:T(8,128)(2,1)}), bf16[32,16,1024]{2,1,0:T(8,128)(2,1)S(1)}, u32[]{:S(2)}, u32[]{:S(2)}) %all-to-all-start.4) | async-done | bytes 1048608 | tf_op jit(solution)/shard_map/all_to_all | solution.py:333
  177.9 1.2 copy-done.1
  179.1 5.5 %branch.1 = bf16[512,2048]{1,0:T(8,128)(2,1)} custom-call(s32[3]{0:T(128)S(1)} %get-tuple-element.538, bf16[512,1024]{1,0:T(8,128)(2,1)S(1)} %bitcast.161, bf16[512,1024]{1,0:T(8,128)(2,1)S(1)} %copy-done.1, bf16[512,1024]{1,0:T(8,128)(2,1)} %collective-permute-done.5.rest_1_, bf16[512,1024]{1,0:T(8,128)(2,1)} %collective-permute-done.6.rest_2_, ...), custom_call_target="tpu_custom_call" | custom-call | tf_op jit(solution)/shard_map/branch/pallas_call | solution.py:163
  184.6 4.8 %all-to-all-start.5 = ((bf16[32,16,2048]{2,1,0:T(8,128)(2,1)}), bf16[32,16,2048]{2,1,0:T(8,128)(2,1)}, u32[]{:S(2)}, u32[]{:S(2)}) async-start(bf16[32,16,2048]{2,1,0:T(8,128)(2,1)} %bitcast.168), calls=%async_computation.5 | async-start | bytes 4194304 | tf_op jit(solution)/shard_map/all_to_all | solution.py:337
  189.4 0.7 reshape_reshape.3
  190.1 0.7 fusion.62
  190.9 25.9 %all-to-all-done.5 = bf16[32,16,2048]{2,1,0:T(8,128)(2,1)} async-done(((bf16[32,16,2048]{2,1,0:T(8,128)(2,1)}), bf16[32,16,2048]{2,1,0:T(8,128)(2,1)}, u32[]{:S(2)}, u32[]{:S(2)}) %all-to-all-start.5) | async-done | bytes 2097184 | tf_op jit(solution)/shard_map/all_to_all | solution.py:337
  216.8 2.5 %hidden_sum.1 = bf16[16,8192]{1,0:T(8,128)(2,1)S(1)} custom-call(bf16[4,8,16,2048]{3,2,1,0:T(8,128)(2,1)} %bitcast.35.branch_ref, bf16[4,8,16,1536]{3,2,1,0:T(8,128)(2,1)S(1)} %bitcast.159), custom_call_target="tpu_custom_call" | custom-call | tf_op jit(solution)/shard_map/hidden_sum/pallas_call | solution.py:188
  219.3 0.8 reshape.436
  (49 shorter events, 1.0 us)
Async XLA Ops:
  2.9 20.4 %all-to-all-start.1 = ((s32[128,1,16]{2,1,0:T(1,128)}), s32[128,1,16]{2,1,0:T(1,128)S(1)}, u32[]{:S(2)}, u32[]{:S(2)}) async-start(s32[128,1,16]{2,1,0:T(1,128)} %broadcast_in_dim.179), calls=%async_computation.1 | async-start | bytes 131072 | tf_op jit(solution)/shard_map/all_to_all | solution.py:240
  33.6 0.9 copy-start.8
  33.6 1.1 copy-start.9
  33.6 1.4 copy-start.7
  33.7 3.3 %collective-permute-start.1 = (bf16[2,80,1024]{2,1,0:T(8,128)(2,1)S(1)}, bf16[2,80,1024]{2,1,0:T(8,128)(2,1)S(1)}, u32[]{:S(2)}, u32[]{:S(2)}) collective-permute-start(bf16[2,80,1024]{2,1,0:T(8,128)(2,1)S(1)} %fusion.35), channel_id=1, source_target_pairs={{0,1},{1,0},{2,3},{3,2},{4,5},{5,4},{6,7},{7,6},{8,9},{9,8},{10,11... | collective-permute-start | bytes 983048 | tf_op jit(solution)/shard_map/ppermute | solution.py:84
  36.2 53.0 %collective-permute-start.3 = (bf16[1024,640]{1,0:T(8,128)(2,1)}, bf16[1024,640]{1,0:T(8,128)(2,1)}, u32[]{:S(2)}, u32[]{:S(2)}) collective-permute-start(bf16[1024,640]{1,0:T(8,128)(2,1)} %pad_maximum_fusion.rest_0_), channel_id=1, source_target_pairs={{0,16},{16,0},{1,17},{17,1},{2,18},{18,2},{3,19},{19,3},{4,20},{20... | collective-permute-start | bytes 3932168 | tf_op jit(solution)/shard_map/ppermute | solution.py:88
  38.9 63.7 %all-to-all-start.2 = ((bf16[16,80,1024]{2,1,0:T(8,128)(2,1)}), bf16[16,80,1024]{2,1,0:T(8,128)(2,1)S(1)}, u32[]{:S(2)}, u32[]{:S(2)}) async-start(bf16[16,80,1024]{2,1,0:T(8,128)(2,1)} %bitcast.167), calls=%async_computation.2 | async-start | bytes 5242880 | tf_op jit(solution)/shard_map/all_to_all | solution.py:286
  42.6 60.0 %collective-permute-start.2 = (bf16[1024,640]{1,0:T(8,128)(2,1)}, bf16[1024,640]{1,0:T(8,128)(2,1)}, u32[]{:S(2)}, u32[]{:S(2)}) collective-permute-start(bf16[1024,640]{1,0:T(8,128)(2,1)} %pad_maximum_fusion.rest_0_), channel_id=1, source_target_pairs={{0,1},{1,0},{2,3},{3,2},{4,5},{5,4},{6,7},{7,6},{8,9},{9,8},{10,11... | collective-permute-start | bytes 3932168 | tf_op jit(solution)/shard_map/ppermute | solution.py:84
  89.2 13.3 %collective-permute-start.4 = (bf16[1024,640]{1,0:T(8,128)(2,1)}, bf16[1024,640]{1,0:T(8,128)(2,1)}, u32[]{:S(2)}, u32[]{:S(2)}) collective-permute-start(bf16[1024,640]{1,0:T(8,128)(2,1)} %collective-permute-done.3.rest_2_), channel_id=1, source_target_pairs={{0,1},{1,0},{2,3},{3,2},{4,5},{5,4},{6,7},{7,6},{8,9},{9,8},{10,11... | collective-permute-start | bytes 3932168 | tf_op jit(solution)/shard_map/ppermute | solution.py:84
  89.2 34.6 %collective-permute-start.6 = (bf16[512,1024]{1,0:T(8,128)(2,1)}, bf16[512,1024]{1,0:T(8,128)(2,1)}, u32[]{:S(2)}, u32[]{:S(2)}) collective-permute-start(bf16[512,1024]{1,0:T(8,128)(2,1)} %rest_0_.1), channel_id=1, source_target_pairs={{0,16},{16,0},{1,17},{17,1},{2,18},{18,2},{3,19},{19,3},{4,20},{20... | collective-permute-start | bytes 3145736 | tf_op jit(solution)/shard_map/ppermute | solution.py:88
  90.1 70.6 %collective-permute-start.5 = (bf16[512,1024]{1,0:T(8,128)(2,1)}, bf16[512,1024]{1,0:T(8,128)(2,1)}, u32[]{:S(2)}, u32[]{:S(2)}) collective-permute-start(bf16[512,1024]{1,0:T(8,128)(2,1)} %rest_0_.1), channel_id=1, source_target_pairs={{0,1},{1,0},{2,3},{3,2},{4,5},{5,4},{6,7},{7,6},{8,9},{9,8},{10,11... | collective-permute-start | bytes 3145736 | tf_op jit(solution)/shard_map/ppermute | solution.py:84
  90.3 5.5 %copy-start.6 = (bf16[4,512,1024]{2,1,0:T(8,128)(2,1)S(1)}, bf16[4,512,1024]{2,1,0:T(8,128)(2,1)}, u32[]{:S(2)}) copy-start(bf16[4,512,1024]{2,1,0:T(8,128)(2,1)} %param.27) | copy-start | bytes 12582916
  95.8 3.9 %copy-start.10 = (s32[4]{0:T(128)S(1)}, s32[4]{0:T(128)}, u32[]{:S(2)}) copy-start(s32[4]{0:T(128)} %param.16) | copy-start | bytes 52
  102.6 9.7 %copy-start = (bf16[16,80,1024]{2,1,0:T(8,128)(2,1)}, bf16[16,80,1024]{2,1,0:T(8,128)(2,1)S(1)}, u32[]{:S(2)}) copy-start(bf16[16,80,1024]{2,1,0:T(8,128)(2,1)S(1)} %all-to-all-done.2) | copy-start | bytes 7864324
  112.3 28.5 %all-to-all-start.3 = ((bf16[32,16,1536]{2,1,0:T(8,128)(2,1)}), bf16[32,16,1536]{2,1,0:T(8,128)(2,1)S(1)}, u32[]{:S(2)}, u32[]{:S(2)}) async-start(bf16[32,16,1536]{2,1,0:T(8,128)(2,1)} %bitcast.163), calls=%async_computation.3 | async-start | bytes 3145728 | tf_op jit(solution)/shard_map/all_to_all | solution.py:313
  117.0 4.6 %copy-start.4 = (bf16[256,8,8,128]{3,2,1,0:T(8,128)(2,1)S(1)}, bf16[256,8,8,128]{3,2,1,0:T(8,128)(2,1)}, u32[]{:S(2)}) copy-start(bf16[256,8,8,128]{3,2,1,0:T(8,128)(2,1)} %copy.185) | copy-start | bytes 12582916
  123.8 36.8 %collective-permute-start.7 = (bf16[512,1024]{1,0:T(8,128)(2,1)}, bf16[512,1024]{1,0:T(8,128)(2,1)}, u32[]{:S(2)}, u32[]{:S(2)}) collective-permute-start(bf16[512,1024]{1,0:T(8,128)(2,1)} %collective-permute-done.6.rest_2_), channel_id=1, source_target_pairs={{0,1},{1,0},{2,3},{3,2},{4,5},{5,4},{6,7},{7,6},{8,9},{9,8},{10,11... | collective-permute-start | bytes 3145736 | tf_op jit(solution)/shard_map/ppermute | solution.py:84
  146.8 1.8 copy-start.5
  155.4 22.5 %all-to-all-start.4 = ((bf16[32,16,1024]{2,1,0:T(8,128)(2,1)}), bf16[32,16,1024]{2,1,0:T(8,128)(2,1)S(1)}, u32[]{:S(2)}, u32[]{:S(2)}) async-start(bf16[32,16,1024]{2,1,0:T(8,128)(2,1)} %bitcast.169), calls=%async_computation.4 | async-start | bytes 2097152 | tf_op jit(solution)/shard_map/all_to_all | solution.py:333
  177.9 1.2 copy-start.1
  184.6 32.1 %all-to-all-start.5 = ((bf16[32,16,2048]{2,1,0:T(8,128)(2,1)}), bf16[32,16,2048]{2,1,0:T(8,128)(2,1)}, u32[]{:S(2)}, u32[]{:S(2)}) async-start(bf16[32,16,2048]{2,1,0:T(8,128)(2,1)} %bitcast.168), calls=%async_computation.5 | async-start | bytes 4194304 | tf_op jit(solution)/shard_map/all_to_all | solution.py:337

commit v3 on v2

--- a/solution.py
+++ b/solution.py
@@ -9,6 +9,7 @@
 HD = 128
 ROUND_ROWS = 72
 SENT_ROWS = 80
+CHIP_COUNT = 8
 
 norm_epsilon = 1e-06
 rope_base = 1000000.0
@@ -21,65 +22,6 @@
 EVERY = ("y", "zl", "zh", "x", "core")
 
 
-def rotate(features, positions):
-    head_width = features.shape[-1]
-    half_width = head_width // 2
-    frequency = rope_base ** (-(2.0 * jnp.arange(half_width, dtype=jnp.float32)) / head_width)
-    angles = positions.astype(jnp.float32)[..., None, None] * frequency
-    cosine = jnp.cos(angles)
-    sine_part = jnp.sin(angles)
-    leading = features[..., :half_width]
-    trailing = features[..., half_width:]
-    return jnp.concatenate(
-        [leading * cosine - trailing * sine_part, trailing * cosine + leading * sine_part], axis=-1
-    )
-
-
-def attend(rotated, fresh_keys, fresh_values, key_cache, value_cache, lengths):
-    seq_here, step_span, heads, head_width = rotated.shape
-    kv_heads = fresh_keys.shape[2]
-    group_size = heads // kv_heads
-    cache_len = key_cache.shape[1]
-    cache_keys = key_cache.reshape(seq_here, cache_len, kv_heads, head_width)
-    cache_values = value_cache.reshape(seq_here, cache_len, kv_heads, head_width)
-    grouped = rotated.reshape(seq_here, step_span, kv_heads, group_size, head_width)
-    score_scale = head_width ** (-0.5)
-    cached = (
-        jnp.einsum("skgrd,sjgd->skgrj", grouped, cache_keys, preferred_element_type=jnp.float32)
-        * score_scale
-    )
-    fresh_scores = (
-        jnp.einsum("skgrd,sjgd->skgrj", grouped, fresh_keys, preferred_element_type=jnp.float32)
-        * score_scale
-    )
-    cache_valid = (jnp.arange(cache_len, dtype=jnp.int32)[None, :] < lengths[:, None])[
-        :, None, None, None, :
-    ]
-    fresh_count = fresh_keys.shape[1]
-    fresh_valid = (
-        jnp.arange(fresh_count, dtype=jnp.int32)[None, :]
-        <= jnp.arange(step_span, dtype=jnp.int32)[:, None]
-    )[None, :, None, None, :]
-    row_top = jnp.maximum(
-        jnp.max(jnp.where(cache_valid, cached, masked_low), axis=-1),
-        jnp.max(jnp.where(fresh_valid, fresh_scores, masked_low), axis=-1),
-    )[..., None]
-    cache_exp = jnp.exp(jnp.where(cache_valid, cached - row_top, masked_low))
-    fresh_exp = jnp.exp(jnp.where(fresh_valid, fresh_scores - row_top, masked_low))
-    denominator = jnp.sum(cache_exp, axis=-1, keepdims=True) + jnp.sum(
-        fresh_exp, axis=-1, keepdims=True
-    )
-    cache_weights = (cache_exp / denominator).astype(jnp.bfloat16)
-    fresh_weights = (fresh_exp / denominator).astype(jnp.bfloat16)
-    attended = jnp.einsum(
-        "skgrj,sjgd->skgrd", cache_weights, cache_values, preferred_element_type=jnp.float32
-    )
-    attended = attended + jnp.einsum(
-        "skgrj,sjgd->skgrd", fresh_weights, fresh_values, preferred_element_type=jnp.float32
-    )
-    return attended.reshape(seq_here, step_span, heads * head_width).astype(jnp.bfloat16)
-
-
 def swap_cores(value):
     return lax.ppermute(value, "core", [(0, 1), (1, 0)])
 
@@ -90,6 +32,219 @@
 
 VMEM = pl.BlockSpec(memory_space=pltpu.VMEM)
 SMEM = pl.BlockSpec(memory_space=pltpu.SMEM)
+
+
+def lookup_kernel(place_ref, id_row_ref, id_col_ref, bias_ref, hold_ref, vocab_ref, *rest):
+    mine_ref, theirs_ref, rank_ref, list_ref, total_ref = rest
+    step = pl.program_id(0)
+    chip, core, first = place_ref[0], place_ref[2], place_ref[3]
+    planes, _, rows = id_row_ref.shape
+    span = vocab_ref.shape[0]
+    vocab_here = span * pl.num_programs(0)
+
+    @pl.when(step == 0)
+    def _():
+        total_ref[...] = jnp.zeros_like(total_ref)
+        across = lax.broadcasted_iota(jnp.int32, (rows, rows), 1)
+        down = lax.broadcasted_iota(jnp.int32, (rows, rows), 0)
+        slot = lax.broadcasted_iota(jnp.int32, (SENT_ROWS, rows), 0)
+        for plane in range(planes):
+            id_row = id_row_ref[plane]
+            id_col = id_col_ref[plane]
+            same = id_row == id_col
+            leader_row = jnp.min(jnp.where(same, down, rows), axis=0, keepdims=True)
+            leader_col = jnp.min(jnp.where(same, across, rows), axis=1, keepdims=True)
+            lead_col = leader_col == lax.broadcasted_iota(jnp.int32, (rows, 1), 0)
+            start_row = jnp.zeros_like(id_row)
+            start_col = jnp.zeros_like(id_col)
+            for other in range(1, CHIP_COUNT):
+                edge = other * 2 * vocab_here
+                start_row = start_row + (id_row >= edge).astype(jnp.int32)
+                start_col = start_col + (id_col >= edge).astype(jnp.int32)
+            key_col = jnp.where(lead_col, start_col, -1)
+            before = (key_col == start_row) & (down < leader_row)
+            rank = jnp.sum(before.astype(jnp.int32), axis=0, keepdims=True)
+            rank_ref[plane] = rank
+            offset = id_row - (2 * chip + core) * vocab_here
+            leads = leader_row == lax.broadcasted_iota(jnp.int32, (1, rows), 1)
+            listed = leads & (offset >= 0) & (offset < vocab_here)
+            wanted = jnp.where(listed, rank - first, -1)
+            chosen = (wanted == slot) & (slot < ROUND_ROWS)
+            list_ref[plane * SENT_ROWS : (plane + 1) * SENT_ROWS, :] = jnp.max(
+                jnp.where(chosen, offset, -1), axis=1, keepdims=True
+            )
+
+    entry = lax.broadcasted_iota(jnp.int32, (planes * SENT_ROWS, span), 1) + step * span
+    chosen = (entry == list_ref[...]).astype(jnp.bfloat16)
+    total_ref[...] += jnp.dot(chosen, vocab_ref[...], preferred_element_type=jnp.float32)
+
+    @pl.when(step == pl.num_programs(0) - 1)
+    def _():
+        for layer in range(planes // 2):
+            for side, target in ((0, mine_ref), (1, theirs_ref)):
+                plane = 2 * layer + (core + side) % 2
+                start = pl.multiple_of(plane * SENT_ROWS, SENT_ROWS)
+                target[layer] = (total_ref[pl.ds(start, SENT_ROWS), :] + bias_ref[...]).astype(
+                    jnp.bfloat16
+                )
+
+
+def look_up(place, plane_ids, bias_rows, held, embedding):
+    planes, rows = plane_ids.shape
+    vocab_here, width = embedding.shape
+    steps = 3
+    whole = lambda *dims: pl.BlockSpec(dims, lambda i: (0,) * len(dims))
+    return pl.pallas_call(
+        lookup_kernel,
+        out_shape=(
+            jax.ShapeDtypeStruct((planes // 2, SENT_ROWS, width), jnp.bfloat16),
+            jax.ShapeDtypeStruct((planes // 2, SENT_ROWS, width), jnp.bfloat16),
+            jax.ShapeDtypeStruct((planes, 1, rows), jnp.int32),
+        ),
+        grid=(steps,),
+        in_specs=[
+            SMEM,
+            whole(planes, 1, rows),
+            whole(planes, rows, 1),
+            whole(SENT_ROWS, width),
+            pl.BlockSpec(memory_space=pl.ANY),
+            pl.BlockSpec((vocab_here // steps, width), lambda i: (i, 0)),
+        ],
+        out_specs=(
+            whole(planes // 2, SENT_ROWS, width),
+            whole(planes // 2, SENT_ROWS, width),
+            whole(planes, 1, rows),
+        ),
+        scratch_shapes=[
+            pltpu.VMEM((planes * SENT_ROWS, 1), jnp.int32),
+            pltpu.VMEM((planes * SENT_ROWS, width), jnp.float32),
+        ],
+        compiler_params=pltpu.CompilerParams(vmem_limit_bytes=48 * 1024 * 1024),
+        name="look_up",
+    )(place, plane_ids.reshape(planes, 1, rows), plane_ids.reshape(planes, rows, 1), bias_rows, held, embedding)
+
+
+def attention_kernel(
+    arrived_ref, bias_ref, cosine_ref, sine_ref, length_ref, keys_ref, values_ref, *rest
+):
+    out_ref, new_keys_ref, new_values_ref, key_buf, value_buf, key_sem, value_sem = rest
+    groups, chips, rows, _ = arrived_ref.shape
+    seqs, cache_len, _ = keys_ref.shape
+    steps = rows // seqs
+    core_cols = bias_ref.shape[2] // 2
+    heads = out_ref.shape[3] // HD
+    half_heads = heads // 2
+    many = heads * rows
+    copies = []
+    for seq in range(seqs):
+        copies.append(pltpu.make_async_copy(keys_ref.at[seq], key_buf.at[seq], key_sem.at[seq]))
+        copies.append(
+            pltpu.make_async_copy(values_ref.at[seq], value_buf.at[seq], value_sem.at[seq])
+        )
+    for copy in copies:
+        copy.start()
+    square = None
+    for group in range(groups):
+        for chip in range(chips):
+            part = arrived_ref[group, chip, :, 2 * core_cols :].astype(jnp.float32)
+            square = part * part if square is None else square + part * part
+    width = groups * chips * square.shape[1]
+    scale = lax.rsqrt(jnp.sum(square, axis=1, keepdims=True) / width + norm_epsilon)
+    cosine = cosine_ref[...]
+    sine = sine_ref[...]
+    lane = lax.broadcasted_iota(jnp.int32, (rows, HD), 1)
+
+    def rotated(features):
+        return (features * cosine + pltpu.roll(features, HD // 2, 1) * sine).astype(jnp.bfloat16)
+
+    row_at = lax.broadcasted_iota(jnp.int32, (many, 1), 0) % rows
+    row_seq = row_at // steps
+    row_step = row_at % steps
+    fresh_at = lax.broadcasted_iota(jnp.int32, (many, rows), 1)
+    fresh_valid = (fresh_at // steps == row_seq) & (fresh_at % steps <= row_step)
+    cache_valid = lax.broadcasted_iota(jnp.int32, (many, cache_len), 1) < length_ref[...]
+    score_scale = HD ** (-0.5)
+    for copy in copies:
+        copy.wait()
+    for chip in range(chips):
+        span = slice(chip * HD, (chip + 1) * HD)
+        joined = arrived_ref[0, chip, :, : 2 * core_cols].astype(jnp.float32)
+        for group in range(1, groups):
+            joined = joined + arrived_ref[group, chip, :, : 2 * core_cols].astype(jnp.float32)
+        joined = (joined * scale + bias_ref[chip]).astype(jnp.bfloat16).astype(jnp.float32)
+        parts = []
+        for head in range(heads):
+            start = (head // half_heads) * core_cols + (head % half_heads) * HD
+            parts.append(rotated(joined[:, start : start + HD]))
+        queries = jnp.concatenate(parts, axis=0)
+        low = joined[:, core_cols - HD : core_cols]
+        high = joined[:, 2 * core_cols - HD :]
+        fresh_keys = rotated(jnp.where(lane < HD // 2, low, pltpu.roll(high, HD // 2, 1)))
+        fresh_values = jnp.where(lane < HD // 2, pltpu.roll(low, HD // 2, 1), high).astype(
+            jnp.bfloat16
+        )
+        new_keys_ref[:, span] = fresh_keys
+        new_values_ref[:, span] = fresh_values
+        scores = None
+        for seq in range(seqs):
+            found = lax.dot_general(
+                queries,
+                key_buf[seq, :, span],
+                (((1,), (1,)), ((), ())),
+                preferred_element_type=jnp.float32,
+            )
+            scores = found if scores is None else jnp.where(row_seq == seq, found, scores)
+        fresh_scores = lax.dot_general(
+            queries, fresh_keys, (((1,), (1,)), ((), ())), preferred_element_type=jnp.float32
+        )
+        scores = jnp.where(cache_valid, scores * score_scale, masked_low)
+        fresh_scores = jnp.where(fresh_valid, fresh_scores * score_scale, masked_low)
+        top = jnp.maximum(
+            jnp.max(scores, axis=1, keepdims=True), jnp.max(fresh_scores, axis=1, keepdims=True)
+        )
+        scores = jnp.exp(scores - top)
+        fresh_scores = jnp.exp(fresh_scores - top)
+        share = 1.0 / (
+            jnp.sum(scores, axis=1, keepdims=True) + jnp.sum(fresh_scores, axis=1, keepdims=True)
+        )
+        weights = (scores * share).astype(jnp.bfloat16)
+        fresh_weights = (fresh_scores * share).astype(jnp.bfloat16)
+        attended = jnp.dot(fresh_weights, fresh_values, preferred_element_type=jnp.float32)
+        for seq in range(seqs):
+            found = jnp.dot(
+                weights, value_buf[seq, :, span], preferred_element_type=jnp.float32
+            )
+            attended = attended + jnp.where(row_seq == seq, found, 0.0)
+        attended = attended.astype(jnp.bfloat16)
+        for head in range(heads):
+            piece = attended[head * rows : (head + 1) * rows]
+            for group in range(groups):
+                out_ref[group, chip, :, head * HD : (head + 1) * HD] = piece
+
+
+def attend(arrived, bias, cosine, sine, row_lengths, key_cache, value_cache):
+    groups, chips, rows, _ = arrived.shape
+    seqs, cache_len, kv_cols = key_cache.shape
+    heads = 8
+    anywhere = pl.BlockSpec(memory_space=pl.ANY)
+    return pl.pallas_call(
+        attention_kernel,
+        out_shape=(
+            jax.ShapeDtypeStruct((groups, chips, rows, heads * HD), jnp.bfloat16),
+            jax.ShapeDtypeStruct((rows, kv_cols), jnp.bfloat16),
+            jax.ShapeDtypeStruct((rows, kv_cols), jnp.bfloat16),
+        ),
+        in_specs=[VMEM] * 5 + [anywhere] * 2,
+        out_specs=(VMEM, VMEM, VMEM),
+        scratch_shapes=[
+            pltpu.VMEM(key_cache.shape, jnp.bfloat16),
+            pltpu.VMEM(key_cache.shape, jnp.bfloat16),
+            pltpu.SemaphoreType.DMA((seqs,)),
+            pltpu.SemaphoreType.DMA((seqs,)),
+        ],
+        compiler_params=pltpu.CompilerParams(vmem_limit_bytes=48 * 1024 * 1024),
+        name="attend",
+    )(arrived, bias, cosine, sine, row_lengths, key_cache, value_cache)
 
 
 def projection_kernel(place_ref, slot_ref, table_ref, gain_ref, *rest):
@@ -243,45 +398,20 @@
         .transpose(1, 3, 0, 2, 4)
         .reshape(4, plane_rows)
     )
-    holder = plane_ids // (2 * vocab_here)
-    spot = jnp.arange(plane_rows, dtype=jnp.int32)
-    same = plane_ids[:, :, None] == plane_ids[:, None, :]
-    leader = jnp.min(jnp.where(same, spot[None, None, :], plane_rows), axis=2)
-    leads = leader == spot[None, :]
-    before = (
-        leads[:, None, :]
-        & (holder[:, :, None] == holder[:, None, :])
-        & (spot[None, None, :] < leader[:, :, None])
-    )
-    rank = jnp.sum(before.astype(jnp.int32), axis=2)
-    rounds = jnp.max(rank) // ROUND_ROWS + 1
     own_plane = 2 * layer + core
-    own_holder = lax.dynamic_index_in_dim(holder, own_plane, 0, keepdims=False)
-    own_rank = lax.dynamic_index_in_dim(rank, own_plane, 0, keepdims=False)
-    own_offset = plane_ids - (2 * chip + core) * vocab_here
-    listed_here = leads & (own_offset >= 0) & (own_offset < vocab_here)
+    own_holder = lax.dynamic_index_in_dim(plane_ids, own_plane, 0, keepdims=False)
+    own_holder = own_holder // (2 * vocab_here)
     row_at = jnp.arange(SENT_ROWS, dtype=jnp.int32)
     bias_rows = jnp.where(
         row_at[:, None] == ROUND_ROWS + core,
         jnp.pad(own_bias, (0, width_here - core_cols))[None, :],
         jnp.zeros((), jnp.bfloat16),
-    )
+    ).astype(jnp.float32)
 
     def exchange(turn):
         first = turn * ROUND_ROWS
-        wanted_rank = jnp.where(row_at < ROUND_ROWS, first + row_at, -1)
-        wanted = listed_here[:, None, :] & (rank[:, None, :] == wanted_rank[None, :, None])
-        listed = jnp.max(jnp.where(wanted, own_offset[:, None, :], -1), axis=2)
-        picked = jnp.dot(
-            (
-                listed.reshape(-1, 1) == jnp.arange(vocab_here, dtype=jnp.int32)[None, :]
-            ).astype(jnp.bfloat16),
-            embedding,
-            preferred_element_type=jnp.float32,
-        ).astype(jnp.bfloat16)
-        picked = picked.reshape(2, 2, SENT_ROWS, width_here) + bias_rows
-        mine = jnp.where(core == 0, picked[:, 0], picked[:, 1])
-        theirs = jnp.where(core == 0, picked[:, 1], picked[:, 0])
+        turn_place = jnp.concatenate([place, jnp.asarray(first, jnp.int32).reshape(1)])
+        mine, theirs, rank = look_up(turn_place, plane_ids, bias_rows, both_layer, embedding)
         merged = mine + swap_cores(theirs)
         table = lax.all_to_all(
             jnp.broadcast_to(merged[:, None], (2, chips, SENT_ROWS, width_here)).reshape(
@@ -292,44 +422,44 @@
             concat_axis=0,
             tiled=True,
         ).reshape(2, chips * SENT_ROWS, width_here)
+        own_rank = lax.dynamic_index_in_dim(rank, own_plane, 0, keepdims=False).reshape(-1)
         here = (own_rank >= first) & (own_rank < first + ROUND_ROWS)
         slot = jnp.where(here, own_holder * SENT_ROWS + own_rank - first, -1)
-        return slot.reshape(plane_rows, 1), table
+        return slot.reshape(plane_rows, 1), table, jnp.max(rank) // ROUND_ROWS + 1
 
     near_gain = lax.dynamic_slice_in_dim(
         norm_gain, lax.axis_index("y") * 2 * width_here, 2 * width_here
     )
     near_gain = near_gain.reshape(2, 1, width_here).astype(jnp.float32)
-    slot, table = exchange(0)
+    slot, table, rounds = exchange(0)
     pair_bias = table[0].reshape(chips, SENT_ROWS, width_here)
     pair_bias = pair_bias[:, ROUND_ROWS : ROUND_ROWS + 2, :core_cols].astype(jnp.float32)
+    pair_bias = pair_bias.reshape(chips, 1, 2 * core_cols)
     payload = project(place, slot, table, near_gain, weights, chips)
 
     def further(turn, sofar):
-        turn_slot, turn_table = exchange(turn)
+        turn_slot, turn_table, _ = exchange(turn)
         return sofar + project(place, turn_slot, turn_table, near_gain, weights, chips)
 
     payload = lax.fori_loop(1, rounds, further, payload)
     arrived = lax.all_to_all(payload, PLANE, split_axis=0, concat_axis=0, tiled=True)
     arrived = arrived.reshape(groups, chips, rows_here, -1)
-    pair_cols = 2 * core_cols
-    inputs = arrived[..., pair_cols:].astype(jnp.float32)
-    square = jnp.sum(inputs * inputs, axis=(0, 1, 3))
-    scale = lax.rsqrt(square / norm_gain.shape[0] + norm_epsilon)
-    summed = jnp.sum(arrived[..., :pair_cols].astype(jnp.float32), axis=0)
-    summed = summed.reshape(chips, rows_here, 2, core_cols)
-    joined = (summed * scale[None, :, None, None] + pair_bias[:, None]).astype(jnp.bfloat16)
-    joined = joined.transpose(1, 0, 2, 3)
-    queries = joined[..., :q_cols].reshape(seq_here, step_count, -1, HD)
-    fresh_keys = joined[..., q_cols : q_cols + k_cols].reshape(seq_here, step_count, -1, HD)
-    fresh_values = joined[..., q_cols + k_cols :].reshape(seq_here, step_count, -1, HD)
-    positions = lengths[:, None] + jnp.arange(step_count, dtype=jnp.int32)[None, :]
-    rotated = rotate(queries.astype(jnp.float32), positions).astype(jnp.bfloat16)
-    new_keys = rotate(fresh_keys.astype(jnp.float32), positions).astype(jnp.bfloat16)
-    attended = attend(rotated, new_keys, fresh_values, key_cache, value_cache, lengths)
-
-    spread = attended.reshape(rows_here, chips, 2 * q_cols).transpose(1, 0, 2)
-    spread = jnp.broadcast_to(spread[None], (groups,) + spread.shape)
+    positions = (lengths[:, None] + jnp.arange(step_count, dtype=jnp.int32)[None, :]).reshape(-1)
+    frequency = rope_base ** (-(2.0 * jnp.arange(HD // 2, dtype=jnp.float32)) / HD)
+    angles = positions.astype(jnp.float32)[:, None] * frequency
+    cosine, sine = jnp.cos(angles), jnp.sin(angles)
+    kv_heads = key_cache.shape[2] // HD
+    row_lengths = jnp.tile(jnp.repeat(lengths, step_count), 8 * kv_heads // chips).reshape(-1, 1)
+    spread, new_keys, new_values = attend(
+        arrived,
+        pair_bias,
+        jnp.concatenate([cosine, cosine], axis=1),
+        jnp.concatenate([-sine, sine], axis=1),
+        row_lengths,
+        key_cache,
+        value_cache,
+    )
+
     gathered = lax.all_to_all(
         spread.reshape(parties, rows_here, 2 * q_cols), PLANE, split_axis=0, concat_axis=0, tiled=True
     ).reshape(plane_rows, 2 * q_cols)
@@ -339,7 +469,7 @@
     return (
         hidden.reshape(seq_here, step_count, -1),
         new_keys.reshape(seq_here, step_count, -1),
-        fresh_values.reshape(seq_here, step_count, -1),
+        new_values.reshape(seq_here, step_count, -1),
     )
 
 

time: 221 us -> 243 us (1.100)
  waiting for transfers between devices: 115 us -> 143 us
  Pallas kernels: 17.7 us -> 38.1 us
  matrix products: 16.9 us -> 0 us
  local copies, waits for them, and re-layouts: 25.6 us -> 10.3 us
  starting transfers between devices: 31.4 us -> 40.5 us
  other arithmetic: 10.5 us -> 6.51 us
    all_to_all x1, waiting for transfers between devices: 0.01 us -> 34.8 us  [exchange(): lax.all_to_all(jnp.broadcast_to(merged[:, None], (2, chips, SENT_ROWS, wi...]
    pallas_call x0 -> x2, Pallas kernels: none -> 20 us  [the longest x1 11.3 us: look_up(): pl.pallas_call(lookup_kernel, out_shape=(jax.ShapeDtypeStruct((planes //...]
    dot_general x5 -> x0, matrix products: 16.9 us -> none  [the longest x1 7.18 us: exchange(): jnp.dot((listed.reshape(-1, 1) == jnp.arange(vocab_here, dtype=jnp.int32)...]
    all_to_all x1, waiting for transfers between devices: 16 us -> 0.01 us  [per_device(): lax.all_to_all(payload, PLANE, split_axis=0, concat_axis=0, tiled=True)]
    all_to_all x1, waiting for transfers between devices: 9.22 us -> 21.3 us  [per_device(): lax.all_to_all(sent_ids, EVERY, split_axis=0, concat_axis=0, tiled=True)]
    unnamed x22 -> x18, local copies, waits for them, and re-layouts: 11 us -> 3.21 us
    ppermute x2, waiting for transfers between devices: 46.5 us -> 39.3 us  [swap_layers(): return lax.ppermute(value, 'zl', [(0, 1), (1, 0)])]
    reshape x3 -> x6, local copies, waits for them, and re-layouts: 6.93 us -> 2.3 us  [the longest x2 0.87 us: exchange(): lax.dynamic_index_in_dim(rank, own_plane, 0, keepdims=False).reshape(-1)]
  transfers between devices with their start and end apart: 12 -> 12, of which waited for: 5 -> 6; matrix products, arithmetic and copies ran while one was open for 17% -> 3% of each run, Pallas kernels for 4% -> 4%
where the time goes in v3:
time: 243 us; the launch traced here: 241 us
  waiting for transfers between devices  143 us (59%)
  starting transfers between devices  40.5 us (17%)
  Pallas kernels  38.1 us (16%)
  local copies, waits for them, and re-layouts  10.3 us (4%)
  other arithmetic  6.51 us (3%)
  between operations  2.94 us (1%)
    ppermute x2, waiting for transfers between devices, swap_layers(): return lax.ppermute(value, 'zl', [(0, 1), (1, 0)])  39.3 us
    all_to_all x1, waiting for transfers between devices, exchange(): lax.all_to_all(jnp.broadcast_to(merged[:, None], (2, chips, SENT_ROWS, wi...  34.8 us
    all_to_all x1, waiting for transfers between devices, per_device(): lax.all_to_all(branch, PLANE, split_axis=0, concat_axis=0, tiled=True)  27.5 us
    all_to_all x1, waiting for transfers between devices, per_device(): lax.all_to_all(sent_ids, EVERY, split_axis=0, concat_axis=0, tiled=True)  21.3 us
    all_to_all x1, waiting for transfers between devices, per_device(): lax.all_to_all(spread.reshape(parties, rows_here, 2 * q_cols), PLANE, spl...  18.5 us
    pallas_call x1, Pallas kernels, look_up(): pl.pallas_call(lookup_kernel, out_shape=(jax.ShapeDtypeStruct((planes //...  11.3 us
    all_to_all x1, starting transfers between devices, per_device(): lax.all_to_all(sent_ids, EVERY, split_axis=0, concat_axis=0, tiled=True)  10.6 us
    pallas_call x1, Pallas kernels, project(): pl.pallas_call(projection_kernel, out_shape=jax.ShapeDtypeStruct((rows, 2...  9.77 us
  transfers between devices with their start and end apart: 12, of which 6 were waited for; matrix products, arithmetic and copies ran while one was open for 3% of the time, Pallas kernels for 4%

profile of v3, /device:TPU:0, one launch (start us, length us, event | category | flops | bytes accessed | tf_op | source)
XLA Modules:
  0.0 241.3 jit_solution(14233190237823533622)
XLA Ops:
  0.7 1.1 copy.84
  1.8 1.1 copy.85
  2.9 2.5 %pad_maximum_fusion.rest_0_ = bf16[1024,640]{1,0:T(8,128)(2,1)} fusion(bf16[1024,64]{1,0:T(8,128)(2,1)S(1)} %copy.85, bf16[1024,64]{1,0:T(8,128)(2,1)S(1)} %copy.84, bf16[1024,512]{1,0:T(8,128)(2,1)} %param.19), kind=kLoop, calls=%fused_computation.6 | loop fusion | flops 3932160 | bytes 2621440 | tf_op jit(solution)/shard_map/concatenate | solution.py:384
  5.4 2.0 collective-permute-start.1
  7.4 0.1 broadcast_in_dim.54
  7.5 0.0 copy-done.9
  7.5 0.1 fusion.10
  7.6 0.1 select_convert_fusion.1.bias_ref
  7.7 0.7 broadcast_in_dim.55
  8.3 10.6 %all-to-all-start.1 = ((s32[128,1,16]{2,1,0:T(1,128)}), s32[128,1,16]{2,1,0:T(1,128)S(1)}, u32[]{:S(2)}, u32[]{:S(2)}) async-start(s32[128,1,16]{2,1,0:T(1,128)} %broadcast_in_dim.55), calls=%async_computation.1 | async-start | bytes 131072 | tf_op jit(solution)/shard_map/all_to_all | solution.py:395
  18.9 0.1 pad_add_fusion.2.place_ref
  19.0 21.3 %all-to-all-done.1 = s32[128,1,16]{2,1,0:T(1,128)S(1)} async-done(((s32[128,1,16]{2,1,0:T(1,128)}), s32[128,1,16]{2,1,0:T(1,128)S(1)}, u32[]{:S(2)}, u32[]{:S(2)}) %all-to-all-start.1) | async-done | bytes 8224 | tf_op jit(solution)/shard_map/all_to_all | solution.py:395
  40.3 0.6 reshape_reshape.16.id_col_ref
  40.9 0.1 reshape_reshape.12.id_row_ref
  41.0 0.0 collective-permute-done.1.hold_ref.rest_2_
  41.0 11.3 %look_up.4 = (bf16[2,80,1024]{2,1,0:T(8,128)(2,1)S(1)}, bf16[2,80,1024]{2,1,0:T(8,128)(2,1)S(1)}, s32[4,1,512]{2,1,0:T(1,128)S(1)}) custom-call(s32[4]{0:T(128)S(1)} %pad_add_fusion.2.place_ref, s32[4,1,512]{2,1,0:T(1,128)S(1)} %reshape_reshape.12.id_row_ref, s32[4,512,1]{2,1,0:T(8,128)S(1)} %reshape_reshape.16.id_col_ref, ...), custom_call_target="tpu_custom_call" | custom-call | tf_op jit(solution)/shard_map/look_up/pallas_call | solution.py:97
  52.3 0.1 collective-permute-start.2
  52.4 1.6 collective-permute-done.2
  54.0 0.1 add.108
  54.1 1.8 broadcast_in_dim.59
  55.9 4.5 %all-to-all-start.2 = ((bf16[16,80,1024]{2,1,0:T(8,128)(2,1)}), bf16[16,80,1024]{2,1,0:T(8,128)(2,1)S(1)}, u32[]{:S(2)}, u32[]{:S(2)}) async-start(bf16[16,80,1024]{2,1,0:T(8,128)(2,1)} %bitcast.60), calls=%async_computation.2 | async-start | bytes 5242880 | tf_op jit(solution)/shard_map/all_to_all | solution.py:416
  60.5 0.1 collective-permute-start.3
  60.5 0.5 collective-permute-start.4
  61.0 0.1 pad_add_fusion.1.place_ref
  61.1 0.7 dynamic-slice_convert_fusion
  61.8 0.1 reshape.284
  61.9 0.1 reshape_reshape.18
  62.0 0.2 copy.91
  62.3 0.1 copy.90
  62.4 0.6 reduce_max.8
  65.1 0.9 copy.87
  65.9 1.0 fusion.4.slot_ref
  67.0 0.0 collective-permute-done.3.rest_1_
  67.0 0.0 collective-permute-done.4.rest_3_
  67.0 34.8 %all-to-all-done.2 = bf16[16,80,1024]{2,1,0:T(8,128)(2,1)S(1)} async-done(((bf16[16,80,1024]{2,1,0:T(8,128)(2,1)}), bf16[16,80,1024]{2,1,0:T(8,128)(2,1)S(1)}, u32[]{:S(2)}, u32[]{:S(2)}) %all-to-all-start.2) | async-done | bytes 2621472 | tf_op jit(solution)/shard_map/all_to_all | solution.py:416
  101.8 9.8 %project.4 = bf16[512,1536]{1,0:T(8,128)(2,1)} custom-call(s32[3]{0:T(128)S(1)} %pad_add_fusion.1.place_ref, s32[512,1]{1,0:T(8,128)S(1)} %fusion.4.slot_ref, bf16[2,640,1024]{2,1,0:T(8,128)(2,1)S(1)} %bitcast.55, f32[2,1,1024]{2,1,0:T(1,128)S(1)} %bitcast.62, bf16[1024,640]{1,0:T(8,128)(2,1)} %pad_maximum_fusion.rest_0_, ...), custom_call_target="tpu_custom_call" | custom-call | tf_op jit(solution)/shard_map/project/pallas_call | solution.py:284
  111.6 7.3 %all-to-all-start.3 = ((bf16[32,16,1536]{2,1,0:T(8,128)(2,1)}), bf16[32,16,1536]{2,1,0:T(8,128)(2,1)S(1)}, u32[]{:S(2)}, u32[]{:S(2)}) async-start(bf16[32,16,1536]{2,1,0:T(8,128)(2,1)} %bitcast.59), calls=%async_computation.3 | async-start | bytes 3145728 | tf_op jit(solution)/shard_map/all_to_all | solution.py:445
  118.9 0.7 collective-permute-start.6
  119.6 0.0 collective-permute-start.5
  119.6 0.1 add.111
  119.7 0.1 add.112
  119.8 0.1 add.114
  119.9 0.1 reshape_tile.4.length_ref
  120.0 0.1 fusion.8
  120.1 0.1 pad_maximum_fusion.1
  120.2 39.3 %collective-permute-done.6.rest_2_ = bf16[512,1024]{1,0:T(8,128)(2,1)} collective-permute-done((bf16[512,1024]{1,0:T(8,128)(2,1)}, bf16[512,1024]{1,0:T(8,128)(2,1)}, u32[]{:S(2)}, u32[]{:S(2)}) %collective-permute-start.6) | collective-permute-done | bytes 1048608 | tf_op jit(solution)/shard_map/ppermute | solution.py:30
  159.5 0.0 collective-permute-start.7
  159.5 0.9 slice_convert_fusion
  160.4 0.1 reshape.298.bias_ref
  160.4 0.0 all-to-all-done.3
  160.4 8.7 %attend.1 = (bf16[4,8,16,1024]{3,2,1,0:T(8,128)(2,1)S(1)}, bf16[16,1024]{1,0:T(8,128)(2,1)S(1)}, bf16[16,1024]{1,0:T(8,128)(2,1)S(1)}) custom-call(bf16[4,8,16,1536]{3,2,1,0:T(8,128)(2,1)S(1)} %bitcast.53, f32[8,1,1280]{2,1,0:T(1,128)S(1)} %reshape.298.bias_ref, f32[16,128]{1,0:T(8,128)S(1)} %get-tuple-element.309.cosine_ref, ...), custom_call_target="tpu_custom_call" | custom-call | tf_op jit(solution)/shard_map/attend/pallas_call | solution.py:230
  169.2 0.0 copy-start.1
  169.2 1.0 copy-done.1
  170.2 9.3 %all-to-all-start.4 = ((bf16[32,16,1024]{2,1,0:T(8,128)(2,1)}), bf16[32,16,1024]{2,1,0:T(8,128)(2,1)S(1)}, u32[]{:S(2)}, u32[]{:S(2)}) async-start(bf16[32,16,1024]{2,1,0:T(8,128)(2,1)} %bitcast.57), calls=%async_computation.4 | async-start | bytes 2097152 | tf_op jit(solution)/shard_map/all_to_all | solution.py:463
  179.5 0.0 collective-permute-done.5.rest_1_
  179.5 0.0 collective-permute-done.7.rest_3_
  179.5 18.5 %all-to-all-done.4 = bf16[32,16,1024]{2,1,0:T(8,128)(2,1)S(1)} async-done(((bf16[32,16,1024]{2,1,0:T(8,128)(2,1)}), bf16[32,16,1024]{2,1,0:T(8,128)(2,1)S(1)}, u32[]{:S(2)}, u32[]{:S(2)}) %all-to-all-start.4) | async-done | bytes 1048608 | tf_op jit(solution)/shard_map/all_to_all | solution.py:463
  198.0 5.9 %branch.1 = bf16[512,2048]{1,0:T(8,128)(2,1)} custom-call(s32[3]{0:T(128)S(1)} %get-tuple-element.554, bf16[512,1024]{1,0:T(8,128)(2,1)S(1)} %bitcast.56, bf16[512,1024]{1,0:T(8,128)(2,1)} %rest_0_.1, bf16[512,1024]{1,0:T(8,128)(2,1)} %collective-permute-done.5.rest_1_, bf16[512,1024]{1,0:T(8,128)(2,1)} %collective-permute-done.6.rest_2_, ...), custom_call_target="tpu_custom_call" | custom-call | tf_op jit(solution)/shard_map/branch/pallas_call | solution.py:318
  203.9 5.4 %all-to-all-start.5 = ((bf16[32,16,2048]{2,1,0:T(8,128)(2,1)}), bf16[32,16,2048]{2,1,0:T(8,128)(2,1)}, u32[]{:S(2)}, u32[]{:S(2)}) async-start(bf16[32,16,2048]{2,1,0:T(8,128)(2,1)} %bitcast.61), calls=%async_computation.5 | async-start | bytes 4194304 | tf_op jit(solution)/shard_map/all_to_all | solution.py:467
  209.3 0.6 reshape.294
  209.9 0.6 reshape.295
  210.5 27.5 %all-to-all-done.5 = bf16[32,16,2048]{2,1,0:T(8,128)(2,1)} async-done(((bf16[32,16,2048]{2,1,0:T(8,128)(2,1)}), bf16[32,16,2048]{2,1,0:T(8,128)(2,1)}, u32[]{:S(2)}, u32[]{:S(2)}) %all-to-all-start.5) | async-done | bytes 2097184 | tf_op jit(solution)/shard_map/all_to_all | solution.py:467
  238.0 2.5 %hidden_sum.1 = bf16[16,8192]{1,0:T(8,128)(2,1)S(1)} custom-call(bf16[4,8,16,2048]{3,2,1,0:T(8,128)(2,1)} %bitcast.17.branch_ref, bf16[4,8,16,1536]{3,2,1,0:T(8,128)(2,1)S(1)} %bitcast.54), custom_call_target="tpu_custom_call" | custom-call | tf_op jit(solution)/shard_map/hidden_sum/pallas_call | solution.py:343
  240.5 0.8 reshape.293
  (25 shorter events, 0.1 us)
Async XLA Ops:
  0.6 6.7 %copy-start.5 = (s32[4,4]{1,0:T(4,128)S(1)}, s32[4,4]{1,0:T(4,128)}, u32[]{:S(2)}) copy-start(s32[4,4]{1,0:T(4,128)} %param.15) | copy-start | bytes 196
  0.6 6.8 %copy-start.6 = (bf16[512]{0:T(512)(128)(2,1)S(1)}, bf16[512]{0:T(512)(128)(2,1)}, u32[]{:S(2)}) copy-start(bf16[512]{0:T(512)(128)(2,1)} %param.22) | copy-start | bytes 3076
  0.7 6.8 %copy-start.9 = (bf16[64]{0:T(256)(128)(2,1)S(1)}, bf16[64]{0:T(256)(128)(2,1)}, u32[]{:S(2)}) copy-start(bf16[64]{0:T(256)(128)(2,1)} %param.23) | copy-start | bytes 388
  0.7 6.8 %copy-start.8 = (bf16[64]{0:T(256)(128)(2,1)S(1)}, bf16[64]{0:T(256)(128)(2,1)}, u32[]{:S(2)}) copy-start(bf16[64]{0:T(256)(128)(2,1)} %param.24) | copy-start | bytes 388
  5.4 35.6 %collective-permute-start.1 = (bf16[1024,640]{1,0:T(8,128)(2,1)}, bf16[1024,640]{1,0:T(8,128)(2,1)S(1)}, u32[]{:S(2)}, u32[]{:S(2)}) collective-permute-start(bf16[1024,640]{1,0:T(8,128)(2,1)} %pad_maximum_fusion.rest_0_), channel_id=1, source_target_pairs={{0,16},{16,0},{1,17},{17,1},{2,18},{18,2},{3,19},{19,3},{4,20},{20... | collective-permute-start | bytes 3932168 | tf_op jit(solution)/shard_map/ppermute | solution.py:30
  8.3 32.0 %all-to-all-start.1 = ((s32[128,1,16]{2,1,0:T(1,128)}), s32[128,1,16]{2,1,0:T(1,128)S(1)}, u32[]{:S(2)}, u32[]{:S(2)}) async-start(s32[128,1,16]{2,1,0:T(1,128)} %broadcast_in_dim.55), calls=%async_computation.1 | async-start | bytes 131072 | tf_op jit(solution)/shard_map/all_to_all | solution.py:395
  41.0 11.3 %copy-start.2 = (bf16[1024,640]{1,0:T(8,128)(2,1)}, bf16[1024,640]{1,0:T(8,128)(2,1)S(1)}, u32[]{:S(2)}) copy-start(bf16[1024,640]{1,0:T(8,128)(2,1)S(1)} %collective-permute-done.1.hold_ref.rest_2_) | copy-start | bytes 3932164
  52.3 1.7 collective-permute-start.2
  55.9 45.9 %all-to-all-start.2 = ((bf16[16,80,1024]{2,1,0:T(8,128)(2,1)}), bf16[16,80,1024]{2,1,0:T(8,128)(2,1)S(1)}, u32[]{:S(2)}, u32[]{:S(2)}) async-start(bf16[16,80,1024]{2,1,0:T(8,128)(2,1)} %bitcast.60), calls=%async_computation.2 | async-start | bytes 5242880 | tf_op jit(solution)/shard_map/all_to_all | solution.py:416
  60.5 6.5 %collective-permute-start.3 = (bf16[1024,640]{1,0:T(8,128)(2,1)}, bf16[1024,640]{1,0:T(8,128)(2,1)}, u32[]{:S(2)}, u32[]{:S(2)}) collective-permute-start(bf16[1024,640]{1,0:T(8,128)(2,1)} %pad_maximum_fusion.rest_0_), channel_id=1, source_target_pairs={{0,1},{1,0},{2,3},{3,2},{4,5},{5,4},{6,7},{7,6},{8,9},{9,8},{10,11... | collective-permute-start | bytes 3932168 | tf_op jit(solution)/shard_map/ppermute | solution.py:26
  60.5 6.4 %collective-permute-start.4 = (bf16[1024,640]{1,0:T(8,128)(2,1)}, bf16[1024,640]{1,0:T(8,128)(2,1)}, u32[]{:S(2)}, u32[]{:S(2)}) collective-permute-start(bf16[1024,640]{1,0:T(8,128)(2,1)} %copy-done.2), channel_id=1, source_target_pairs={{0,1},{1,0},{2,3},{3,2},{4,5},{5,4},{6,7},{7,6},{8,9},{9,8},{10,11... | collective-permute-start | bytes 3932168 | tf_op jit(solution)/shard_map/ppermute | solution.py:26
  101.8 9.8 %copy-start = (bf16[16,80,1024]{2,1,0:T(8,128)(2,1)}, bf16[16,80,1024]{2,1,0:T(8,128)(2,1)S(1)}, u32[]{:S(2)}) copy-start(bf16[16,80,1024]{2,1,0:T(8,128)(2,1)S(1)} %all-to-all-done.2) | copy-start | bytes 7864324
  111.6 8.0 %copy-start.7 = (s32[4]{0:T(128)S(1)}, s32[4]{0:T(128)}, u32[]{:S(2)}) copy-start(s32[4]{0:T(128)} %param.16) | copy-start | bytes 52
  111.6 48.8 %all-to-all-start.3 = ((bf16[32,16,1536]{2,1,0:T(8,128)(2,1)}), bf16[32,16,1536]{2,1,0:T(8,128)(2,1)S(1)}, u32[]{:S(2)}, u32[]{:S(2)}) async-start(bf16[32,16,1536]{2,1,0:T(8,128)(2,1)} %bitcast.59), calls=%async_computation.3 | async-start | bytes 3145728 | tf_op jit(solution)/shard_map/all_to_all | solution.py:445
  118.9 40.5 %collective-permute-start.6 = (bf16[512,1024]{1,0:T(8,128)(2,1)}, bf16[512,1024]{1,0:T(8,128)(2,1)}, u32[]{:S(2)}, u32[]{:S(2)}) collective-permute-start(bf16[512,1024]{1,0:T(8,128)(2,1)} %rest_0_.1), channel_id=1, source_target_pairs={{0,16},{16,0},{1,17},{17,1},{2,18},{18,2},{3,19},{19,3},{4,20},{20... | collective-permute-start | bytes 3145736 | tf_op jit(solution)/shard_map/ppermute | solution.py:30
  119.6 59.9 %collective-permute-start.5 = (bf16[512,1024]{1,0:T(8,128)(2,1)}, bf16[512,1024]{1,0:T(8,128)(2,1)}, u32[]{:S(2)}, u32[]{:S(2)}) collective-permute-start(bf16[512,1024]{1,0:T(8,128)(2,1)} %rest_0_.1), channel_id=1, source_target_pairs={{0,1},{1,0},{2,3},{3,2},{4,5},{5,4},{6,7},{7,6},{8,9},{9,8},{10,11... | collective-permute-start | bytes 3145736 | tf_op jit(solution)/shard_map/ppermute | solution.py:26
  159.5 20.1 %collective-permute-start.7 = (bf16[512,1024]{1,0:T(8,128)(2,1)}, bf16[512,1024]{1,0:T(8,128)(2,1)}, u32[]{:S(2)}, u32[]{:S(2)}) collective-permute-start(bf16[512,1024]{1,0:T(8,128)(2,1)} %collective-permute-done.6.rest_2_), channel_id=1, source_target_pairs={{0,1},{1,0},{2,3},{3,2},{4,5},{5,4},{6,7},{7,6},{8,9},{9,8},{10,11... | collective-permute-start | bytes 3145736 | tf_op jit(solution)/shard_map/ppermute | solution.py:26
  169.2 1.0 copy-start.1
  170.2 27.8 %all-to-all-start.4 = ((bf16[32,16,1024]{2,1,0:T(8,128)(2,1)}), bf16[32,16,1024]{2,1,0:T(8,128)(2,1)S(1)}, u32[]{:S(2)}, u32[]{:S(2)}) async-start(bf16[32,16,1024]{2,1,0:T(8,128)(2,1)} %bitcast.57), calls=%async_computation.4 | async-start | bytes 2097152 | tf_op jit(solution)/shard_map/all_to_all | solution.py:463
  203.9 34.1 %all-to-all-start.5 = ((bf16[32,16,2048]{2,1,0:T(8,128)(2,1)}), bf16[32,16,2048]{2,1,0:T(8,128)(2,1)}, u32[]{:S(2)}, u32[]{:S(2)}) async-start(bf16[32,16,2048]{2,1,0:T(8,128)(2,1)} %bitcast.61), calls=%async_computation.5 | async-start | bytes 4194304 | tf_op jit(solution)/shard_map/all_to_all | solution.py:467

commit v4 on v3

v4 whole, which is shorter than its diff:
```python
import jax
import jax.numpy as jnp
from jax import lax
from jax.experimental import pallas as pl
from jax.experimental.pallas import tpu as pltpu
from jax.sharding import Mesh
from jax.sharding import PartitionSpec as P

HD = 128
ROUND_ROWS = 126
SENT_ROWS = 128
CHIP_COUNT = 8

norm_epsilon = 1e-06
rope_base = 1000000.0
masked_low = -1e30

DP = ("y", "zl")
CHIPS = ("zh", "x")
LAYER = ("zl", "zh", "x")
PLANE = ("y", "zl", "zh", "x")
EVERY = ("y", "zl", "zh", "x", "core")


def swap_cores(value):
    return lax.ppermute(value, "core", [(0, 1), (1, 0)])


def shift(value, count, step):
    return lax.ppermute(value, "y", [(i, (i + step) % count) for i in range(count)])


VMEM = pl.BlockSpec(memory_space=pltpu.VMEM)
SMEM = pl.BlockSpec(memory_space=pltpu.SMEM)


def lookup_kernel(place_ref, id_row_ref, id_col_ref, bias_ref, vocab_ref, *rest):
    mine_ref, theirs_ref, rank_ref, list_ref, total_ref = rest
    step = pl.program_id(0)
    chip, core, first = place_ref[0], place_ref[1], place_ref[3]
    planes, _, rows = id_row_ref.shape
    span = vocab_ref.shape[0]
    vocab_here = span * pl.num_programs(0)

    @pl.when(step == 0)
    def _():
        total_ref[...] = jnp.zeros_like(total_ref)
        across = lax.broadcasted_iota(jnp.int32, (rows, rows), 1)
        down = lax.broadcasted_iota(jnp.int32, (rows, rows), 0)
        earlier = across < down
        slot = lax.broadcasted_iota(jnp.int32, (SENT_ROWS, rows), 0)
        for plane in range(planes):
            id_row = id_row_ref[plane]
            id_col = id_col_ref[plane]
            again = jnp.where((id_row == id_col) & earlier, 1, 0)
            key_col = jnp.where(jnp.max(again, axis=1, keepdims=True) == 0, id_col, -1)
            edge_row = jnp.zeros_like(id_row)
            for other in range(1, CHIP_COUNT):
                edge = other * 2 * vocab_here
                edge_row = jnp.where(id_row >= edge, edge, edge_row)
            before = (key_col >= edge_row) & (key_col < id_row)
            rank = jnp.sum(before.astype(jnp.int32), axis=0, keepdims=True)
            rank_ref[plane] = rank
            offset = id_row - (2 * chip + core) * vocab_here
            listed = (offset >= 0) & (offset < vocab_here)
            wanted = jnp.where(listed, rank - first, -1)
            chosen = (wanted == slot) & (slot < ROUND_ROWS)
            list_ref[plane * SENT_ROWS : (plane + 1) * SENT_ROWS, :] = jnp.max(
                jnp.where(chosen, offset, -1), axis=1, keepdims=True
            )

    entry = lax.broadcasted_iota(jnp.int32, (planes * SENT_ROWS, span), 1) + step * span
    chosen = (entry == list_ref[...]).astype(jnp.bfloat16)
    total_ref[...] += jnp.dot(chosen, vocab_ref[...], preferred_element_type=jnp.float32)

    @pl.when(step == pl.num_programs(0) - 1)
    def _():
        for side, target in ((0, mine_ref), (1, theirs_ref)):
            plane = (core + side) % 2
            start = pl.multiple_of(plane * SENT_ROWS, SENT_ROWS)
            target[...] = (total_ref[pl.ds(start, SENT_ROWS), :] + bias_ref[...]).astype(
                jnp.bfloat16
            )


def look_up(place, plane_ids, bias_rows, embedding):
    planes, rows = plane_ids.shape
    vocab_here, width = embedding.shape
    steps = 3
    whole = lambda *dims: pl.BlockSpec(dims, lambda i: (0,) * len(dims))
    return pl.pallas_call(
        lookup_kernel,
        out_shape=(
            jax.ShapeDtypeStruct((SENT_ROWS, width), jnp.bfloat16),
            jax.ShapeDtypeStruct((SENT_ROWS, width), jnp.bfloat16),
            jax.ShapeDtypeStruct((planes, 1, rows), jnp.int32),
        ),
        grid=(steps,),
        in_specs=[
            SMEM,
            whole(planes, 1, rows),
            whole(planes, rows, 1),
            whole(SENT_ROWS, width),
            pl.BlockSpec((vocab_here // steps, width), lambda i: (i, 0)),
        ],
        out_specs=(
            whole(SENT_ROWS, width),
            whole(SENT_ROWS, width),
            whole(planes, 1, rows),
        ),
        scratch_shapes=[
            pltpu.VMEM((planes * SENT_ROWS, 1), jnp.int32),
            pltpu.VMEM((planes * SENT_ROWS, width), jnp.float32),
        ],
        compiler_params=pltpu.CompilerParams(vmem_limit_bytes=48 * 1024 * 1024),
        name="look_up",
    )(place, plane_ids.reshape(planes, 1, rows), plane_ids.reshape(planes, rows, 1), bias_rows, embedding)


def attention_kernel(
    arrived_ref, bias_ref, cosine_ref, sine_ref, length_ref, keys_ref, values_ref, *rest
):
    out_ref, new_keys_ref, new_values_ref, key_buf, value_buf, key_sem, value_sem = rest
    groups, chips, rows, _ = arrived_ref.shape
    seqs, cache_len, _ = keys_ref.shape
    steps = rows // seqs
    core_cols = bias_ref.shape[2] // 2
    heads = out_ref.shape[3] // HD
    half_heads = heads // 2
    many = heads * rows
    copies = []
    for seq in range(seqs):
        copies.append(pltpu.make_async_copy(keys_ref.at[seq], key_buf.at[seq], key_sem.at[seq]))
        copies.append(
            pltpu.make_async_copy(values_ref.at[seq], value_buf.at[seq], value_sem.at[seq])
        )
    for copy in copies:
        copy.start()
    square = None
    for group in range(groups):
        for chip in range(chips):
            part = arrived_ref[group, chip, :, 2 * core_cols :].astype(jnp.float32)
            square = part * part if square is None else square + part * part
    width = groups * chips * square.shape[1]
    scale = lax.rsqrt(jnp.sum(square, axis=1, keepdims=True) / width + norm_epsilon)
    cosine = cosine_ref[...]
    sine = sine_ref[...]
    lane = lax.broadcasted_iota(jnp.int32, (rows, HD), 1)

    def rotated(features):
        return (features * cosine + pltpu.roll(features, HD // 2, 1) * sine).astype(jnp.bfloat16)

    row_at = lax.broadcasted_iota(jnp.int32, (many, 1), 0) % rows
    row_seq = row_at // steps
    row_step = row_at % steps
    fresh_at = lax.broadcasted_iota(jnp.int32, (many, rows), 1)
    fresh_valid = (fresh_at // steps == row_seq) & (fresh_at % steps <= row_step)
    cache_valid = lax.broadcasted_iota(jnp.int32, (many, cache_len), 1) < length_ref[...]
    score_scale = HD ** (-0.5)
    for copy in copies:
        copy.wait()
    for chip in range(chips):
        span = slice(chip * HD, (chip + 1) * HD)
        joined = arrived_ref[0, chip, :, : 2 * core_cols].astype(jnp.float32)
        for group in range(1, groups):
            joined = joined + arrived_ref[group, chip, :, : 2 * core_cols].astype(jnp.float32)
        joined = (joined * scale + bias_ref[chip]).astype(jnp.bfloat16).astype(jnp.float32)
        parts = []
        for head in range(heads):
            start = (head // half_heads) * core_cols + (head % half_heads) * HD
            parts.append(rotated(joined[:, start : start + HD]))
        queries = jnp.concatenate(parts, axis=0)
        low = joined[:, core_cols - HD : core_cols]
        high = joined[:, 2 * core_cols - HD :]
        fresh_keys = rotated(jnp.where(lane < HD // 2, low, pltpu.roll(high, HD // 2, 1)))
        fresh_values = jnp.where(lane < HD // 2, pltpu.roll(low, HD // 2, 1), high).astype(
            jnp.bfloat16
        )
        new_keys_ref[:, span] = fresh_keys
        new_values_ref[:, span] = fresh_values
        scores = None
        for seq in range(seqs):
            found = lax.dot_general(
                queries,
                key_buf[seq, :, span],
                (((1,), (1,)), ((), ())),
                preferred_element_type=jnp.float32,
            )
            scores = found if scores is None else jnp.where(row_seq == seq, found, scores)
        fresh_scores = lax.dot_general(
            queries, fresh_keys, (((1,), (1,)), ((), ())), preferred_element_type=jnp.float32
        )
        scores = jnp.where(cache_valid, scores * score_scale, masked_low)
        fresh_scores = jnp.where(fresh_valid, fresh_scores * score_scale, masked_low)
        top = jnp.maximum(
            jnp.max(scores, axis=1, keepdims=True), jnp.max(fresh_scores, axis=1, keepdims=True)
        )
        scores = jnp.exp(scores - top)
        fresh_scores = jnp.exp(fresh_scores - top)
        share = 1.0 / (
            jnp.sum(scores, axis=1, keepdims=True) + jnp.sum(fresh_scores, axis=1, keepdims=True)
        )
        weights = (scores * share).astype(jnp.bfloat16)
        fresh_weights = (fresh_scores * share).astype(jnp.bfloat16)
        attended = jnp.dot(fresh_weights, fresh_values, preferred_element_type=jnp.float32)
        for seq in range(seqs):
            found = jnp.dot(
                weights, value_buf[seq, :, span], preferred_element_type=jnp.float32
            )
            attended = attended + jnp.where(row_seq == seq, found, 0.0)
        attended = attended.astype(jnp.bfloat16)
        for head in range(heads):
            piece = attended[head * rows : (head + 1) * rows]
            for group in range(out_ref.shape[0]):
                out_ref[group, chip, :, head * HD : (head + 1) * HD] = piece


def attend(arrived, bias, cosine, sine, row_lengths, key_cache, value_cache, copies):
    _, chips, rows, _ = arrived.shape
    seqs, cache_len, kv_cols = key_cache.shape
    heads = 8
    anywhere = pl.BlockSpec(memory_space=pl.ANY)
    return pl.pallas_call(
        attention_kernel,
        out_shape=(
            jax.ShapeDtypeStruct((copies, chips, rows, heads * HD), jnp.bfloat16),
            jax.ShapeDtypeStruct((rows, kv_cols), jnp.bfloat16),
            jax.ShapeDtypeStruct((rows, kv_cols), jnp.bfloat16),
        ),
        in_specs=[VMEM] * 5 + [anywhere] * 2,
        out_specs=(VMEM, VMEM, VMEM),
        scratch_shapes=[
            pltpu.VMEM(key_cache.shape, jnp.bfloat16),
            pltpu.VMEM(key_cache.shape, jnp.bfloat16),
            pltpu.SemaphoreType.DMA((seqs,)),
            pltpu.SemaphoreType.DMA((seqs,)),
        ],
        compiler_params=pltpu.CompilerParams(vmem_limit_bytes=48 * 1024 * 1024),
        name="attend",
    )(arrived, bias, cosine, sine, row_lengths, key_cache, value_cache)


def projection_kernel(place_ref, slot_ref, table_ref, gain_ref, mine_ref, theirs_ref, *rest):
    out_ref, wide_ref, weight_buf, sem = rest[-4:]
    chip, core = place_ref[0], place_ref[1]
    rows = slot_ref.shape[0]
    table_rows = table_ref.shape[0]
    cols = mine_ref.shape[1]
    step = pl.program_id(0)
    copies = [
        pltpu.make_async_copy(source, weight_buf.at[side], sem.at[side])
        for side, source in enumerate((mine_ref, theirs_ref))
    ]

    @pl.when(step == 0)
    def _():
        for copy in copies:
            copy.start()

    chosen = (
        lax.broadcasted_iota(jnp.int32, (rows, table_rows), 1) == slot_ref[...]
    ).astype(jnp.bfloat16)
    found = jnp.dot(chosen, table_ref[...], preferred_element_type=jnp.float32)
    wide_ref[...] = found.astype(jnp.bfloat16)
    gained = (found * gain_ref[...]).astype(jnp.bfloat16)

    @pl.when(step == 0)
    def _():
        for copy in copies:
            copy.wait()

    for side in range(2):
        product = jnp.dot(gained, weight_buf[side], preferred_element_type=jnp.float32)
        where = pl.multiple_of(((core + side) % 2) * cols, cols)
        out_ref[:, pl.ds(where, cols)] = product.astype(jnp.bfloat16)
    strip = out_ref.shape[1] - 2 * cols
    out_ref[:, 2 * cols :] = wide_ref[:, pl.ds(pl.multiple_of(chip * strip, strip), strip)]


def project(place, slot, table, gain, mine, theirs, held, chips):
    rows = slot.shape[0]
    table_rows, width = table.shape
    cols = mine.shape[1]
    out_cols = 2 * cols + width // chips
    block = 256
    anywhere = pl.BlockSpec(memory_space=pl.ANY)
    return pl.pallas_call(
        projection_kernel,
        out_shape=jax.ShapeDtypeStruct((rows, out_cols), jnp.bfloat16),
        grid=(rows // block,),
        in_specs=[
            SMEM,
            pl.BlockSpec((block, 1), lambda i: (i, 0)),
            pl.BlockSpec((table_rows, width), lambda i: (0, 0)),
            pl.BlockSpec((1, width), lambda i: (0, 0)),
        ]
        + [anywhere] * (2 + len(held)),
        out_specs=pl.BlockSpec((block, out_cols), lambda i: (i, 0)),
        scratch_shapes=[
            pltpu.VMEM((block, width), jnp.bfloat16),
            pltpu.VMEM((2, width, cols), jnp.bfloat16),
            pltpu.SemaphoreType.DMA((2,)),
        ],
        compiler_params=pltpu.CompilerParams(vmem_limit_bytes=48 * 1024 * 1024),
        name="project",
    )(place, slot, table, gain, mine, theirs, *held)


def branch_kernel(place_ref, rows_ref, *rest):
    weight_refs, (out_ref, weight_buf, sem) = rest[:-3], rest[-3:]
    core, line = place_ref[1], place_ref[2]
    depth, width = weight_refs[0].shape
    count = len(weight_refs) // 2
    copies = [
        pltpu.make_async_copy(source, weight_buf.at[k], sem.at[k])
        for k, source in enumerate(weight_refs)
    ]
    for copy in copies:
        copy.start()
    for turn in range(count):
        block = pl.multiple_of(((line + count - turn) % count) * width, width)
        parts = []
        for side in range(2):
            where = pl.multiple_of(((core + side) % 2) * depth, depth)
            copies[2 * turn + side].wait()
            parts.append(
                jnp.dot(
                    rows_ref[:, pl.ds(where, depth)],
                    weight_buf[2 * turn + side],
                    preferred_element_type=jnp.float32,
                )
            )
        out_ref[:, pl.ds(block, width)] = (parts[0] + parts[1]).astype(jnp.bfloat16)


def branch_out(place, rows, weights):
    count = len(weights)
    depth, width = weights[0].shape
    return pl.pallas_call(
        branch_kernel,
        out_shape=jax.ShapeDtypeStruct((rows.shape[0], count // 2 * width), jnp.bfloat16),
        in_specs=[SMEM, VMEM] + [pl.BlockSpec(memory_space=pl.ANY)] * count,
        out_specs=VMEM,
        scratch_shapes=[
            pltpu.VMEM((count, depth, width), jnp.bfloat16),
            pltpu.SemaphoreType.DMA((count,)),
        ],
        compiler_params=pltpu.CompilerParams(vmem_limit_bytes=48 * 1024 * 1024),
        name="branch",
    )(place, rows, *weights)


def hidden_kernel(branch_ref, strip_ref, out_ref):
    layers, chips, _, width = branch_ref.shape
    strip = strip_ref.shape[3]
    for layer in range(layers):
        for part in range(width // strip):
            span = slice(part * strip, (part + 1) * strip)
            total = strip_ref[layer, part].astype(jnp.float32)
            for chip in range(chips):
                total = total + branch_ref[layer, chip, :, span].astype(jnp.float32)
            start = layer * width + part * strip
            out_ref[:, start : start + strip] = total.astype(jnp.bfloat16)


def hidden_sum(branches, arrived, width):
    layers, chips, rows, all_width = branches.shape
    groups = all_width // width
    strip = width // chips
    last = arrived.shape[3] // strip - 1
    return pl.pallas_call(
        hidden_kernel,
        out_shape=jax.ShapeDtypeStruct((rows, layers * all_width), jnp.bfloat16),
        grid=(groups,),
        in_specs=[
            pl.BlockSpec((layers, chips, rows, width), lambda y: (0, 0, 0, y)),
            pl.BlockSpec((layers, chips, rows, strip), lambda y: (y, 0, 0, last)),
        ],
        out_specs=pl.BlockSpec((rows, layers * width), lambda y: (0, y)),
        compiler_params=pltpu.CompilerParams(vmem_limit_bytes=48 * 1024 * 1024),
        name="hidden_sum",
    )(branches, arrived)


def per_device(
    token_ids,
    lengths,
    embedding,
    norm_gain,
    q_weight,
    k_weight,
    v_weight,
    q_bias,
    k_bias,
    v_bias,
    o_weight,
    key_cache,
    value_cache,
):
    seq_here, step_count = token_ids.shape
    rows_here = seq_here * step_count
    vocab_here, width_here = embedding.shape
    lines = lax.axis_size("y")
    line = lax.axis_index("y")
    replicas = lax.axis_size(DP)
    chips = lax.axis_size(CHIPS)
    chip = lax.axis_index(CHIPS)
    core = lax.axis_index("core")
    parties = replicas * chips
    plane_rows = parties * rows_here
    place = jnp.stack([chip, core, line]).astype(jnp.int32)

    both = jnp.concatenate([q_weight, k_weight, v_weight], axis=1)
    both_other = swap_cores(both)
    o_lines = [o_weight, shift(o_weight, lines, 1), None, shift(o_weight, lines, -1)]
    o_lines[2] = shift(o_lines[1], lines, 1)
    o_held = (o_lines[1], o_lines[3])
    o_weights = [piece for own in o_lines for piece in (own, swap_cores(own))]
    own_bias = jnp.concatenate([q_bias, k_bias, v_bias])
    core_cols = own_bias.shape[0]
    q_cols = q_bias.shape[0]

    sent_ids = jnp.broadcast_to(token_ids.reshape(1, rows_here), (parties * 2, rows_here))
    every_id = lax.all_to_all(sent_ids, EVERY, split_axis=0, concat_axis=0, tiled=True)
    plane_ids = every_id.reshape(parties, 2, rows_here).transpose(1, 0, 2).reshape(2, plane_rows)
    own_holder = lax.dynamic_index_in_dim(plane_ids, core, 0, keepdims=False) // (2 * vocab_here)
    row_at = jnp.arange(SENT_ROWS, dtype=jnp.int32)
    bias_rows = jnp.where(
        row_at[:, None] == ROUND_ROWS + core,
        jnp.pad(own_bias, (0, width_here - core_cols))[None, :],
        jnp.zeros((), jnp.bfloat16),
    ).astype(jnp.float32)

    def exchange(turn):
        first = turn * ROUND_ROWS
        turn_place = jnp.concatenate([place, jnp.asarray(first, jnp.int32).reshape(1)])
        mine, theirs, rank = look_up(turn_place, plane_ids, bias_rows, embedding)
        merged = mine + swap_cores(theirs)
        table = lax.all_to_all(
            jnp.broadcast_to(merged[None], (chips, SENT_ROWS, width_here)),
            CHIPS,
            split_axis=0,
            concat_axis=0,
            tiled=True,
        ).reshape(chips * SENT_ROWS, width_here)
        own_rank = lax.dynamic_index_in_dim(rank, core, 0, keepdims=False).reshape(-1)
        here = (own_rank >= first) & (own_rank < first + ROUND_ROWS)
        slot = jnp.where(here, own_holder * SENT_ROWS + own_rank - first, -1)
        return slot.reshape(plane_rows, 1), table, jnp.max(rank) // ROUND_ROWS + 1

    own_gain = lax.dynamic_slice_in_dim(norm_gain, lax.axis_index(DP) * width_here, width_here)
    own_gain = own_gain.reshape(1, width_here).astype(jnp.float32)
    slot, table, rounds = exchange(0)
    pair_bias = table.reshape(chips, SENT_ROWS, width_here)
    pair_bias = pair_bias[:, ROUND_ROWS : ROUND_ROWS + 2, :core_cols].astype(jnp.float32)
    pair_bias = pair_bias.reshape(chips, 1, 2 * core_cols)
    payload = project(place, slot, table, own_gain, both, both_other, o_held, chips)

    def further(turn, sofar):
        turn_slot, turn_table, _ = exchange(turn)
        return sofar + project(
            place, turn_slot, turn_table, own_gain, both, both_other, (), chips
        )

    payload = lax.fori_loop(1, rounds, further, payload)
    arrived = lax.all_to_all(payload, PLANE, split_axis=0, concat_axis=0, tiled=True)
    arrived = arrived.reshape(replicas, chips, rows_here, -1)
    positions = (lengths[:, None] + jnp.arange(step_count, dtype=jnp.int32)[None, :]).reshape(-1)
    frequency = rope_base ** (-(2.0 * jnp.arange(HD // 2, dtype=jnp.float32)) / HD)
    angles = positions.astype(jnp.float32)[:, None] * frequency
    cosine, sine = jnp.cos(angles), jnp.sin(angles)
    kv_heads = key_cache.shape[2] // HD
    row_lengths = jnp.tile(jnp.repeat(lengths, step_count), 8 * kv_heads // chips).reshape(-1, 1)
    spread, new_keys, new_values = attend(
        arrived,
        pair_bias,
        jnp.concatenate([cosine, cosine], axis=1),
        jnp.concatenate([-sine, sine], axis=1),
        row_lengths,
        key_cache,
        value_cache,
        replicas // lines,
    )

    gathered = lax.all_to_all(
        spread.reshape(-1, rows_here, 2 * q_cols), LAYER, split_axis=0, concat_axis=0, tiled=True
    ).reshape(-1, 2 * q_cols)
    branch = branch_out(place, gathered, o_weights)
    branches = lax.all_to_all(branch, LAYER, split_axis=0, concat_axis=0, tiled=True)
    branches = branches.reshape(replicas // lines, chips, rows_here, -1)
    hidden = hidden_sum(branches, arrived, o_weight.shape[1])
    return (
        hidden.reshape(seq_here, step_count, -1),
        new_keys.reshape(seq_here, step_count, -1),
        new_values.reshape(seq_here, step_count, -1),
    )


def solution(mesh):
    fine = Mesh(mesh.devices.reshape(4, 2, 2, 4, 2), EVERY)
    tensor = CHIPS + ("core",)
    placed = (
        P(EVERY, None),
        P(EVERY),
        P(tensor, DP),
        P(),
        P(DP, tensor),
        P(DP, tensor),
        P(DP, tensor),
        P(tensor),
        P(tensor),
        P(tensor),
        P(tensor, DP),
        P(EVERY, None, None),
        P(EVERY, None, None),
    )
    return jax.shard_map(
        per_device,
        mesh=fine,
        in_specs=placed,
        out_specs=(
            P(EVERY, None, None),
            P(EVERY, None, None),
            P(EVERY, None, None),
        ),
        check_vma=False,
    )
```

time: 243 us -> 229 us (0.942)
  waiting for transfers between devices: 143 us -> 121 us
  local copies, waits for them, and re-layouts: 10.3 us -> 16.3 us
    all_to_all x3, waiting for transfers between devices: 80.8 us -> 41.6 us  [the longest x1 29.5 us: per_device(): lax.all_to_all(branch, LAYER, split_axis=0, concat_axis=0, tiled=True)]
    ppermute x2 -> x3, waiting for transfers between devices: 39.3 us -> 68.9 us  [shift(): lax.ppermute(value, 'y', [(i, (i + step) % count) for i in range(count)])]
    all_to_all x1, waiting for transfers between devices: 21.3 us -> 9.17 us  [per_device(): lax.all_to_all(sent_ids, EVERY, split_axis=0, concat_axis=0, tiled=True)]
    all_to_all x3, starting transfers between devices: 19.2 us -> 14.9 us  [the longest x1 6.7 us: per_device(): lax.all_to_all(spread.reshape(-1, rows_here, 2 * q_cols), LAYER, split_ax...]
    unnamed x18, local copies, waits for them, and re-layouts: 3.21 us -> 7.52 us
    all_to_all x1, starting transfers between devices: 7.3 us -> 10.6 us  [per_device(): lax.all_to_all(payload, PLANE, split_axis=0, concat_axis=0, tiled=True)]
    ppermute x2 -> x3, starting transfers between devices: 2.7 us -> 4.9 us  [shift(): lax.ppermute(value, 'y', [(i, (i + step) % count) for i in range(count)])]
  transfers between devices with their start and end apart: 12 -> 14, of which waited for: 6 -> 6; matrix products, arithmetic and copies ran while one was open for 3% -> 6% of each run, Pallas kernels for 4% -> 4%
where the time goes in v4:
time: 229 us; the launch traced here: 228 us
  waiting for transfers between devices  121 us (53%)
  starting transfers between devices  42.4 us (19%)
  Pallas kernels  36.6 us (16%)
  local copies, waits for them, and re-layouts  16.3 us (7%)
  other arithmetic  8.17 us (4%)
  between operations  2.93 us (1%)
    ppermute x3, waiting for transfers between devices, shift(): lax.ppermute(value, 'y', [(i, (i + step) % count) for i in range(count)])  68.9 us
    all_to_all x1, waiting for transfers between devices, per_device(): lax.all_to_all(branch, LAYER, split_axis=0, concat_axis=0, tiled=True)  29.5 us
    all_to_all x1, waiting for transfers between devices, per_device(): lax.all_to_all(spread.reshape(-1, rows_here, 2 * q_cols), LAYER, split_ax...  12.2 us
    all_to_all x1, starting transfers between devices, per_device(): lax.all_to_all(sent_ids, EVERY, split_axis=0, concat_axis=0, tiled=True)  11.1 us
    all_to_all x1, starting transfers between devices, per_device(): lax.all_to_all(payload, PLANE, split_axis=0, concat_axis=0, tiled=True)  10.6 us
    pallas_call x1, Pallas kernels, project(): pl.pallas_call(projection_kernel, out_shape=jax.ShapeDtypeStruct((rows, o...  9.55 us
    pallas_call x1, Pallas kernels, look_up(): pl.pallas_call(lookup_kernel, out_shape=(jax.ShapeDtypeStruct((SENT_ROWS,...  9.42 us
    all_to_all x1, waiting for transfers between devices, per_device(): lax.all_to_all(sent_ids, EVERY, split_axis=0, concat_axis=0, tiled=True)  9.17 us
  transfers between devices with their start and end apart: 14, of which 6 were waited for; matrix products, arithmetic and copies ran while one was open for 6% of the time, Pallas kernels for 4%

profile of v4, /device:TPU:0, one launch (start us, length us, event | category | flops | bytes accessed | tf_op | source)
XLA Modules:
  0.0 227.9 jit_solution(8827909006013922472)
XLA Ops:
  0.7 0.8 broadcast_in_dim.54
  1.4 0.8 fusion.10
  2.2 0.1 select_convert_fusion.1.bias_ref
  2.3 0.7 broadcast_in_dim.55
  3.0 11.1 %all-to-all-start.1 = ((s32[128,1,16]{2,1,0:T(1,128)}), s32[128,1,16]{2,1,0:T(1,128)S(1)}, u32[]{:S(2)}, u32[]{:S(2)}) async-start(s32[128,1,16]{2,1,0:T(1,128)} %broadcast_in_dim.55), calls=%async_computation.1 | async-start | bytes 131072 | tf_op jit(solution)/shard_map/all_to_all | solution.py:424
  14.1 0.1 pad_add_fusion.2.place_ref
  14.2 9.2 %all-to-all-done.1 = s32[128,1,16]{2,1,0:T(1,128)S(1)} async-done(((s32[128,1,16]{2,1,0:T(1,128)}), s32[128,1,16]{2,1,0:T(1,128)S(1)}, u32[]{:S(2)}, u32[]{:S(2)}) %all-to-all-start.1) | async-done | bytes 8224 | tf_op jit(solution)/shard_map/all_to_all | solution.py:424
  23.4 0.6 reshape_reshape.17.id_col_ref
  24.0 0.1 reshape_reshape.16.id_row_ref
  24.1 9.4 %look_up.4 = (bf16[128,1024]{1,0:T(8,128)(2,1)S(1)}, bf16[128,1024]{1,0:T(8,128)(2,1)S(1)}, s32[2,1,1024]{2,1,0:T(1,128)S(1)}) custom-call(s32[4]{0:T(128)S(1)} %pad_add_fusion.2.place_ref, s32[2,1,1024]{2,1,0:T(1,128)S(1)} %reshape_reshape.16.id_row_ref, s32[2,1024,1]{2,1,0:T(8,128)S(1)} %reshape_reshape.17.id_col_ref, ...), custom_call_target="tpu_custom_call" | custom-call | tf_op jit(solution)/shard_map/look_up/pallas_call | solution.py:91
  33.5 0.1 collective-permute-start.1
  33.6 1.5 collective-permute-done.1
  35.1 0.1 add.107
  35.2 1.6 broadcast_in_dim.59
  36.8 3.7 %all-to-all-start.2 = ((bf16[8,128,1024]{2,1,0:T(8,128)(2,1)}), bf16[8,128,1024]{2,1,0:T(8,128)(2,1)S(1)}, u32[]{:S(2)}, u32[]{:S(2)}) async-start(bf16[8,128,1024]{2,1,0:T(8,128)(2,1)} %broadcast_in_dim.59), calls=%async_computation.2 | async-start | bytes 4194304 | tf_op jit(solution)/shard_map/all_to_all | solution.py:439
  40.6 1.1 copy.80
  41.6 1.7 copy.81
  43.4 2.3 %pad_maximum_fusion.mine_ref = bf16[1024,640]{1,0:T(8,128)(2,1)} fusion(bf16[1024,64]{1,0:T(8,128)(2,1)} %copy.81, bf16[1024,64]{1,0:T(8,128)(2,1)S(1)} %copy.80, bf16[1024,512]{1,0:T(8,128)(2,1)S(1)} %copy-done.8), kind=kLoop, calls=%fused_computation.6 | loop fusion | flops 3932160 | bytes 2621440 | tf_op jit(solution)/shard_map/concatenate | solution.py:413
  45.7 0.1 collective-permute-start.2
  45.8 0.7 collective-permute-start.3
  46.5 2.6 %collective-permute-start.4 = (bf16[512,1024]{1,0:T(8,128)(2,1)}, bf16[512,1024]{1,0:T(8,128)(2,1)}, u32[]{:S(2)}, u32[]{:S(2)}) collective-permute-start(bf16[512,1024]{1,0:T(8,128)(2,1)} %rest_0_.1), channel_id=1, source_target_pairs={{0,96},{32,0},{64,32},{96,64},{1,97},{33,1},{65,33},{97,65},{2,98}... | collective-permute-start | bytes 3145736 | tf_op jit(solution)/shard_map/ppermute | solution.py:30
  49.1 0.7 dynamic-slice_convert_fusion
  49.8 0.1 pad_add_fusion.1.place_ref
  49.8 0.1 reshape.262
  49.9 0.6 reduce_max.8
  52.5 0.1 reshape_reshape.20
  52.6 1.1 copy.73
  53.8 0.3 copy.77
  54.1 1.0 copy.76
  55.1 2.2 fusion.4.slot_ref
  57.4 15.3 %collective-permute-done.3.rest_0_.rest_2_ = bf16[512,1024]{1,0:T(8,128)(2,1)S(1)} collective-permute-done((bf16[512,1024]{1,0:T(8,128)(2,1)}, bf16[512,1024]{1,0:T(8,128)(2,1)S(1)}, u32[]{:S(2)}, u32[]{:S(2)}) %collective-permute-start.3) | collective-permute-done | bytes 1048608 | tf_op jit(solution)/shard_map/ppermute | solution.py:30
  72.7 0.0 collective-permute-done.4.rest_1_.rest_6_
  72.7 0.0 collective-permute-done.2.theirs_ref
  72.7 1.4 copy-done.3
  74.1 9.6 %project.4 = bf16[1024,1408]{1,0:T(8,128)(2,1)} custom-call(s32[3]{0:T(128)S(1)} %pad_add_fusion.1.place_ref, s32[1024,1]{1,0:T(8,128)S(1)} %copy-done.3, bf16[1024,1024]{1,0:T(8,128)(2,1)S(1)} %bitcast.40, f32[1,1024]{1,0:T(1,128)S(1)} %bitcast.47, bf16[1024,640]{1,0:T(8,128)(2,1)} %pad_maximum_fusion.mine_ref, ...), custom_call_target="tpu_custom_call" | custom-call | tf_op jit(solution)/shard_map/project/pallas_call | solution.py:287
  83.7 0.2 while.14
  83.9 0.0 copy-start.9
  83.9 10.6 %all-to-all-start.3 = ((bf16[64,16,1408]{2,1,0:T(8,128)(2,1)}), bf16[64,16,1408]{2,1,0:T(8,128)(2,1)S(1)}, u32[]{:S(2)}, u32[]{:S(2)}) async-start(bf16[64,16,1408]{2,1,0:T(8,128)(2,1)} %bitcast.43), calls=%async_computation.3 | async-start | bytes 5767168 | tf_op jit(solution)/shard_map/all_to_all | solution.py:466
  94.5 1.6 collective-permute-start.7
  96.2 0.1 add.111
  96.3 0.1 add.112
  96.4 0.1 add.114
  96.4 0.1 reshape_tile.4.length_ref
  96.6 0.6 collective-permute-start.6
  97.2 0.1 collective-permute-start.9
  97.2 53.6 %collective-permute-done.7.rest_4_ = bf16[512,1024]{1,0:T(8,128)(2,1)} collective-permute-done((bf16[512,1024]{1,0:T(8,128)(2,1)}, bf16[512,1024]{1,0:T(8,128)(2,1)}, u32[]{:S(2)}, u32[]{:S(2)}) %collective-permute-start.7) | collective-permute-done | bytes 1048608 | tf_op jit(solution)/shard_map/ppermute | solution.py:30
  150.8 0.0 collective-permute-start.8
  150.8 0.1 fusion.8
  151.0 0.1 pad_maximum_fusion.1
  151.0 0.9 slice_convert_fusion
  151.9 0.1 reshape.275.bias_ref
  152.0 8.7 %attend.1 = (bf16[2,8,16,1024]{3,2,1,0:T(8,128)(2,1)S(1)}, bf16[16,1024]{1,0:T(8,128)(2,1)S(1)}, bf16[16,1024]{1,0:T(8,128)(2,1)S(1)}) custom-call(bf16[8,8,16,1408]{3,2,1,0:T(8,128)(2,1)S(1)} %bitcast.38, f32[8,1,1280]{2,1,0:T(1,128)S(1)} %reshape.275.bias_ref, f32[16,128]{1,0:T(8,128)S(1)} %get-tuple-element.260.cosine_ref, ...), custom_call_target="tpu_custom_call" | custom-call | tf_op jit(solution)/shard_map/attend/pallas_call | solution.py:223
  160.8 0.8 copy-done.5
  161.6 6.7 %all-to-all-start.4 = ((bf16[16,16,1024]{2,1,0:T(8,128)(2,1)}), bf16[16,16,1024]{2,1,0:T(8,128)(2,1)S(1)}, u32[]{:S(2)}, u32[]{:S(2)}) async-start(bf16[16,16,1024]{2,1,0:T(8,128)(2,1)} %bitcast.42), calls=%async_computation.4 | async-start | bytes 1048576 | tf_op jit(solution)/shard_map/all_to_all | solution.py:485
  168.3 12.2 %all-to-all-done.4 = bf16[16,16,1024]{2,1,0:T(8,128)(2,1)S(1)} async-done(((bf16[16,16,1024]{2,1,0:T(8,128)(2,1)}), bf16[16,16,1024]{2,1,0:T(8,128)(2,1)S(1)}, u32[]{:S(2)}, u32[]{:S(2)}) %all-to-all-start.4) | async-done | bytes 524320 | tf_op jit(solution)/shard_map/all_to_all | solution.py:485
  180.5 1.2 copy-done.2
  181.7 1.2 copy-done.4
  183.0 6.4 %branch.1 = bf16[256,4096]{1,0:T(8,128)(2,1)} custom-call(s32[3]{0:T(128)S(1)} %get-tuple-element.483, bf16[256,1024]{1,0:T(8,128)(2,1)S(1)} %bitcast.41, bf16[512,1024]{1,0:T(8,128)(2,1)S(1)} %copy-done.4, bf16[512,1024]{1,0:T(8,128)(2,1)} %collective-permute-done.5.rest_1_, bf16[512,1024]{1,0:T(8,128)(2,1)S(1)} %copy-done.2, ...), custom_call_target="tpu_custom_call" | custom-call | tf_op jit(solution)/shard_map/branch/pallas_call | solution.py:339
  189.4 4.4 %all-to-all-start.5 = ((bf16[16,16,4096]{2,1,0:T(8,128)(2,1)}), bf16[16,16,4096]{2,1,0:T(8,128)(2,1)}, u32[]{:S(2)}, u32[]{:S(2)}) async-start(bf16[16,16,4096]{2,1,0:T(8,128)(2,1)} %bitcast.44), calls=%async_computation.5 | async-start | bytes 4194304 | tf_op jit(solution)/shard_map/all_to_all | solution.py:489
  193.8 0.6 reshape.271
  194.5 0.6 reshape.272
  195.1 29.5 %all-to-all-done.5 = bf16[16,16,4096]{2,1,0:T(8,128)(2,1)} async-done(((bf16[16,16,4096]{2,1,0:T(8,128)(2,1)}), bf16[16,16,4096]{2,1,0:T(8,128)(2,1)}, u32[]{:S(2)}, u32[]{:S(2)}) %all-to-all-start.5) | async-done | bytes 2097184 | tf_op jit(solution)/shard_map/all_to_all | solution.py:489
  224.6 2.5 %hidden_sum.1 = bf16[16,8192]{1,0:T(8,128)(2,1)S(1)} custom-call(bf16[2,8,16,4096]{3,2,1,0:T(8,128)(2,1)} %bitcast.16.branch_ref, bf16[8,8,16,1408]{3,2,1,0:T(8,128)(2,1)S(1)} %bitcast.39), custom_call_target="tpu_custom_call" | custom-call | tf_op jit(solution)/shard_map/hidden_sum/pallas_call | solution.py:371
  227.1 0.8 reshape.270
  (29 shorter events, 0.2 us)
Async XLA Ops:
  3.0 20.4 %all-to-all-start.1 = ((s32[128,1,16]{2,1,0:T(1,128)}), s32[128,1,16]{2,1,0:T(1,128)S(1)}, u32[]{:S(2)}, u32[]{:S(2)}) async-start(s32[128,1,16]{2,1,0:T(1,128)} %broadcast_in_dim.55), calls=%async_computation.1 | async-start | bytes 131072 | tf_op jit(solution)/shard_map/all_to_all | solution.py:424
  33.5 1.6 collective-permute-start.1
  36.8 6.6 %copy-start.8 = (bf16[1024,512]{1,0:T(8,128)(2,1)S(1)}, bf16[1024,512]{1,0:T(8,128)(2,1)}, u32[]{:S(2)}) copy-start(bf16[1024,512]{1,0:T(8,128)(2,1)} %param.19) | copy-start | bytes 3145732
  36.8 35.9 %all-to-all-start.2 = ((bf16[8,128,1024]{2,1,0:T(8,128)(2,1)}), bf16[8,128,1024]{2,1,0:T(8,128)(2,1)S(1)}, u32[]{:S(2)}, u32[]{:S(2)}) async-start(bf16[8,128,1024]{2,1,0:T(8,128)(2,1)} %broadcast_in_dim.59), calls=%async_computation.2 | async-start | bytes 4194304 | tf_op jit(solution)/shard_map/all_to_all | solution.py:439
  45.7 27.0 %collective-permute-start.2 = (bf16[1024,640]{1,0:T(8,128)(2,1)}, bf16[1024,640]{1,0:T(8,128)(2,1)}, u32[]{:S(2)}, u32[]{:S(2)}) collective-permute-start(bf16[1024,640]{1,0:T(8,128)(2,1)} %pad_maximum_fusion.mine_ref), channel_id=1, source_target_pairs={{0,1},{1,0},{2,3},{3,2},{4,5},{5,4},{6,7},{7,6},{8,9},{9,8},{10,11... | collective-permute-start | bytes 3932168 | tf_op jit(solution)/shard_map/ppermute | solution.py:26
  45.8 26.9 %collective-permute-start.3 = (bf16[512,1024]{1,0:T(8,128)(2,1)}, bf16[512,1024]{1,0:T(8,128)(2,1)S(1)}, u32[]{:S(2)}, u32[]{:S(2)}) collective-permute-start(bf16[512,1024]{1,0:T(8,128)(2,1)} %rest_0_.1), channel_id=1, source_target_pairs={{0,32},{32,64},{64,96},{96,0},{1,33},{33,65},{65,97},{97,1},{2,34}... | collective-permute-start | bytes 3145736 | tf_op jit(solution)/shard_map/ppermute | solution.py:30
  46.5 26.2 %collective-permute-start.4 = (bf16[512,1024]{1,0:T(8,128)(2,1)}, bf16[512,1024]{1,0:T(8,128)(2,1)}, u32[]{:S(2)}, u32[]{:S(2)}) collective-permute-start(bf16[512,1024]{1,0:T(8,128)(2,1)} %rest_0_.1), channel_id=1, source_target_pairs={{0,96},{32,0},{64,32},{96,64},{1,97},{33,1},{65,33},{97,65},{2,98}... | collective-permute-start | bytes 3145736 | tf_op jit(solution)/shard_map/ppermute | solution.py:30
  72.7 11.0 %copy-start.1 = (bf16[512,1024]{1,0:T(8,128)(2,1)}, bf16[512,1024]{1,0:T(8,128)(2,1)S(1)}, u32[]{:S(2)}) copy-start(bf16[512,1024]{1,0:T(8,128)(2,1)S(1)} %collective-permute-done.3.rest_0_.rest_2_) | copy-start | bytes 3145732
  72.7 11.0 %copy-start = (bf16[8,128,1024]{2,1,0:T(8,128)(2,1)}, bf16[8,128,1024]{2,1,0:T(8,128)(2,1)S(1)}, u32[]{:S(2)}) copy-start(bf16[8,128,1024]{2,1,0:T(8,128)(2,1)S(1)} %all-to-all-done.2) | copy-start | bytes 6291460
  72.7 1.4 copy-start.3
  83.9 12.3 %copy-start.9 = (s32[4]{0:T(128)S(1)}, s32[4]{0:T(128)}, u32[]{:S(2)}) copy-start(s32[4]{0:T(128)} %param.16) | copy-start | bytes 52
  83.9 68.1 %all-to-all-start.3 = ((bf16[64,16,1408]{2,1,0:T(8,128)(2,1)}), bf16[64,16,1408]{2,1,0:T(8,128)(2,1)S(1)}, u32[]{:S(2)}, u32[]{:S(2)}) async-start(bf16[64,16,1408]{2,1,0:T(8,128)(2,1)} %bitcast.43), calls=%async_computation.3 | async-start | bytes 5767168 | tf_op jit(solution)/shard_map/all_to_all | solution.py:466
  94.5 56.3 %collective-permute-start.7 = (bf16[512,1024]{1,0:T(8,128)(2,1)}, bf16[512,1024]{1,0:T(8,128)(2,1)}, u32[]{:S(2)}, u32[]{:S(2)}) collective-permute-start(bf16[512,1024]{1,0:T(8,128)(2,1)} %copy-done.1), channel_id=1, source_target_pairs={{0,32},{32,64},{64,96},{96,0},{1,33},{33,65},{65,97},{97,1},{2,34}... | collective-permute-start | bytes 3145736 | tf_op jit(solution)/shard_map/ppermute | solution.py:30
  96.2 72.1 %collective-permute-start.5 = (bf16[512,1024]{1,0:T(8,128)(2,1)}, bf16[512,1024]{1,0:T(8,128)(2,1)}, u32[]{:S(2)}, u32[]{:S(2)}) collective-permute-start(bf16[512,1024]{1,0:T(8,128)(2,1)} %rest_0_.1), channel_id=1, source_target_pairs={{0,1},{1,0},{2,3},{3,2},{4,5},{5,4},{6,7},{7,6},{8,9},{9,8},{10,11... | collective-permute-start | bytes 3145736 | tf_op jit(solution)/shard_map/ppermute | solution.py:26
  96.6 71.7 %collective-permute-start.6 = (bf16[512,1024]{1,0:T(8,128)(2,1)}, bf16[512,1024]{1,0:T(8,128)(2,1)}, u32[]{:S(2)}, u32[]{:S(2)}) collective-permute-start(bf16[512,1024]{1,0:T(8,128)(2,1)} %copy-done.1), channel_id=1, source_target_pairs={{0,1},{1,0},{2,3},{3,2},{4,5},{5,4},{6,7},{7,6},{8,9},{9,8},{10,11... | collective-permute-start | bytes 3145736 | tf_op jit(solution)/shard_map/ppermute | solution.py:26
  97.2 71.2 %collective-permute-start.9 = (bf16[512,1024]{1,0:T(8,128)(2,1)}, bf16[512,1024]{1,0:T(8,128)(2,1)}, u32[]{:S(2)}, u32[]{:S(2)}) collective-permute-start(bf16[512,1024]{1,0:T(8,128)(2,1)} %collective-permute-done.4.rest_1_.rest_6_), channel_id=1, source_target_pairs={{0,1},{1,0},{2,3},{3,2},{4,5},{5,4},{6,7},{7,6},{8,9},{9,8},{10,11... | collective-permute-start | bytes 3145736 | tf_op jit(solution)/shard_map/ppermute | solution.py:26
  150.8 17.5 %collective-permute-start.8 = (bf16[512,1024]{1,0:T(8,128)(2,1)}, bf16[512,1024]{1,0:T(8,128)(2,1)}, u32[]{:S(2)}, u32[]{:S(2)}) collective-permute-start(bf16[512,1024]{1,0:T(8,128)(2,1)} %collective-permute-done.7.rest_4_), channel_id=1, source_target_pairs={{0,1},{1,0},{2,3},{3,2},{4,5},{5,4},{6,7},{7,6},{8,9},{9,8},{10,11... | collective-permute-start | bytes 3145736 | tf_op jit(solution)/shard_map/ppermute | solution.py:26
  160.8 0.8 copy-start.5
  161.6 18.9 %all-to-all-start.4 = ((bf16[16,16,1024]{2,1,0:T(8,128)(2,1)}), bf16[16,16,1024]{2,1,0:T(8,128)(2,1)S(1)}, u32[]{:S(2)}, u32[]{:S(2)}) async-start(bf16[16,16,1024]{2,1,0:T(8,128)(2,1)} %bitcast.42), calls=%async_computation.4 | async-start | bytes 1048576 | tf_op jit(solution)/shard_map/all_to_all | solution.py:485
  180.5 1.2 copy-start.2
  181.7 1.2 copy-start.4
  189.4 35.2 %all-to-all-start.5 = ((bf16[16,16,4096]{2,1,0:T(8,128)(2,1)}), bf16[16,16,4096]{2,1,0:T(8,128)(2,1)}, u32[]{:S(2)}, u32[]{:S(2)}) async-start(bf16[16,16,4096]{2,1,0:T(8,128)(2,1)} %bitcast.44), calls=%async_computation.5 | async-start | bytes 4194304 | tf_op jit(solution)/shard_map/all_to_all | solution.py:489

commit v5 on v4

--- a/solution.py
+++ b/solution.py
@@ -1,3 +1,5 @@
+import functools
+
 import jax
 import jax.numpy as jnp
 from jax import lax
@@ -10,28 +12,30 @@
 ROUND_ROWS = 126
 SENT_ROWS = 128
 CHIP_COUNT = 8
+HALVES = 1
 
 norm_epsilon = 1e-06
 rope_base = 1000000.0
 masked_low = -1e30
 
-DP = ("y", "zl")
+DP = ("yh", "yl", "zl")
 CHIPS = ("zh", "x")
-LAYER = ("zl", "zh", "x")
-PLANE = ("y", "zl", "zh", "x")
-EVERY = ("y", "zl", "zh", "x", "core")
+LAYER = ("yh", "zl", "zh", "x")
+PLANE = ("yh", "yl", "zl", "zh", "x")
+EVERY = ("yh", "yl", "zl", "zh", "x", "core")
 
 
 def swap_cores(value):
     return lax.ppermute(value, "core", [(0, 1), (1, 0)])
 
 
-def shift(value, count, step):
-    return lax.ppermute(value, "y", [(i, (i + step) % count) for i in range(count)])
+def swap_lines(value):
+    return lax.ppermute(value, "yl", [(0, 1), (1, 0)])
 
 
 VMEM = pl.BlockSpec(memory_space=pltpu.VMEM)
 SMEM = pl.BlockSpec(memory_space=pltpu.SMEM)
+HBM = pl.BlockSpec(memory_space=pltpu.HBM)
 
 
 def lookup_kernel(place_ref, id_row_ref, id_col_ref, bias_ref, vocab_ref, *rest):
@@ -118,11 +122,12 @@
 
 
 def attention_kernel(
+    half,
     arrived_ref, bias_ref, cosine_ref, sine_ref, length_ref, keys_ref, values_ref, *rest
 ):
     out_ref, new_keys_ref, new_values_ref, key_buf, value_buf, key_sem, value_sem = rest
     groups, chips, rows, _ = arrived_ref.shape
-    seqs, cache_len, _ = keys_ref.shape
+    seqs, cache_len, _ = key_buf.shape
     steps = rows // seqs
     core_cols = bias_ref.shape[2] // 2
     heads = out_ref.shape[3] // HD
@@ -130,9 +135,11 @@
     many = heads * rows
     copies = []
     for seq in range(seqs):
-        copies.append(pltpu.make_async_copy(keys_ref.at[seq], key_buf.at[seq], key_sem.at[seq]))
+        copies.append(pltpu.make_async_copy(keys_ref.at[half * seqs + seq], key_buf.at[seq], key_sem.at[seq]))
         copies.append(
-            pltpu.make_async_copy(values_ref.at[seq], value_buf.at[seq], value_sem.at[seq])
+            pltpu.make_async_copy(
+                values_ref.at[half * seqs + seq], value_buf.at[seq], value_sem.at[seq]
+            )
         )
     for copy in copies:
         copy.start()
@@ -148,7 +155,7 @@
     lane = lax.broadcasted_iota(jnp.int32, (rows, HD), 1)
 
     def rotated(features):
-        return (features * cosine + pltpu.roll(features, HD // 2, 1) * sine).astype(jnp.bfloat16)
+        return features * cosine + pltpu.roll(features, HD // 2, 1) * sine
 
     row_at = lax.broadcasted_iota(jnp.int32, (many, 1), 0) % rows
     row_seq = row_at // steps
@@ -169,10 +176,12 @@
         for head in range(heads):
             start = (head // half_heads) * core_cols + (head % half_heads) * HD
             parts.append(rotated(joined[:, start : start + HD]))
-        queries = jnp.concatenate(parts, axis=0)
+        queries = jnp.concatenate(parts, axis=0).astype(jnp.bfloat16)
         low = joined[:, core_cols - HD : core_cols]
         high = joined[:, 2 * core_cols - HD :]
-        fresh_keys = rotated(jnp.where(lane < HD // 2, low, pltpu.roll(high, HD // 2, 1)))
+        fresh_keys = rotated(jnp.where(lane < HD // 2, low, pltpu.roll(high, HD // 2, 1))).astype(
+            jnp.bfloat16
+        )
         fresh_values = jnp.where(lane < HD // 2, pltpu.roll(low, HD // 2, 1), high).astype(
             jnp.bfloat16
         )
@@ -208,30 +217,29 @@
                 weights, value_buf[seq, :, span], preferred_element_type=jnp.float32
             )
             attended = attended + jnp.where(row_seq == seq, found, 0.0)
-        attended = attended.astype(jnp.bfloat16)
         for head in range(heads):
-            piece = attended[head * rows : (head + 1) * rows]
+            piece = attended[head * rows : (head + 1) * rows].astype(jnp.bfloat16)
             for group in range(out_ref.shape[0]):
                 out_ref[group, chip, :, head * HD : (head + 1) * HD] = piece
 
 
-def attend(arrived, bias, cosine, sine, row_lengths, key_cache, value_cache, copies):
+def attend(half, arrived, bias, cosine, sine, row_lengths, key_cache, value_cache, copies):
     _, chips, rows, _ = arrived.shape
     seqs, cache_len, kv_cols = key_cache.shape
+    seqs = seqs // HALVES
     heads = 8
-    anywhere = pl.BlockSpec(memory_space=pl.ANY)
     return pl.pallas_call(
-        attention_kernel,
+        functools.partial(attention_kernel, half),
         out_shape=(
             jax.ShapeDtypeStruct((copies, chips, rows, heads * HD), jnp.bfloat16),
             jax.ShapeDtypeStruct((rows, kv_cols), jnp.bfloat16),
             jax.ShapeDtypeStruct((rows, kv_cols), jnp.bfloat16),
         ),
-        in_specs=[VMEM] * 5 + [anywhere] * 2,
+        in_specs=[VMEM] * 5 + [HBM] * 2,
         out_specs=(VMEM, VMEM, VMEM),
         scratch_shapes=[
-            pltpu.VMEM(key_cache.shape, jnp.bfloat16),
-            pltpu.VMEM(key_cache.shape, jnp.bfloat16),
+            pltpu.VMEM((seqs, cache_len, kv_cols), jnp.bfloat16),
+            pltpu.VMEM((seqs, cache_len, kv_cols), jnp.bfloat16),
             pltpu.SemaphoreType.DMA((seqs,)),
             pltpu.SemaphoreType.DMA((seqs,)),
         ],
@@ -283,7 +291,6 @@
     cols = mine.shape[1]
     out_cols = 2 * cols + width // chips
     block = 256
-    anywhere = pl.BlockSpec(memory_space=pl.ANY)
     return pl.pallas_call(
         projection_kernel,
         out_shape=jax.ShapeDtypeStruct((rows, out_cols), jnp.bfloat16),
@@ -294,7 +301,7 @@
             pl.BlockSpec((table_rows, width), lambda i: (0, 0)),
             pl.BlockSpec((1, width), lambda i: (0, 0)),
         ]
-        + [anywhere] * (2 + len(held)),
+        + [HBM] * (2 + len(held)),
         out_specs=pl.BlockSpec((block, out_cols), lambda i: (i, 0)),
         scratch_shapes=[
             pltpu.VMEM((block, width), jnp.bfloat16),
@@ -339,7 +346,7 @@
     return pl.pallas_call(
         branch_kernel,
         out_shape=jax.ShapeDtypeStruct((rows.shape[0], count // 2 * width), jnp.bfloat16),
-        in_specs=[SMEM, VMEM] + [pl.BlockSpec(memory_space=pl.ANY)] * count,
+        in_specs=[SMEM, VMEM] + [HBM] * count,
         out_specs=VMEM,
         scratch_shapes=[
             pltpu.VMEM((count, depth, width), jnp.bfloat16),
@@ -350,36 +357,46 @@
     )(place, rows, *weights)
 
 
-def hidden_kernel(branch_ref, strip_ref, out_ref):
-    layers, chips, _, width = branch_ref.shape
-    strip = strip_ref.shape[3]
-    for layer in range(layers):
-        for part in range(width // strip):
-            span = slice(part * strip, (part + 1) * strip)
-            total = strip_ref[layer, part].astype(jnp.float32)
-            for chip in range(chips):
-                total = total + branch_ref[layer, chip, :, span].astype(jnp.float32)
-            start = layer * width + part * strip
-            out_ref[:, start : start + strip] = total.astype(jnp.bfloat16)
-
-
-def hidden_sum(branches, arrived, width):
-    layers, chips, rows, all_width = branches.shape
-    groups = all_width // width
+def hidden_kernel(steps, *refs):
+    out_ref = refs[-1]
+    branch_refs, strip_refs = refs[:HALVES], refs[HALVES:-1]
+    _, layers, chips, rows, width = branch_refs[0].shape
+    strip = strip_refs[0].shape[3]
+    for half in range(HALVES):
+        for layer in range(layers):
+            for part in range(width // strip):
+                span = slice(part * strip, (part + 1) * strip)
+                total = strip_refs[half][layer, part].astype(jnp.float32)
+                for chip in range(chips):
+                    total = total + branch_refs[half][0, layer, chip, :, span].astype(jnp.float32)
+                start = layer * width + part * strip
+                for seq in range(rows // steps):
+                    out_ref[half * (rows // steps) + seq, :, start : start + strip] = total[
+                        seq * steps : (seq + 1) * steps
+                    ].astype(jnp.bfloat16)
+
+
+def hidden_sum(branches, arrived, width, steps):
+    upper, layers, chips, rows, pair_width = branches[0].shape
+    lower = pair_width // width
     strip = width // chips
-    last = arrived.shape[3] // strip - 1
+    last = arrived[0].shape[3] // strip - 1
+    seqs = HALVES * rows // steps
     return pl.pallas_call(
-        hidden_kernel,
-        out_shape=jax.ShapeDtypeStruct((rows, layers * all_width), jnp.bfloat16),
-        grid=(groups,),
+        functools.partial(hidden_kernel, steps),
+        out_shape=jax.ShapeDtypeStruct((seqs, steps, upper * layers * pair_width), jnp.bfloat16),
+        grid=(upper * lower,),
         in_specs=[
-            pl.BlockSpec((layers, chips, rows, width), lambda y: (0, 0, 0, y)),
-            pl.BlockSpec((layers, chips, rows, strip), lambda y: (y, 0, 0, last)),
-        ],
-        out_specs=pl.BlockSpec((rows, layers * width), lambda y: (0, y)),
+            pl.BlockSpec(
+                (1, layers, chips, rows, width), lambda y: (y // lower, 0, 0, 0, y % lower)
+            )
+        ]
+        * HALVES
+        + [pl.BlockSpec((layers, chips, rows, strip), lambda y: (y, 0, 0, last))] * HALVES,
+        out_specs=pl.BlockSpec((seqs, steps, layers * width), lambda y: (0, 0, y)),
         compiler_params=pltpu.CompilerParams(vmem_limit_bytes=48 * 1024 * 1024),
         name="hidden_sum",
-    )(branches, arrived)
+    )(*branches, *arrived)
 
 
 def per_device(
@@ -400,8 +417,7 @@
     seq_here, step_count = token_ids.shape
     rows_here = seq_here * step_count
     vocab_here, width_here = embedding.shape
-    lines = lax.axis_size("y")
-    line = lax.axis_index("y")
+    line = lax.axis_index("yl")
     replicas = lax.axis_size(DP)
     chips = lax.axis_size(CHIPS)
     chip = lax.axis_index(CHIPS)
@@ -412,10 +428,8 @@
 
     both = jnp.concatenate([q_weight, k_weight, v_weight], axis=1)
     both_other = swap_cores(both)
-    o_lines = [o_weight, shift(o_weight, lines, 1), None, shift(o_weight, lines, -1)]
-    o_lines[2] = shift(o_lines[1], lines, 1)
-    o_held = (o_lines[1], o_lines[3])
-    o_weights = [piece for own in o_lines for piece in (own, swap_cores(own))]
+    o_line = swap_lines(o_weight)
+    o_weights = (o_weight, swap_cores(o_weight), o_line, swap_cores(o_line))
     own_bias = jnp.concatenate([q_bias, k_bias, v_bias])
     core_cols = own_bias.shape[0]
     q_cols = q_bias.shape[0]
@@ -446,7 +460,7 @@
         own_rank = lax.dynamic_index_in_dim(rank, core, 0, keepdims=False).reshape(-1)
         here = (own_rank >= first) & (own_rank < first + ROUND_ROWS)
         slot = jnp.where(here, own_holder * SENT_ROWS + own_rank - first, -1)
-        return slot.reshape(plane_rows, 1), table, jnp.max(rank) // ROUND_ROWS + 1
+        return slot, table, jnp.max(rank) // ROUND_ROWS + 1
 
     own_gain = lax.dynamic_slice_in_dim(norm_gain, lax.axis_index(DP) * width_here, width_here)
     own_gain = own_gain.reshape(1, width_here).astype(jnp.float32)
@@ -454,50 +468,73 @@
     pair_bias = table.reshape(chips, SENT_ROWS, width_here)
     pair_bias = pair_bias[:, ROUND_ROWS : ROUND_ROWS + 2, :core_cols].astype(jnp.float32)
     pair_bias = pair_bias.reshape(chips, 1, 2 * core_cols)
-    payload = project(place, slot, table, own_gain, both, both_other, o_held, chips)
-
-    def further(turn, sofar):
-        turn_slot, turn_table, _ = exchange(turn)
-        return sofar + project(
-            place, turn_slot, turn_table, own_gain, both, both_other, (), chips
-        )
-
-    payload = lax.fori_loop(1, rounds, further, payload)
-    arrived = lax.all_to_all(payload, PLANE, split_axis=0, concat_axis=0, tiled=True)
-    arrived = arrived.reshape(replicas, chips, rows_here, -1)
+    half_rows = rows_here // HALVES
+    kv_heads = key_cache.shape[2] // HD
     positions = (lengths[:, None] + jnp.arange(step_count, dtype=jnp.int32)[None, :]).reshape(-1)
     frequency = rope_base ** (-(2.0 * jnp.arange(HD // 2, dtype=jnp.float32)) / HD)
     angles = positions.astype(jnp.float32)[:, None] * frequency
     cosine, sine = jnp.cos(angles), jnp.sin(angles)
-    kv_heads = key_cache.shape[2] // HD
-    row_lengths = jnp.tile(jnp.repeat(lengths, step_count), 8 * kv_heads // chips).reshape(-1, 1)
-    spread, new_keys, new_values = attend(
-        arrived,
-        pair_bias,
-        jnp.concatenate([cosine, cosine], axis=1),
-        jnp.concatenate([-sine, sine], axis=1),
-        row_lengths,
-        key_cache,
-        value_cache,
-        replicas // lines,
+    cosine = jnp.concatenate([cosine, cosine], axis=1)
+    sine = jnp.concatenate([-sine, sine], axis=1)
+    row_lengths = jnp.repeat(lengths, step_count)
+
+    def part_of(values, half):
+        return values.reshape(parties, HALVES, half_rows)[:, half].reshape(-1, 1)
+
+    payloads = tuple(
+        project(place, part_of(slot, half), table, own_gain, both, both_other, (o_line,), chips)
+        for half in range(HALVES)
     )
 
-    gathered = lax.all_to_all(
-        spread.reshape(-1, rows_here, 2 * q_cols), LAYER, split_axis=0, concat_axis=0, tiled=True
-    ).reshape(-1, 2 * q_cols)
-    branch = branch_out(place, gathered, o_weights)
-    branches = lax.all_to_all(branch, LAYER, split_axis=0, concat_axis=0, tiled=True)
-    branches = branches.reshape(replicas // lines, chips, rows_here, -1)
-    hidden = hidden_sum(branches, arrived, o_weight.shape[1])
+    def further(turn, sofar):
+        turn_slot, turn_table, _ = exchange(turn)
+        return tuple(
+            sofar[half]
+            + project(
+                place, part_of(turn_slot, half), turn_table, own_gain, both, both_other, (), chips
+            )
+            for half in range(HALVES)
+        )
+
+    payloads = lax.fori_loop(1, rounds, further, payloads)
+    layer_count = lax.axis_size(("yh", "zl"))
+    arrived, new_keys, new_values, branches = [], [], [], []
+    for half in range(HALVES):
+        here = lax.all_to_all(payloads[half], PLANE, split_axis=0, concat_axis=0, tiled=True)
+        here = here.reshape(replicas, chips, half_rows, -1)
+        rows = slice(half * half_rows, (half + 1) * half_rows)
+        spread, keys, values = attend(
+            half,
+            here,
+            pair_bias,
+            cosine[rows],
+            sine[rows],
+            jnp.tile(row_lengths[rows], 8 * kv_heads // chips).reshape(-1, 1),
+            key_cache,
+            value_cache,
+            layer_count,
+        )
+        gathered = lax.all_to_all(
+            spread.reshape(-1, half_rows, 2 * q_cols), LAYER, split_axis=0, concat_axis=0, tiled=True
+        ).reshape(-1, 2 * q_cols)
+        branch = branch_out(place, gathered, o_weights)
+        back = lax.all_to_all(branch, LAYER, split_axis=0, concat_axis=0, tiled=True)
+        branches.append(back.reshape(2, layer_count // 2, chips, half_rows, -1))
+        arrived.append(here)
+        new_keys.append(keys)
+        new_values.append(values)
+    hidden = hidden_sum(branches, arrived, o_weight.shape[1], step_count)
+    new_keys = jnp.concatenate(new_keys, axis=0)
+    new_values = jnp.concatenate(new_values, axis=0)
     return (
-        hidden.reshape(seq_here, step_count, -1),
+        hidden,
         new_keys.reshape(seq_here, step_count, -1),
         new_values.reshape(seq_here, step_count, -1),
     )
 
 
 def solution(mesh):
-    fine = Mesh(mesh.devices.reshape(4, 2, 2, 4, 2), EVERY)
+    fine = Mesh(mesh.devices.reshape(2, 2, 2, 2, 4, 2), EVERY)
     tensor = CHIPS + ("core",)
     placed = (
         P(EVERY, None),

time: 229 us -> 208 us (0.908)
  waiting for transfers between devices: 121 us -> 107 us
  starting transfers between devices: 42.4 us -> 35 us
    ppermute x3 -> x1, waiting for transfers between devices: 68.9 us -> 16.7 us  [swap_lines(): return lax.ppermute(value, 'yl', [(0, 1), (1, 0)])]
    all_to_all x2, waiting for transfers between devices: 12.2 us -> 53.3 us  [the longest x1 36.6 us: per_device(): lax.all_to_all(payloads[half], PLANE, split_axis=0, concat_axis=0, tiled=...]
    ppermute x3 -> x1, starting transfers between devices: 4.9 us -> 0.66 us  [swap_lines(): return lax.ppermute(value, 'yl', [(0, 1), (1, 0)])]
    all_to_all x2, starting transfers between devices: 17.3 us -> 13.4 us  [the longest x1 8.7 us: per_device(): lax.all_to_all(payloads[half], PLANE, split_axis=0, concat_axis=0, tiled=...]
    all_to_all x1, waiting for transfers between devices: 29.5 us -> 26.1 us  [per_device(): lax.all_to_all(branch, LAYER, split_axis=0, concat_axis=0, tiled=True)]
  transfers between devices with their start and end apart: 14 -> 10, of which waited for: 6 -> 6; matrix products, arithmetic and copies ran while one was open for 6% -> 7% of each run, Pallas kernels for 4% -> 4%
where the time goes in v5:
time: 208 us; the launch traced here: 207 us
  waiting for transfers between devices  107 us (51%)
  Pallas kernels  37.8 us (18%)
  starting transfers between devices  35 us (17%)
  local copies, waits for them, and re-layouts  15.7 us (8%)
  other arithmetic  8.18 us (4%)
  between operations  2.91 us (1%)
    all_to_all x1, waiting for transfers between devices, per_device(): lax.all_to_all(payloads[half], PLANE, split_axis=0, concat_axis=0, tiled=...  36.6 us
    all_to_all x1, waiting for transfers between devices, per_device(): lax.all_to_all(branch, LAYER, split_axis=0, concat_axis=0, tiled=True)  26.1 us
    all_to_all x1, waiting for transfers between devices, per_device(): lax.all_to_all(spread.reshape(-1, half_rows, 2 * q_cols), LAYER, split_ax...  16.7 us
    ppermute x1, waiting for transfers between devices, swap_lines(): return lax.ppermute(value, 'yl', [(0, 1), (1, 0)])  16.7 us
    all_to_all x1, starting transfers between devices, per_device(): lax.all_to_all(sent_ids, EVERY, split_axis=0, concat_axis=0, tiled=True)  11.1 us
    pallas_call x1, Pallas kernels, project(): pl.pallas_call(projection_kernel, out_shape=jax.ShapeDtypeStruct((rows, o...  9.56 us
    pallas_call x1, Pallas kernels, look_up(): pl.pallas_call(lookup_kernel, out_shape=(jax.ShapeDtypeStruct((SENT_ROWS,...  9.42 us
    all_to_all x1, waiting for transfers between devices, per_device(): lax.all_to_all(sent_ids, EVERY, split_axis=0, concat_axis=0, tiled=True)  9.17 us
  transfers between devices with their start and end apart: 10, of which 6 were waited for; matrix products, arithmetic and copies ran while one was open for 7% of the time, Pallas kernels for 4%

profile of v5, /device:TPU:0, one launch (start us, length us, event | category | flops | bytes accessed | tf_op | source)
XLA Modules:
  0.0 206.7 jit_solution(4712006401373612061)
XLA Ops:
  0.7 0.8 broadcast_in_dim.54
  1.4 0.8 fusion.10
  2.2 0.1 select_convert_fusion.1.bias_ref
  2.3 0.7 broadcast_in_dim.55
  3.0 11.1 %all-to-all-start.1 = ((s32[128,1,16]{2,1,0:T(1,128)}), s32[128,1,16]{2,1,0:T(1,128)S(1)}, u32[]{:S(2)}, u32[]{:S(2)}) async-start(s32[128,1,16]{2,1,0:T(1,128)} %broadcast_in_dim.55), calls=%async_computation.1 | async-start | bytes 131072 | tf_op jit(solution)/shard_map/all_to_all | solution.py:438
  14.1 0.1 pad_add_fusion.2.place_ref
  14.2 9.2 %all-to-all-done.1 = s32[128,1,16]{2,1,0:T(1,128)S(1)} async-done(((s32[128,1,16]{2,1,0:T(1,128)}), s32[128,1,16]{2,1,0:T(1,128)S(1)}, u32[]{:S(2)}, u32[]{:S(2)}) %all-to-all-start.1) | async-done | bytes 8224 | tf_op jit(solution)/shard_map/all_to_all | solution.py:438
  23.4 0.6 reshape_reshape.17.id_col_ref
  24.0 0.1 reshape_reshape.16.id_row_ref
  24.1 9.4 %look_up.4 = (bf16[128,1024]{1,0:T(8,128)(2,1)S(1)}, bf16[128,1024]{1,0:T(8,128)(2,1)S(1)}, s32[2,1,1024]{2,1,0:T(1,128)S(1)}) custom-call(s32[4]{0:T(128)S(1)} %pad_add_fusion.2.place_ref, s32[2,1,1024]{2,1,0:T(1,128)S(1)} %reshape_reshape.16.id_row_ref, s32[2,1024,1]{2,1,0:T(8,128)S(1)} %reshape_reshape.17.id_col_ref, ...), custom_call_target="tpu_custom_call" | custom-call | tf_op jit(solution)/shard_map/look_up/pallas_call | solution.py:95
  33.5 0.1 collective-permute-start.1
  33.6 1.5 collective-permute-done.1
  35.1 0.1 add.110
  35.2 1.6 broadcast_in_dim.59
  36.8 3.7 %all-to-all-start.2 = ((bf16[8,128,1024]{2,1,0:T(8,128)(2,1)}), bf16[8,128,1024]{2,1,0:T(8,128)(2,1)S(1)}, u32[]{:S(2)}, u32[]{:S(2)}) async-start(bf16[8,128,1024]{2,1,0:T(8,128)(2,1)} %broadcast_in_dim.59), calls=%async_computation.2 | async-start | bytes 4194304 | tf_op jit(solution)/shard_map/all_to_all | solution.py:453
  40.5 1.1 copy.80
  41.6 1.7 copy.81
  43.4 2.3 %pad_maximum_fusion.mine_ref = bf16[1024,640]{1,0:T(8,128)(2,1)} fusion(bf16[1024,64]{1,0:T(8,128)(2,1)} %copy.81, bf16[1024,64]{1,0:T(8,128)(2,1)S(1)} %copy.80, bf16[1024,512]{1,0:T(8,128)(2,1)S(1)} %copy-done.8), kind=kLoop, calls=%fused_computation.6 | loop fusion | flops 3932160 | bytes 2621440 | tf_op jit(solution)/shard_map/concatenate | solution.py:429
  45.7 0.1 collective-permute-start.2
  45.8 0.7 collective-permute-start.3
  46.5 0.7 dynamic-slice_convert_fusion
  47.1 0.1 pad_add_fusion.1.place_ref
  47.2 0.1 reshape.258
  47.3 0.6 reduce_max.8
  49.9 0.1 reshape_reshape.20
  50.0 1.1 copy.73
  51.2 0.3 copy.77
  51.5 1.0 copy.76
  52.6 2.2 %fusion.4.slot_ref = s32[1024,1]{1,0:T(8,128)} fusion(s32[1024,1]{1,0:T(8,128)} %copy.73, pred[1024,1]{1,0:T(8,128)(4,1)S(1)} %copy.77, s32[1024,1]{1,0:T(8,128)} %copy.76), kind=kLoop, calls=%fused_computation.10 | loop fusion | flops 8192 | bytes 13312 | tf_op jit(solution)/shard_map/jit(_where)/select_n | solution.py:462
  54.8 16.7 %collective-permute-done.3.rest_0_.rest_2_ = bf16[512,1024]{1,0:T(8,128)(2,1)S(1)} collective-permute-done((bf16[512,1024]{1,0:T(8,128)(2,1)}, bf16[512,1024]{1,0:T(8,128)(2,1)S(1)}, u32[]{:S(2)}, u32[]{:S(2)}) %collective-permute-start.3) | collective-permute-done | bytes 1048608 | tf_op jit(solution)/shard_map/ppermute | solution.py:33
  71.5 0.0 collective-permute-done.2.theirs_ref
  71.5 0.0 all-to-all-done.2
  71.5 0.0 copy-start
  71.5 0.0 copy-start.3
  71.5 1.4 copy-done.3
  72.9 9.6 %project.4 = bf16[1024,1408]{1,0:T(8,128)(2,1)} custom-call(s32[3]{0:T(128)S(1)} %pad_add_fusion.1.place_ref, s32[1024,1]{1,0:T(8,128)S(1)} %copy-done.3, bf16[1024,1024]{1,0:T(8,128)(2,1)S(1)} %bitcast.40, f32[1,1024]{1,0:T(1,128)S(1)} %bitcast.46, bf16[1024,640]{1,0:T(8,128)(2,1)} %pad_maximum_fusion.mine_ref, ...), custom_call_target="tpu_custom_call" | custom-call | tf_op jit(solution)/shard_map/project/pallas_call | solution.py:294
  82.5 0.2 while.14
  82.7 0.0 copy-start.9
  82.7 8.7 %all-to-all-start.3 = ((bf16[64,16,1408]{2,1,0:T(8,128)(2,1)}), bf16[64,16,1408]{2,1,0:T(8,128)(2,1)S(1)}, u32[]{:S(2)}, u32[]{:S(2)}) async-start(bf16[64,16,1408]{2,1,0:T(8,128)(2,1)} %bitcast.42), calls=%async_computation.3 | async-start | bytes 5767168 | tf_op jit(solution)/shard_map/all_to_all | solution.py:503
  91.4 0.1 collective-permute-start.4
  91.5 0.1 add.115
  91.6 0.1 add.116
  91.7 0.1 add.118
  91.8 0.1 reshape_tile.4.length_ref
  91.9 0.1 fusion.8
  92.0 0.1 pad_maximum_fusion.1
  92.1 0.7 collective-permute-start.5
  92.8 0.9 slice_convert_fusion
  93.7 0.1 reshape.270.bias_ref
  93.8 36.6 %all-to-all-done.3 = bf16[64,16,1408]{2,1,0:T(8,128)(2,1)S(1)} async-done(((bf16[64,16,1408]{2,1,0:T(8,128)(2,1)}), bf16[64,16,1408]{2,1,0:T(8,128)(2,1)S(1)}, u32[]{:S(2)}, u32[]{:S(2)}) %all-to-all-start.3) | async-done | bytes 2883616 | tf_op jit(solution)/shard_map/all_to_all | solution.py:503
  130.4 8.7 %attend.1 = (bf16[4,8,16,1024]{3,2,1,0:T(8,128)(2,1)S(1)}, bf16[16,1024]{1,0:T(8,128)(2,1)S(1)}, bf16[16,1024]{1,0:T(8,128)(2,1)S(1)}) custom-call(bf16[8,8,16,1408]{3,2,1,0:T(8,128)(2,1)S(1)} %bitcast.38, f32[8,1,1280]{2,1,0:T(1,128)S(1)} %reshape.270.bias_ref, f32[16,128]{1,0:T(8,128)S(1)} %get-tuple-element.260.cosine_ref, ...), custom_call_target="tpu_custom_call" | custom-call | tf_op jit(solution)/shard_map/attend/pallas_call | solution.py:231
  139.2 1.1 copy-done.4
  140.2 4.7 %all-to-all-start.4 = ((bf16[32,16,1024]{2,1,0:T(8,128)(2,1)}), bf16[32,16,1024]{2,1,0:T(8,128)(2,1)}, u32[]{:S(2)}, u32[]{:S(2)}) async-start(bf16[32,16,1024]{2,1,0:T(8,128)(2,1)} %bitcast.41), calls=%async_computation.4 | async-start | bytes 2097152 | tf_op jit(solution)/shard_map/all_to_all | solution.py:517
  144.9 0.0 collective-permute-done.4.rest_1_
  144.9 0.0 collective-permute-done.5.rest_3_
  144.9 16.7 %all-to-all-done.4 = bf16[32,16,1024]{2,1,0:T(8,128)(2,1)} async-done(((bf16[32,16,1024]{2,1,0:T(8,128)(2,1)}), bf16[32,16,1024]{2,1,0:T(8,128)(2,1)}, u32[]{:S(2)}, u32[]{:S(2)}) %all-to-all-start.4) | async-done | bytes 1048608 | tf_op jit(solution)/shard_map/all_to_all | solution.py:517
  161.6 1.2 copy-done.2
  162.8 1.2 copy-done.5
  164.1 6.5 %branch.1 = bf16[512,2048]{1,0:T(8,128)(2,1)} custom-call(s32[3]{0:T(128)S(1)} %get-tuple-element.480, bf16[512,1024]{1,0:T(8,128)(2,1)} %bitcast.14.rows_ref, bf16[512,1024]{1,0:T(8,128)(2,1)S(1)} %copy-done.5, bf16[512,1024]{1,0:T(8,128)(2,1)} %collective-permute-done.4.rest_1_, bf16[512,1024]{1,0:T(8,128)(2,1)S(1)} %copy-done.2, ...), custom_call_target="tpu_custom_call" | custom-call | tf_op jit(solution)/shard_map/branch/pallas_call | solution.py:346
  170.6 5.1 %all-to-all-start.5 = ((bf16[32,16,2048]{2,1,0:T(8,128)(2,1)}), bf16[32,16,2048]{2,1,0:T(8,128)(2,1)}, u32[]{:S(2)}, u32[]{:S(2)}) async-start(bf16[32,16,2048]{2,1,0:T(8,128)(2,1)} %bitcast.43), calls=%async_computation.5 | async-start | bytes 4194304 | tf_op jit(solution)/shard_map/all_to_all | solution.py:521
  175.7 0.6 reshape.266
  176.3 0.6 reshape.267
  177.0 26.1 %all-to-all-done.5 = bf16[32,16,2048]{2,1,0:T(8,128)(2,1)} async-done(((bf16[32,16,2048]{2,1,0:T(8,128)(2,1)}), bf16[32,16,2048]{2,1,0:T(8,128)(2,1)}, u32[]{:S(2)}, u32[]{:S(2)}) %all-to-all-start.5) | async-done | bytes 2097184 | tf_op jit(solution)/shard_map/all_to_all | solution.py:521
  203.1 3.6 %hidden_sum.1 = bf16[4,4,8192]{2,1,0:T(4,128)(2,1)} custom-call(bf16[2,2,8,16,2048]{4,3,2,1,0:T(8,128)(2,1)} %bitcast.16.refs_0_, bf16[8,8,16,1408]{3,2,1,0:T(8,128)(2,1)S(1)} %bitcast.39), custom_call_target="tpu_custom_call" | custom-call | tf_op jit(solution)/shard_map/hidden_sum/pallas_call | solution.py:385
  (20 shorter events, 0.2 us)
Async XLA Ops:
  3.0 20.4 %all-to-all-start.1 = ((s32[128,1,16]{2,1,0:T(1,128)}), s32[128,1,16]{2,1,0:T(1,128)S(1)}, u32[]{:S(2)}, u32[]{:S(2)}) async-start(s32[128,1,16]{2,1,0:T(1,128)} %broadcast_in_dim.55), calls=%async_computation.1 | async-start | bytes 131072 | tf_op jit(solution)/shard_map/all_to_all | solution.py:438
  33.5 1.6 collective-permute-start.1
  36.8 6.6 %copy-start.8 = (bf16[1024,512]{1,0:T(8,128)(2,1)S(1)}, bf16[1024,512]{1,0:T(8,128)(2,1)}, u32[]{:S(2)}) copy-start(bf16[1024,512]{1,0:T(8,128)(2,1)} %param.19) | copy-start | bytes 3145732
  36.8 34.7 %all-to-all-start.2 = ((bf16[8,128,1024]{2,1,0:T(8,128)(2,1)}), bf16[8,128,1024]{2,1,0:T(8,128)(2,1)S(1)}, u32[]{:S(2)}, u32[]{:S(2)}) async-start(bf16[8,128,1024]{2,1,0:T(8,128)(2,1)} %broadcast_in_dim.59), calls=%async_computation.2 | async-start | bytes 4194304 | tf_op jit(solution)/shard_map/all_to_all | solution.py:453
  45.7 25.8 %collective-permute-start.2 = (bf16[1024,640]{1,0:T(8,128)(2,1)}, bf16[1024,640]{1,0:T(8,128)(2,1)}, u32[]{:S(2)}, u32[]{:S(2)}) collective-permute-start(bf16[1024,640]{1,0:T(8,128)(2,1)} %pad_maximum_fusion.mine_ref), channel_id=1, source_target_pairs={{0,1},{1,0},{2,3},{3,2},{4,5},{5,4},{6,7},{7,6},{8,9},{9,8},{10,11... | collective-permute-start | bytes 3932168 | tf_op jit(solution)/shard_map/ppermute | solution.py:29
  45.8 25.6 %collective-permute-start.3 = (bf16[512,1024]{1,0:T(8,128)(2,1)}, bf16[512,1024]{1,0:T(8,128)(2,1)S(1)}, u32[]{:S(2)}, u32[]{:S(2)}) collective-permute-start(bf16[512,1024]{1,0:T(8,128)(2,1)} %rest_0_.1), channel_id=1, source_target_pairs={{0,32},{32,0},{1,33},{33,1},{2,34},{34,2},{3,35},{35,3},{4,36},{36... | collective-permute-start | bytes 3145736 | tf_op jit(solution)/shard_map/ppermute | solution.py:33
  71.5 11.0 %copy-start.1 = (bf16[512,1024]{1,0:T(8,128)(2,1)}, bf16[512,1024]{1,0:T(8,128)(2,1)S(1)}, u32[]{:S(2)}) copy-start(bf16[512,1024]{1,0:T(8,128)(2,1)S(1)} %collective-permute-done.3.rest_0_.rest_2_) | copy-start | bytes 3145732
  71.5 11.0 %copy-start = (bf16[8,128,1024]{2,1,0:T(8,128)(2,1)}, bf16[8,128,1024]{2,1,0:T(8,128)(2,1)S(1)}, u32[]{:S(2)}) copy-start(bf16[8,128,1024]{2,1,0:T(8,128)(2,1)S(1)} %all-to-all-done.2) | copy-start | bytes 6291460
  71.5 1.4 copy-start.3
  82.7 8.8 %copy-start.9 = (s32[4]{0:T(128)S(1)}, s32[4]{0:T(128)}, u32[]{:S(2)}) copy-start(s32[4]{0:T(128)} %param.16) | copy-start | bytes 52
  82.7 47.7 %all-to-all-start.3 = ((bf16[64,16,1408]{2,1,0:T(8,128)(2,1)}), bf16[64,16,1408]{2,1,0:T(8,128)(2,1)S(1)}, u32[]{:S(2)}, u32[]{:S(2)}) async-start(bf16[64,16,1408]{2,1,0:T(8,128)(2,1)} %bitcast.42), calls=%async_computation.3 | async-start | bytes 5767168 | tf_op jit(solution)/shard_map/all_to_all | solution.py:503
  91.4 53.5 %collective-permute-start.4 = (bf16[512,1024]{1,0:T(8,128)(2,1)}, bf16[512,1024]{1,0:T(8,128)(2,1)}, u32[]{:S(2)}, u32[]{:S(2)}) collective-permute-start(bf16[512,1024]{1,0:T(8,128)(2,1)} %rest_0_.1), channel_id=1, source_target_pairs={{0,1},{1,0},{2,3},{3,2},{4,5},{5,4},{6,7},{7,6},{8,9},{9,8},{10,11... | collective-permute-start | bytes 3145736 | tf_op jit(solution)/shard_map/ppermute | solution.py:29
  92.1 52.8 %collective-permute-start.5 = (bf16[512,1024]{1,0:T(8,128)(2,1)}, bf16[512,1024]{1,0:T(8,128)(2,1)}, u32[]{:S(2)}, u32[]{:S(2)}) collective-permute-start(bf16[512,1024]{1,0:T(8,128)(2,1)} %copy-done.1), channel_id=1, source_target_pairs={{0,1},{1,0},{2,3},{3,2},{4,5},{5,4},{6,7},{7,6},{8,9},{9,8},{10,11... | collective-permute-start | bytes 3145736 | tf_op jit(solution)/shard_map/ppermute | solution.py:29
  139.1 1.1 copy-start.4
  140.2 21.4 %all-to-all-start.4 = ((bf16[32,16,1024]{2,1,0:T(8,128)(2,1)}), bf16[32,16,1024]{2,1,0:T(8,128)(2,1)}, u32[]{:S(2)}, u32[]{:S(2)}) async-start(bf16[32,16,1024]{2,1,0:T(8,128)(2,1)} %bitcast.41), calls=%async_computation.4 | async-start | bytes 2097152 | tf_op jit(solution)/shard_map/all_to_all | solution.py:517
  161.6 1.2 copy-start.2
  162.8 1.2 copy-start.5
  170.6 32.5 %all-to-all-start.5 = ((bf16[32,16,2048]{2,1,0:T(8,128)(2,1)}), bf16[32,16,2048]{2,1,0:T(8,128)(2,1)}, u32[]{:S(2)}, u32[]{:S(2)}) async-start(bf16[32,16,2048]{2,1,0:T(8,128)(2,1)} %bitcast.43), calls=%async_computation.5 | async-start | bytes 4194304 | tf_op jit(solution)/shard_map/all_to_all | solution.py:521

commit v6 on v5

--- a/solution.py
+++ b/solution.py
@@ -12,7 +12,7 @@
 ROUND_ROWS = 126
 SENT_ROWS = 128
 CHIP_COUNT = 8
-HALVES = 1
+HALVES = 2
 
 norm_epsilon = 1e-06
 rope_base = 1000000.0
@@ -38,7 +38,12 @@
 HBM = pl.BlockSpec(memory_space=pltpu.HBM)
 
 
-def lookup_kernel(place_ref, id_row_ref, id_col_ref, bias_ref, vocab_ref, *rest):
+def turned(row):
+    wide = jnp.broadcast_to(row.astype(jnp.float32), (8, row.shape[1]))
+    return jnp.transpose(wide)[:, :1].astype(jnp.int32)
+
+
+def lookup_kernel(place_ref, id_row_ref, bias_ref, vocab_ref, *rest):
     mine_ref, theirs_ref, rank_ref, list_ref, total_ref = rest
     step = pl.program_id(0)
     chip, core, first = place_ref[0], place_ref[1], place_ref[3]
@@ -55,7 +60,7 @@
         slot = lax.broadcasted_iota(jnp.int32, (SENT_ROWS, rows), 0)
         for plane in range(planes):
             id_row = id_row_ref[plane]
-            id_col = id_col_ref[plane]
+            id_col = turned(id_row)
             again = jnp.where((id_row == id_col) & earlier, 1, 0)
             key_col = jnp.where(jnp.max(again, axis=1, keepdims=True) == 0, id_col, -1)
             edge_row = jnp.zeros_like(id_row)
@@ -103,7 +108,6 @@
         in_specs=[
             SMEM,
             whole(planes, 1, rows),
-            whole(planes, rows, 1),
             whole(SENT_ROWS, width),
             pl.BlockSpec((vocab_here // steps, width), lambda i: (i, 0)),
         ],
@@ -118,7 +122,7 @@
         ],
         compiler_params=pltpu.CompilerParams(vmem_limit_bytes=48 * 1024 * 1024),
         name="look_up",
-    )(place, plane_ids.reshape(planes, 1, rows), plane_ids.reshape(planes, rows, 1), bias_rows, embedding)
+    )(place, plane_ids.reshape(planes, 1, rows), bias_rows, embedding)
 
 
 def attention_kernel(
@@ -251,10 +255,11 @@
 def projection_kernel(place_ref, slot_ref, table_ref, gain_ref, mine_ref, theirs_ref, *rest):
     out_ref, wide_ref, weight_buf, sem = rest[-4:]
     chip, core = place_ref[0], place_ref[1]
-    rows = slot_ref.shape[0]
     table_rows = table_ref.shape[0]
     cols = mine_ref.shape[1]
     step = pl.program_id(0)
+    slot = turned(slot_ref[...])
+    rows = slot.shape[0]
     copies = [
         pltpu.make_async_copy(source, weight_buf.at[side], sem.at[side])
         for side, source in enumerate((mine_ref, theirs_ref))
@@ -266,7 +271,7 @@
             copy.start()
 
     chosen = (
-        lax.broadcasted_iota(jnp.int32, (rows, table_rows), 1) == slot_ref[...]
+        lax.broadcasted_iota(jnp.int32, (rows, table_rows), 1) == slot
     ).astype(jnp.bfloat16)
     found = jnp.dot(chosen, table_ref[...], preferred_element_type=jnp.float32)
     wide_ref[...] = found.astype(jnp.bfloat16)
@@ -286,7 +291,7 @@
 
 
 def project(place, slot, table, gain, mine, theirs, held, chips):
-    rows = slot.shape[0]
+    rows = slot.shape[1]
     table_rows, width = table.shape
     cols = mine.shape[1]
     out_cols = 2 * cols + width // chips
@@ -297,7 +302,7 @@
         grid=(rows // block,),
         in_specs=[
             SMEM,
-            pl.BlockSpec((block, 1), lambda i: (i, 0)),
+            pl.BlockSpec((1, block), lambda i: (0, i)),
             pl.BlockSpec((table_rows, width), lambda i: (0, 0)),
             pl.BlockSpec((1, width), lambda i: (0, 0)),
         ]
@@ -314,26 +319,19 @@
 
 
 def branch_kernel(place_ref, rows_ref, *rest):
-    weight_refs, (out_ref, weight_buf, sem) = rest[:-3], rest[-3:]
+    weight_refs, out_ref = rest[:-1], rest[-1]
     core, line = place_ref[1], place_ref[2]
     depth, width = weight_refs[0].shape
     count = len(weight_refs) // 2
-    copies = [
-        pltpu.make_async_copy(source, weight_buf.at[k], sem.at[k])
-        for k, source in enumerate(weight_refs)
-    ]
-    for copy in copies:
-        copy.start()
     for turn in range(count):
         block = pl.multiple_of(((line + count - turn) % count) * width, width)
         parts = []
         for side in range(2):
             where = pl.multiple_of(((core + side) % 2) * depth, depth)
-            copies[2 * turn + side].wait()
             parts.append(
                 jnp.dot(
                     rows_ref[:, pl.ds(where, depth)],
-                    weight_buf[2 * turn + side],
+                    weight_refs[2 * turn + side][...],
                     preferred_element_type=jnp.float32,
                 )
             )
@@ -342,16 +340,12 @@
 
 def branch_out(place, rows, weights):
     count = len(weights)
-    depth, width = weights[0].shape
+    width = weights[0].shape[1]
     return pl.pallas_call(
         branch_kernel,
         out_shape=jax.ShapeDtypeStruct((rows.shape[0], count // 2 * width), jnp.bfloat16),
-        in_specs=[SMEM, VMEM] + [HBM] * count,
+        in_specs=[SMEM, VMEM] + [VMEM] * count,
         out_specs=VMEM,
-        scratch_shapes=[
-            pltpu.VMEM((count, depth, width), jnp.bfloat16),
-            pltpu.SemaphoreType.DMA((count,)),
-        ],
         compiler_params=pltpu.CompilerParams(vmem_limit_bytes=48 * 1024 * 1024),
         name="branch",
     )(place, rows, *weights)
@@ -479,7 +473,7 @@
     row_lengths = jnp.repeat(lengths, step_count)
 
     def part_of(values, half):
-        return values.reshape(parties, HALVES, half_rows)[:, half].reshape(-1, 1)
+        return values.reshape(parties, HALVES, half_rows)[:, half].reshape(1, -1)
 
     payloads = tuple(
         project(place, part_of(slot, half), table, own_gain, both, both_other, (o_line,), chips)

time: 208 us -> 227 us (1.091)
  waiting for transfers between devices: 107 us -> 70.4 us
  blocking collectives: 0 us -> 31.5 us
  starting transfers between devices: 35 us -> 46.2 us
  Pallas kernels: 37.8 us -> 46.3 us
  local copies, waits for them, and re-layouts: 15.7 us -> 20 us
    all_to_all x0 -> x1, blocking collectives: none -> 31.5 us  [per_device(): lax.all_to_all(payloads[half], PLANE, split_axis=0, concat_axis=0, tiled=...]
    all_to_all x1, waiting for transfers between devices: 36.6 us -> 6.16 us  [per_device(): lax.all_to_all(payloads[half], PLANE, split_axis=0, concat_axis=0, tiled=...]
    all_to_all x1 -> x2, starting transfers between devices: 4.67 us -> 14.5 us  [per_device(): lax.all_to_all(spread.reshape(-1, half_rows, 2 * q_cols), LAYER, split_ax...]
    all_to_all x1 -> x2, waiting for transfers between devices: 16.7 us -> 7.71 us  [per_device(): lax.all_to_all(spread.reshape(-1, half_rows, 2 * q_cols), LAYER, split_ax...]
    all_to_all x1 -> x2, starting transfers between devices: 5.09 us -> 9.54 us  [per_device(): lax.all_to_all(branch, LAYER, split_axis=0, concat_axis=0, tiled=True)]
    pallas_call x1 -> x2, Pallas kernels: 8.75 us -> 13 us  [attend(): pl.pallas_call(functools.partial(attention_kernel, half), out_shape=(jax....]
    all_to_all x1, starting transfers between devices: 8.7 us -> 5.63 us  [per_device(): lax.all_to_all(payloads[half], PLANE, split_axis=0, concat_axis=0, tiled=...]
    pallas_call x1 -> x2, Pallas kernels: 9.56 us -> 12.3 us  [project(): pl.pallas_call(projection_kernel, out_shape=jax.ShapeDtypeStruct((rows, o...]
  transfers between devices with their start and end apart: 10 -> 12, of which waited for: 6 -> 7; matrix products, arithmetic and copies ran while one was open for 7% -> 7% of each run, Pallas kernels for 4% -> 9%
where the time goes in v6:
time: 227 us; the launch traced here: 225 us
  waiting for transfers between devices  70.4 us (31%)
  Pallas kernels  46.3 us (20%)
  starting transfers between devices  46.2 us (20%)
  blocking collectives  31.5 us (14%)
  local copies, waits for them, and re-layouts  20 us (9%)
  other arithmetic  7.46 us (3%)
  between operations  2.99 us (1%)
    all_to_all x1, blocking collectives, per_device(): lax.all_to_all(payloads[half], PLANE, split_axis=0, concat_axis=0, tiled=...  31.5 us
    all_to_all x2, waiting for transfers between devices, per_device(): lax.all_to_all(branch, LAYER, split_axis=0, concat_axis=0, tiled=True)  26.6 us
    ppermute x1, waiting for transfers between devices, swap_lines(): return lax.ppermute(value, 'yl', [(0, 1), (1, 0)])  19.2 us
    all_to_all x2, starting transfers between devices, per_device(): lax.all_to_all(spread.reshape(-1, half_rows, 2 * q_cols), LAYER, split_ax...  14.5 us
    pallas_call x2, Pallas kernels, attend(): pl.pallas_call(functools.partial(attention_kernel, half), out_shape=(jax....  13 us
    pallas_call x2, Pallas kernels, project(): pl.pallas_call(projection_kernel, out_shape=jax.ShapeDtypeStruct((rows, o...  12.3 us
    all_to_all x1, starting transfers between devices, per_device(): lax.all_to_all(sent_ids, EVERY, split_axis=0, concat_axis=0, tiled=True)  11.1 us
    unnamed x44, local copies, waits for them, and re-layouts  9.69 us
  transfers between devices with their start and end apart: 12, of which 7 were waited for; matrix products, arithmetic and copies ran while one was open for 7% of the time, Pallas kernels for 9%

profile of v6, /device:TPU:0, one launch (start us, length us, event | category | flops | bytes accessed | tf_op | source)
XLA Modules:
  0.0 225.1 jit_solution(10569498390832668683)
XLA Ops:
  0.7 0.8 broadcast_in_dim.58
  1.4 0.8 fusion.11
  2.2 0.1 select_convert_fusion.1.bias_ref
  2.3 0.7 broadcast_in_dim.59
  3.0 11.1 %all-to-all-start.1 = ((s32[128,1,16]{2,1,0:T(1,128)}), s32[128,1,16]{2,1,0:T(1,128)S(1)}, u32[]{:S(2)}, u32[]{:S(2)}) async-start(s32[128,1,16]{2,1,0:T(1,128)} %broadcast_in_dim.59), calls=%async_computation.1 | async-start | bytes 131072 | tf_op jit(solution)/shard_map/all_to_all | solution.py:432
  14.2 9.2 %all-to-all-done.1 = s32[128,1,16]{2,1,0:T(1,128)S(1)} async-done(((s32[128,1,16]{2,1,0:T(1,128)}), s32[128,1,16]{2,1,0:T(1,128)S(1)}, u32[]{:S(2)}, u32[]{:S(2)}) %all-to-all-start.1) | async-done | bytes 8224 | tf_op jit(solution)/shard_map/all_to_all | solution.py:432
  23.5 9.7 %look_up.4 = (bf16[128,1024]{1,0:T(8,128)(2,1)S(1)}, bf16[128,1024]{1,0:T(8,128)(2,1)S(1)}, s32[2,1,1024]{2,1,0:T(1,128)S(1)}) custom-call(s32[4]{0:T(128)S(1)} %pad_add_fusion.2.place_ref, s32[2,1,1024]{2,1,0:T(1,128)S(1)} %reshape_reshape.8.id_row_ref, f32[128,1024]{1,0:T(8,128)S(1)} %select_convert_fusion.1.bias_ref, bf16[4752,1024]{1,0:T(8,128)(2,1)} %vocab_ref.1), custom_call_target="tpu_custom_call" | custom-call | tf_op jit(solution)/shard_map/look_up/pallas_call | solution.py:100
  33.3 1.5 collective-permute-done.1
  34.9 1.6 broadcast_in_dim.63
  36.5 3.7 %all-to-all-start.2 = ((bf16[8,128,1024]{2,1,0:T(8,128)(2,1)}), bf16[8,128,1024]{2,1,0:T(8,128)(2,1)S(1)}, u32[]{:S(2)}, u32[]{:S(2)}) async-start(bf16[8,128,1024]{2,1,0:T(8,128)(2,1)} %broadcast_in_dim.63), calls=%async_computation.2 | async-start | bytes 4194304 | tf_op jit(solution)/shard_map/all_to_all | solution.py:447
  40.2 0.8 copy.33
  41.1 1.7 copy.34
  42.8 2.4 %pad_maximum_fusion.mine_ref = bf16[1024,640]{1,0:T(8,128)(2,1)} fusion(bf16[1024,64]{1,0:T(8,128)(2,1)} %copy.34, bf16[1024,64]{1,0:T(8,128)(2,1)} %copy.33, bf16[1024,512]{1,0:T(8,128)(2,1)S(1)} %copy-done.20), kind=kLoop, calls=%fused_computation.8 | loop fusion | flops 3932160 | bytes 2621440 | tf_op jit(solution)/shard_map/concatenate | solution.py:423
  45.2 0.1 collective-permute-start.2
  45.3 0.7 collective-permute-start.3
  46.0 0.7 dynamic-slice_convert_fusion
  46.7 0.1 reshape.165
  46.8 0.6 reduce_max.8
  49.6 0.1 reshape.164
  49.7 0.5 broadcast.120
  50.2 0.7 fusion.12
  50.9 0.1 div.25
  51.1 0.1 and.34
  51.2 0.1 and_select_fusion.1
  51.3 0.2 slice_reduce_fusion.2
  51.7 19.2 %collective-permute-done.3.rest_0_.rest_2_ = bf16[512,1024]{1,0:T(8,128)(2,1)S(1)} collective-permute-done((bf16[512,1024]{1,0:T(8,128)(2,1)}, bf16[512,1024]{1,0:T(8,128)(2,1)S(1)}, u32[]{:S(2)}, u32[]{:S(2)}) %collective-permute-start.3) | collective-permute-done | bytes 1048608 | tf_op jit(solution)/shard_map/ppermute | solution.py:33
  71.0 6.2 %project.9 = bf16[512,1408]{1,0:T(8,128)(2,1)} custom-call(s32[3]{0:T(128)S(1)} %pad_add_fusion.1.place_ref, s32[1,512]{1,0:T(1,128)S(1)} %reshape_squeeze.7.slot_ref, bf16[1024,1024]{1,0:T(8,128)(2,1)S(1)} %bitcast.31, f32[1,1024]{1,0:T(1,128)S(1)} %bitcast.40, bf16[1024,640]{1,0:T(8,128)(2,1)} %pad_maximum_fusion.mine_ref, ...), custom_call_target="tpu_custom_call" | custom-call | tf_op jit(solution)/shard_map/project/pallas_call | solution.py:299
  77.2 6.1 %project.8 = bf16[512,1408]{1,0:T(8,128)(2,1)} custom-call(s32[3]{0:T(128)S(1)} %pad_add_fusion.1.place_ref, s32[1,512]{1,0:T(1,128)S(1)} %reshape_squeeze.6.slot_ref, bf16[1024,1024]{1,0:T(8,128)(2,1)S(1)} %bitcast.32, f32[1,1024]{1,0:T(1,128)S(1)} %bitcast.41, bf16[1024,640]{1,0:T(8,128)(2,1)} %pad_maximum_fusion.mine_ref, ...), custom_call_target="tpu_custom_call" | custom-call | tf_op jit(solution)/shard_map/project/pallas_call | solution.py:299
  83.3 0.2 while.16
  83.5 31.5 %all_to_all.67 = bf16[64,8,1408]{2,1,0:T(8,128)(2,1)S(1)} all-to-all(bf16[64,8,1408]{2,1,0:T(8,128)(2,1)} %bitcast.38), channel_id=1, replica_groups=mesh['yh'=2,'yl'=2,'zl'=2,'zh'=2,'x'=4,'core'=2] {'yh','yl','zl','zh','x'}, dimensions={0} | all-to-all | bytes 2883584 | tf_op jit(solution)/shard_map/all_to_all | solution.py:497
  115.0 5.6 %all-to-all-start.3 = ((bf16[64,8,1408]{2,1,0:T(8,128)(2,1)}), bf16[64,8,1408]{2,1,0:T(8,128)(2,1)}, u32[]{:S(2)}, u32[]{:S(2)}) async-start(bf16[64,8,1408]{2,1,0:T(8,128)(2,1)} %bitcast.39), calls=%async_computation.3 | async-start | bytes 2883584 | tf_op jit(solution)/shard_map/all_to_all | solution.py:497
  120.9 0.6 fusion.13
  121.6 0.7 reshape_tile.9.length_ref
  122.4 0.1 multiply_sine_fusion
  122.6 0.7 collective-permute-start.5
  123.3 1.5 slice_convert_fusion
  124.8 1.5 reshape.181.bias_ref
  126.3 0.8 copy-done.3
  127.0 0.8 copy-done.5
  127.8 5.8 %attend.3 = (bf16[4,8,8,1024]{3,2,1,0:T(8,128)(2,1)S(1)}, bf16[8,1024]{1,0:T(8,128)(2,1)S(1)}, bf16[8,1024]{1,0:T(8,128)(2,1)S(1)}) custom-call(bf16[8,8,8,1408]{3,2,1,0:T(8,128)(2,1)S(1)} %bitcast.33, f32[8,1,1280]{2,1,0:T(1,128)S(1)} %copy-done.3, f32[8,128]{1,0:T(8,128)S(1)} %get-tuple-element.283.cosine_ref, f32[8,128]{1,0:T(8,128)S(1)} %get-tuple-element.273.sine_ref, ...), custom_call_target="tpu_custom_call" | custom-call | tf_op jit(solution)/shard_map/attend/pallas_call | solution.py:235
  133.6 0.8 copy-done.1
  134.4 0.6 copy-done.7
  135.0 0.6 copy-done.9
  135.6 6.2 %all-to-all-done.3 = bf16[64,8,1408]{2,1,0:T(8,128)(2,1)} async-done(((bf16[64,8,1408]{2,1,0:T(8,128)(2,1)}), bf16[64,8,1408]{2,1,0:T(8,128)(2,1)}, u32[]{:S(2)}, u32[]{:S(2)}) %all-to-all-start.3) | async-done | bytes 1441824 | tf_op jit(solution)/shard_map/all_to_all | solution.py:497
  141.8 4.6 %all-to-all-start.7 = ((bf16[32,8,1024]{2,1,0:T(8,128)(2,1)}), bf16[32,8,1024]{2,1,0:T(8,128)(2,1)}, u32[]{:S(2)}, u32[]{:S(2)}) async-start(bf16[32,8,1024]{2,1,0:T(8,128)(2,1)} %bitcast.36), calls=%async_computation.7 | async-start | bytes 1048576 | tf_op jit(solution)/shard_map/all_to_all | solution.py:511
  146.4 0.7 broadcast_in_dim.64
  147.2 0.7 reshape_tile.8.length_ref
  147.9 0.8 copy-done.4
  148.7 0.8 copy-done.6
  149.5 7.2 %attend.2 = (bf16[4,8,8,1024]{3,2,1,0:T(8,128)(2,1)S(1)}, bf16[8,1024]{1,0:T(8,128)(2,1)S(1)}, bf16[8,1024]{1,0:T(8,128)(2,1)S(1)}) custom-call(bf16[8,8,8,1408]{3,2,1,0:T(8,128)(2,1)} %bitcast.9.arrived_ref.refs_2_, f32[8,1,1280]{2,1,0:T(1,128)S(1)} %copy-done.4, f32[8,128]{1,0:T(8,128)S(1)} %get-tuple-element.282.cosine_ref, ...), custom_call_target="tpu_custom_call" | custom-call | tf_op jit(solution)/shard_map/attend/pallas_call | solution.py:235
  156.7 0.8 copy-done.2
  157.5 0.6 copy-done.11
  158.1 0.6 copy-done.13
  158.7 9.9 %all-to-all-start.4 = ((bf16[32,8,1024]{2,1,0:T(8,128)(2,1)}), bf16[32,8,1024]{2,1,0:T(8,128)(2,1)}, u32[]{:S(2)}, u32[]{:S(2)}) async-start(bf16[32,8,1024]{2,1,0:T(8,128)(2,1)} %bitcast.37), calls=%async_computation.4 | async-start | bytes 1048576 | tf_op jit(solution)/shard_map/all_to_all | solution.py:511
  168.6 3.9 %branch.3 = bf16[256,2048]{1,0:T(8,128)(2,1)} custom-call(s32[3]{0:T(128)S(1)} %copy-done.23, bf16[256,1024]{1,0:T(8,128)(2,1)} %bitcast.17.rows_ref, bf16[512,1024]{1,0:T(8,128)(2,1)} %rest_0_.3, bf16[512,1024]{1,0:T(8,128)(2,1)S(1)} %collective-permute-done.4.rest_1_, bf16[512,1024]{1,0:T(8,128)(2,1)S(1)} %collective-permute-done.3.rest_0_.rest_2_, ...), custom_call_target="tpu_custom_call" | custom-call | tf_op jit(solution)/shard_map/branch/pallas_call | solution.py:344
  172.5 7.7 %all-to-all-done.4 = bf16[32,8,1024]{2,1,0:T(8,128)(2,1)} async-done(((bf16[32,8,1024]{2,1,0:T(8,128)(2,1)}), bf16[32,8,1024]{2,1,0:T(8,128)(2,1)}, u32[]{:S(2)}, u32[]{:S(2)}) %all-to-all-start.4) | async-done | bytes 524320 | tf_op jit(solution)/shard_map/all_to_all | solution.py:511
  180.2 4.7 %all-to-all-start.8 = ((bf16[32,8,2048]{2,1,0:T(8,128)(2,1)}), bf16[32,8,2048]{2,1,0:T(8,128)(2,1)}, u32[]{:S(2)}, u32[]{:S(2)}) async-start(bf16[32,8,2048]{2,1,0:T(8,128)(2,1)} %bitcast.18), calls=%async_computation.8 | async-start | bytes 2097152 | tf_op jit(solution)/shard_map/all_to_all | solution.py:515
  184.9 4.0 %branch.2 = bf16[256,2048]{1,0:T(8,128)(2,1)} custom-call(s32[3]{0:T(128)S(1)} %copy-done.23, bf16[256,1024]{1,0:T(8,128)(2,1)} %bitcast.11.rows_ref, bf16[512,1024]{1,0:T(8,128)(2,1)} %rest_0_.3, bf16[512,1024]{1,0:T(8,128)(2,1)S(1)} %collective-permute-done.4.rest_1_, bf16[512,1024]{1,0:T(8,128)(2,1)S(1)} %collective-permute-done.3.rest_0_.rest_2_, ...), custom_call_target="tpu_custom_call" | custom-call | tf_op jit(solution)/shard_map/branch/pallas_call | solution.py:344
  188.9 11.8 %all-to-all-done.8 = bf16[32,8,2048]{2,1,0:T(8,128)(2,1)} async-done(((bf16[32,8,2048]{2,1,0:T(8,128)(2,1)}), bf16[32,8,2048]{2,1,0:T(8,128)(2,1)}, u32[]{:S(2)}, u32[]{:S(2)}) %all-to-all-start.8) | async-done | bytes 1048608 | tf_op jit(solution)/shard_map/all_to_all | solution.py:515
  200.7 4.9 %all-to-all-start.5 = ((bf16[32,8,2048]{2,1,0:T(8,128)(2,1)}), bf16[32,8,2048]{2,1,0:T(8,128)(2,1)S(1)}, u32[]{:S(2)}, u32[]{:S(2)}) async-start(bf16[32,8,2048]{2,1,0:T(8,128)(2,1)} %bitcast.12), calls=%async_computation.5 | async-start | bytes 2097152 | tf_op jit(solution)/shard_map/all_to_all | solution.py:515
  205.6 0.6 reshape.178
  206.2 0.6 reshape.177
  206.9 14.8 %all-to-all-done.5 = bf16[32,8,2048]{2,1,0:T(8,128)(2,1)S(1)} async-done(((bf16[32,8,2048]{2,1,0:T(8,128)(2,1)}), bf16[32,8,2048]{2,1,0:T(8,128)(2,1)S(1)}, u32[]{:S(2)}, u32[]{:S(2)}) %all-to-all-start.5) | async-done | bytes 1048608 | tf_op jit(solution)/shard_map/all_to_all | solution.py:515
  221.7 3.4 %hidden_sum.1 = bf16[4,4,8192]{2,1,0:T(4,128)(2,1)} custom-call(bf16[2,2,8,8,2048]{4,3,2,1,0:T(8,128)(2,1)S(1)} %bitcast.35, bf16[2,2,8,8,2048]{4,3,2,1,0:T(8,128)(2,1)} %bitcast.19.refs_1_, bf16[8,8,8,1408]{3,2,1,0:T(8,128)(2,1)} %bitcast.9.arrived_ref.refs_2_, bf16[8,8,8,1408]{3,2,1,0:T(8,128)(2,1)S(1)} %bitcast.34), custom_call_target="tpu_custom_call" | custom-call | tf_op jit(solution)/shard_map/hidden_sum/pallas_call | solution.py:379
  (62 shorter events, 1.4 us)
Async XLA Ops:
  3.0 20.4 %all-to-all-start.1 = ((s32[128,1,16]{2,1,0:T(1,128)}), s32[128,1,16]{2,1,0:T(1,128)S(1)}, u32[]{:S(2)}, u32[]{:S(2)}) async-start(s32[128,1,16]{2,1,0:T(1,128)} %broadcast_in_dim.59), calls=%async_computation.1 | async-start | bytes 131072 | tf_op jit(solution)/shard_map/all_to_all | solution.py:432
  23.4 26.0 %copy-start.19 = (s32[2,64,16]{2,1,0:T(8,128)}, s32[2,64,16]{2,1,0:T(8,128)S(1)}, u32[]{:S(2)}) copy-start(s32[2,64,16]{2,1,0:T(8,128)S(1)} %copy.30) | copy-start | bytes 24580
  33.2 1.6 collective-permute-start.1
  36.5 3.7 %copy-start.21 = (bf16[1024,64]{0,1:T(8,128)(2,1)S(1)}, bf16[1024,64]{0,1:T(8,128)(2,1)}, u32[]{:S(2)}) copy-start(bf16[1024,64]{0,1:T(8,128)(2,1)} %param.20) | copy-start | bytes 393220
  36.5 6.3 %copy-start.20 = (bf16[1024,512]{1,0:T(8,128)(2,1)S(1)}, bf16[1024,512]{1,0:T(8,128)(2,1)}, u32[]{:S(2)}) copy-start(bf16[1024,512]{1,0:T(8,128)(2,1)} %param.19) | copy-start | bytes 3145732
  36.5 34.5 %all-to-all-start.2 = ((bf16[8,128,1024]{2,1,0:T(8,128)(2,1)}), bf16[8,128,1024]{2,1,0:T(8,128)(2,1)S(1)}, u32[]{:S(2)}, u32[]{:S(2)}) async-start(bf16[8,128,1024]{2,1,0:T(8,128)(2,1)} %broadcast_in_dim.63), calls=%async_computation.2 | async-start | bytes 4194304 | tf_op jit(solution)/shard_map/all_to_all | solution.py:447
  45.2 25.8 %collective-permute-start.2 = (bf16[1024,640]{1,0:T(8,128)(2,1)}, bf16[1024,640]{1,0:T(8,128)(2,1)}, u32[]{:S(2)}, u32[]{:S(2)}) collective-permute-start(bf16[1024,640]{1,0:T(8,128)(2,1)} %pad_maximum_fusion.mine_ref), channel_id=1, source_target_pairs={{0,1},{1,0},{2,3},{3,2},{4,5},{5,4},{6,7},{7,6},{8,9},{9,8},{10,11... | collective-permute-start | bytes 3932168 | tf_op jit(solution)/shard_map/ppermute | solution.py:29
  45.3 25.6 %collective-permute-start.3 = (bf16[512,1024]{1,0:T(8,128)(2,1)}, bf16[512,1024]{1,0:T(8,128)(2,1)S(1)}, u32[]{:S(2)}, u32[]{:S(2)}) collective-permute-start(bf16[512,1024]{1,0:T(8,128)(2,1)} %rest_0_.3), channel_id=1, source_target_pairs={{0,32},{32,0},{1,33},{33,1},{2,34},{34,2},{3,35},{35,3},{4,36},{36... | collective-permute-start | bytes 3145736 | tf_op jit(solution)/shard_map/ppermute | solution.py:33
  71.0 6.2 %copy-start = (bf16[8,128,1024]{2,1,0:T(8,128)(2,1)}, bf16[8,128,1024]{2,1,0:T(8,128)(2,1)S(1)}, u32[]{:S(2)}) copy-start(bf16[8,128,1024]{2,1,0:T(8,128)(2,1)S(1)} %all-to-all-done.2) | copy-start | bytes 6291460
  83.5 31.5 %copy-start.22 = (s32[3]{0:T(128)}, s32[3]{0:T(128)S(1)}, u32[]{:S(2)}) copy-start(s32[3]{0:T(128)S(1)} %get-tuple-element.520) | copy-start | bytes 40
  115.0 5.7 %copy-start.24 = (s32[4]{0:T(128)S(1)}, s32[4]{0:T(128)}, u32[]{:S(2)}) copy-start(s32[4]{0:T(128)} %param.16) | copy-start | bytes 52
  115.0 26.8 %all-to-all-start.3 = ((bf16[64,8,1408]{2,1,0:T(8,128)(2,1)}), bf16[64,8,1408]{2,1,0:T(8,128)(2,1)}, u32[]{:S(2)}, u32[]{:S(2)}) async-start(bf16[64,8,1408]{2,1,0:T(8,128)(2,1)} %bitcast.39), calls=%async_computation.3 | async-start | bytes 2883584 | tf_op jit(solution)/shard_map/all_to_all | solution.py:497
  120.7 47.9 %collective-permute-start.4 = (bf16[512,1024]{1,0:T(8,128)(2,1)}, bf16[512,1024]{1,0:T(8,128)(2,1)S(1)}, u32[]{:S(2)}, u32[]{:S(2)}) collective-permute-start(bf16[512,1024]{1,0:T(8,128)(2,1)} %rest_0_.3), channel_id=1, source_target_pairs={{0,1},{1,0},{2,3},{3,2},{4,5},{5,4},{6,7},{7,6},{8,9},{9,8},{10,11... | collective-permute-start | bytes 3145736 | tf_op jit(solution)/shard_map/ppermute | solution.py:29
  122.6 46.0 %collective-permute-start.5 = (bf16[512,1024]{1,0:T(8,128)(2,1)S(1)}, bf16[512,1024]{1,0:T(8,128)(2,1)}, u32[]{:S(2)}, u32[]{:S(2)}) collective-permute-start(bf16[512,1024]{1,0:T(8,128)(2,1)S(1)} %collective-permute-done.3.rest_0_.rest_2_), channel_id=1, source_target_pairs={{0,1},{1,0},{2,3},{3,2},{4,5},{5,4},{6,7},{7,6},{8,9},{9,8},{10,11... | collective-permute-start | bytes 3145736 | tf_op jit(solution)/shard_map/ppermute | solution.py:29
  126.3 0.8 copy-start.3
  127.0 0.8 copy-start.5
  133.6 0.8 copy-start.1
  134.4 0.6 copy-start.7
  135.0 0.6 copy-start.9
  141.8 16.9 %all-to-all-start.7 = ((bf16[32,8,1024]{2,1,0:T(8,128)(2,1)}), bf16[32,8,1024]{2,1,0:T(8,128)(2,1)}, u32[]{:S(2)}, u32[]{:S(2)}) async-start(bf16[32,8,1024]{2,1,0:T(8,128)(2,1)} %bitcast.36), calls=%async_computation.7 | async-start | bytes 1048576 | tf_op jit(solution)/shard_map/all_to_all | solution.py:511
  147.9 0.8 copy-start.4
  148.7 0.8 copy-start.6
  149.5 19.1 %copy-start.23 = (s32[3]{0:T(128)S(1)}, s32[3]{0:T(128)}, u32[]{:S(2)}) copy-start(s32[3]{0:T(128)} %copy-done.22) | copy-start | bytes 40
  156.7 0.8 copy-start.2
  157.5 0.6 copy-start.11
  158.1 0.6 copy-start.13
  158.7 21.5 %all-to-all-start.4 = ((bf16[32,8,1024]{2,1,0:T(8,128)(2,1)}), bf16[32,8,1024]{2,1,0:T(8,128)(2,1)}, u32[]{:S(2)}, u32[]{:S(2)}) async-start(bf16[32,8,1024]{2,1,0:T(8,128)(2,1)} %bitcast.37), calls=%async_computation.4 | async-start | bytes 1048576 | tf_op jit(solution)/shard_map/all_to_all | solution.py:511
  180.2 20.5 %all-to-all-start.8 = ((bf16[32,8,2048]{2,1,0:T(8,128)(2,1)}), bf16[32,8,2048]{2,1,0:T(8,128)(2,1)}, u32[]{:S(2)}, u32[]{:S(2)}) async-start(bf16[32,8,2048]{2,1,0:T(8,128)(2,1)} %bitcast.18), calls=%async_computation.8 | async-start | bytes 2097152 | tf_op jit(solution)/shard_map/all_to_all | solution.py:515
  188.8 16.7 %copy-start.10 = (bf16[8,1024]{1,0:T(8,128)(2,1)S(1)}, bf16[8,1024]{1,0:T(8,128)(2,1)}, u32[]{:S(2)}) copy-start(bf16[8,1024]{1,0:T(8,128)(2,1)} %copy-done.9) | copy-start | bytes 49156
  188.8 16.7 %copy-start.14 = (bf16[8,1024]{1,0:T(8,128)(2,1)S(1)}, bf16[8,1024]{1,0:T(8,128)(2,1)}, u32[]{:S(2)}) copy-start(bf16[8,1024]{1,0:T(8,128)(2,1)} %copy-done.13) | copy-start | bytes 49156
  188.8 17.4 %copy-start.8 = (bf16[8,1024]{1,0:T(8,128)(2,1)S(1)}, bf16[8,1024]{1,0:T(8,128)(2,1)}, u32[]{:S(2)}) copy-start(bf16[8,1024]{1,0:T(8,128)(2,1)} %copy-done.7) | copy-start | bytes 49156
  188.9 17.4 %copy-start.12 = (bf16[8,1024]{1,0:T(8,128)(2,1)S(1)}, bf16[8,1024]{1,0:T(8,128)(2,1)}, u32[]{:S(2)}) copy-start(bf16[8,1024]{1,0:T(8,128)(2,1)} %copy-done.11) | copy-start | bytes 49156
  200.7 21.0 %all-to-all-start.5 = ((bf16[32,8,2048]{2,1,0:T(8,128)(2,1)}), bf16[32,8,2048]{2,1,0:T(8,128)(2,1)S(1)}, u32[]{:S(2)}, u32[]{:S(2)}) async-start(bf16[32,8,2048]{2,1,0:T(8,128)(2,1)} %bitcast.12), calls=%async_computation.5 | async-start | bytes 2097152 | tf_op jit(solution)/shard_map/all_to_all | solution.py:515

commit v7 on v6

--- a/solution.py
+++ b/solution.py
@@ -12,7 +12,8 @@
 ROUND_ROWS = 126
 SENT_ROWS = 128
 CHIP_COUNT = 8
-HALVES = 2
+WHOLE_VMEM = 60 * 1024 * 1024
+HALVES = 1
 
 norm_epsilon = 1e-06
 rope_base = 1000000.0
@@ -43,7 +44,7 @@
     return jnp.transpose(wide)[:, :1].astype(jnp.int32)
 
 
-def lookup_kernel(place_ref, id_row_ref, bias_ref, vocab_ref, *rest):
+def lookup_kernel(place_ref, id_row_ref, q_ref, k_ref, v_ref, vocab_ref, *rest):
     mine_ref, theirs_ref, rank_ref, list_ref, total_ref = rest
     step = pl.program_id(0)
     chip, core, first = place_ref[0], place_ref[1], place_ref[3]
@@ -84,15 +85,24 @@
 
     @pl.when(step == pl.num_programs(0) - 1)
     def _():
+        width = total_ref.shape[1]
+        pieces = [piece[...].astype(jnp.float32) for piece in (q_ref, k_ref, v_ref)]
+        filled = sum(piece.shape[1] for piece in pieces)
+        pieces.append(jnp.zeros((1, width - filled), jnp.float32))
+        bias = jnp.broadcast_to(jnp.concatenate(pieces, axis=1), (16, width))
+        is_bias = (
+            lax.broadcasted_iota(jnp.int32, (16, 1), 0) == ROUND_ROWS + core - (SENT_ROWS - 16)
+        )
         for side, target in ((0, mine_ref), (1, theirs_ref)):
             plane = (core + side) % 2
             start = pl.multiple_of(plane * SENT_ROWS, SENT_ROWS)
-            target[...] = (total_ref[pl.ds(start, SENT_ROWS), :] + bias_ref[...]).astype(
-                jnp.bfloat16
-            )
-
-
-def look_up(place, plane_ids, bias_rows, embedding):
+            target[...] = total_ref[pl.ds(start, SENT_ROWS), :].astype(jnp.bfloat16)
+            tail = total_ref[pl.ds(start + SENT_ROWS - 16, 16), :]
+            tail = jnp.where(is_bias, bias, tail)
+            target[SENT_ROWS - 16 :, :] = tail.astype(jnp.bfloat16)
+
+
+def look_up(place, plane_ids, biases, embedding):
     planes, rows = plane_ids.shape
     vocab_here, width = embedding.shape
     steps = 3
@@ -108,7 +118,7 @@
         in_specs=[
             SMEM,
             whole(planes, 1, rows),
-            whole(SENT_ROWS, width),
+            *[whole(1, bias.shape[0]) for bias in biases],
             pl.BlockSpec((vocab_here // steps, width), lambda i: (i, 0)),
         ],
         out_specs=(
@@ -122,14 +132,20 @@
         ],
         compiler_params=pltpu.CompilerParams(vmem_limit_bytes=48 * 1024 * 1024),
         name="look_up",
-    )(place, plane_ids.reshape(planes, 1, rows), bias_rows, embedding)
+    )(
+        place,
+        plane_ids.reshape(planes, 1, rows),
+        *[bias.reshape(1, -1) for bias in biases],
+        embedding,
+    )
 
 
 def attention_kernel(
     half,
     arrived_ref, bias_ref, cosine_ref, sine_ref, length_ref, keys_ref, values_ref, *rest
 ):
-    out_ref, new_keys_ref, new_values_ref, key_buf, value_buf, key_sem, value_sem = rest
+    out_ref, new_keys_ref, new_values_ref = rest[:3]
+    key_buf, value_buf, query_buf, key_sem, value_sem = rest[3:]
     groups, chips, rows, _ = arrived_ref.shape
     seqs, cache_len, _ = key_buf.shape
     steps = rows // seqs
@@ -168,8 +184,6 @@
     fresh_valid = (fresh_at // steps == row_seq) & (fresh_at % steps <= row_step)
     cache_valid = lax.broadcasted_iota(jnp.int32, (many, cache_len), 1) < length_ref[...]
     score_scale = HD ** (-0.5)
-    for copy in copies:
-        copy.wait()
     for chip in range(chips):
         span = slice(chip * HD, (chip + 1) * HD)
         joined = arrived_ref[0, chip, :, : 2 * core_cols].astype(jnp.float32)
@@ -180,7 +194,7 @@
         for head in range(heads):
             start = (head // half_heads) * core_cols + (head % half_heads) * HD
             parts.append(rotated(joined[:, start : start + HD]))
-        queries = jnp.concatenate(parts, axis=0).astype(jnp.bfloat16)
+        query_buf[chip] = jnp.concatenate(parts, axis=0).astype(jnp.bfloat16)
         low = joined[:, core_cols - HD : core_cols]
         high = joined[:, 2 * core_cols - HD :]
         fresh_keys = rotated(jnp.where(lane < HD // 2, low, pltpu.roll(high, HD // 2, 1))).astype(
@@ -191,6 +205,13 @@
         )
         new_keys_ref[:, span] = fresh_keys
         new_values_ref[:, span] = fresh_values
+    for copy in copies:
+        copy.wait()
+    for chip in range(chips):
+        span = slice(chip * HD, (chip + 1) * HD)
+        queries = query_buf[chip]
+        fresh_keys = new_keys_ref[:, span]
+        fresh_values = new_values_ref[:, span]
         scores = None
         for seq in range(seqs):
             found = lax.dot_general(
@@ -244,10 +265,11 @@
         scratch_shapes=[
             pltpu.VMEM((seqs, cache_len, kv_cols), jnp.bfloat16),
             pltpu.VMEM((seqs, cache_len, kv_cols), jnp.bfloat16),
+            pltpu.VMEM((chips, heads * rows, HD), jnp.bfloat16),
             pltpu.SemaphoreType.DMA((seqs,)),
             pltpu.SemaphoreType.DMA((seqs,)),
         ],
-        compiler_params=pltpu.CompilerParams(vmem_limit_bytes=48 * 1024 * 1024),
+        compiler_params=pltpu.CompilerParams(vmem_limit_bytes=WHOLE_VMEM),
         name="attend",
     )(arrived, bias, cosine, sine, row_lengths, key_cache, value_cache)
 
@@ -260,10 +282,12 @@
     step = pl.program_id(0)
     slot = turned(slot_ref[...])
     rows = slot.shape[0]
-    copies = [
-        pltpu.make_async_copy(source, weight_buf.at[side], sem.at[side])
-        for side, source in enumerate((mine_ref, theirs_ref))
-    ]
+    copies = []
+    for side, source in enumerate((mine_ref, theirs_ref)):
+        where = pl.multiple_of(((core + side) % 2) * cols, cols)
+        copies.append(
+            pltpu.make_async_copy(source, weight_buf.at[:, pl.ds(where, cols)], sem.at[side])
+        )
 
     @pl.when(step == 0)
     def _():
@@ -282,10 +306,8 @@
         for copy in copies:
             copy.wait()
 
-    for side in range(2):
-        product = jnp.dot(gained, weight_buf[side], preferred_element_type=jnp.float32)
-        where = pl.multiple_of(((core + side) % 2) * cols, cols)
-        out_ref[:, pl.ds(where, cols)] = product.astype(jnp.bfloat16)
+    product = jnp.dot(gained, weight_buf[...], preferred_element_type=jnp.float32)
+    out_ref[:, : 2 * cols] = product.astype(jnp.bfloat16)
     strip = out_ref.shape[1] - 2 * cols
     out_ref[:, 2 * cols :] = wide_ref[:, pl.ds(pl.multiple_of(chip * strip, strip), strip)]
 
@@ -310,7 +332,7 @@
         out_specs=pl.BlockSpec((block, out_cols), lambda i: (i, 0)),
         scratch_shapes=[
             pltpu.VMEM((block, width), jnp.bfloat16),
-            pltpu.VMEM((2, width, cols), jnp.bfloat16),
+            pltpu.VMEM((width, 2 * cols), jnp.bfloat16),
             pltpu.SemaphoreType.DMA((2,)),
         ],
         compiler_params=pltpu.CompilerParams(vmem_limit_bytes=48 * 1024 * 1024),
@@ -346,7 +368,7 @@
         out_shape=jax.ShapeDtypeStruct((rows.shape[0], count // 2 * width), jnp.bfloat16),
         in_specs=[SMEM, VMEM] + [VMEM] * count,
         out_specs=VMEM,
-        compiler_params=pltpu.CompilerParams(vmem_limit_bytes=48 * 1024 * 1024),
+        compiler_params=pltpu.CompilerParams(vmem_limit_bytes=WHOLE_VMEM),
         name="branch",
     )(place, rows, *weights)
 
@@ -424,25 +446,17 @@
     both_other = swap_cores(both)
     o_line = swap_lines(o_weight)
     o_weights = (o_weight, swap_cores(o_weight), o_line, swap_cores(o_line))
-    own_bias = jnp.concatenate([q_bias, k_bias, v_bias])
-    core_cols = own_bias.shape[0]
+    core_cols = q_bias.shape[0] + k_bias.shape[0] + v_bias.shape[0]
     q_cols = q_bias.shape[0]
 
     sent_ids = jnp.broadcast_to(token_ids.reshape(1, rows_here), (parties * 2, rows_here))
     every_id = lax.all_to_all(sent_ids, EVERY, split_axis=0, concat_axis=0, tiled=True)
     plane_ids = every_id.reshape(parties, 2, rows_here).transpose(1, 0, 2).reshape(2, plane_rows)
     own_holder = lax.dynamic_index_in_dim(plane_ids, core, 0, keepdims=False) // (2 * vocab_here)
-    row_at = jnp.arange(SENT_ROWS, dtype=jnp.int32)
-    bias_rows = jnp.where(
-        row_at[:, None] == ROUND_ROWS + core,
-        jnp.pad(own_bias, (0, width_here - core_cols))[None, :],
-        jnp.zeros((), jnp.bfloat16),
-    ).astype(jnp.float32)
-
     def exchange(turn):
         first = turn * ROUND_ROWS
         turn_place = jnp.concatenate([place, jnp.asarray(first, jnp.int32).reshape(1)])
-        mine, theirs, rank = look_up(turn_place, plane_ids, bias_rows, embedding)
+        mine, theirs, rank = look_up(turn_place, plane_ids, (q_bias, k_bias, v_bias), embedding)
         merged = mine + swap_cores(theirs)
         table = lax.all_to_all(
             jnp.broadcast_to(merged[None], (chips, SENT_ROWS, width_here)),

time: 227 us -> 208 us (0.916)
  waiting for transfers between devices: 70.4 us -> 110 us
  blocking collectives: 31.5 us -> 0 us
  starting transfers between devices: 46.2 us -> 34.4 us
  local copies, waits for them, and re-layouts: 20 us -> 12.4 us
  Pallas kernels: 46.3 us -> 41.6 us
    all_to_all x1 -> x0, blocking collectives: 31.5 us -> none  [per_device(): lax.all_to_all(payloads[half], PLANE, split_axis=0, concat_axis=0, tiled=...]
    all_to_all x1, waiting for transfers between devices: 6.16 us -> 35 us  [per_device(): lax.all_to_all(payloads[half], PLANE, split_axis=0, concat_axis=0, tiled=...]
    all_to_all x2 -> x1, starting transfers between devices: 14.5 us -> 3.97 us  [per_device(): lax.all_to_all(spread.reshape(-1, half_rows, 2 * q_cols), LAYER, split_ax...]
    all_to_all x2 -> x1, waiting for transfers between devices: 7.71 us -> 17.3 us  [per_device(): lax.all_to_all(spread.reshape(-1, half_rows, 2 * q_cols), LAYER, split_ax...]
    unnamed x44 -> x28, local copies, waits for them, and re-layouts: 9.69 us -> 5.48 us
    all_to_all x2 -> x1, starting transfers between devices: 9.54 us -> 5.46 us  [per_device(): lax.all_to_all(branch, LAYER, split_axis=0, concat_axis=0, tiled=True)]
    all_to_all x1, starting transfers between devices: 5.63 us -> 8.69 us  [per_device(): lax.all_to_all(payloads[half], PLANE, split_axis=0, concat_axis=0, tiled=...]
    pallas_call x2 -> x1, Pallas kernels: 7.88 us -> 6.2 us  [branch_out(): pl.pallas_call(branch_kernel, out_shape=jax.ShapeDtypeStruct((rows.shape[...]
  transfers between devices with their start and end apart: 12 -> 10, of which waited for: 7 -> 6; matrix products, arithmetic and copies ran while one was open for 7% -> 6% of each run, Pallas kernels for 9% -> 6%
where the time goes in v7:
time: 208 us; the launch traced here: 207 us
  waiting for transfers between devices  110 us (53%)
  Pallas kernels  41.6 us (20%)
  starting transfers between devices  34.4 us (17%)
  local copies, waits for them, and re-layouts  12.4 us (6%)
  other arithmetic  5.65 us (3%)
  between operations  2.9 us (1%)
    all_to_all x1, waiting for transfers between devices, per_device(): lax.all_to_all(payloads[half], PLANE, split_axis=0, concat_axis=0, tiled=...  35 us
    all_to_all x1, waiting for transfers between devices, per_device(): lax.all_to_all(branch, LAYER, split_axis=0, concat_axis=0, tiled=True)  26.5 us
    ppermute x1, waiting for transfers between devices, swap_lines(): return lax.ppermute(value, 'yl', [(0, 1), (1, 0)])  21.3 us
    all_to_all x1, waiting for transfers between devices, per_device(): lax.all_to_all(spread.reshape(-1, half_rows, 2 * q_cols), LAYER, split_ax...  17.3 us
    pallas_call x1, Pallas kernels, attend(): pl.pallas_call(functools.partial(attention_kernel, half), out_shape=(jax....  11.4 us
    all_to_all x1, starting transfers between devices, per_device(): lax.all_to_all(sent_ids, EVERY, split_axis=0, concat_axis=0, tiled=True)  11.1 us
    pallas_call x1, Pallas kernels, project(): pl.pallas_call(projection_kernel, out_shape=jax.ShapeDtypeStruct((rows, o...  10.7 us
    pallas_call x1, Pallas kernels, look_up(): pl.pallas_call(lookup_kernel, out_shape=(jax.ShapeDtypeStruct((SENT_ROWS,...  9.67 us
  transfers between devices with their start and end apart: 10, of which 6 were waited for; matrix products, arithmetic and copies ran while one was open for 6% of the time, Pallas kernels for 6%

profile of v7, /device:TPU:0, one launch (start us, length us, event | category | flops | bytes accessed | tf_op | source)
XLA Modules:
  0.0 207.3 jit_solution(3128825859268754516)
XLA Ops:
  0.6 0.8 broadcast_in_dim.15
  1.4 0.7 broadcast_in_dim.16
  2.1 11.1 %all-to-all-start.1 = ((s32[128,1,16]{2,1,0:T(1,128)}), s32[128,1,16]{2,1,0:T(1,128)S(1)}, u32[]{:S(2)}, u32[]{:S(2)}) async-start(s32[128,1,16]{2,1,0:T(1,128)} %broadcast_in_dim.16), calls=%async_computation.1 | async-start | bytes 131072 | tf_op jit(solution)/shard_map/all_to_all | solution.py:453
  13.2 0.1 pad_add_fusion.2.place_ref
  13.3 0.7 reshape.201.q_ref
  14.0 8.5 %all-to-all-done.1 = s32[128,1,16]{2,1,0:T(1,128)S(1)} async-done(((s32[128,1,16]{2,1,0:T(1,128)}), s32[128,1,16]{2,1,0:T(1,128)S(1)}, u32[]{:S(2)}, u32[]{:S(2)}) %all-to-all-start.1) | async-done | bytes 8224 | tf_op jit(solution)/shard_map/all_to_all | solution.py:453
  22.5 0.1 reshape_reshape.8.id_row_ref
  22.6 9.7 %look_up.4 = (bf16[128,1024]{1,0:T(8,128)(2,1)S(1)}, bf16[128,1024]{1,0:T(8,128)(2,1)S(1)}, s32[2,1,1024]{2,1,0:T(1,128)S(1)}) custom-call(s32[4]{0:T(128)S(1)} %pad_add_fusion.2.place_ref, s32[2,1,1024]{2,1,0:T(1,128)S(1)} %reshape_reshape.8.id_row_ref, bf16[1,512]{1,0:T(2,128)(2,1)S(1)} %reshape.201.q_ref, bf16[1,64]{1,0:T(2,128)(2,1)} %bitcast.61, ...), custom_call_target="tpu_custom_call" | custom-call | tf_op jit(solution)/shard_map/look_up/pallas_call | solution.py:110
  32.3 0.1 collective-permute-start.1
  32.3 1.5 collective-permute-done.1
  33.9 0.1 add.92
  33.9 1.6 broadcast_in_dim.17
  35.6 3.7 %all-to-all-start.2 = ((bf16[8,128,1024]{2,1,0:T(8,128)(2,1)}), bf16[8,128,1024]{2,1,0:T(8,128)(2,1)S(1)}, u32[]{:S(2)}, u32[]{:S(2)}) async-start(bf16[8,128,1024]{2,1,0:T(8,128)(2,1)} %broadcast_in_dim.17), calls=%async_computation.2 | async-start | bytes 4194304 | tf_op jit(solution)/shard_map/all_to_all | solution.py:461
  39.3 1.1 copy.31
  40.4 1.7 copy.32
  42.1 2.3 %pad_maximum_fusion.mine_ref = bf16[1024,640]{1,0:T(8,128)(2,1)} fusion(bf16[1024,64]{1,0:T(8,128)(2,1)} %copy.32, bf16[1024,64]{1,0:T(8,128)(2,1)S(1)} %copy.31, bf16[1024,512]{1,0:T(8,128)(2,1)S(1)} %copy-done.8), kind=kLoop, calls=%fused_computation.5 | loop fusion | flops 3932160 | bytes 2621440 | tf_op jit(solution)/shard_map/concatenate | solution.py:445
  44.4 0.1 collective-permute-start.2
  44.6 0.6 collective-permute-start.3
  45.2 0.1 pad_add_fusion.1.place_ref
  45.3 0.7 dynamic-slice_convert_fusion
  46.0 0.1 reshape.205
  46.1 0.6 reduce_max.8
  48.7 0.1 reshape_reshape.9
  48.8 0.1 fusion.4
  48.9 21.3 %collective-permute-done.3.rest_0_.rest_2_ = bf16[512,1024]{1,0:T(8,128)(2,1)S(1)} collective-permute-done((bf16[512,1024]{1,0:T(8,128)(2,1)}, bf16[512,1024]{1,0:T(8,128)(2,1)S(1)}, u32[]{:S(2)}, u32[]{:S(2)}) %collective-permute-start.3) | collective-permute-done | bytes 1048608 | tf_op jit(solution)/shard_map/ppermute | solution.py:34
  70.2 0.0 collective-permute-done.2.theirs_ref
  70.2 0.0 all-to-all-done.2
  70.2 0.0 copy-start.9
  70.2 0.0 copy-start.12
  70.2 0.0 copy-start.13
  70.3 10.7 %project.4 = bf16[1024,1408]{1,0:T(8,128)(2,1)} custom-call(s32[3]{0:T(128)S(1)} %pad_add_fusion.1.place_ref, s32[1,1024]{1,0:T(1,128)S(1)} %get-tuple-element.237.slot_ref, bf16[1024,1024]{1,0:T(8,128)(2,1)S(1)} %bitcast.52, f32[1,1024]{1,0:T(1,128)S(1)} %bitcast.59, bf16[1024,640]{1,0:T(8,128)(2,1)} %pad_maximum_fusion.mine_ref, ...), custom_call_target="tpu_custom_call" | custom-call | tf_op jit(solution)/shard_map/project/pallas_call | solution.py:321
  81.0 0.0 copy-done.3
  81.0 0.0 copy-done.2
  81.0 0.0 copy-done.9
  81.0 0.0 copy-done.12
  81.0 0.0 copy-done.13
  81.0 0.2 while.13
  81.2 0.0 copy-start.14
  81.3 8.7 %all-to-all-start.3 = ((bf16[64,16,1408]{2,1,0:T(8,128)(2,1)}), bf16[64,16,1408]{2,1,0:T(8,128)(2,1)S(1)}, u32[]{:S(2)}, u32[]{:S(2)}) async-start(bf16[64,16,1408]{2,1,0:T(8,128)(2,1)} %bitcast.53), calls=%async_computation.3 | async-start | bytes 5767168 | tf_op jit(solution)/shard_map/all_to_all | solution.py:511
  90.0 0.1 collective-permute-start.4
  90.1 0.0 copy-done.14
  90.1 0.1 add.97
  90.1 0.1 add.98
  90.2 0.1 add.100
  90.3 0.7 reshape_tile.4.length_ref
  91.0 0.1 fusion.3
  91.2 0.7 pad_maximum_fusion.1
  91.9 0.5 collective-permute-start.5
  92.3 0.9 slice_convert_fusion
  93.2 0.7 reshape.217.bias_ref
  93.9 35.0 %all-to-all-done.3 = bf16[64,16,1408]{2,1,0:T(8,128)(2,1)S(1)} async-done(((bf16[64,16,1408]{2,1,0:T(8,128)(2,1)}), bf16[64,16,1408]{2,1,0:T(8,128)(2,1)S(1)}, u32[]{:S(2)}, u32[]{:S(2)}) %all-to-all-start.3) | async-done | bytes 2883616 | tf_op jit(solution)/shard_map/all_to_all | solution.py:511
  128.9 1.6 copy-done
  130.5 11.4 %attend.1 = (bf16[4,8,16,1024]{3,2,1,0:T(8,128)(2,1)}, bf16[16,1024]{1,0:T(8,128)(2,1)}, bf16[16,1024]{1,0:T(8,128)(2,1)}) custom-call(bf16[8,8,16,1408]{3,2,1,0:T(8,128)(2,1)} %bitcast.50, f32[8,1,1280]{2,1,0:T(1,128)} %reshape.217.bias_ref, f32[16,128]{1,0:T(8,128)} %get-tuple-element.242.cosine_ref, f32[16,128]{1,0:T(8,128)} %get-tuple-element.243.sine_ref, ...), custom_call_target="tpu_custom_call" | custom-call | tf_op jit(solution)/shard_map/attend/pallas_call | solution.py:256
  142.0 4.0 %all-to-all-start.4 = ((bf16[32,16,1024]{2,1,0:T(8,128)(2,1)}), bf16[32,16,1024]{2,1,0:T(8,128)(2,1)S(1)}, u32[]{:S(2)}, u32[]{:S(2)}) async-start(bf16[32,16,1024]{2,1,0:T(8,128)(2,1)} %bitcast.56), calls=%async_computation.4 | async-start | bytes 2097152 | tf_op jit(solution)/shard_map/all_to_all | solution.py:525
  145.9 0.0 collective-permute-done.4.rest_1_
  145.9 0.0 collective-permute-done.5.rest_3_
  146.0 17.3 %all-to-all-done.4 = bf16[32,16,1024]{2,1,0:T(8,128)(2,1)S(1)} async-done(((bf16[32,16,1024]{2,1,0:T(8,128)(2,1)}), bf16[32,16,1024]{2,1,0:T(8,128)(2,1)S(1)}, u32[]{:S(2)}, u32[]{:S(2)}) %all-to-all-start.4) | async-done | bytes 1048608 | tf_op jit(solution)/shard_map/all_to_all | solution.py:525
  163.3 1.0 copy-done.6
  164.3 6.2 %branch.1 = bf16[512,2048]{1,0:T(8,128)(2,1)} custom-call(s32[3]{0:T(128)S(1)} %get-tuple-element.474, bf16[512,1024]{1,0:T(8,128)(2,1)} %bitcast.55, bf16[512,1024]{1,0:T(8,128)(2,1)} %rest_0_.1, bf16[512,1024]{1,0:T(8,128)(2,1)} %collective-permute-done.4.rest_1_, bf16[512,1024]{1,0:T(8,128)(2,1)} %copy-done.3, ...), custom_call_target="tpu_custom_call" | custom-call | tf_op jit(solution)/shard_map/branch/pallas_call | solution.py:366
  170.5 5.5 %all-to-all-start.5 = ((bf16[32,16,2048]{2,1,0:T(8,128)(2,1)}), bf16[32,16,2048]{2,1,0:T(8,128)(2,1)}, u32[]{:S(2)}, u32[]{:S(2)}) async-start(bf16[32,16,2048]{2,1,0:T(8,128)(2,1)} %bitcast.54), calls=%async_computation.5 | async-start | bytes 4194304 | tf_op jit(solution)/shard_map/all_to_all | solution.py:529
  176.0 0.6 reshape.213
  176.6 0.6 reshape.214
  177.3 26.5 %all-to-all-done.5 = bf16[32,16,2048]{2,1,0:T(8,128)(2,1)} async-done(((bf16[32,16,2048]{2,1,0:T(8,128)(2,1)}), bf16[32,16,2048]{2,1,0:T(8,128)(2,1)}, u32[]{:S(2)}, u32[]{:S(2)}) %all-to-all-start.5) | async-done | bytes 2097184 | tf_op jit(solution)/shard_map/all_to_all | solution.py:529
  203.7 3.6 %hidden_sum.1 = bf16[4,4,8192]{2,1,0:T(4,128)(2,1)} custom-call(bf16[2,2,8,16,2048]{4,3,2,1,0:T(8,128)(2,1)} %bitcast.22.refs_0_, bf16[8,8,16,1408]{3,2,1,0:T(8,128)(2,1)S(1)} %bitcast.51), custom_call_target="tpu_custom_call" | custom-call | tf_op jit(solution)/shard_map/hidden_sum/pallas_call | solution.py:401
  (21 shorter events, 0.1 us)
Async XLA Ops:
  2.1 20.4 %all-to-all-start.1 = ((s32[128,1,16]{2,1,0:T(1,128)}), s32[128,1,16]{2,1,0:T(1,128)S(1)}, u32[]{:S(2)}, u32[]{:S(2)}) async-start(s32[128,1,16]{2,1,0:T(1,128)} %broadcast_in_dim.16), calls=%async_computation.1 | async-start | bytes 131072 | tf_op jit(solution)/shard_map/all_to_all | solution.py:453
  22.5 26.2 %copy-start.7 = (s32[2,64,16]{2,1,0:T(8,128)}, s32[2,64,16]{2,1,0:T(8,128)S(1)}, u32[]{:S(2)}) copy-start(s32[2,64,16]{2,1,0:T(8,128)S(1)} %copy.28) | copy-start | bytes 24580
  32.3 1.6 collective-permute-start.1
  35.6 6.6 %copy-start.8 = (bf16[1024,512]{1,0:T(8,128)(2,1)S(1)}, bf16[1024,512]{1,0:T(8,128)(2,1)}, u32[]{:S(2)}) copy-start(bf16[1024,512]{1,0:T(8,128)(2,1)} %param.19) | copy-start | bytes 3145732
  35.6 34.7 %all-to-all-start.2 = ((bf16[8,128,1024]{2,1,0:T(8,128)(2,1)}), bf16[8,128,1024]{2,1,0:T(8,128)(2,1)S(1)}, u32[]{:S(2)}, u32[]{:S(2)}) async-start(bf16[8,128,1024]{2,1,0:T(8,128)(2,1)} %broadcast_in_dim.17), calls=%async_computation.2 | async-start | bytes 4194304 | tf_op jit(solution)/shard_map/all_to_all | solution.py:461
  44.4 25.8 %collective-permute-start.2 = (bf16[1024,640]{1,0:T(8,128)(2,1)}, bf16[1024,640]{1,0:T(8,128)(2,1)}, u32[]{:S(2)}, u32[]{:S(2)}) collective-permute-start(bf16[1024,640]{1,0:T(8,128)(2,1)} %pad_maximum_fusion.mine_ref), channel_id=1, source_target_pairs={{0,1},{1,0},{2,3},{3,2},{4,5},{5,4},{6,7},{7,6},{8,9},{9,8},{10,11... | collective-permute-start | bytes 3932168 | tf_op jit(solution)/shard_map/ppermute | solution.py:30
  44.6 25.6 %collective-permute-start.3 = (bf16[512,1024]{1,0:T(8,128)(2,1)}, bf16[512,1024]{1,0:T(8,128)(2,1)S(1)}, u32[]{:S(2)}, u32[]{:S(2)}) collective-permute-start(bf16[512,1024]{1,0:T(8,128)(2,1)} %rest_0_.1), channel_id=1, source_target_pairs={{0,32},{32,0},{1,33},{33,1},{2,34},{34,2},{3,35},{35,3},{4,36},{36... | collective-permute-start | bytes 3145736 | tf_op jit(solution)/shard_map/ppermute | solution.py:34
  70.2 10.8 %copy-start.3 = (bf16[512,1024]{1,0:T(8,128)(2,1)}, bf16[512,1024]{1,0:T(8,128)(2,1)S(1)}, u32[]{:S(2)}) copy-start(bf16[512,1024]{1,0:T(8,128)(2,1)S(1)} %collective-permute-done.3.rest_0_.rest_2_) | copy-start | bytes 3145732
  70.2 10.8 %copy-start.2 = (bf16[8,128,1024]{2,1,0:T(8,128)(2,1)}, bf16[8,128,1024]{2,1,0:T(8,128)(2,1)S(1)}, u32[]{:S(2)}) copy-start(bf16[8,128,1024]{2,1,0:T(8,128)(2,1)S(1)} %all-to-all-done.2) | copy-start | bytes 6291460
  70.2 10.8 %copy-start.9 = (bf16[512]{0:T(512)(128)(2,1)S(1)}, bf16[512]{0:T(512)(128)(2,1)}, u32[]{:S(2)}) copy-start(bf16[512]{0:T(512)(128)(2,1)} %param.22) | copy-start | bytes 3076
  70.2 10.8 %copy-start.12 = (bf16[64]{0:T(256)(128)(2,1)S(1)}, bf16[64]{0:T(256)(128)(2,1)}, u32[]{:S(2)}) copy-start(bf16[64]{0:T(256)(128)(2,1)} %param.23) | copy-start | bytes 388
  70.2 10.8 %copy-start.13 = (bf16[64]{0:T(256)(128)(2,1)S(1)}, bf16[64]{0:T(256)(128)(2,1)}, u32[]{:S(2)}) copy-start(bf16[64]{0:T(256)(128)(2,1)} %param.24) | copy-start | bytes 388
  81.2 8.8 %copy-start.14 = (s32[4]{0:T(128)S(1)}, s32[4]{0:T(128)}, u32[]{:S(2)}) copy-start(s32[4]{0:T(128)} %param.16) | copy-start | bytes 52
  81.3 47.7 %all-to-all-start.3 = ((bf16[64,16,1408]{2,1,0:T(8,128)(2,1)}), bf16[64,16,1408]{2,1,0:T(8,128)(2,1)S(1)}, u32[]{:S(2)}, u32[]{:S(2)}) async-start(bf16[64,16,1408]{2,1,0:T(8,128)(2,1)} %bitcast.53), calls=%async_computation.3 | async-start | bytes 5767168 | tf_op jit(solution)/shard_map/all_to_all | solution.py:511
  90.0 56.0 %collective-permute-start.4 = (bf16[512,1024]{1,0:T(8,128)(2,1)}, bf16[512,1024]{1,0:T(8,128)(2,1)}, u32[]{:S(2)}, u32[]{:S(2)}) collective-permute-start(bf16[512,1024]{1,0:T(8,128)(2,1)} %rest_0_.1), channel_id=1, source_target_pairs={{0,1},{1,0},{2,3},{3,2},{4,5},{5,4},{6,7},{7,6},{8,9},{9,8},{10,11... | collective-permute-start | bytes 3145736 | tf_op jit(solution)/shard_map/ppermute | solution.py:30
  91.9 54.1 %collective-permute-start.5 = (bf16[512,1024]{1,0:T(8,128)(2,1)}, bf16[512,1024]{1,0:T(8,128)(2,1)}, u32[]{:S(2)}, u32[]{:S(2)}) collective-permute-start(bf16[512,1024]{1,0:T(8,128)(2,1)} %copy-done.3), channel_id=1, source_target_pairs={{0,1},{1,0},{2,3},{3,2},{4,5},{5,4},{6,7},{7,6},{8,9},{9,8},{10,11... | collective-permute-start | bytes 3145736 | tf_op jit(solution)/shard_map/ppermute | solution.py:30
  128.9 1.6 copy-start
  142.0 21.3 %all-to-all-start.4 = ((bf16[32,16,1024]{2,1,0:T(8,128)(2,1)}), bf16[32,16,1024]{2,1,0:T(8,128)(2,1)S(1)}, u32[]{:S(2)}, u32[]{:S(2)}) async-start(bf16[32,16,1024]{2,1,0:T(8,128)(2,1)} %bitcast.56), calls=%async_computation.4 | async-start | bytes 2097152 | tf_op jit(solution)/shard_map/all_to_all | solution.py:525
  163.3 1.0 copy-start.6
  170.5 5.5 %copy-start.11 = (bf16[16,1024]{1,0:T(8,128)(2,1)S(1)}, bf16[16,1024]{1,0:T(8,128)(2,1)}, u32[]{:S(2)}) copy-start(bf16[16,1024]{1,0:T(8,128)(2,1)} %get-tuple-element.177) | copy-start | bytes 98308
  170.5 6.1 %copy-start.10 = (bf16[16,1024]{1,0:T(8,128)(2,1)S(1)}, bf16[16,1024]{1,0:T(8,128)(2,1)}, u32[]{:S(2)}) copy-start(bf16[16,1024]{1,0:T(8,128)(2,1)} %get-tuple-element.178) | copy-start | bytes 98308
  170.5 33.2 %copy-start.1 = (bf16[64,16,1408]{2,1,0:T(8,128)(2,1)S(1)}, bf16[64,16,1408]{2,1,0:T(8,128)(2,1)}, u32[]{:S(2)}) copy-start(bf16[64,16,1408]{2,1,0:T(8,128)(2,1)} %copy-done) | copy-start | bytes 8650756
  170.5 33.2 %all-to-all-start.5 = ((bf16[32,16,2048]{2,1,0:T(8,128)(2,1)}), bf16[32,16,2048]{2,1,0:T(8,128)(2,1)}, u32[]{:S(2)}, u32[]{:S(2)}) async-start(bf16[32,16,2048]{2,1,0:T(8,128)(2,1)} %bitcast.54), calls=%async_computation.5 | async-start | bytes 4194304 | tf_op jit(solution)/shard_map/all_to_all | solution.py:529

commit v8 on v7

--- a/solution.py
+++ b/solution.py
@@ -151,7 +151,6 @@
     steps = rows // seqs
     core_cols = bias_ref.shape[2] // 2
     heads = out_ref.shape[3] // HD
-    half_heads = heads // 2
     many = heads * rows
     copies = []
     for seq in range(seqs):
@@ -192,11 +191,10 @@
         joined = (joined * scale + bias_ref[chip]).astype(jnp.bfloat16).astype(jnp.float32)
         parts = []
         for head in range(heads):
-            start = (head // half_heads) * core_cols + (head % half_heads) * HD
-            parts.append(rotated(joined[:, start : start + HD]))
+            parts.append(rotated(joined[:, head * HD : (head + 1) * HD]))
         query_buf[chip] = jnp.concatenate(parts, axis=0).astype(jnp.bfloat16)
-        low = joined[:, core_cols - HD : core_cols]
-        high = joined[:, 2 * core_cols - HD :]
+        low = joined[:, heads * HD : (heads + 1) * HD]
+        high = joined[:, (heads + 1) * HD :]
         fresh_keys = rotated(jnp.where(lane < HD // 2, low, pltpu.roll(high, HD // 2, 1))).astype(
             jnp.bfloat16
         )
@@ -269,25 +267,30 @@
             pltpu.SemaphoreType.DMA((seqs,)),
             pltpu.SemaphoreType.DMA((seqs,)),
         ],
-        compiler_params=pltpu.CompilerParams(vmem_limit_bytes=WHOLE_VMEM),
+        compiler_params=pltpu.CompilerParams(vmem_limit_bytes=48 * 1024 * 1024),
         name="attend",
     )(arrived, bias, cosine, sine, row_lengths, key_cache, value_cache)
 
 
-def projection_kernel(place_ref, slot_ref, table_ref, gain_ref, mine_ref, theirs_ref, *rest):
-    out_ref, wide_ref, weight_buf, sem = rest[-4:]
+def projection_kernel(place_ref, slot_ref, table_ref, gain_ref, *rest):
+    out_ref, wide_ref, weight_buf, kv_buf, sem = rest[-5:]
     chip, core = place_ref[0], place_ref[1]
     table_rows = table_ref.shape[0]
-    cols = mine_ref.shape[1]
+    q_cols, kv_cols = rest[0].shape[1], rest[2].shape[0]
+    cols = q_cols + 2 * kv_cols
     step = pl.program_id(0)
     slot = turned(slot_ref[...])
     rows = slot.shape[0]
     copies = []
-    for side, source in enumerate((mine_ref, theirs_ref)):
-        where = pl.multiple_of(((core + side) % 2) * cols, cols)
-        copies.append(
-            pltpu.make_async_copy(source, weight_buf.at[:, pl.ds(where, cols)], sem.at[side])
-        )
+    for side in range(2):
+        owner = (core + side) % 2
+        spots = [weight_buf.at[:, pl.ds(pl.multiple_of(owner * q_cols, q_cols), q_cols)]]
+        for part in range(2):
+            first = pl.multiple_of((2 * owner + part) * kv_cols, kv_cols)
+            spots.append(kv_buf.at[pl.ds(first, kv_cols), :])
+        for part, spot in enumerate(spots):
+            number = 2 * part + side
+            copies.append(pltpu.make_async_copy(rest[number], spot, sem.at[number]))
 
     @pl.when(step == 0)
     def _():
@@ -307,15 +310,20 @@
             copy.wait()
 
     product = jnp.dot(gained, weight_buf[...], preferred_element_type=jnp.float32)
-    out_ref[:, : 2 * cols] = product.astype(jnp.bfloat16)
+    out_ref[:, : 2 * q_cols] = product.astype(jnp.bfloat16)
+    product = lax.dot_general(
+        gained, kv_buf[...], (((1,), (1,)), ((), ())), preferred_element_type=jnp.float32
+    )
+    out_ref[:, 2 * q_cols : 2 * cols] = product.astype(jnp.bfloat16)
     strip = out_ref.shape[1] - 2 * cols
     out_ref[:, 2 * cols :] = wide_ref[:, pl.ds(pl.multiple_of(chip * strip, strip), strip)]
 
 
-def project(place, slot, table, gain, mine, theirs, held, chips):
+def project(place, slot, table, gain, weights, held, chips):
     rows = slot.shape[1]
     table_rows, width = table.shape
-    cols = mine.shape[1]
+    q_cols, kv_cols = weights[0].shape[1], weights[2].shape[0]
+    cols = q_cols + 2 * kv_cols
     out_cols = 2 * cols + width // chips
     block = 256
     return pl.pallas_call(
@@ -328,16 +336,17 @@
             pl.BlockSpec((table_rows, width), lambda i: (0, 0)),
             pl.BlockSpec((1, width), lambda i: (0, 0)),
         ]
-        + [HBM] * (2 + len(held)),
+        + [HBM] * (len(weights) + len(held)),
         out_specs=pl.BlockSpec((block, out_cols), lambda i: (i, 0)),
         scratch_shapes=[
             pltpu.VMEM((block, width), jnp.bfloat16),
-            pltpu.VMEM((width, 2 * cols), jnp.bfloat16),
-            pltpu.SemaphoreType.DMA((2,)),
+            pltpu.VMEM((width, 2 * q_cols), jnp.bfloat16),
+            pltpu.VMEM((4 * kv_cols, width), jnp.bfloat16),
+            pltpu.SemaphoreType.DMA((len(weights),)),
         ],
         compiler_params=pltpu.CompilerParams(vmem_limit_bytes=48 * 1024 * 1024),
         name="project",
-    )(place, slot, table, gain, mine, theirs, *held)
+    )(place, slot, table, gain, *weights, *held)
 
 
 def branch_kernel(place_ref, rows_ref, *rest):
@@ -373,46 +382,40 @@
     )(place, rows, *weights)
 
 
-def hidden_kernel(steps, *refs):
-    out_ref = refs[-1]
-    branch_refs, strip_refs = refs[:HALVES], refs[HALVES:-1]
-    _, layers, chips, rows, width = branch_refs[0].shape
-    strip = strip_refs[0].shape[3]
-    for half in range(HALVES):
-        for layer in range(layers):
-            for part in range(width // strip):
-                span = slice(part * strip, (part + 1) * strip)
-                total = strip_refs[half][layer, part].astype(jnp.float32)
-                for chip in range(chips):
-                    total = total + branch_refs[half][0, layer, chip, :, span].astype(jnp.float32)
-                start = layer * width + part * strip
-                for seq in range(rows // steps):
-                    out_ref[half * (rows // steps) + seq, :, start : start + strip] = total[
-                        seq * steps : (seq + 1) * steps
-                    ].astype(jnp.bfloat16)
-
-
-def hidden_sum(branches, arrived, width, steps):
-    upper, layers, chips, rows, pair_width = branches[0].shape
+def hidden_kernel(steps, branch_ref, strip_ref, out_ref):
+    upper, layers, chips, rows, pair_width = branch_ref.shape
+    groups = strip_ref.shape[0]
+    strip = out_ref.shape[2] // (groups * chips)
+    width = strip * chips
     lower = pair_width // width
-    strip = width // chips
-    last = arrived[0].shape[3] // strip - 1
-    seqs = HALVES * rows // steps
+    for group in range(groups):
+        high, low, layer = group // (lower * layers), group // layers % lower, group % layers
+        for part in range(chips):
+            start = low * width + part * strip
+            total = strip_ref[group, part, :, strip_ref.shape[3] - strip :].astype(jnp.float32)
+            for chip in range(chips):
+                total = total + branch_ref[high, layer, chip, :, start : start + strip].astype(
+                    jnp.float32
+                )
+            start = group * width + part * strip
+            for seq in range(rows // steps):
+                out_ref[seq, :, start : start + strip] = total[
+                    seq * steps : (seq + 1) * steps
+                ].astype(jnp.bfloat16)
+
+
+def hidden_sum(branches, arrived, steps):
+    upper, layers, _, rows, pair_width = branches.shape
     return pl.pallas_call(
         functools.partial(hidden_kernel, steps),
-        out_shape=jax.ShapeDtypeStruct((seqs, steps, upper * layers * pair_width), jnp.bfloat16),
-        grid=(upper * lower,),
-        in_specs=[
-            pl.BlockSpec(
-                (1, layers, chips, rows, width), lambda y: (y // lower, 0, 0, 0, y % lower)
-            )
-        ]
-        * HALVES
-        + [pl.BlockSpec((layers, chips, rows, strip), lambda y: (y, 0, 0, last))] * HALVES,
-        out_specs=pl.BlockSpec((seqs, steps, layers * width), lambda y: (0, 0, y)),
+        out_shape=jax.ShapeDtypeStruct(
+            (rows // steps, steps, upper * layers * pair_width), jnp.bfloat16
+        ),
+        in_specs=[VMEM] * 2,
+        out_specs=VMEM,
         compiler_params=pltpu.CompilerParams(vmem_limit_bytes=48 * 1024 * 1024),
         name="hidden_sum",
-    )(*branches, *arrived)
+    )(branches, arrived)
 
 
 def per_device(
@@ -442,8 +445,9 @@
     plane_rows = parties * rows_here
     place = jnp.stack([chip, core, line]).astype(jnp.int32)
 
-    both = jnp.concatenate([q_weight, k_weight, v_weight], axis=1)
-    both_other = swap_cores(both)
+    weights = []
+    for own in (q_weight, k_weight.T, v_weight.T):
+        weights += [own, swap_cores(own)]
     o_line = swap_lines(o_weight)
     o_weights = (o_weight, swap_cores(o_weight), o_line, swap_cores(o_line))
     core_cols = q_bias.shape[0] + k_bias.shape[0] + v_bias.shape[0]
@@ -475,7 +479,13 @@
     slot, table, rounds = exchange(0)
     pair_bias = table.reshape(chips, SENT_ROWS, width_here)
     pair_bias = pair_bias[:, ROUND_ROWS : ROUND_ROWS + 2, :core_cols].astype(jnp.float32)
-    pair_bias = pair_bias.reshape(chips, 1, 2 * core_cols)
+    pair_bias = jnp.concatenate(
+        [
+            pair_bias[:, :, :q_cols].reshape(chips, 1, -1),
+            pair_bias[:, :, q_cols:].reshape(chips, 1, -1),
+        ],
+        axis=2,
+    )
     half_rows = rows_here // HALVES
     kv_heads = key_cache.shape[2] // HD
     positions = (lengths[:, None] + jnp.arange(step_count, dtype=jnp.int32)[None, :]).reshape(-1)
@@ -490,7 +500,7 @@
         return values.reshape(parties, HALVES, half_rows)[:, half].reshape(1, -1)
 
     payloads = tuple(
-        project(place, part_of(slot, half), table, own_gain, both, both_other, (o_line,), chips)
+        project(place, part_of(slot, half), table, own_gain, weights, (o_line,), chips)
         for half in range(HALVES)
     )
 
@@ -499,7 +509,7 @@
         return tuple(
             sofar[half]
             + project(
-                place, part_of(turn_slot, half), turn_table, own_gain, both, both_other, (), chips
+                place, part_of(turn_slot, half), turn_table, own_gain, weights, (), chips
             )
             for half in range(HALVES)
         )
@@ -531,7 +541,7 @@
         arrived.append(here)
         new_keys.append(keys)
         new_values.append(values)
-    hidden = hidden_sum(branches, arrived, o_weight.shape[1], step_count)
+    hidden = hidden_sum(branches[0], arrived[0], step_count)
     new_keys = jnp.concatenate(new_keys, axis=0)
     new_values = jnp.concatenate(new_values, axis=0)
     return (

time: 208 us -> 203 us (0.976)
  Pallas kernels: 41.6 us -> 38.1 us
  starting transfers between devices: 34.4 us -> 36.7 us
  local copies, waits for them, and re-layouts: 12.4 us -> 10.1 us
    ppermute x1, waiting for transfers between devices: 21.3 us -> 15.1 us  [swap_lines(): return lax.ppermute(value, 'yl', [(0, 1), (1, 0)])]
    unnamed x28 -> x18, local copies, waits for them, and re-layouts: 5.48 us -> 1.53 us
    all_to_all x1, waiting for transfers between devices: 0.01 us -> 3.46 us  [exchange(): lax.all_to_all(jnp.broadcast_to(merged[None], (chips, SENT_ROWS, width_he...]
    pallas_call x1, Pallas kernels: 11.4 us -> 8.91 us  [attend(): pl.pallas_call(functools.partial(attention_kernel, half), out_shape=(jax....]
    concatenate x1, other arithmetic: 2.29 us -> 0.04 us  [per_device(): jnp.concatenate([pair_bias[:, :, :q_cols].reshape(chips, 1, -1), pair_bia...]
  transfers between devices with their start and end apart: 10 -> 12, of which waited for: 6 -> 7; matrix products, arithmetic and copies ran while one was open for 6% -> 5% of each run, Pallas kernels for 6% -> 4%
where the time goes in v8:
time: 203 us; the launch traced here: 201 us
  waiting for transfers between devices  108 us (53%)
  Pallas kernels  38.1 us (19%)
  starting transfers between devices  36.7 us (18%)
  local copies, waits for them, and re-layouts  10.1 us (5%)
  other arithmetic  5.36 us (3%)
  between operations  2.86 us (1%)
    all_to_all x1, waiting for transfers between devices, per_device(): lax.all_to_all(payloads[half], PLANE, split_axis=0, concat_axis=0, tiled=...  35.8 us
    all_to_all x1, waiting for transfers between devices, per_device(): lax.all_to_all(branch, LAYER, split_axis=0, concat_axis=0, tiled=True)  26.4 us
    all_to_all x1, waiting for transfers between devices, per_device(): lax.all_to_all(spread.reshape(-1, half_rows, 2 * q_cols), LAYER, split_ax...  17.2 us
    ppermute x1, waiting for transfers between devices, swap_lines(): return lax.ppermute(value, 'yl', [(0, 1), (1, 0)])  15.1 us
    all_to_all x1, starting transfers between devices, per_device(): lax.all_to_all(sent_ids, EVERY, split_axis=0, concat_axis=0, tiled=True)  11.1 us
    pallas_call x1, Pallas kernels, project(): pl.pallas_call(projection_kernel, out_shape=jax.ShapeDtypeStruct((rows, o...  10.7 us
    all_to_all x1, starting transfers between devices, per_device(): lax.all_to_all(payloads[half], PLANE, split_axis=0, concat_axis=0, tiled=...  9.92 us
    pallas_call x1, Pallas kernels, look_up(): pl.pallas_call(lookup_kernel, out_shape=(jax.ShapeDtypeStruct((SENT_ROWS,...  9.64 us
  transfers between devices with their start and end apart: 12, of which 7 were waited for; matrix products, arithmetic and copies ran while one was open for 5% of the time, Pallas kernels for 4%

profile of v8, /device:TPU:0, one launch (start us, length us, event | category | flops | bytes accessed | tf_op | source)
XLA Modules:
  0.0 201.3 jit_solution(8364804163523046653)
XLA Ops:
  0.6 0.8 broadcast_in_dim.15
  1.4 0.7 broadcast_in_dim.16
  2.1 11.1 %all-to-all-start.1 = ((s32[128,1,16]{2,1,0:T(1,128)}), s32[128,1,16]{2,1,0:T(1,128)S(1)}, u32[]{:S(2)}, u32[]{:S(2)}) async-start(s32[128,1,16]{2,1,0:T(1,128)} %broadcast_in_dim.16), calls=%async_computation.1 | async-start | bytes 131072 | tf_op jit(solution)/shard_map/all_to_all | solution.py:457
  13.2 0.1 pad_add_fusion.2.place_ref
  13.3 0.7 reshape.202.q_ref
  14.0 8.5 %all-to-all-done.1 = s32[128,1,16]{2,1,0:T(1,128)S(1)} async-done(((s32[128,1,16]{2,1,0:T(1,128)}), s32[128,1,16]{2,1,0:T(1,128)S(1)}, u32[]{:S(2)}, u32[]{:S(2)}) %all-to-all-start.1) | async-done | bytes 8224 | tf_op jit(solution)/shard_map/all_to_all | solution.py:457
  22.5 0.1 reshape_reshape.8.id_row_ref
  22.6 0.5 copy-done.8
  23.1 9.6 %look_up.4 = (bf16[128,1024]{1,0:T(8,128)(2,1)S(1)}, bf16[128,1024]{1,0:T(8,128)(2,1)S(1)}, s32[2,1,1024]{2,1,0:T(1,128)S(1)}) custom-call(s32[4]{0:T(128)S(1)} %pad_add_fusion.2.place_ref, s32[2,1,1024]{2,1,0:T(1,128)S(1)} %reshape_reshape.8.id_row_ref, bf16[1,512]{1,0:T(2,128)(2,1)S(1)} %reshape.202.q_ref, bf16[1,64]{1,0:T(2,128)(2,1)} %bitcast.70, ...), custom_call_target="tpu_custom_call" | custom-call | tf_op jit(solution)/shard_map/look_up/pallas_call | solution.py:110
  32.8 0.1 collective-permute-start.1
  32.9 1.5 collective-permute-done.1
  34.4 0.1 add.92
  34.4 0.0 copy-start.6
  34.5 0.0 copy-start.7
  34.5 1.6 broadcast_in_dim.17
  36.1 3.6 %all-to-all-start.2 = ((bf16[8,128,1024]{2,1,0:T(8,128)(2,1)}), bf16[8,128,1024]{2,1,0:T(8,128)(2,1)S(1)}, u32[]{:S(2)}, u32[]{:S(2)}) async-start(bf16[8,128,1024]{2,1,0:T(8,128)(2,1)} %broadcast_in_dim.17), calls=%async_computation.2 | async-start | bytes 4194304 | tf_op jit(solution)/shard_map/all_to_all | solution.py:465
  39.7 0.7 collective-permute-start.5
  40.4 0.0 collective-permute-start.2
  40.4 0.0 copy-done.6
  40.4 0.5 collective-permute-start.3
  40.9 0.0 copy-done.7
  40.9 0.1 collective-permute-start.4
  41.0 0.7 pad_add_fusion.1.place_ref
  41.7 0.7 dynamic-slice_convert_fusion
  42.4 1.5 reshape.206
  43.9 0.6 reduce_max.8
  46.5 1.5 reshape_reshape.9
  48.0 0.7 fusion.4
  48.8 0.7 and_select_fusion.1
  49.5 0.6 add_select_fusion
  50.1 0.0 collective-permute-done.3.rest_3_
  50.1 0.0 collective-permute-done.4.rest_5_
  50.1 15.1 %collective-permute-done.5.rest_6_.rest_2_ = bf16[512,1024]{1,0:T(8,128)(2,1)S(1)} collective-permute-done((bf16[512,1024]{1,0:T(8,128)(2,1)}, bf16[512,1024]{1,0:T(8,128)(2,1)S(1)}, u32[]{:S(2)}, u32[]{:S(2)}) %collective-permute-start.5) | collective-permute-done | bytes 1048608 | tf_op jit(solution)/shard_map/ppermute | solution.py:34
  65.2 0.0 collective-permute-done.2.rest_1_
  65.2 3.5 %all-to-all-done.2 = bf16[8,128,1024]{2,1,0:T(8,128)(2,1)S(1)} async-done(((bf16[8,128,1024]{2,1,0:T(8,128)(2,1)}), bf16[8,128,1024]{2,1,0:T(8,128)(2,1)S(1)}, u32[]{:S(2)}, u32[]{:S(2)}) %all-to-all-start.2) | async-done | bytes 2097184 | tf_op jit(solution)/shard_map/all_to_all | solution.py:465
  68.6 10.7 %project.4 = bf16[1024,1408]{1,0:T(8,128)(2,1)} custom-call(s32[3]{0:T(128)} %pad_add_fusion.1.place_ref, s32[1,1024]{1,0:T(1,128)S(1)} %get-tuple-element.293.slot_ref, bf16[1024,1024]{1,0:T(8,128)(2,1)S(1)} %bitcast.55, f32[1,1024]{1,0:T(1,128)S(1)} %bitcast.67, bf16[1024,512]{1,0:T(8,128)(2,1)} %rest_0_.2, ...), custom_call_target="tpu_custom_call" | custom-call | tf_op jit(solution)/shard_map/project/pallas_call | solution.py:329
  79.4 0.0 copy-done.1
  79.4 0.0 copy-done
  79.4 0.2 while.13
  79.6 0.0 copy-start.13
  79.6 9.9 %all-to-all-start.3 = ((bf16[64,16,1408]{2,1,0:T(8,128)(2,1)}), bf16[64,16,1408]{2,1,0:T(8,128)(2,1)S(1)}, u32[]{:S(2)}, u32[]{:S(2)}) async-start(bf16[64,16,1408]{2,1,0:T(8,128)(2,1)} %bitcast.57), calls=%async_computation.3 | async-start | bytes 5767168 | tf_op jit(solution)/shard_map/all_to_all | solution.py:521
  89.5 0.1 collective-permute-start.6
  89.6 0.1 add.97
  89.7 0.1 add.98
  89.8 0.1 add.100
  89.9 0.1 reshape_tile.4.length_ref
  90.0 0.1 fusion.3
  90.1 0.1 pad_maximum_fusion.1
  90.2 0.7 collective-permute-start.7
  90.9 0.9 slice_convert_fusion
  91.9 0.1 reshape.209
  92.0 35.8 %all-to-all-done.3 = bf16[64,16,1408]{2,1,0:T(8,128)(2,1)S(1)} async-done(((bf16[64,16,1408]{2,1,0:T(8,128)(2,1)}), bf16[64,16,1408]{2,1,0:T(8,128)(2,1)S(1)}, u32[]{:S(2)}, u32[]{:S(2)}) %all-to-all-start.3) | async-done | bytes 2883616 | tf_op jit(solution)/shard_map/all_to_all | solution.py:521
  127.8 8.9 %attend.1 = (bf16[4,8,16,1024]{3,2,1,0:T(8,128)(2,1)S(1)}, bf16[16,1024]{1,0:T(8,128)(2,1)S(1)}, bf16[16,1024]{1,0:T(8,128)(2,1)S(1)}) custom-call(bf16[8,8,16,1408]{3,2,1,0:T(8,128)(2,1)S(1)} %bitcast.53, f32[8,1,1280]{2,1,0:T(1,128)S(1)} %pad_maximum_fusion.bias_ref, f32[16,128]{1,0:T(8,128)S(1)} %get-tuple-element.298.cosine_ref, ...), custom_call_target="tpu_custom_call" | custom-call | tf_op jit(solution)/shard_map/attend/pallas_call | solution.py:254
  136.7 1.0 copy-done.2
  137.7 4.7 %all-to-all-start.4 = ((bf16[32,16,1024]{2,1,0:T(8,128)(2,1)}), bf16[32,16,1024]{2,1,0:T(8,128)(2,1)}, u32[]{:S(2)}, u32[]{:S(2)}) async-start(bf16[32,16,1024]{2,1,0:T(8,128)(2,1)} %bitcast.56), calls=%async_computation.4 | async-start | bytes 2097152 | tf_op jit(solution)/shard_map/all_to_all | solution.py:535
  142.4 0.0 collective-permute-done.6.rest_1_
  142.4 0.0 collective-permute-done.7.rest_3_
  142.4 17.2 %all-to-all-done.4 = bf16[32,16,1024]{2,1,0:T(8,128)(2,1)} async-done(((bf16[32,16,1024]{2,1,0:T(8,128)(2,1)}), bf16[32,16,1024]{2,1,0:T(8,128)(2,1)}, u32[]{:S(2)}, u32[]{:S(2)}) %all-to-all-start.4) | async-done | bytes 1048608 | tf_op jit(solution)/shard_map/all_to_all | solution.py:535
  159.6 6.2 %branch.1 = bf16[512,2048]{1,0:T(8,128)(2,1)} custom-call(s32[3]{0:T(128)S(1)} %copy-done.12, bf16[512,1024]{1,0:T(8,128)(2,1)} %bitcast.23.rows_ref, bf16[512,1024]{1,0:T(8,128)(2,1)} %rest_0_.3, bf16[512,1024]{1,0:T(8,128)(2,1)} %collective-permute-done.6.rest_1_, bf16[512,1024]{1,0:T(8,128)(2,1)} %copy-done.1, ...), custom_call_target="tpu_custom_call" | custom-call | tf_op jit(solution)/shard_map/branch/pallas_call | solution.py:375
  165.8 5.2 %all-to-all-start.5 = ((bf16[32,16,2048]{2,1,0:T(8,128)(2,1)}), bf16[32,16,2048]{2,1,0:T(8,128)(2,1)}, u32[]{:S(2)}, u32[]{:S(2)}) async-start(bf16[32,16,2048]{2,1,0:T(8,128)(2,1)} %bitcast.58), calls=%async_computation.5 | async-start | bytes 4194304 | tf_op jit(solution)/shard_map/all_to_all | solution.py:539
  171.0 0.6 reshape.214
  171.6 0.6 reshape.215
  172.2 26.4 %all-to-all-done.5 = bf16[32,16,2048]{2,1,0:T(8,128)(2,1)} async-done(((bf16[32,16,2048]{2,1,0:T(8,128)(2,1)}), bf16[32,16,2048]{2,1,0:T(8,128)(2,1)}, u32[]{:S(2)}, u32[]{:S(2)}) %all-to-all-start.5) | async-done | bytes 2097184 | tf_op jit(solution)/shard_map/all_to_all | solution.py:539
  198.7 2.6 %hidden_sum.1 = bf16[4,4,8192]{2,1,0:T(4,128)(2,1)} custom-call(bf16[2,2,8,16,2048]{4,3,2,1,0:T(8,128)(2,1)} %bitcast.25.branch_ref, bf16[8,8,16,1408]{3,2,1,0:T(8,128)(2,1)S(1)} %bitcast.54), custom_call_target="tpu_custom_call" | custom-call | tf_op jit(solution)/shard_map/hidden_sum/pallas_call | solution.py:409
  (17 shorter events, 0.1 us)
Async XLA Ops:
  2.1 20.4 %all-to-all-start.1 = ((s32[128,1,16]{2,1,0:T(1,128)}), s32[128,1,16]{2,1,0:T(1,128)S(1)}, u32[]{:S(2)}, u32[]{:S(2)}) async-start(s32[128,1,16]{2,1,0:T(1,128)} %broadcast_in_dim.16), calls=%async_computation.1 | async-start | bytes 131072 | tf_op jit(solution)/shard_map/all_to_all | solution.py:457
  22.5 0.6 copy-start.8
  32.8 1.6 collective-permute-start.1
  34.4 6.0 %copy-start.6 = (bf16[1024,64]{0,1:T(8,128)(2,1)S(1)}, bf16[1024,64]{0,1:T(8,128)(2,1)}, u32[]{:S(2)}) copy-start(bf16[1024,64]{0,1:T(8,128)(2,1)} %param.20) | copy-start | bytes 393220
  34.5 6.5 %copy-start.7 = (bf16[1024,64]{0,1:T(8,128)(2,1)S(1)}, bf16[1024,64]{0,1:T(8,128)(2,1)}, u32[]{:S(2)}) copy-start(bf16[1024,64]{0,1:T(8,128)(2,1)} %param.21) | copy-start | bytes 393220
  36.1 32.6 %all-to-all-start.2 = ((bf16[8,128,1024]{2,1,0:T(8,128)(2,1)}), bf16[8,128,1024]{2,1,0:T(8,128)(2,1)S(1)}, u32[]{:S(2)}, u32[]{:S(2)}) async-start(bf16[8,128,1024]{2,1,0:T(8,128)(2,1)} %broadcast_in_dim.17), calls=%async_computation.2 | async-start | bytes 4194304 | tf_op jit(solution)/shard_map/all_to_all | solution.py:465
  39.7 25.5 %collective-permute-start.5 = (bf16[512,1024]{1,0:T(8,128)(2,1)}, bf16[512,1024]{1,0:T(8,128)(2,1)S(1)}, u32[]{:S(2)}, u32[]{:S(2)}) collective-permute-start(bf16[512,1024]{1,0:T(8,128)(2,1)} %rest_0_.3), channel_id=1, source_target_pairs={{0,32},{32,0},{1,33},{33,1},{2,34},{34,2},{3,35},{35,3},{4,36},{36... | collective-permute-start | bytes 3145736 | tf_op jit(solution)/shard_map/ppermute | solution.py:34
  40.4 24.8 %collective-permute-start.2 = (bf16[1024,512]{1,0:T(8,128)(2,1)}, bf16[1024,512]{1,0:T(8,128)(2,1)}, u32[]{:S(2)}, u32[]{:S(2)}) collective-permute-start(bf16[1024,512]{1,0:T(8,128)(2,1)} %rest_0_.2), channel_id=1, source_target_pairs={{0,1},{1,0},{2,3},{3,2},{4,5},{5,4},{6,7},{7,6},{8,9},{9,8},{10,11... | collective-permute-start | bytes 3145736 | tf_op jit(solution)/shard_map/ppermute | solution.py:30
  40.4 9.7 %collective-permute-start.3 = (bf16[64,1024]{1,0:T(8,128)(2,1)S(1)}, bf16[64,1024]{1,0:T(8,128)(2,1)S(1)}, u32[]{:S(2)}, u32[]{:S(2)}) collective-permute-start(bf16[64,1024]{1,0:T(8,128)(2,1)S(1)} %bitcast.59), channel_id=1, source_target_pairs={{0,1},{1,0},{2,3},{3,2},{4,5},{5,4},{6,7},{7,6},{8,9},{9,8},{10,11... | collective-permute-start | bytes 393224 | tf_op jit(solution)/shard_map/ppermute | solution.py:30
  40.9 9.2 %collective-permute-start.4 = (bf16[64,1024]{1,0:T(8,128)(2,1)S(1)}, bf16[64,1024]{1,0:T(8,128)(2,1)}, u32[]{:S(2)}, u32[]{:S(2)}) collective-permute-start(bf16[64,1024]{1,0:T(8,128)(2,1)S(1)} %bitcast.62), channel_id=1, source_target_pairs={{0,1},{1,0},{2,3},{3,2},{4,5},{5,4},{6,7},{7,6},{8,9},{9,8},{10,11... | collective-permute-start | bytes 393224 | tf_op jit(solution)/shard_map/ppermute | solution.py:30
  65.2 14.2 %copy-start.1 = (bf16[512,1024]{1,0:T(8,128)(2,1)}, bf16[512,1024]{1,0:T(8,128)(2,1)S(1)}, u32[]{:S(2)}) copy-start(bf16[512,1024]{1,0:T(8,128)(2,1)S(1)} %collective-permute-done.5.rest_6_.rest_2_) | copy-start | bytes 3145732
  68.6 10.7 %copy-start = (bf16[8,128,1024]{2,1,0:T(8,128)(2,1)}, bf16[8,128,1024]{2,1,0:T(8,128)(2,1)S(1)}, u32[]{:S(2)}) copy-start(bf16[8,128,1024]{2,1,0:T(8,128)(2,1)S(1)} %all-to-all-done.2) | copy-start | bytes 6291460
  68.6 10.7 %copy-start.9 = (s32[2,1,1024]{2,1,0:T(1,128)S(1)}, s32[2,1,1024]{2,1,0:T(1,128)}, u32[]{:S(2)}) copy-start(s32[2,1,1024]{2,1,0:T(1,128)} %reshape_reshape.9) | copy-start | bytes 24580
  79.6 10.0 %copy-start.13 = (s32[4]{0:T(128)S(1)}, s32[4]{0:T(128)}, u32[]{:S(2)}) copy-start(s32[4]{0:T(128)} %param.16) | copy-start | bytes 52
  79.6 48.2 %all-to-all-start.3 = ((bf16[64,16,1408]{2,1,0:T(8,128)(2,1)}), bf16[64,16,1408]{2,1,0:T(8,128)(2,1)S(1)}, u32[]{:S(2)}, u32[]{:S(2)}) async-start(bf16[64,16,1408]{2,1,0:T(8,128)(2,1)} %bitcast.57), calls=%async_computation.3 | async-start | bytes 5767168 | tf_op jit(solution)/shard_map/all_to_all | solution.py:521
  89.5 52.8 %collective-permute-start.6 = (bf16[512,1024]{1,0:T(8,128)(2,1)}, bf16[512,1024]{1,0:T(8,128)(2,1)}, u32[]{:S(2)}, u32[]{:S(2)}) collective-permute-start(bf16[512,1024]{1,0:T(8,128)(2,1)} %rest_0_.3), channel_id=1, source_target_pairs={{0,1},{1,0},{2,3},{3,2},{4,5},{5,4},{6,7},{7,6},{8,9},{9,8},{10,11... | collective-permute-start | bytes 3145736 | tf_op jit(solution)/shard_map/ppermute | solution.py:30
  90.2 52.2 %collective-permute-start.7 = (bf16[512,1024]{1,0:T(8,128)(2,1)}, bf16[512,1024]{1,0:T(8,128)(2,1)}, u32[]{:S(2)}, u32[]{:S(2)}) collective-permute-start(bf16[512,1024]{1,0:T(8,128)(2,1)} %copy-done.1), channel_id=1, source_target_pairs={{0,1},{1,0},{2,3},{3,2},{4,5},{5,4},{6,7},{7,6},{8,9},{9,8},{10,11... | collective-permute-start | bytes 3145736 | tf_op jit(solution)/shard_map/ppermute | solution.py:30
  127.8 31.8 %copy-start.12 = (s32[3]{0:T(128)S(1)}, s32[3]{0:T(128)}, u32[]{:S(2)}) copy-start(s32[3]{0:T(128)} %get-tuple-element.588) | copy-start | bytes 40
  136.7 1.0 copy-start.2
  137.7 21.9 %all-to-all-start.4 = ((bf16[32,16,1024]{2,1,0:T(8,128)(2,1)}), bf16[32,16,1024]{2,1,0:T(8,128)(2,1)}, u32[]{:S(2)}, u32[]{:S(2)}) async-start(bf16[32,16,1024]{2,1,0:T(8,128)(2,1)} %bitcast.56), calls=%async_computation.4 | async-start | bytes 2097152 | tf_op jit(solution)/shard_map/all_to_all | solution.py:535
  165.8 32.9 %all-to-all-start.5 = ((bf16[32,16,2048]{2,1,0:T(8,128)(2,1)}), bf16[32,16,2048]{2,1,0:T(8,128)(2,1)}, u32[]{:S(2)}, u32[]{:S(2)}) async-start(bf16[32,16,2048]{2,1,0:T(8,128)(2,1)} %bitcast.58), calls=%async_computation.5 | async-start | bytes 4194304 | tf_op jit(solution)/shard_map/all_to_all | solution.py:539

commit v9 on v8

--- a/solution.py
+++ b/solution.py
@@ -9,8 +9,8 @@
 from jax.sharding import PartitionSpec as P
 
 HD = 128
-ROUND_ROWS = 126
-SENT_ROWS = 128
+ROUND_ROWS = 118
+SENT_ROWS = 120
 CHIP_COUNT = 8
 WHOLE_VMEM = 60 * 1024 * 1024
 HALVES = 1
@@ -62,8 +62,14 @@
         for plane in range(planes):
             id_row = id_row_ref[plane]
             id_col = turned(id_row)
-            again = jnp.where((id_row == id_col) & earlier, 1, 0)
-            key_col = jnp.where(jnp.max(again, axis=1, keepdims=True) == 0, id_col, -1)
+            keys = []
+            for low in range(0, rows, rows // 4):
+                high = low + rows // 4
+                own_col = id_col[low:high]
+                again = (id_row[:, :high] == own_col) & earlier[low:high, :high]
+                found = jnp.max(jnp.where(again, 1, 0), axis=1, keepdims=True)
+                keys.append(jnp.where(found == 0, own_col, -1))
+            key_col = jnp.concatenate(keys, axis=0)
             edge_row = jnp.zeros_like(id_row)
             for other in range(1, CHIP_COUNT):
                 edge = other * 2 * vocab_here
@@ -89,17 +95,16 @@
         pieces = [piece[...].astype(jnp.float32) for piece in (q_ref, k_ref, v_ref)]
         filled = sum(piece.shape[1] for piece in pieces)
         pieces.append(jnp.zeros((1, width - filled), jnp.float32))
-        bias = jnp.broadcast_to(jnp.concatenate(pieces, axis=1), (16, width))
+        bias = jnp.broadcast_to(jnp.concatenate(pieces, axis=1), (8, width))
         is_bias = (
-            lax.broadcasted_iota(jnp.int32, (16, 1), 0) == ROUND_ROWS + core - (SENT_ROWS - 16)
+            lax.broadcasted_iota(jnp.int32, (8, 1), 0) == ROUND_ROWS + core - (SENT_ROWS - 8)
         )
         for side, target in ((0, mine_ref), (1, theirs_ref)):
             plane = (core + side) % 2
             start = pl.multiple_of(plane * SENT_ROWS, SENT_ROWS)
+            tail = pl.ds(start + SENT_ROWS - 8, 8)
+            total_ref[tail, :] = jnp.where(is_bias, bias, total_ref[tail, :])
             target[...] = total_ref[pl.ds(start, SENT_ROWS), :].astype(jnp.bfloat16)
-            tail = total_ref[pl.ds(start + SENT_ROWS - 16, 16), :]
-            tail = jnp.where(is_bias, bias, tail)
-            target[SENT_ROWS - 16 :, :] = tail.astype(jnp.bfloat16)
 
 
 def look_up(place, plane_ids, biases, embedding):
@@ -152,15 +157,16 @@
     core_cols = bias_ref.shape[2] // 2
     heads = out_ref.shape[3] // HD
     many = heads * rows
-    copies = []
+    key_copies, value_copies = [], []
     for seq in range(seqs):
-        copies.append(pltpu.make_async_copy(keys_ref.at[half * seqs + seq], key_buf.at[seq], key_sem.at[seq]))
-        copies.append(
-            pltpu.make_async_copy(
-                values_ref.at[half * seqs + seq], value_buf.at[seq], value_sem.at[seq]
-            )
-        )
-    for copy in copies:
+        source = half * seqs + seq
+        key_copies.append(
+            pltpu.make_async_copy(keys_ref.at[source], key_buf.at[seq], key_sem.at[seq])
+        )
+        value_copies.append(
+            pltpu.make_async_copy(values_ref.at[source], value_buf.at[seq], value_sem.at[seq])
+        )
+    for copy in key_copies + value_copies:
         copy.start()
     square = None
     for group in range(groups):
@@ -203,7 +209,7 @@
         )
         new_keys_ref[:, span] = fresh_keys
         new_values_ref[:, span] = fresh_values
-    for copy in copies:
+    for copy in key_copies:
         copy.wait()
     for chip in range(chips):
         span = slice(chip * HD, (chip + 1) * HD)
@@ -235,6 +241,9 @@
         weights = (scores * share).astype(jnp.bfloat16)
         fresh_weights = (fresh_scores * share).astype(jnp.bfloat16)
         attended = jnp.dot(fresh_weights, fresh_values, preferred_element_type=jnp.float32)
+        if chip == 0:
+            for copy in value_copies:
+                copy.wait()
         for seq in range(seqs):
             found = jnp.dot(
                 weights, value_buf[seq, :, span], preferred_element_type=jnp.float32
@@ -325,7 +334,7 @@
     q_cols, kv_cols = weights[0].shape[1], weights[2].shape[0]
     cols = q_cols + 2 * kv_cols
     out_cols = 2 * cols + width // chips
-    block = 256
+    block = 512
     return pl.pallas_call(
         projection_kernel,
         out_shape=jax.ShapeDtypeStruct((rows, out_cols), jnp.bfloat16),

time: 203 us -> 200 us (0.985)
  no operation moved by 1% of the time
where the time goes in v9:
time: 200 us; the launch traced here: 199 us
  waiting for transfers between devices  107 us (54%)
  Pallas kernels  37.9 us (19%)
  starting transfers between devices  35.9 us (18%)
  local copies, waits for them, and re-layouts  10 us (5%)
  other arithmetic  5.29 us (3%)
  between operations  2.85 us (1%)
    all_to_all x1, waiting for transfers between devices, per_device(): lax.all_to_all(payloads[half], PLANE, split_axis=0, concat_axis=0, tiled=...  35.8 us
    all_to_all x1, waiting for transfers between devices, per_device(): lax.all_to_all(branch, LAYER, split_axis=0, concat_axis=0, tiled=True)  26.5 us
    all_to_all x1, waiting for transfers between devices, per_device(): lax.all_to_all(spread.reshape(-1, half_rows, 2 * q_cols), LAYER, split_ax...  17.3 us
    ppermute x1, waiting for transfers between devices, swap_lines(): return lax.ppermute(value, 'yl', [(0, 1), (1, 0)])  15.2 us
    all_to_all x1, starting transfers between devices, per_device(): lax.all_to_all(sent_ids, EVERY, split_axis=0, concat_axis=0, tiled=True)  11.1 us
    pallas_call x1, Pallas kernels, look_up(): pl.pallas_call(lookup_kernel, out_shape=(jax.ShapeDtypeStruct((SENT_ROWS,...  10.5 us
    pallas_call x1, Pallas kernels, project(): pl.pallas_call(projection_kernel, out_shape=jax.ShapeDtypeStruct((rows, o...  9.86 us
    all_to_all x1, starting transfers between devices, per_device(): lax.all_to_all(payloads[half], PLANE, split_axis=0, concat_axis=0, tiled=...  9.15 us
  transfers between devices with their start and end apart: 12, of which 7 were waited for; matrix products, arithmetic and copies ran while one was open for 5% of the time, Pallas kernels for 4%

profile of v9, /device:TPU:0, one launch (start us, length us, event | category | flops | bytes accessed | tf_op | source)
XLA Modules:
  0.0 198.9 jit_solution(1728091494296589368)
XLA Ops:
  0.6 0.8 broadcast_in_dim.15
  1.4 0.7 broadcast_in_dim.16
  2.1 11.1 %all-to-all-start.1 = ((s32[128,1,16]{2,1,0:T(1,128)}), s32[128,1,16]{2,1,0:T(1,128)S(1)}, u32[]{:S(2)}, u32[]{:S(2)}) async-start(s32[128,1,16]{2,1,0:T(1,128)} %broadcast_in_dim.16), calls=%async_computation.1 | async-start | bytes 131072 | tf_op jit(solution)/shard_map/all_to_all | solution.py:466
  13.2 0.1 pad_add_fusion.2.place_ref
  13.3 0.7 reshape.202.q_ref
  14.0 8.5 %all-to-all-done.1 = s32[128,1,16]{2,1,0:T(1,128)S(1)} async-done(((s32[128,1,16]{2,1,0:T(1,128)}), s32[128,1,16]{2,1,0:T(1,128)S(1)}, u32[]{:S(2)}, u32[]{:S(2)}) %all-to-all-start.1) | async-done | bytes 8224 | tf_op jit(solution)/shard_map/all_to_all | solution.py:466
  22.5 0.1 reshape_reshape.8.id_row_ref
  22.6 0.5 copy-done.8
  23.1 10.5 %look_up.4 = (bf16[120,1024]{1,0:T(8,128)(2,1)S(1)}, bf16[120,1024]{1,0:T(8,128)(2,1)S(1)}, s32[2,1,1024]{2,1,0:T(1,128)S(1)}) custom-call(s32[4]{0:T(128)S(1)} %pad_add_fusion.2.place_ref, s32[2,1,1024]{2,1,0:T(1,128)S(1)} %reshape_reshape.8.id_row_ref, bf16[1,512]{1,0:T(2,128)(2,1)S(1)} %reshape.202.q_ref, bf16[1,64]{1,0:T(2,128)(2,1)} %bitcast.70, ...), custom_call_target="tpu_custom_call" | custom-call | tf_op jit(solution)/shard_map/look_up/pallas_call | solution.py:115
  33.6 0.1 collective-permute-start.1
  33.7 1.5 collective-permute-done.1
  35.2 0.1 add.92
  35.3 0.0 copy-start.6
  35.3 0.0 copy-start.7
  35.3 1.6 broadcast_in_dim.17
  36.8 3.6 %all-to-all-start.2 = ((bf16[8,120,1024]{2,1,0:T(8,128)(2,1)}), bf16[8,120,1024]{2,1,0:T(8,128)(2,1)S(1)}, u32[]{:S(2)}, u32[]{:S(2)}) async-start(bf16[8,120,1024]{2,1,0:T(8,128)(2,1)} %broadcast_in_dim.17), calls=%async_computation.2 | async-start | bytes 3932160 | tf_op jit(solution)/shard_map/all_to_all | solution.py:474
  40.5 0.7 collective-permute-start.5
  41.2 0.0 collective-permute-start.2
  41.2 0.0 copy-done.6
  41.2 0.5 collective-permute-start.3
  41.7 0.0 copy-done.7
  41.7 0.1 collective-permute-start.4
  41.8 0.6 pad_add_fusion.1.place_ref
  42.4 0.7 dynamic-slice_convert_fusion
  43.0 1.5 reshape.206
  44.6 0.6 reduce_max.8
  47.2 1.5 reshape_reshape.9
  48.7 0.7 fusion.4
  49.5 0.7 and_select_fusion.1
  50.2 0.6 add_select_fusion
  50.8 0.0 collective-permute-done.3.rest_3_
  50.8 0.0 collective-permute-done.4.rest_5_
  50.8 15.2 %collective-permute-done.5.rest_6_.rest_2_ = bf16[512,1024]{1,0:T(8,128)(2,1)S(1)} collective-permute-done((bf16[512,1024]{1,0:T(8,128)(2,1)}, bf16[512,1024]{1,0:T(8,128)(2,1)S(1)}, u32[]{:S(2)}, u32[]{:S(2)}) %collective-permute-start.5) | collective-permute-done | bytes 1048608 | tf_op jit(solution)/shard_map/ppermute | solution.py:34
  65.9 0.0 collective-permute-done.2.rest_1_
  65.9 2.1 %all-to-all-done.2 = bf16[8,120,1024]{2,1,0:T(8,128)(2,1)S(1)} async-done(((bf16[8,120,1024]{2,1,0:T(8,128)(2,1)}), bf16[8,120,1024]{2,1,0:T(8,128)(2,1)S(1)}, u32[]{:S(2)}, u32[]{:S(2)}) %all-to-all-start.2) | async-done | bytes 1966112 | tf_op jit(solution)/shard_map/all_to_all | solution.py:474
  68.0 9.9 %project.4 = bf16[1024,1408]{1,0:T(8,128)(2,1)} custom-call(s32[3]{0:T(128)} %pad_add_fusion.1.place_ref, s32[1,1024]{1,0:T(1,128)S(1)} %get-tuple-element.293.slot_ref, bf16[960,1024]{1,0:T(8,128)(2,1)S(1)} %bitcast.55, f32[1,1024]{1,0:T(1,128)S(1)} %bitcast.67, bf16[1024,512]{1,0:T(8,128)(2,1)} %rest_0_.2, ...), custom_call_target="tpu_custom_call" | custom-call | tf_op jit(solution)/shard_map/project/pallas_call | solution.py:338
  77.9 0.2 while.13
  78.1 0.0 copy-start.13
  78.1 9.1 %all-to-all-start.3 = ((bf16[64,16,1408]{2,1,0:T(8,128)(2,1)}), bf16[64,16,1408]{2,1,0:T(8,128)(2,1)S(1)}, u32[]{:S(2)}, u32[]{:S(2)}) async-start(bf16[64,16,1408]{2,1,0:T(8,128)(2,1)} %bitcast.57), calls=%async_computation.3 | async-start | bytes 5767168 | tf_op jit(solution)/shard_map/all_to_all | solution.py:530
  87.3 0.1 collective-permute-start.6
  87.4 0.0 copy-done.13
  87.4 0.1 add.97
  87.5 0.1 add.98
  87.5 0.1 add.100
  87.6 0.1 reshape_tile.4.length_ref
  87.8 0.1 fusion.3
  87.9 0.1 pad_maximum_fusion.1
  88.0 0.7 collective-permute-start.7
  88.7 0.9 slice_convert_fusion
  89.6 0.1 reshape.209
  89.7 35.8 %all-to-all-done.3 = bf16[64,16,1408]{2,1,0:T(8,128)(2,1)S(1)} async-done(((bf16[64,16,1408]{2,1,0:T(8,128)(2,1)}), bf16[64,16,1408]{2,1,0:T(8,128)(2,1)S(1)}, u32[]{:S(2)}, u32[]{:S(2)}) %all-to-all-start.3) | async-done | bytes 2883616 | tf_op jit(solution)/shard_map/all_to_all | solution.py:530
  125.5 8.7 %attend.1 = (bf16[4,8,16,1024]{3,2,1,0:T(8,128)(2,1)S(1)}, bf16[16,1024]{1,0:T(8,128)(2,1)S(1)}, bf16[16,1024]{1,0:T(8,128)(2,1)S(1)}) custom-call(bf16[8,8,16,1408]{3,2,1,0:T(8,128)(2,1)S(1)} %bitcast.53, f32[8,1,1280]{2,1,0:T(1,128)S(1)} %pad_maximum_fusion.bias_ref, f32[16,128]{1,0:T(8,128)S(1)} %get-tuple-element.298.cosine_ref, ...), custom_call_target="tpu_custom_call" | custom-call | tf_op jit(solution)/shard_map/attend/pallas_call | solution.py:263
  134.2 0.0 copy-start.2
  134.2 1.0 copy-done.2
  135.2 4.7 %all-to-all-start.4 = ((bf16[32,16,1024]{2,1,0:T(8,128)(2,1)}), bf16[32,16,1024]{2,1,0:T(8,128)(2,1)}, u32[]{:S(2)}, u32[]{:S(2)}) async-start(bf16[32,16,1024]{2,1,0:T(8,128)(2,1)} %bitcast.56), calls=%async_computation.4 | async-start | bytes 2097152 | tf_op jit(solution)/shard_map/all_to_all | solution.py:544
  139.9 0.0 collective-permute-done.6.rest_1_
  139.9 0.0 collective-permute-done.7.rest_3_
  139.9 17.3 %all-to-all-done.4 = bf16[32,16,1024]{2,1,0:T(8,128)(2,1)} async-done(((bf16[32,16,1024]{2,1,0:T(8,128)(2,1)}), bf16[32,16,1024]{2,1,0:T(8,128)(2,1)}, u32[]{:S(2)}, u32[]{:S(2)}) %all-to-all-start.4) | async-done | bytes 1048608 | tf_op jit(solution)/shard_map/all_to_all | solution.py:544
  157.2 6.2 %branch.1 = bf16[512,2048]{1,0:T(8,128)(2,1)} custom-call(s32[3]{0:T(128)S(1)} %copy-done.12, bf16[512,1024]{1,0:T(8,128)(2,1)} %bitcast.23.rows_ref, bf16[512,1024]{1,0:T(8,128)(2,1)} %rest_0_.3, bf16[512,1024]{1,0:T(8,128)(2,1)} %collective-permute-done.6.rest_1_, bf16[512,1024]{1,0:T(8,128)(2,1)} %copy-done.1, ...), custom_call_target="tpu_custom_call" | custom-call | tf_op jit(solution)/shard_map/branch/pallas_call | solution.py:384
  163.3 5.2 %all-to-all-start.5 = ((bf16[32,16,2048]{2,1,0:T(8,128)(2,1)}), bf16[32,16,2048]{2,1,0:T(8,128)(2,1)}, u32[]{:S(2)}, u32[]{:S(2)}) async-start(bf16[32,16,2048]{2,1,0:T(8,128)(2,1)} %bitcast.58), calls=%async_computation.5 | async-start | bytes 4194304 | tf_op jit(solution)/shard_map/all_to_all | solution.py:548
  168.5 0.6 reshape.214
  169.2 0.6 reshape.215
  169.8 26.5 %all-to-all-done.5 = bf16[32,16,2048]{2,1,0:T(8,128)(2,1)} async-done(((bf16[32,16,2048]{2,1,0:T(8,128)(2,1)}), bf16[32,16,2048]{2,1,0:T(8,128)(2,1)}, u32[]{:S(2)}, u32[]{:S(2)}) %all-to-all-start.5) | async-done | bytes 2097184 | tf_op jit(solution)/shard_map/all_to_all | solution.py:548
  196.3 2.6 %hidden_sum.1 = bf16[4,4,8192]{2,1,0:T(4,128)(2,1)} custom-call(bf16[2,2,8,16,2048]{4,3,2,1,0:T(8,128)(2,1)} %bitcast.25.branch_ref, bf16[8,8,16,1408]{3,2,1,0:T(8,128)(2,1)S(1)} %bitcast.54), custom_call_target="tpu_custom_call" | custom-call | tf_op jit(solution)/shard_map/hidden_sum/pallas_call | solution.py:418
  (17 shorter events, 0.1 us)
Async XLA Ops:
  2.1 20.4 %all-to-all-start.1 = ((s32[128,1,16]{2,1,0:T(1,128)}), s32[128,1,16]{2,1,0:T(1,128)S(1)}, u32[]{:S(2)}, u32[]{:S(2)}) async-start(s32[128,1,16]{2,1,0:T(1,128)} %broadcast_in_dim.16), calls=%async_computation.1 | async-start | bytes 131072 | tf_op jit(solution)/shard_map/all_to_all | solution.py:466
  22.5 0.6 copy-start.8
  33.6 1.6 collective-permute-start.1
  35.3 5.9 %copy-start.6 = (bf16[1024,64]{0,1:T(8,128)(2,1)S(1)}, bf16[1024,64]{0,1:T(8,128)(2,1)}, u32[]{:S(2)}) copy-start(bf16[1024,64]{0,1:T(8,128)(2,1)} %param.20) | copy-start | bytes 393220
  35.3 6.4 %copy-start.7 = (bf16[1024,64]{0,1:T(8,128)(2,1)S(1)}, bf16[1024,64]{0,1:T(8,128)(2,1)}, u32[]{:S(2)}) copy-start(bf16[1024,64]{0,1:T(8,128)(2,1)} %param.21) | copy-start | bytes 393220
  36.8 31.2 %all-to-all-start.2 = ((bf16[8,120,1024]{2,1,0:T(8,128)(2,1)}), bf16[8,120,1024]{2,1,0:T(8,128)(2,1)S(1)}, u32[]{:S(2)}, u32[]{:S(2)}) async-start(bf16[8,120,1024]{2,1,0:T(8,128)(2,1)} %broadcast_in_dim.17), calls=%async_computation.2 | async-start | bytes 3932160 | tf_op jit(solution)/shard_map/all_to_all | solution.py:474
  40.5 25.5 %collective-permute-start.5 = (bf16[512,1024]{1,0:T(8,128)(2,1)}, bf16[512,1024]{1,0:T(8,128)(2,1)S(1)}, u32[]{:S(2)}, u32[]{:S(2)}) collective-permute-start(bf16[512,1024]{1,0:T(8,128)(2,1)} %rest_0_.3), channel_id=1, source_target_pairs={{0,32},{32,0},{1,33},{33,1},{2,34},{34,2},{3,35},{35,3},{4,36},{36... | collective-permute-start | bytes 3145736 | tf_op jit(solution)/shard_map/ppermute | solution.py:34
  41.2 24.8 %collective-permute-start.2 = (bf16[1024,512]{1,0:T(8,128)(2,1)}, bf16[1024,512]{1,0:T(8,128)(2,1)}, u32[]{:S(2)}, u32[]{:S(2)}) collective-permute-start(bf16[1024,512]{1,0:T(8,128)(2,1)} %rest_0_.2), channel_id=1, source_target_pairs={{0,1},{1,0},{2,3},{3,2},{4,5},{5,4},{6,7},{7,6},{8,9},{9,8},{10,11... | collective-permute-start | bytes 3145736 | tf_op jit(solution)/shard_map/ppermute | solution.py:30
  41.2 9.6 %collective-permute-start.3 = (bf16[64,1024]{1,0:T(8,128)(2,1)S(1)}, bf16[64,1024]{1,0:T(8,128)(2,1)S(1)}, u32[]{:S(2)}, u32[]{:S(2)}) collective-permute-start(bf16[64,1024]{1,0:T(8,128)(2,1)S(1)} %bitcast.59), channel_id=1, source_target_pairs={{0,1},{1,0},{2,3},{3,2},{4,5},{5,4},{6,7},{7,6},{8,9},{9,8},{10,11... | collective-permute-start | bytes 393224 | tf_op jit(solution)/shard_map/ppermute | solution.py:30
  41.7 9.1 %collective-permute-start.4 = (bf16[64,1024]{1,0:T(8,128)(2,1)S(1)}, bf16[64,1024]{1,0:T(8,128)(2,1)S(1)}, u32[]{:S(2)}, u32[]{:S(2)}) collective-permute-start(bf16[64,1024]{1,0:T(8,128)(2,1)S(1)} %bitcast.62), channel_id=1, source_target_pairs={{0,1},{1,0},{2,3},{3,2},{4,5},{5,4},{6,7},{7,6},{8,9},{9,8},{10,11... | collective-permute-start | bytes 393224 | tf_op jit(solution)/shard_map/ppermute | solution.py:30
  65.9 11.9 %copy-start.1 = (bf16[512,1024]{1,0:T(8,128)(2,1)}, bf16[512,1024]{1,0:T(8,128)(2,1)S(1)}, u32[]{:S(2)}) copy-start(bf16[512,1024]{1,0:T(8,128)(2,1)S(1)} %collective-permute-done.5.rest_6_.rest_2_) | copy-start | bytes 3145732
  68.0 9.9 %copy-start = (bf16[8,120,1024]{2,1,0:T(8,128)(2,1)}, bf16[8,120,1024]{2,1,0:T(8,128)(2,1)S(1)}, u32[]{:S(2)}) copy-start(bf16[8,120,1024]{2,1,0:T(8,128)(2,1)S(1)} %all-to-all-done.2) | copy-start | bytes 5898244
  68.0 9.9 %copy-start.9 = (s32[2,1,1024]{2,1,0:T(1,128)S(1)}, s32[2,1,1024]{2,1,0:T(1,128)}, u32[]{:S(2)}) copy-start(s32[2,1,1024]{2,1,0:T(1,128)} %reshape_reshape.9) | copy-start | bytes 24580
  78.1 9.3 %copy-start.13 = (s32[4]{0:T(128)S(1)}, s32[4]{0:T(128)}, u32[]{:S(2)}) copy-start(s32[4]{0:T(128)} %param.16) | copy-start | bytes 52
  78.1 47.4 %all-to-all-start.3 = ((bf16[64,16,1408]{2,1,0:T(8,128)(2,1)}), bf16[64,16,1408]{2,1,0:T(8,128)(2,1)S(1)}, u32[]{:S(2)}, u32[]{:S(2)}) async-start(bf16[64,16,1408]{2,1,0:T(8,128)(2,1)} %bitcast.57), calls=%async_computation.3 | async-start | bytes 5767168 | tf_op jit(solution)/shard_map/all_to_all | solution.py:530
  87.3 52.6 %collective-permute-start.6 = (bf16[512,1024]{1,0:T(8,128)(2,1)}, bf16[512,1024]{1,0:T(8,128)(2,1)}, u32[]{:S(2)}, u32[]{:S(2)}) collective-permute-start(bf16[512,1024]{1,0:T(8,128)(2,1)} %rest_0_.3), channel_id=1, source_target_pairs={{0,1},{1,0},{2,3},{3,2},{4,5},{5,4},{6,7},{7,6},{8,9},{9,8},{10,11... | collective-permute-start | bytes 3145736 | tf_op jit(solution)/shard_map/ppermute | solution.py:30
  88.0 51.9 %collective-permute-start.7 = (bf16[512,1024]{1,0:T(8,128)(2,1)}, bf16[512,1024]{1,0:T(8,128)(2,1)}, u32[]{:S(2)}, u32[]{:S(2)}) collective-permute-start(bf16[512,1024]{1,0:T(8,128)(2,1)} %copy-done.1), channel_id=1, source_target_pairs={{0,1},{1,0},{2,3},{3,2},{4,5},{5,4},{6,7},{7,6},{8,9},{9,8},{10,11... | collective-permute-start | bytes 3145736 | tf_op jit(solution)/shard_map/ppermute | solution.py:30
  125.5 31.6 %copy-start.12 = (s32[3]{0:T(128)S(1)}, s32[3]{0:T(128)}, u32[]{:S(2)}) copy-start(s32[3]{0:T(128)} %get-tuple-element.589) | copy-start | bytes 40
  134.2 1.0 copy-start.2
  135.2 22.0 %all-to-all-start.4 = ((bf16[32,16,1024]{2,1,0:T(8,128)(2,1)}), bf16[32,16,1024]{2,1,0:T(8,128)(2,1)}, u32[]{:S(2)}, u32[]{:S(2)}) async-start(bf16[32,16,1024]{2,1,0:T(8,128)(2,1)} %bitcast.56), calls=%async_computation.4 | async-start | bytes 2097152 | tf_op jit(solution)/shard_map/all_to_all | solution.py:544
  163.3 32.9 %all-to-all-start.5 = ((bf16[32,16,2048]{2,1,0:T(8,128)(2,1)}), bf16[32,16,2048]{2,1,0:T(8,128)(2,1)}, u32[]{:S(2)}, u32[]{:S(2)}) async-start(bf16[32,16,2048]{2,1,0:T(8,128)(2,1)} %bitcast.58), calls=%async_computation.5 | async-start | bytes 4194304 | tf_op jit(solution)/shard_map/all_to_all | solution.py:548

commit v10 on v9

--- a/solution.py
+++ b/solution.py
@@ -45,73 +45,76 @@
 
 
 def lookup_kernel(place_ref, id_row_ref, q_ref, k_ref, v_ref, vocab_ref, *rest):
-    mine_ref, theirs_ref, rank_ref, list_ref, total_ref = rest
-    step = pl.program_id(0)
+    mine_ref, theirs_ref, rank_ref, list_ref, total_ref, vocab_buf, sem = rest
     chip, core, first = place_ref[0], place_ref[1], place_ref[3]
     planes, _, rows = id_row_ref.shape
-    span = vocab_ref.shape[0]
-    vocab_here = span * pl.num_programs(0)
-
-    @pl.when(step == 0)
-    def _():
-        total_ref[...] = jnp.zeros_like(total_ref)
-        across = lax.broadcasted_iota(jnp.int32, (rows, rows), 1)
-        down = lax.broadcasted_iota(jnp.int32, (rows, rows), 0)
-        earlier = across < down
-        slot = lax.broadcasted_iota(jnp.int32, (SENT_ROWS, rows), 0)
-        for plane in range(planes):
-            id_row = id_row_ref[plane]
-            id_col = turned(id_row)
-            keys = []
-            for low in range(0, rows, rows // 4):
-                high = low + rows // 4
-                own_col = id_col[low:high]
-                again = (id_row[:, :high] == own_col) & earlier[low:high, :high]
-                found = jnp.max(jnp.where(again, 1, 0), axis=1, keepdims=True)
-                keys.append(jnp.where(found == 0, own_col, -1))
-            key_col = jnp.concatenate(keys, axis=0)
-            edge_row = jnp.zeros_like(id_row)
-            for other in range(1, CHIP_COUNT):
-                edge = other * 2 * vocab_here
-                edge_row = jnp.where(id_row >= edge, edge, edge_row)
-            before = (key_col >= edge_row) & (key_col < id_row)
-            rank = jnp.sum(before.astype(jnp.int32), axis=0, keepdims=True)
-            rank_ref[plane] = rank
-            offset = id_row - (2 * chip + core) * vocab_here
-            listed = (offset >= 0) & (offset < vocab_here)
-            wanted = jnp.where(listed, rank - first, -1)
-            chosen = (wanted == slot) & (slot < ROUND_ROWS)
-            list_ref[plane * SENT_ROWS : (plane + 1) * SENT_ROWS, :] = jnp.max(
-                jnp.where(chosen, offset, -1), axis=1, keepdims=True
-            )
-
-    entry = lax.broadcasted_iota(jnp.int32, (planes * SENT_ROWS, span), 1) + step * span
-    chosen = (entry == list_ref[...]).astype(jnp.bfloat16)
-    total_ref[...] += jnp.dot(chosen, vocab_ref[...], preferred_element_type=jnp.float32)
-
-    @pl.when(step == pl.num_programs(0) - 1)
-    def _():
-        width = total_ref.shape[1]
-        pieces = [piece[...].astype(jnp.float32) for piece in (q_ref, k_ref, v_ref)]
-        filled = sum(piece.shape[1] for piece in pieces)
-        pieces.append(jnp.zeros((1, width - filled), jnp.float32))
-        bias = jnp.broadcast_to(jnp.concatenate(pieces, axis=1), (8, width))
-        is_bias = (
-            lax.broadcasted_iota(jnp.int32, (8, 1), 0) == ROUND_ROWS + core - (SENT_ROWS - 8)
-        )
-        for side, target in ((0, mine_ref), (1, theirs_ref)):
-            plane = (core + side) % 2
-            start = pl.multiple_of(plane * SENT_ROWS, SENT_ROWS)
-            tail = pl.ds(start + SENT_ROWS - 8, 8)
-            total_ref[tail, :] = jnp.where(is_bias, bias, total_ref[tail, :])
-            target[...] = total_ref[pl.ds(start, SENT_ROWS), :].astype(jnp.bfloat16)
+    vocab_here = vocab_ref.shape[0]
+    steps = sem.shape[0]
+    span = vocab_here // steps
+    copies = [
+        pltpu.make_async_copy(
+            vocab_ref.at[pl.ds(step * span, span), :],
+            vocab_buf.at[pl.ds(step * span, span), :],
+            sem.at[step],
+        )
+        for step in range(steps)
+    ]
+    for copy in copies:
+        copy.start()
+    across = lax.broadcasted_iota(jnp.int32, (rows, rows), 1)
+    down = lax.broadcasted_iota(jnp.int32, (rows, rows), 0)
+    earlier = across < down
+    slot = lax.broadcasted_iota(jnp.int32, (SENT_ROWS, rows), 0)
+    for plane in range(planes):
+        id_row = id_row_ref[plane]
+        id_col = turned(id_row)
+        again = jnp.where((id_row == id_col) & earlier, 1, 0)
+        key_col = jnp.where(jnp.max(again, axis=1, keepdims=True) == 0, id_col, -1)
+        edge_row = jnp.zeros_like(id_row)
+        for other in range(1, CHIP_COUNT):
+            edge = other * 2 * vocab_here
+            edge_row = jnp.where(id_row >= edge, edge, edge_row)
+        before = (key_col >= edge_row) & (key_col < id_row)
+        rank = jnp.sum(before.astype(jnp.int32), axis=0, keepdims=True)
+        rank_ref[plane] = rank
+        offset = id_row - (2 * chip + core) * vocab_here
+        listed = (offset >= 0) & (offset < vocab_here)
+        wanted = jnp.where(listed, rank - first, -1)
+        chosen = (wanted == slot) & (slot < ROUND_ROWS)
+        list_ref[plane * SENT_ROWS : (plane + 1) * SENT_ROWS, :] = jnp.max(
+            jnp.where(chosen, offset, -1), axis=1, keepdims=True
+        )
+
+    total = None
+    for step in range(steps):
+        entry = lax.broadcasted_iota(jnp.int32, (planes * SENT_ROWS, span), 1) + step * span
+        chosen = (entry == list_ref[...]).astype(jnp.bfloat16)
+        copies[step].wait()
+        found = jnp.dot(
+            chosen, vocab_buf[step * span : (step + 1) * span, :], preferred_element_type=jnp.float32
+        )
+        total = found if total is None else total + found
+    total_ref[...] = total
+    width = total_ref.shape[1]
+    pieces = [piece[...].astype(jnp.float32) for piece in (q_ref, k_ref, v_ref)]
+    filled = sum(piece.shape[1] for piece in pieces)
+    pieces.append(jnp.zeros((1, width - filled), jnp.float32))
+    bias = jnp.broadcast_to(jnp.concatenate(pieces, axis=1), (8, width))
+    is_bias = (
+        lax.broadcasted_iota(jnp.int32, (8, 1), 0) == ROUND_ROWS + core - (SENT_ROWS - 8)
+    )
+    for side, target in ((0, mine_ref), (1, theirs_ref)):
+        plane = (core + side) % 2
+        start = pl.multiple_of(plane * SENT_ROWS, SENT_ROWS)
+        tail = pl.ds(start + SENT_ROWS - 8, 8)
+        total_ref[tail, :] = jnp.where(is_bias, bias, total_ref[tail, :])
+        target[...] = total_ref[pl.ds(start, SENT_ROWS), :].astype(jnp.bfloat16)
 
 
 def look_up(place, plane_ids, biases, embedding):
     planes, rows = plane_ids.shape
     vocab_here, width = embedding.shape
     steps = 3
-    whole = lambda *dims: pl.BlockSpec(dims, lambda i: (0,) * len(dims))
     return pl.pallas_call(
         lookup_kernel,
         out_shape=(
@@ -119,21 +122,13 @@
             jax.ShapeDtypeStruct((SENT_ROWS, width), jnp.bfloat16),
             jax.ShapeDtypeStruct((planes, 1, rows), jnp.int32),
         ),
-        grid=(steps,),
-        in_specs=[
-            SMEM,
-            whole(planes, 1, rows),
-            *[whole(1, bias.shape[0]) for bias in biases],
-            pl.BlockSpec((vocab_here // steps, width), lambda i: (i, 0)),
-        ],
-        out_specs=(
-            whole(SENT_ROWS, width),
-            whole(SENT_ROWS, width),
-            whole(planes, 1, rows),
-        ),
+        in_specs=[SMEM] + [VMEM] * (1 + len(biases)) + [HBM],
+        out_specs=(VMEM, VMEM, VMEM),
         scratch_shapes=[
             pltpu.VMEM((planes * SENT_ROWS, 1), jnp.int32),
             pltpu.VMEM((planes * SENT_ROWS, width), jnp.float32),
+            pltpu.VMEM((vocab_here, width), jnp.bfloat16),
+            pltpu.SemaphoreType.DMA((steps,)),
         ],
         compiler_params=pltpu.CompilerParams(vmem_limit_bytes=48 * 1024 * 1024),
         name="look_up",

time: 200 us -> 197 us (0.985)
  Pallas kernels: 37.9 us -> 35 us
    pallas_call x1, Pallas kernels: 10.5 us -> 7.64 us  [look_up(): pl.pallas_call(lookup_kernel, out_shape=(jax.ShapeDtypeStruct((SENT_ROWS,...]
where the time goes in v10:
time: 197 us; the launch traced here: 196 us
  waiting for transfers between devices  107 us (54%)
  starting transfers between devices  36 us (18%)
  Pallas kernels  35 us (18%)
  local copies, waits for them, and re-layouts  10 us (5%)
  other arithmetic  5.29 us (3%)
  between operations  2.85 us (1%)
    all_to_all x1, waiting for transfers between devices, per_device(): lax.all_to_all(payloads[half], PLANE, split_axis=0, concat_axis=0, tiled=...  35.8 us
    all_to_all x1, waiting for transfers between devices, per_device(): lax.all_to_all(branch, LAYER, split_axis=0, concat_axis=0, tiled=True)  26.5 us
    all_to_all x1, waiting for transfers between devices, per_device(): lax.all_to_all(spread.reshape(-1, half_rows, 2 * q_cols), LAYER, split_ax...  17.3 us
    ppermute x1, waiting for transfers between devices, swap_lines(): return lax.ppermute(value, 'yl', [(0, 1), (1, 0)])  15.1 us
    all_to_all x1, starting transfers between devices, per_device(): lax.all_to_all(sent_ids, EVERY, split_axis=0, concat_axis=0, tiled=True)  11.1 us
    pallas_call x1, Pallas kernels, project(): pl.pallas_call(projection_kernel, out_shape=jax.ShapeDtypeStruct((rows, o...  9.86 us
    all_to_all x1, starting transfers between devices, per_device(): lax.all_to_all(payloads[half], PLANE, split_axis=0, concat_axis=0, tiled=...  9.16 us
    pallas_call x1, Pallas kernels, attend(): pl.pallas_call(functools.partial(attention_kernel, half), out_shape=(jax....  8.68 us
  transfers between devices with their start and end apart: 12, of which 7 were waited for; matrix products, arithmetic and copies ran while one was open for 5% of the time, Pallas kernels for 4%

profile of v10, /device:TPU:0, one launch (start us, length us, event | category | flops | bytes accessed | tf_op | source)
XLA Modules:
  0.0 196.1 jit_solution(17244020586517823635)
XLA Ops:
  0.6 0.8 broadcast_in_dim.15
  1.4 0.7 broadcast_in_dim.16
  2.1 11.1 %all-to-all-start.1 = ((s32[128,1,16]{2,1,0:T(1,128)}), s32[128,1,16]{2,1,0:T(1,128)S(1)}, u32[]{:S(2)}, u32[]{:S(2)}) async-start(s32[128,1,16]{2,1,0:T(1,128)} %broadcast_in_dim.16), calls=%async_computation.1 | async-start | bytes 131072 | tf_op jit(solution)/shard_map/all_to_all | solution.py:461
  13.2 0.1 pad_add_fusion.2.place_ref
  13.3 0.7 reshape.202.q_ref
  14.0 8.5 %all-to-all-done.1 = s32[128,1,16]{2,1,0:T(1,128)S(1)} async-done(((s32[128,1,16]{2,1,0:T(1,128)}), s32[128,1,16]{2,1,0:T(1,128)S(1)}, u32[]{:S(2)}, u32[]{:S(2)}) %all-to-all-start.1) | async-done | bytes 8224 | tf_op jit(solution)/shard_map/all_to_all | solution.py:461
  22.5 0.1 reshape_reshape.8.id_row_ref
  22.6 0.5 copy-done.8
  23.1 7.6 %look_up.4 = (bf16[120,1024]{1,0:T(8,128)(2,1)S(1)}, bf16[120,1024]{1,0:T(8,128)(2,1)S(1)}, s32[2,1,1024]{2,1,0:T(1,128)S(1)}) custom-call(s32[4]{0:T(128)S(1)} %pad_add_fusion.2.place_ref, s32[2,1,1024]{2,1,0:T(1,128)S(1)} %reshape_reshape.8.id_row_ref, bf16[1,512]{1,0:T(2,128)(2,1)S(1)} %reshape.202.q_ref, bf16[1,64]{1,0:T(2,128)(2,1)} %bitcast.70, ...), custom_call_target="tpu_custom_call" | custom-call | tf_op jit(solution)/shard_map/look_up/pallas_call | solution.py:118
  30.8 0.1 collective-permute-start.1
  30.8 1.5 collective-permute-done.1
  32.3 0.1 add.92
  32.4 0.0 copy-start.6
  32.4 0.0 copy-start.7
  32.4 1.6 broadcast_in_dim.17
  34.0 3.6 %all-to-all-start.2 = ((bf16[8,120,1024]{2,1,0:T(8,128)(2,1)}), bf16[8,120,1024]{2,1,0:T(8,128)(2,1)S(1)}, u32[]{:S(2)}, u32[]{:S(2)}) async-start(bf16[8,120,1024]{2,1,0:T(8,128)(2,1)} %broadcast_in_dim.17), calls=%async_computation.2 | async-start | bytes 3932160 | tf_op jit(solution)/shard_map/all_to_all | solution.py:469
  37.6 0.7 collective-permute-start.5
  38.3 0.0 collective-permute-start.2
  38.3 0.0 copy-done.6
  38.3 0.5 collective-permute-start.3
  38.8 0.1 collective-permute-start.4
  38.9 0.6 pad_add_fusion.1.place_ref
  39.5 0.7 dynamic-slice_convert_fusion
  40.2 1.5 reshape.206
  41.7 0.6 reduce_max.8
  44.3 1.5 reshape_reshape.9
  45.9 0.7 fusion.4
  46.6 0.7 and_select_fusion.1
  47.3 0.6 add_select_fusion
  47.9 0.0 collective-permute-done.3.rest_3_
  47.9 0.0 collective-permute-done.4.rest_5_
  47.9 15.1 %collective-permute-done.5.rest_6_.rest_2_ = bf16[512,1024]{1,0:T(8,128)(2,1)S(1)} collective-permute-done((bf16[512,1024]{1,0:T(8,128)(2,1)}, bf16[512,1024]{1,0:T(8,128)(2,1)S(1)}, u32[]{:S(2)}, u32[]{:S(2)}) %collective-permute-start.5) | collective-permute-done | bytes 1048608 | tf_op jit(solution)/shard_map/ppermute | solution.py:34
  63.1 0.0 collective-permute-done.2.rest_1_
  63.1 2.1 %all-to-all-done.2 = bf16[8,120,1024]{2,1,0:T(8,128)(2,1)S(1)} async-done(((bf16[8,120,1024]{2,1,0:T(8,128)(2,1)}), bf16[8,120,1024]{2,1,0:T(8,128)(2,1)S(1)}, u32[]{:S(2)}, u32[]{:S(2)}) %all-to-all-start.2) | async-done | bytes 1966112 | tf_op jit(solution)/shard_map/all_to_all | solution.py:469
  65.2 9.9 %project.4 = bf16[1024,1408]{1,0:T(8,128)(2,1)} custom-call(s32[3]{0:T(128)} %pad_add_fusion.1.place_ref, s32[1,1024]{1,0:T(1,128)S(1)} %get-tuple-element.293.slot_ref, bf16[960,1024]{1,0:T(8,128)(2,1)S(1)} %bitcast.55, f32[1,1024]{1,0:T(1,128)S(1)} %bitcast.67, bf16[1024,512]{1,0:T(8,128)(2,1)} %rest_0_.2, ...), custom_call_target="tpu_custom_call" | custom-call | tf_op jit(solution)/shard_map/project/pallas_call | solution.py:333
  75.0 0.0 copy-done.1
  75.0 0.0 copy-done
  75.0 0.0 copy-done.9
  75.0 0.2 while.13
  75.2 0.0 copy-start.13
  75.3 9.2 %all-to-all-start.3 = ((bf16[64,16,1408]{2,1,0:T(8,128)(2,1)}), bf16[64,16,1408]{2,1,0:T(8,128)(2,1)S(1)}, u32[]{:S(2)}, u32[]{:S(2)}) async-start(bf16[64,16,1408]{2,1,0:T(8,128)(2,1)} %bitcast.57), calls=%async_computation.3 | async-start | bytes 5767168 | tf_op jit(solution)/shard_map/all_to_all | solution.py:525
  84.4 0.1 collective-permute-start.6
  84.5 0.1 add.97
  84.6 0.1 add.98
  84.7 0.1 add.100
  84.8 0.1 reshape_tile.4.length_ref
  84.9 0.1 fusion.3
  85.0 0.1 pad_maximum_fusion.1
  85.1 0.7 collective-permute-start.7
  85.8 0.9 slice_convert_fusion
  86.8 0.1 reshape.209
  86.9 35.8 %all-to-all-done.3 = bf16[64,16,1408]{2,1,0:T(8,128)(2,1)S(1)} async-done(((bf16[64,16,1408]{2,1,0:T(8,128)(2,1)}), bf16[64,16,1408]{2,1,0:T(8,128)(2,1)S(1)}, u32[]{:S(2)}, u32[]{:S(2)}) %all-to-all-start.3) | async-done | bytes 2883616 | tf_op jit(solution)/shard_map/all_to_all | solution.py:525
  122.7 8.7 %attend.1 = (bf16[4,8,16,1024]{3,2,1,0:T(8,128)(2,1)S(1)}, bf16[16,1024]{1,0:T(8,128)(2,1)S(1)}, bf16[16,1024]{1,0:T(8,128)(2,1)S(1)}) custom-call(bf16[8,8,16,1408]{3,2,1,0:T(8,128)(2,1)S(1)} %bitcast.53, f32[8,1,1280]{2,1,0:T(1,128)S(1)} %pad_maximum_fusion.bias_ref, f32[16,128]{1,0:T(8,128)S(1)} %get-tuple-element.298.cosine_ref, ...), custom_call_target="tpu_custom_call" | custom-call | tf_op jit(solution)/shard_map/attend/pallas_call | solution.py:258
  131.4 1.0 copy-done.2
  132.4 4.7 %all-to-all-start.4 = ((bf16[32,16,1024]{2,1,0:T(8,128)(2,1)}), bf16[32,16,1024]{2,1,0:T(8,128)(2,1)}, u32[]{:S(2)}, u32[]{:S(2)}) async-start(bf16[32,16,1024]{2,1,0:T(8,128)(2,1)} %bitcast.56), calls=%async_computation.4 | async-start | bytes 2097152 | tf_op jit(solution)/shard_map/all_to_all | solution.py:539
  137.0 0.0 collective-permute-done.6.rest_1_
  137.0 0.0 collective-permute-done.7.rest_3_
  137.1 17.3 %all-to-all-done.4 = bf16[32,16,1024]{2,1,0:T(8,128)(2,1)} async-done(((bf16[32,16,1024]{2,1,0:T(8,128)(2,1)}), bf16[32,16,1024]{2,1,0:T(8,128)(2,1)}, u32[]{:S(2)}, u32[]{:S(2)}) %all-to-all-start.4) | async-done | bytes 1048608 | tf_op jit(solution)/shard_map/all_to_all | solution.py:539
  154.3 6.2 %branch.1 = bf16[512,2048]{1,0:T(8,128)(2,1)} custom-call(s32[3]{0:T(128)S(1)} %copy-done.12, bf16[512,1024]{1,0:T(8,128)(2,1)} %bitcast.23.rows_ref, bf16[512,1024]{1,0:T(8,128)(2,1)} %rest_0_.3, bf16[512,1024]{1,0:T(8,128)(2,1)} %collective-permute-done.6.rest_1_, bf16[512,1024]{1,0:T(8,128)(2,1)} %copy-done.1, ...), custom_call_target="tpu_custom_call" | custom-call | tf_op jit(solution)/shard_map/branch/pallas_call | solution.py:379
  160.5 5.2 %all-to-all-start.5 = ((bf16[32,16,2048]{2,1,0:T(8,128)(2,1)}), bf16[32,16,2048]{2,1,0:T(8,128)(2,1)}, u32[]{:S(2)}, u32[]{:S(2)}) async-start(bf16[32,16,2048]{2,1,0:T(8,128)(2,1)} %bitcast.58), calls=%async_computation.5 | async-start | bytes 4194304 | tf_op jit(solution)/shard_map/all_to_all | solution.py:543
  165.7 0.6 reshape.214
  166.3 0.6 reshape.215
  167.0 26.5 %all-to-all-done.5 = bf16[32,16,2048]{2,1,0:T(8,128)(2,1)} async-done(((bf16[32,16,2048]{2,1,0:T(8,128)(2,1)}), bf16[32,16,2048]{2,1,0:T(8,128)(2,1)}, u32[]{:S(2)}, u32[]{:S(2)}) %all-to-all-start.5) | async-done | bytes 2097184 | tf_op jit(solution)/shard_map/all_to_all | solution.py:543
  193.4 2.6 %hidden_sum.1 = bf16[4,4,8192]{2,1,0:T(4,128)(2,1)} custom-call(bf16[2,2,8,16,2048]{4,3,2,1,0:T(8,128)(2,1)} %bitcast.25.branch_ref, bf16[8,8,16,1408]{3,2,1,0:T(8,128)(2,1)S(1)} %bitcast.54), custom_call_target="tpu_custom_call" | custom-call | tf_op jit(solution)/shard_map/hidden_sum/pallas_call | solution.py:413
  (17 shorter events, 0.1 us)
Async XLA Ops:
  2.1 20.4 %all-to-all-start.1 = ((s32[128,1,16]{2,1,0:T(1,128)}), s32[128,1,16]{2,1,0:T(1,128)S(1)}, u32[]{:S(2)}, u32[]{:S(2)}) async-start(s32[128,1,16]{2,1,0:T(1,128)} %broadcast_in_dim.16), calls=%async_computation.1 | async-start | bytes 131072 | tf_op jit(solution)/shard_map/all_to_all | solution.py:461
  22.5 0.6 copy-start.8
  30.8 1.6 collective-permute-start.1
  32.4 5.9 %copy-start.6 = (bf16[1024,64]{0,1:T(8,128)(2,1)S(1)}, bf16[1024,64]{0,1:T(8,128)(2,1)}, u32[]{:S(2)}) copy-start(bf16[1024,64]{0,1:T(8,128)(2,1)} %param.20) | copy-start | bytes 393220
  32.4 6.4 %copy-start.7 = (bf16[1024,64]{0,1:T(8,128)(2,1)S(1)}, bf16[1024,64]{0,1:T(8,128)(2,1)}, u32[]{:S(2)}) copy-start(bf16[1024,64]{0,1:T(8,128)(2,1)} %param.21) | copy-start | bytes 393220
  34.0 31.2 %all-to-all-start.2 = ((bf16[8,120,1024]{2,1,0:T(8,128)(2,1)}), bf16[8,120,1024]{2,1,0:T(8,128)(2,1)S(1)}, u32[]{:S(2)}, u32[]{:S(2)}) async-start(bf16[8,120,1024]{2,1,0:T(8,128)(2,1)} %broadcast_in_dim.17), calls=%async_computation.2 | async-start | bytes 3932160 | tf_op jit(solution)/shard_map/all_to_all | solution.py:469
  37.6 25.5 %collective-permute-start.5 = (bf16[512,1024]{1,0:T(8,128)(2,1)}, bf16[512,1024]{1,0:T(8,128)(2,1)S(1)}, u32[]{:S(2)}, u32[]{:S(2)}) collective-permute-start(bf16[512,1024]{1,0:T(8,128)(2,1)} %rest_0_.3), channel_id=1, source_target_pairs={{0,32},{32,0},{1,33},{33,1},{2,34},{34,2},{3,35},{35,3},{4,36},{36... | collective-permute-start | bytes 3145736 | tf_op jit(solution)/shard_map/ppermute | solution.py:34
  38.3 24.8 %collective-permute-start.2 = (bf16[1024,512]{1,0:T(8,128)(2,1)}, bf16[1024,512]{1,0:T(8,128)(2,1)}, u32[]{:S(2)}, u32[]{:S(2)}) collective-permute-start(bf16[1024,512]{1,0:T(8,128)(2,1)} %rest_0_.2), channel_id=1, source_target_pairs={{0,1},{1,0},{2,3},{3,2},{4,5},{5,4},{6,7},{7,6},{8,9},{9,8},{10,11... | collective-permute-start | bytes 3145736 | tf_op jit(solution)/shard_map/ppermute | solution.py:30
  38.3 9.6 %collective-permute-start.3 = (bf16[64,1024]{1,0:T(8,128)(2,1)S(1)}, bf16[64,1024]{1,0:T(8,128)(2,1)S(1)}, u32[]{:S(2)}, u32[]{:S(2)}) collective-permute-start(bf16[64,1024]{1,0:T(8,128)(2,1)S(1)} %bitcast.59), channel_id=1, source_target_pairs={{0,1},{1,0},{2,3},{3,2},{4,5},{5,4},{6,7},{7,6},{8,9},{9,8},{10,11... | collective-permute-start | bytes 393224 | tf_op jit(solution)/shard_map/ppermute | solution.py:30
  38.8 9.1 %collective-permute-start.4 = (bf16[64,1024]{1,0:T(8,128)(2,1)S(1)}, bf16[64,1024]{1,0:T(8,128)(2,1)S(1)}, u32[]{:S(2)}, u32[]{:S(2)}) collective-permute-start(bf16[64,1024]{1,0:T(8,128)(2,1)S(1)} %bitcast.62), channel_id=1, source_target_pairs={{0,1},{1,0},{2,3},{3,2},{4,5},{5,4},{6,7},{7,6},{8,9},{9,8},{10,11... | collective-permute-start | bytes 393224 | tf_op jit(solution)/shard_map/ppermute | solution.py:30
  63.1 11.9 %copy-start.1 = (bf16[512,1024]{1,0:T(8,128)(2,1)}, bf16[512,1024]{1,0:T(8,128)(2,1)S(1)}, u32[]{:S(2)}) copy-start(bf16[512,1024]{1,0:T(8,128)(2,1)S(1)} %collective-permute-done.5.rest_6_.rest_2_) | copy-start | bytes 3145732
  65.1 9.9 %copy-start = (bf16[8,120,1024]{2,1,0:T(8,128)(2,1)}, bf16[8,120,1024]{2,1,0:T(8,128)(2,1)S(1)}, u32[]{:S(2)}) copy-start(bf16[8,120,1024]{2,1,0:T(8,128)(2,1)S(1)} %all-to-all-done.2) | copy-start | bytes 5898244
  65.1 9.9 %copy-start.9 = (s32[2,1,1024]{2,1,0:T(1,128)S(1)}, s32[2,1,1024]{2,1,0:T(1,128)}, u32[]{:S(2)}) copy-start(s32[2,1,1024]{2,1,0:T(1,128)} %reshape_reshape.9) | copy-start | bytes 24580
  75.2 9.3 %copy-start.13 = (s32[4]{0:T(128)S(1)}, s32[4]{0:T(128)}, u32[]{:S(2)}) copy-start(s32[4]{0:T(128)} %param.16) | copy-start | bytes 52
  75.3 47.4 %all-to-all-start.3 = ((bf16[64,16,1408]{2,1,0:T(8,128)(2,1)}), bf16[64,16,1408]{2,1,0:T(8,128)(2,1)S(1)}, u32[]{:S(2)}, u32[]{:S(2)}) async-start(bf16[64,16,1408]{2,1,0:T(8,128)(2,1)} %bitcast.57), calls=%async_computation.3 | async-start | bytes 5767168 | tf_op jit(solution)/shard_map/all_to_all | solution.py:525
  84.4 52.6 %collective-permute-start.6 = (bf16[512,1024]{1,0:T(8,128)(2,1)}, bf16[512,1024]{1,0:T(8,128)(2,1)}, u32[]{:S(2)}, u32[]{:S(2)}) collective-permute-start(bf16[512,1024]{1,0:T(8,128)(2,1)} %rest_0_.3), channel_id=1, source_target_pairs={{0,1},{1,0},{2,3},{3,2},{4,5},{5,4},{6,7},{7,6},{8,9},{9,8},{10,11... | collective-permute-start | bytes 3145736 | tf_op jit(solution)/shard_map/ppermute | solution.py:30
  85.1 51.9 %collective-permute-start.7 = (bf16[512,1024]{1,0:T(8,128)(2,1)}, bf16[512,1024]{1,0:T(8,128)(2,1)}, u32[]{:S(2)}, u32[]{:S(2)}) collective-permute-start(bf16[512,1024]{1,0:T(8,128)(2,1)} %copy-done.1), channel_id=1, source_target_pairs={{0,1},{1,0},{2,3},{3,2},{4,5},{5,4},{6,7},{7,6},{8,9},{9,8},{10,11... | collective-permute-start | bytes 3145736 | tf_op jit(solution)/shard_map/ppermute | solution.py:30
  122.7 31.6 %copy-start.12 = (s32[3]{0:T(128)S(1)}, s32[3]{0:T(128)}, u32[]{:S(2)}) copy-start(s32[3]{0:T(128)} %get-tuple-element.589) | copy-start | bytes 40
  131.4 1.0 copy-start.2
  132.4 22.0 %all-to-all-start.4 = ((bf16[32,16,1024]{2,1,0:T(8,128)(2,1)}), bf16[32,16,1024]{2,1,0:T(8,128)(2,1)}, u32[]{:S(2)}, u32[]{:S(2)}) async-start(bf16[32,16,1024]{2,1,0:T(8,128)(2,1)} %bitcast.56), calls=%async_computation.4 | async-start | bytes 2097152 | tf_op jit(solution)/shard_map/all_to_all | solution.py:539
  160.5 32.9 %all-to-all-start.5 = ((bf16[32,16,2048]{2,1,0:T(8,128)(2,1)}), bf16[32,16,2048]{2,1,0:T(8,128)(2,1)}, u32[]{:S(2)}, u32[]{:S(2)}) async-start(bf16[32,16,2048]{2,1,0:T(8,128)(2,1)} %bitcast.58), calls=%async_computation.5 | async-start | bytes 4194304 | tf_op jit(solution)/shard_map/all_to_all | solution.py:543

commit v11 on v10

--- a/solution.py
+++ b/solution.py
@@ -457,9 +457,22 @@
     core_cols = q_bias.shape[0] + k_bias.shape[0] + v_bias.shape[0]
     q_cols = q_bias.shape[0]
 
-    sent_ids = jnp.broadcast_to(token_ids.reshape(1, rows_here), (parties * 2, rows_here))
-    every_id = lax.all_to_all(sent_ids, EVERY, split_axis=0, concat_axis=0, tiled=True)
-    plane_ids = every_id.reshape(parties, 2, rows_here).transpose(1, 0, 2).reshape(2, plane_rows)
+    layer_parties = parties // 2
+    sent_ids = jnp.broadcast_to(token_ids.reshape(1, rows_here), (layer_parties, rows_here))
+    near_ids = lax.all_to_all(sent_ids, LAYER, split_axis=0, concat_axis=0, tiled=True)
+    other_ids = swap_cores(near_ids)
+    core_ids = jnp.stack(
+        [jnp.where(core == 0, near_ids, other_ids), jnp.where(core == 0, other_ids, near_ids)]
+    )
+    line_ids = swap_lines(core_ids)
+    every_id = jnp.stack(
+        [jnp.where(line == 0, core_ids, line_ids), jnp.where(line == 0, line_ids, core_ids)]
+    )
+    plane_ids = (
+        every_id.reshape(2, 2, 2, layer_parties // 2, rows_here)
+        .transpose(1, 2, 0, 3, 4)
+        .reshape(2, plane_rows)
+    )
     own_holder = lax.dynamic_index_in_dim(plane_ids, core, 0, keepdims=False) // (2 * vocab_here)
     def exchange(turn):
         first = turn * ROUND_ROWS

time: 197 us -> 202 us (1.025)
  blocking collectives: 0 us -> 20.5 us
  starting transfers between devices: 36 us -> 25.2 us
  waiting for transfers between devices: 107 us -> 102 us
    all_to_all x0 -> x1, blocking collectives: none -> 20.5 us  [per_device(): lax.all_to_all(sent_ids, LAYER, split_axis=0, concat_axis=0, tiled=True)]
    all_to_all x1 -> x0, starting transfers between devices: 11.1 us -> none  [per_device(): lax.all_to_all(sent_ids, EVERY, split_axis=0, concat_axis=0, tiled=True)]
    all_to_all x1 -> x0, waiting for transfers between devices: 8.49 us -> none  [per_device(): lax.all_to_all(sent_ids, EVERY, split_axis=0, concat_axis=0, tiled=True)]
    ppermute x1 -> x2, waiting for transfers between devices: 15.1 us -> 17.5 us  [swap_lines(): return lax.ppermute(value, 'yl', [(0, 1), (1, 0)])]
  transfers between devices with their start and end apart: 12 -> 13, of which waited for: 7 -> 8; matrix products, arithmetic and copies ran while one was open for 5% -> 5% of each run, Pallas kernels for 4% -> 4%
where the time goes in v11:
time: 202 us; the launch traced here: 200 us
  waiting for transfers between devices  102 us (50%)
  Pallas kernels  35 us (17%)
  starting transfers between devices  25.2 us (12%)
  blocking collectives  20.5 us (10%)
  local copies, waits for them, and re-layouts  9.37 us (5%)
  other arithmetic  5.39 us (3%)
  between operations  2.86 us (1%)
    all_to_all x1, waiting for transfers between devices, per_device(): lax.all_to_all(payloads[half], PLANE, split_axis=0, concat_axis=0, tiled=...  35.8 us
    all_to_all x1, waiting for transfers between devices, per_device(): lax.all_to_all(branch, LAYER, split_axis=0, concat_axis=0, tiled=True)  26.5 us
    all_to_all x1, blocking collectives, per_device(): lax.all_to_all(sent_ids, LAYER, split_axis=0, concat_axis=0, tiled=True)  20.5 us
    ppermute x2, waiting for transfers between devices, swap_lines(): return lax.ppermute(value, 'yl', [(0, 1), (1, 0)])  17.5 us
    all_to_all x1, waiting for transfers between devices, per_device(): lax.all_to_all(spread.reshape(-1, half_rows, 2 * q_cols), LAYER, split_ax...  17.3 us
    pallas_call x1, Pallas kernels, project(): pl.pallas_call(projection_kernel, out_shape=jax.ShapeDtypeStruct((rows, o...  9.86 us
    all_to_all x1, starting transfers between devices, per_device(): lax.all_to_all(payloads[half], PLANE, split_axis=0, concat_axis=0, tiled=...  8.73 us
    pallas_call x1, Pallas kernels, attend(): pl.pallas_call(functools.partial(attention_kernel, half), out_shape=(jax....  8.68 us
  transfers between devices with their start and end apart: 13, of which 8 were waited for; matrix products, arithmetic and copies ran while one was open for 5% of the time, Pallas kernels for 4%

profile of v11, /device:TPU:0, one launch (start us, length us, event | category | flops | bytes accessed | tf_op | source)
XLA Modules:
  0.0 200.3 jit_solution(1575937608576324756)
XLA Ops:
  0.6 0.8 broadcast_in_dim.15
  1.4 20.5 %all_to_all.46 = s32[32,1,16]{2,1,0:T(1,128)S(1)} all-to-all(s32[32,1,16]{2,1,0:T(1,128)S(1)} %broadcast_in_dim.16), channel_id=1, replica_groups=mesh['yh'=2,'yl'=2,'zl'=2,'zh'=2,'x'=4,'core'=2] {'yh','zl','zh','x'}, dimensions={0} | all-to-all | bytes 4096 | tf_op jit(solution)/shard_map/all_to_all | solution.py:462
  21.9 0.0 collective-permute-start.1
  21.9 1.2 collective-permute-done.1
  23.1 0.8 collective-permute-start.2
  23.8 0.1 pad_add_fusion.3.place_ref
  23.9 0.7 reshape.202.q_ref
  24.6 2.5 %collective-permute-done.2 = s32[2,32,16]{2,1,0:T(8,128)S(1)} collective-permute-done((s32[2,32,16]{2,1,0:T(8,128)S(1)}, s32[2,32,16]{2,1,0:T(8,128)S(1)}, u32[]{:S(2)}, u32[]{:S(2)}) %collective-permute-start.2) | collective-permute-done | bytes 4128 | tf_op jit(solution)/shard_map/ppermute | solution.py:34
  27.1 0.0 copy-start.8
  27.1 0.1 reshape_reshape.6.id_row_ref
  27.2 0.5 copy-done.8
  27.7 7.6 %look_up.4 = (bf16[120,1024]{1,0:T(8,128)(2,1)S(1)}, bf16[120,1024]{1,0:T(8,128)(2,1)S(1)}, s32[2,1,1024]{2,1,0:T(1,128)S(1)}) custom-call(s32[4]{0:T(128)S(1)} %pad_add_fusion.3.place_ref, s32[2,1,1024]{2,1,0:T(1,128)S(1)} %reshape_reshape.6.id_row_ref, bf16[1,512]{1,0:T(2,128)(2,1)S(1)} %reshape.202.q_ref, bf16[1,64]{1,0:T(2,128)(2,1)} %bitcast.89, ...), custom_call_target="tpu_custom_call" | custom-call | tf_op jit(solution)/shard_map/look_up/pallas_call | solution.py:118
  35.4 0.1 collective-permute-start.3
  35.5 1.5 collective-permute-done.3
  37.0 0.1 add.92
  37.0 0.0 copy-start.6
  37.1 0.0 copy-start.7
  37.1 1.6 broadcast_in_dim.17
  38.6 3.6 %all-to-all-start.2 = ((bf16[8,120,1024]{2,1,0:T(8,128)(2,1)}), bf16[8,120,1024]{2,1,0:T(8,128)(2,1)S(1)}, u32[]{:S(2)}, u32[]{:S(2)}) async-start(bf16[8,120,1024]{2,1,0:T(8,128)(2,1)} %broadcast_in_dim.17), calls=%async_computation.2 | async-start | bytes 3932160 | tf_op jit(solution)/shard_map/all_to_all | solution.py:482
  42.2 0.8 collective-permute-start.7
  43.0 0.0 collective-permute-start.4
  43.0 0.5 collective-permute-start.5
  43.5 0.1 collective-permute-start.6
  43.6 0.7 pad_add_fusion.2.place_ref
  44.3 0.7 dynamic-slice_convert_fusion
  44.9 1.5 reshape.206
  46.5 0.6 reduce_max.8
  49.1 1.5 reshape_reshape.7
  50.6 0.7 fusion.4
  51.3 0.7 and_select_fusion.1
  52.1 0.6 add_select_fusion
  52.7 0.0 collective-permute-done.5.rest_3_
  52.7 0.0 collective-permute-done.6.rest_5_
  52.7 15.0 %collective-permute-done.7.rest_6_.rest_2_ = bf16[512,1024]{1,0:T(8,128)(2,1)S(1)} collective-permute-done((bf16[512,1024]{1,0:T(8,128)(2,1)}, bf16[512,1024]{1,0:T(8,128)(2,1)S(1)}, u32[]{:S(2)}, u32[]{:S(2)}) %collective-permute-start.7) | collective-permute-done | bytes 1048608 | tf_op jit(solution)/shard_map/ppermute | solution.py:34
  67.7 0.0 collective-permute-done.4.rest_1_
  67.7 2.1 %all-to-all-done.2 = bf16[8,120,1024]{2,1,0:T(8,128)(2,1)S(1)} async-done(((bf16[8,120,1024]{2,1,0:T(8,128)(2,1)}), bf16[8,120,1024]{2,1,0:T(8,128)(2,1)S(1)}, u32[]{:S(2)}, u32[]{:S(2)}) %all-to-all-start.2) | async-done | bytes 1966112 | tf_op jit(solution)/shard_map/all_to_all | solution.py:482
  69.8 9.9 %project.4 = bf16[1024,1408]{1,0:T(8,128)(2,1)} custom-call(s32[3]{0:T(128)} %pad_add_fusion.2.place_ref, s32[1,1024]{1,0:T(1,128)S(1)} %get-tuple-element.257.slot_ref, bf16[960,1024]{1,0:T(8,128)(2,1)S(1)} %bitcast.71, f32[1,1024]{1,0:T(1,128)S(1)} %bitcast.82, bf16[1024,512]{1,0:T(8,128)(2,1)} %rest_0_.2, ...), custom_call_target="tpu_custom_call" | custom-call | tf_op jit(solution)/shard_map/project/pallas_call | solution.py:333
  79.7 0.0 copy-done.1
  79.7 0.2 while.13
  79.9 0.0 copy-start.13
  79.9 8.7 %all-to-all-start.3 = ((bf16[64,16,1408]{2,1,0:T(8,128)(2,1)}), bf16[64,16,1408]{2,1,0:T(8,128)(2,1)S(1)}, u32[]{:S(2)}, u32[]{:S(2)}) async-start(bf16[64,16,1408]{2,1,0:T(8,128)(2,1)} %bitcast.73), calls=%async_computation.3 | async-start | bytes 5767168 | tf_op jit(solution)/shard_map/all_to_all | solution.py:538
  88.6 0.1 collective-permute-start.8
  88.7 0.1 add.97
  88.8 0.1 add.98
  88.9 0.1 add.100
  89.0 0.1 reshape_tile.4.length_ref
  89.1 0.1 fusion.3
  89.2 0.1 pad_maximum_fusion.1
  89.3 0.7 collective-permute-start.9
  90.0 0.9 slice_convert_fusion
  91.0 0.1 reshape.209
  91.1 35.8 %all-to-all-done.3 = bf16[64,16,1408]{2,1,0:T(8,128)(2,1)S(1)} async-done(((bf16[64,16,1408]{2,1,0:T(8,128)(2,1)}), bf16[64,16,1408]{2,1,0:T(8,128)(2,1)S(1)}, u32[]{:S(2)}, u32[]{:S(2)}) %all-to-all-start.3) | async-done | bytes 2883616 | tf_op jit(solution)/shard_map/all_to_all | solution.py:538
  126.9 8.7 %attend.1 = (bf16[4,8,16,1024]{3,2,1,0:T(8,128)(2,1)S(1)}, bf16[16,1024]{1,0:T(8,128)(2,1)S(1)}, bf16[16,1024]{1,0:T(8,128)(2,1)S(1)}) custom-call(bf16[8,8,16,1408]{3,2,1,0:T(8,128)(2,1)S(1)} %bitcast.69, f32[8,1,1280]{2,1,0:T(1,128)S(1)} %pad_maximum_fusion.bias_ref, f32[16,128]{1,0:T(8,128)S(1)} %get-tuple-element.266.cosine_ref, ...), custom_call_target="tpu_custom_call" | custom-call | tf_op jit(solution)/shard_map/attend/pallas_call | solution.py:258
  135.6 1.0 copy-done.2
  136.6 4.7 %all-to-all-start.4 = ((bf16[32,16,1024]{2,1,0:T(8,128)(2,1)}), bf16[32,16,1024]{2,1,0:T(8,128)(2,1)}, u32[]{:S(2)}, u32[]{:S(2)}) async-start(bf16[32,16,1024]{2,1,0:T(8,128)(2,1)} %bitcast.72), calls=%async_computation.4 | async-start | bytes 2097152 | tf_op jit(solution)/shard_map/all_to_all | solution.py:552
  141.3 0.0 collective-permute-done.8.rest_1_
  141.3 0.0 collective-permute-done.9.rest_3_
  141.3 17.3 %all-to-all-done.4 = bf16[32,16,1024]{2,1,0:T(8,128)(2,1)} async-done(((bf16[32,16,1024]{2,1,0:T(8,128)(2,1)}), bf16[32,16,1024]{2,1,0:T(8,128)(2,1)}, u32[]{:S(2)}, u32[]{:S(2)}) %all-to-all-start.4) | async-done | bytes 1048608 | tf_op jit(solution)/shard_map/all_to_all | solution.py:552
  158.5 6.2 %branch.1 = bf16[512,2048]{1,0:T(8,128)(2,1)} custom-call(s32[3]{0:T(128)S(1)} %copy-done.12, bf16[512,1024]{1,0:T(8,128)(2,1)} %bitcast.29.rows_ref, bf16[512,1024]{1,0:T(8,128)(2,1)} %rest_0_.3, bf16[512,1024]{1,0:T(8,128)(2,1)} %collective-permute-done.8.rest_1_, bf16[512,1024]{1,0:T(8,128)(2,1)} %copy-done.1, ...), custom_call_target="tpu_custom_call" | custom-call | tf_op jit(solution)/shard_map/branch/pallas_call | solution.py:379
  164.7 5.2 %all-to-all-start.5 = ((bf16[32,16,2048]{2,1,0:T(8,128)(2,1)}), bf16[32,16,2048]{2,1,0:T(8,128)(2,1)}, u32[]{:S(2)}, u32[]{:S(2)}) async-start(bf16[32,16,2048]{2,1,0:T(8,128)(2,1)} %bitcast.74), calls=%async_computation.5 | async-start | bytes 4194304 | tf_op jit(solution)/shard_map/all_to_all | solution.py:556
  169.9 0.6 reshape.214
  170.6 0.6 reshape.215
  171.2 26.5 %all-to-all-done.5 = bf16[32,16,2048]{2,1,0:T(8,128)(2,1)} async-done(((bf16[32,16,2048]{2,1,0:T(8,128)(2,1)}), bf16[32,16,2048]{2,1,0:T(8,128)(2,1)}, u32[]{:S(2)}, u32[]{:S(2)}) %all-to-all-start.5) | async-done | bytes 2097184 | tf_op jit(solution)/shard_map/all_to_all | solution.py:556
  197.6 2.6 %hidden_sum.1 = bf16[4,4,8192]{2,1,0:T(4,128)(2,1)} custom-call(bf16[2,2,8,16,2048]{4,3,2,1,0:T(8,128)(2,1)} %bitcast.31.branch_ref, bf16[8,8,16,1408]{3,2,1,0:T(8,128)(2,1)S(1)} %bitcast.70), custom_call_target="tpu_custom_call" | custom-call | tf_op jit(solution)/shard_map/hidden_sum/pallas_call | solution.py:413
  (23 shorter events, 0.1 us)
Async XLA Ops:
  21.9 1.2 collective-permute-start.1
  23.1 4.0 %collective-permute-start.2 = (s32[2,32,16]{2,1,0:T(8,128)S(1)}, s32[2,32,16]{2,1,0:T(8,128)S(1)}, u32[]{:S(2)}, u32[]{:S(2)}) collective-permute-start(s32[2,32,16]{2,1,0:T(8,128)S(1)} %pad_add_fusion.1), channel_id=1, source_target_pairs={{0,32},{32,0},{1,33},{33,1},{2,34},{34,2},{3,35},{35,3},{4,36},{36... | collective-permute-start | bytes 12296 | tf_op jit(solution)/shard_map/ppermute | solution.py:34
  27.1 0.6 copy-start.8
  35.4 1.6 collective-permute-start.3
  37.0 6.0 %copy-start.6 = (bf16[1024,64]{0,1:T(8,128)(2,1)S(1)}, bf16[1024,64]{0,1:T(8,128)(2,1)}, u32[]{:S(2)}) copy-start(bf16[1024,64]{0,1:T(8,128)(2,1)} %param.20) | copy-start | bytes 393220
  37.1 6.5 %copy-start.7 = (bf16[1024,64]{0,1:T(8,128)(2,1)S(1)}, bf16[1024,64]{0,1:T(8,128)(2,1)}, u32[]{:S(2)}) copy-start(bf16[1024,64]{0,1:T(8,128)(2,1)} %param.21) | copy-start | bytes 393220
  38.6 31.2 %all-to-all-start.2 = ((bf16[8,120,1024]{2,1,0:T(8,128)(2,1)}), bf16[8,120,1024]{2,1,0:T(8,128)(2,1)S(1)}, u32[]{:S(2)}, u32[]{:S(2)}) async-start(bf16[8,120,1024]{2,1,0:T(8,128)(2,1)} %broadcast_in_dim.17), calls=%async_computation.2 | async-start | bytes 3932160 | tf_op jit(solution)/shard_map/all_to_all | solution.py:482
  42.2 25.5 %collective-permute-start.7 = (bf16[512,1024]{1,0:T(8,128)(2,1)}, bf16[512,1024]{1,0:T(8,128)(2,1)S(1)}, u32[]{:S(2)}, u32[]{:S(2)}) collective-permute-start(bf16[512,1024]{1,0:T(8,128)(2,1)} %rest_0_.3), channel_id=1, source_target_pairs={{0,32},{32,0},{1,33},{33,1},{2,34},{34,2},{3,35},{35,3},{4,36},{36... | collective-permute-start | bytes 3145736 | tf_op jit(solution)/shard_map/ppermute | solution.py:34
  43.0 24.7 %collective-permute-start.4 = (bf16[1024,512]{1,0:T(8,128)(2,1)}, bf16[1024,512]{1,0:T(8,128)(2,1)}, u32[]{:S(2)}, u32[]{:S(2)}) collective-permute-start(bf16[1024,512]{1,0:T(8,128)(2,1)} %rest_0_.2), channel_id=1, source_target_pairs={{0,1},{1,0},{2,3},{3,2},{4,5},{5,4},{6,7},{7,6},{8,9},{9,8},{10,11... | collective-permute-start | bytes 3145736 | tf_op jit(solution)/shard_map/ppermute | solution.py:30
  43.0 9.7 %collective-permute-start.5 = (bf16[64,1024]{1,0:T(8,128)(2,1)S(1)}, bf16[64,1024]{1,0:T(8,128)(2,1)S(1)}, u32[]{:S(2)}, u32[]{:S(2)}) collective-permute-start(bf16[64,1024]{1,0:T(8,128)(2,1)S(1)} %bitcast.75), channel_id=1, source_target_pairs={{0,1},{1,0},{2,3},{3,2},{4,5},{5,4},{6,7},{7,6},{8,9},{9,8},{10,11... | collective-permute-start | bytes 393224 | tf_op jit(solution)/shard_map/ppermute | solution.py:30
  43.5 9.2 %collective-permute-start.6 = (bf16[64,1024]{1,0:T(8,128)(2,1)S(1)}, bf16[64,1024]{1,0:T(8,128)(2,1)S(1)}, u32[]{:S(2)}, u32[]{:S(2)}) collective-permute-start(bf16[64,1024]{1,0:T(8,128)(2,1)S(1)} %bitcast.78), channel_id=1, source_target_pairs={{0,1},{1,0},{2,3},{3,2},{4,5},{5,4},{6,7},{7,6},{8,9},{9,8},{10,11... | collective-permute-start | bytes 393224 | tf_op jit(solution)/shard_map/ppermute | solution.py:30
  67.7 11.9 %copy-start.1 = (bf16[512,1024]{1,0:T(8,128)(2,1)}, bf16[512,1024]{1,0:T(8,128)(2,1)S(1)}, u32[]{:S(2)}) copy-start(bf16[512,1024]{1,0:T(8,128)(2,1)S(1)} %collective-permute-done.7.rest_6_.rest_2_) | copy-start | bytes 3145732
  69.8 9.9 %copy-start = (bf16[8,120,1024]{2,1,0:T(8,128)(2,1)}, bf16[8,120,1024]{2,1,0:T(8,128)(2,1)S(1)}, u32[]{:S(2)}) copy-start(bf16[8,120,1024]{2,1,0:T(8,128)(2,1)S(1)} %all-to-all-done.2) | copy-start | bytes 5898244
  69.8 9.9 %copy-start.9 = (s32[2,1,1024]{2,1,0:T(1,128)S(1)}, s32[2,1,1024]{2,1,0:T(1,128)}, u32[]{:S(2)}) copy-start(s32[2,1,1024]{2,1,0:T(1,128)} %reshape_reshape.7) | copy-start | bytes 24580
  79.9 8.8 %copy-start.13 = (s32[4]{0:T(128)S(1)}, s32[4]{0:T(128)}, u32[]{:S(2)}) copy-start(s32[4]{0:T(128)} %param.16) | copy-start | bytes 52
  79.9 47.0 %all-to-all-start.3 = ((bf16[64,16,1408]{2,1,0:T(8,128)(2,1)}), bf16[64,16,1408]{2,1,0:T(8,128)(2,1)S(1)}, u32[]{:S(2)}, u32[]{:S(2)}) async-start(bf16[64,16,1408]{2,1,0:T(8,128)(2,1)} %bitcast.73), calls=%async_computation.3 | async-start | bytes 5767168 | tf_op jit(solution)/shard_map/all_to_all | solution.py:538
  88.6 52.6 %collective-permute-start.8 = (bf16[512,1024]{1,0:T(8,128)(2,1)}, bf16[512,1024]{1,0:T(8,128)(2,1)}, u32[]{:S(2)}, u32[]{:S(2)}) collective-permute-start(bf16[512,1024]{1,0:T(8,128)(2,1)} %rest_0_.3), channel_id=1, source_target_pairs={{0,1},{1,0},{2,3},{3,2},{4,5},{5,4},{6,7},{7,6},{8,9},{9,8},{10,11... | collective-permute-start | bytes 3145736 | tf_op jit(solution)/shard_map/ppermute | solution.py:30
  89.3 52.0 %collective-permute-start.9 = (bf16[512,1024]{1,0:T(8,128)(2,1)}, bf16[512,1024]{1,0:T(8,128)(2,1)}, u32[]{:S(2)}, u32[]{:S(2)}) collective-permute-start(bf16[512,1024]{1,0:T(8,128)(2,1)} %copy-done.1), channel_id=1, source_target_pairs={{0,1},{1,0},{2,3},{3,2},{4,5},{5,4},{6,7},{7,6},{8,9},{9,8},{10,11... | collective-permute-start | bytes 3145736 | tf_op jit(solution)/shard_map/ppermute | solution.py:30
  126.9 31.6 %copy-start.12 = (s32[3]{0:T(128)S(1)}, s32[3]{0:T(128)}, u32[]{:S(2)}) copy-start(s32[3]{0:T(128)} %get-tuple-element.557) | copy-start | bytes 40
  135.6 1.0 copy-start.2
  136.6 22.0 %all-to-all-start.4 = ((bf16[32,16,1024]{2,1,0:T(8,128)(2,1)}), bf16[32,16,1024]{2,1,0:T(8,128)(2,1)}, u32[]{:S(2)}, u32[]{:S(2)}) async-start(bf16[32,16,1024]{2,1,0:T(8,128)(2,1)} %bitcast.72), calls=%async_computation.4 | async-start | bytes 2097152 | tf_op jit(solution)/shard_map/all_to_all | solution.py:552
  164.7 32.9 %all-to-all-start.5 = ((bf16[32,16,2048]{2,1,0:T(8,128)(2,1)}), bf16[32,16,2048]{2,1,0:T(8,128)(2,1)}, u32[]{:S(2)}, u32[]{:S(2)}) async-start(bf16[32,16,2048]{2,1,0:T(8,128)(2,1)} %bitcast.74), calls=%async_computation.5 | async-start | bytes 4194304 | tf_op jit(solution)/shard_map/all_to_all | solution.py:556

commit v12 on v10

--- a/solution.py
+++ b/solution.py
@@ -271,7 +271,7 @@
             pltpu.SemaphoreType.DMA((seqs,)),
             pltpu.SemaphoreType.DMA((seqs,)),
         ],
-        compiler_params=pltpu.CompilerParams(vmem_limit_bytes=48 * 1024 * 1024),
+        compiler_params=pltpu.CompilerParams(vmem_limit_bytes=56 * 1024 * 1024),
         name="attend",
     )(arrived, bias, cosine, sine, row_lengths, key_cache, value_cache)
 

time: 197 us -> 203 us (1.030)
  Pallas kernels: 35 us -> 37.6 us
  local copies, waits for them, and re-layouts: 10 us -> 12.2 us
    pallas_call x1, Pallas kernels: 8.68 us -> 11.2 us  [attend(): pl.pallas_call(functools.partial(attention_kernel, half), out_shape=(jax....]
  transfers between devices with their start and end apart: 12 -> 12, of which waited for: 7 -> 7; matrix products, arithmetic and copies ran while one was open for 5% -> 6% of each run, Pallas kernels for 4% -> 6%
where the time goes in v12:
time: 203 us; the launch traced here: 201 us
  waiting for transfers between devices  106 us (52%)
  Pallas kernels  37.6 us (19%)
  starting transfers between devices  35.6 us (18%)
  local copies, waits for them, and re-layouts  12.2 us (6%)
  other arithmetic  6.5 us (3%)
  between operations  2.84 us (1%)
    all_to_all x1, waiting for transfers between devices, per_device(): lax.all_to_all(payloads[half], PLANE, split_axis=0, concat_axis=0, tiled=...  34.2 us
    all_to_all x1, waiting for transfers between devices, per_device(): lax.all_to_all(branch, LAYER, split_axis=0, concat_axis=0, tiled=True)  27.3 us
    all_to_all x1, waiting for transfers between devices, per_device(): lax.all_to_all(spread.reshape(-1, half_rows, 2 * q_cols), LAYER, split_ax...  17.7 us
    ppermute x1, waiting for transfers between devices, swap_lines(): return lax.ppermute(value, 'yl', [(0, 1), (1, 0)])  15.1 us
    pallas_call x1, Pallas kernels, attend(): pl.pallas_call(functools.partial(attention_kernel, half), out_shape=(jax....  11.2 us
    all_to_all x1, starting transfers between devices, per_device(): lax.all_to_all(sent_ids, EVERY, split_axis=0, concat_axis=0, tiled=True)  11.1 us
    pallas_call x1, Pallas kernels, project(): pl.pallas_call(projection_kernel, out_shape=jax.ShapeDtypeStruct((rows, o...  9.87 us
    all_to_all x1, starting transfers between devices, per_device(): lax.all_to_all(payloads[half], PLANE, split_axis=0, concat_axis=0, tiled=...  9.16 us
  transfers between devices with their start and end apart: 12, of which 7 were waited for; matrix products, arithmetic and copies ran while one was open for 6% of the time, Pallas kernels for 6%

profile of v12, /device:TPU:0, one launch (start us, length us, event | category | flops | bytes accessed | tf_op | source)
XLA Modules:
  0.0 201.3 jit_solution(4977245778839232003)
XLA Ops:
  0.6 0.8 broadcast_in_dim.15
  1.4 0.7 broadcast_in_dim.16
  2.1 11.1 %all-to-all-start.1 = ((s32[128,1,16]{2,1,0:T(1,128)}), s32[128,1,16]{2,1,0:T(1,128)S(1)}, u32[]{:S(2)}, u32[]{:S(2)}) async-start(s32[128,1,16]{2,1,0:T(1,128)} %broadcast_in_dim.16), calls=%async_computation.1 | async-start | bytes 131072 | tf_op jit(solution)/shard_map/all_to_all | solution.py:461
  13.2 0.1 pad_add_fusion.2.place_ref
  13.3 0.7 reshape.202.q_ref
  14.0 8.5 %all-to-all-done.1 = s32[128,1,16]{2,1,0:T(1,128)S(1)} async-done(((s32[128,1,16]{2,1,0:T(1,128)}), s32[128,1,16]{2,1,0:T(1,128)S(1)}, u32[]{:S(2)}, u32[]{:S(2)}) %all-to-all-start.1) | async-done | bytes 8224 | tf_op jit(solution)/shard_map/all_to_all | solution.py:461
  22.5 0.1 reshape_reshape.8.id_row_ref
  22.6 0.5 copy-done.10
  23.1 7.6 %look_up.4 = (bf16[120,1024]{1,0:T(8,128)(2,1)S(1)}, bf16[120,1024]{1,0:T(8,128)(2,1)S(1)}, s32[2,1,1024]{2,1,0:T(1,128)S(1)}) custom-call(s32[4]{0:T(128)S(1)} %pad_add_fusion.2.place_ref, s32[2,1,1024]{2,1,0:T(1,128)S(1)} %reshape_reshape.8.id_row_ref, bf16[1,512]{1,0:T(2,128)(2,1)S(1)} %reshape.202.q_ref, bf16[1,64]{1,0:T(2,128)(2,1)} %bitcast.71, ...), custom_call_target="tpu_custom_call" | custom-call | tf_op jit(solution)/shard_map/look_up/pallas_call | solution.py:118
  30.8 0.1 collective-permute-start.1
  30.8 1.5 collective-permute-done.1
  32.3 0.1 add.92
  32.4 0.0 copy-start.7
  32.4 0.0 copy-start.8
  32.4 1.6 broadcast_in_dim.17
  34.0 3.6 %all-to-all-start.2 = ((bf16[8,120,1024]{2,1,0:T(8,128)(2,1)}), bf16[8,120,1024]{2,1,0:T(8,128)(2,1)S(1)}, u32[]{:S(2)}, u32[]{:S(2)}) async-start(bf16[8,120,1024]{2,1,0:T(8,128)(2,1)} %broadcast_in_dim.17), calls=%async_computation.2 | async-start | bytes 3932160 | tf_op jit(solution)/shard_map/all_to_all | solution.py:469
  37.6 0.7 collective-permute-start.5
  38.3 0.0 collective-permute-start.2
  38.3 0.0 copy-done.7
  38.3 0.5 collective-permute-start.3
  38.8 0.1 collective-permute-start.4
  38.9 0.6 pad_add_fusion.1.place_ref
  39.5 0.7 dynamic-slice_convert_fusion
  40.2 1.5 reshape.206
  41.7 0.6 reduce_max.8
  44.3 1.5 reshape_reshape.9
  45.9 0.7 fusion.4
  46.6 0.7 and_select_fusion.1
  47.4 0.6 add_select_fusion
  48.0 0.0 collective-permute-done.3.rest_3_
  48.0 0.0 collective-permute-done.4.rest_5_
  48.0 15.1 %collective-permute-done.5.rest_6_.rest_2_ = bf16[512,1024]{1,0:T(8,128)(2,1)S(1)} collective-permute-done((bf16[512,1024]{1,0:T(8,128)(2,1)}, bf16[512,1024]{1,0:T(8,128)(2,1)S(1)}, u32[]{:S(2)}, u32[]{:S(2)}) %collective-permute-start.5) | collective-permute-done | bytes 1048608 | tf_op jit(solution)/shard_map/ppermute | solution.py:34
  63.1 0.0 collective-permute-done.2.rest_1_
  63.1 2.1 %all-to-all-done.2 = bf16[8,120,1024]{2,1,0:T(8,128)(2,1)S(1)} async-done(((bf16[8,120,1024]{2,1,0:T(8,128)(2,1)}), bf16[8,120,1024]{2,1,0:T(8,128)(2,1)S(1)}, u32[]{:S(2)}, u32[]{:S(2)}) %all-to-all-start.2) | async-done | bytes 1966112 | tf_op jit(solution)/shard_map/all_to_all | solution.py:469
  65.2 9.9 %project.4 = bf16[1024,1408]{1,0:T(8,128)(2,1)} custom-call(s32[3]{0:T(128)} %pad_add_fusion.1.place_ref, s32[1,1024]{1,0:T(1,128)S(1)} %get-tuple-element.293.slot_ref, bf16[960,1024]{1,0:T(8,128)(2,1)S(1)} %bitcast.55, f32[1,1024]{1,0:T(1,128)S(1)} %bitcast.68, bf16[1024,512]{1,0:T(8,128)(2,1)} %rest_0_.2, ...), custom_call_target="tpu_custom_call" | custom-call | tf_op jit(solution)/shard_map/project/pallas_call | solution.py:333
  75.1 0.2 while.13
  75.3 0.0 copy-start.17
  75.3 9.2 %all-to-all-start.3 = ((bf16[64,16,1408]{2,1,0:T(8,128)(2,1)}), bf16[64,16,1408]{2,1,0:T(8,128)(2,1)S(1)}, u32[]{:S(2)}, u32[]{:S(2)}) async-start(bf16[64,16,1408]{2,1,0:T(8,128)(2,1)} %bitcast.56), calls=%async_computation.3 | async-start | bytes 5767168 | tf_op jit(solution)/shard_map/all_to_all | solution.py:525
  84.5 0.1 collective-permute-start.6
  84.6 0.1 add.97
  84.6 0.1 add.98
  84.7 0.1 add.100
  84.8 0.7 reshape_tile.4.length_ref
  85.5 0.1 fusion.3
  85.7 0.7 pad_maximum_fusion.1
  86.3 0.5 collective-permute-start.7
  86.8 0.9 slice_convert_fusion
  87.8 0.1 reshape.209
  87.8 0.6 pad_maximum_fusion.bias_ref
  88.5 34.2 %all-to-all-done.3 = bf16[64,16,1408]{2,1,0:T(8,128)(2,1)S(1)} async-done(((bf16[64,16,1408]{2,1,0:T(8,128)(2,1)}), bf16[64,16,1408]{2,1,0:T(8,128)(2,1)S(1)}, u32[]{:S(2)}, u32[]{:S(2)}) %all-to-all-start.3) | async-done | bytes 2883616 | tf_op jit(solution)/shard_map/all_to_all | solution.py:525
  122.7 1.6 copy-done
  124.3 11.2 %attend.1 = (bf16[4,8,16,1024]{3,2,1,0:T(8,128)(2,1)}, bf16[16,1024]{1,0:T(8,128)(2,1)}, bf16[16,1024]{1,0:T(8,128)(2,1)}) custom-call(bf16[8,8,16,1408]{3,2,1,0:T(8,128)(2,1)} %bitcast.53, f32[8,1,1280]{2,1,0:T(1,128)} %pad_maximum_fusion.bias_ref, f32[16,128]{1,0:T(8,128)} %get-tuple-element.298.cosine_ref, f32[16,128]{1,0:T(8,128)} %get-tuple-element.299.sine_ref, ...), custom_call_target="tpu_custom_call" | custom-call | tf_op jit(solution)/shard_map/attend/pallas_call | solution.py:258
  135.5 4.2 %all-to-all-start.4 = ((bf16[32,16,1024]{2,1,0:T(8,128)(2,1)}), bf16[32,16,1024]{2,1,0:T(8,128)(2,1)S(1)}, u32[]{:S(2)}, u32[]{:S(2)}) async-start(bf16[32,16,1024]{2,1,0:T(8,128)(2,1)} %bitcast.65), calls=%async_computation.4 | async-start | bytes 2097152 | tf_op jit(solution)/shard_map/all_to_all | solution.py:539
  139.6 0.0 collective-permute-done.6.rest_1_
  139.6 0.0 collective-permute-done.7.rest_3_
  139.7 17.7 %all-to-all-done.4 = bf16[32,16,1024]{2,1,0:T(8,128)(2,1)S(1)} async-done(((bf16[32,16,1024]{2,1,0:T(8,128)(2,1)}), bf16[32,16,1024]{2,1,0:T(8,128)(2,1)S(1)}, u32[]{:S(2)}, u32[]{:S(2)}) %all-to-all-start.4) | async-done | bytes 1048608 | tf_op jit(solution)/shard_map/all_to_all | solution.py:539
  157.3 1.0 copy-done.9
  158.3 6.2 %branch.1 = bf16[512,2048]{1,0:T(8,128)(2,1)} custom-call(s32[3]{0:T(128)S(1)} %copy-done.16, bf16[512,1024]{1,0:T(8,128)(2,1)} %bitcast.64, bf16[512,1024]{1,0:T(8,128)(2,1)} %rest_0_.3, bf16[512,1024]{1,0:T(8,128)(2,1)} %collective-permute-done.6.rest_1_, bf16[512,1024]{1,0:T(8,128)(2,1)} %copy-done.3, bf16[512,1024]{1,0:T(8,128)(2,1)} %collective-permute-done.7.rest_3_), custom_call_target="tpu_custom_call" | custom-call | tf_op jit(solution)/shard_map/branch/pallas_call | solution.py:379
  164.5 5.5 %all-to-all-start.5 = ((bf16[32,16,2048]{2,1,0:T(8,128)(2,1)}), bf16[32,16,2048]{2,1,0:T(8,128)(2,1)}, u32[]{:S(2)}, u32[]{:S(2)}) async-start(bf16[32,16,2048]{2,1,0:T(8,128)(2,1)} %bitcast.57), calls=%async_computation.5 | async-start | bytes 4194304 | tf_op jit(solution)/shard_map/all_to_all | solution.py:543
  170.1 0.0 copy-done.15
  170.1 0.6 reshape.214
  170.7 0.6 reshape.215
  171.4 27.3 %all-to-all-done.5 = bf16[32,16,2048]{2,1,0:T(8,128)(2,1)} async-done(((bf16[32,16,2048]{2,1,0:T(8,128)(2,1)}), bf16[32,16,2048]{2,1,0:T(8,128)(2,1)}, u32[]{:S(2)}, u32[]{:S(2)}) %all-to-all-start.5) | async-done | bytes 2097184 | tf_op jit(solution)/shard_map/all_to_all | solution.py:543
  198.7 2.6 %hidden_sum.1 = bf16[4,4,8192]{2,1,0:T(4,128)(2,1)} custom-call(bf16[2,2,8,16,2048]{4,3,2,1,0:T(8,128)(2,1)} %bitcast.25.branch_ref, bf16[8,8,16,1408]{3,2,1,0:T(8,128)(2,1)S(1)} %bitcast.54), custom_call_target="tpu_custom_call" | custom-call | tf_op jit(solution)/shard_map/hidden_sum/pallas_call | solution.py:413
  (25 shorter events, 0.1 us)
Async XLA Ops:
  2.1 20.4 %all-to-all-start.1 = ((s32[128,1,16]{2,1,0:T(1,128)}), s32[128,1,16]{2,1,0:T(1,128)S(1)}, u32[]{:S(2)}, u32[]{:S(2)}) async-start(s32[128,1,16]{2,1,0:T(1,128)} %broadcast_in_dim.16), calls=%async_computation.1 | async-start | bytes 131072 | tf_op jit(solution)/shard_map/all_to_all | solution.py:461
  22.5 0.6 copy-start.10
  30.8 1.6 collective-permute-start.1
  32.4 5.9 %copy-start.7 = (bf16[1024,64]{0,1:T(8,128)(2,1)S(1)}, bf16[1024,64]{0,1:T(8,128)(2,1)}, u32[]{:S(2)}) copy-start(bf16[1024,64]{0,1:T(8,128)(2,1)} %param.20) | copy-start | bytes 393220
  32.4 6.4 %copy-start.8 = (bf16[1024,64]{0,1:T(8,128)(2,1)S(1)}, bf16[1024,64]{0,1:T(8,128)(2,1)}, u32[]{:S(2)}) copy-start(bf16[1024,64]{0,1:T(8,128)(2,1)} %param.21) | copy-start | bytes 393220
  34.0 31.2 %all-to-all-start.2 = ((bf16[8,120,1024]{2,1,0:T(8,128)(2,1)}), bf16[8,120,1024]{2,1,0:T(8,128)(2,1)S(1)}, u32[]{:S(2)}, u32[]{:S(2)}) async-start(bf16[8,120,1024]{2,1,0:T(8,128)(2,1)} %broadcast_in_dim.17), calls=%async_computation.2 | async-start | bytes 3932160 | tf_op jit(solution)/shard_map/all_to_all | solution.py:469
  37.6 25.5 %collective-permute-start.5 = (bf16[512,1024]{1,0:T(8,128)(2,1)}, bf16[512,1024]{1,0:T(8,128)(2,1)S(1)}, u32[]{:S(2)}, u32[]{:S(2)}) collective-permute-start(bf16[512,1024]{1,0:T(8,128)(2,1)} %rest_0_.3), channel_id=1, source_target_pairs={{0,32},{32,0},{1,33},{33,1},{2,34},{34,2},{3,35},{35,3},{4,36},{36... | collective-permute-start | bytes 3145736 | tf_op jit(solution)/shard_map/ppermute | solution.py:34
  38.3 24.8 %collective-permute-start.2 = (bf16[1024,512]{1,0:T(8,128)(2,1)}, bf16[1024,512]{1,0:T(8,128)(2,1)}, u32[]{:S(2)}, u32[]{:S(2)}) collective-permute-start(bf16[1024,512]{1,0:T(8,128)(2,1)} %rest_0_.2), channel_id=1, source_target_pairs={{0,1},{1,0},{2,3},{3,2},{4,5},{5,4},{6,7},{7,6},{8,9},{9,8},{10,11... | collective-permute-start | bytes 3145736 | tf_op jit(solution)/shard_map/ppermute | solution.py:30
  38.3 9.6 %collective-permute-start.3 = (bf16[64,1024]{1,0:T(8,128)(2,1)S(1)}, bf16[64,1024]{1,0:T(8,128)(2,1)S(1)}, u32[]{:S(2)}, u32[]{:S(2)}) collective-permute-start(bf16[64,1024]{1,0:T(8,128)(2,1)S(1)} %bitcast.58), channel_id=1, source_target_pairs={{0,1},{1,0},{2,3},{3,2},{4,5},{5,4},{6,7},{7,6},{8,9},{9,8},{10,11... | collective-permute-start | bytes 393224 | tf_op jit(solution)/shard_map/ppermute | solution.py:30
  38.8 9.1 %collective-permute-start.4 = (bf16[64,1024]{1,0:T(8,128)(2,1)S(1)}, bf16[64,1024]{1,0:T(8,128)(2,1)S(1)}, u32[]{:S(2)}, u32[]{:S(2)}) collective-permute-start(bf16[64,1024]{1,0:T(8,128)(2,1)S(1)} %bitcast.61), channel_id=1, source_target_pairs={{0,1},{1,0},{2,3},{3,2},{4,5},{5,4},{6,7},{7,6},{8,9},{9,8},{10,11... | collective-permute-start | bytes 393224 | tf_op jit(solution)/shard_map/ppermute | solution.py:30
  63.1 11.9 %copy-start.3 = (bf16[512,1024]{1,0:T(8,128)(2,1)}, bf16[512,1024]{1,0:T(8,128)(2,1)S(1)}, u32[]{:S(2)}) copy-start(bf16[512,1024]{1,0:T(8,128)(2,1)S(1)} %collective-permute-done.5.rest_6_.rest_2_) | copy-start | bytes 3145732
  65.2 9.9 %copy-start.2 = (bf16[8,120,1024]{2,1,0:T(8,128)(2,1)}, bf16[8,120,1024]{2,1,0:T(8,128)(2,1)S(1)}, u32[]{:S(2)}) copy-start(bf16[8,120,1024]{2,1,0:T(8,128)(2,1)S(1)} %all-to-all-done.2) | copy-start | bytes 5898244
  65.2 9.9 %copy-start.11 = (s32[2,1,1024]{2,1,0:T(1,128)S(1)}, s32[2,1,1024]{2,1,0:T(1,128)}, u32[]{:S(2)}) copy-start(s32[2,1,1024]{2,1,0:T(1,128)} %reshape_reshape.9) | copy-start | bytes 24580
  75.3 9.3 %copy-start.17 = (s32[4]{0:T(128)S(1)}, s32[4]{0:T(128)}, u32[]{:S(2)}) copy-start(s32[4]{0:T(128)} %param.16) | copy-start | bytes 52
  75.3 47.4 %all-to-all-start.3 = ((bf16[64,16,1408]{2,1,0:T(8,128)(2,1)}), bf16[64,16,1408]{2,1,0:T(8,128)(2,1)S(1)}, u32[]{:S(2)}, u32[]{:S(2)}) async-start(bf16[64,16,1408]{2,1,0:T(8,128)(2,1)} %bitcast.56), calls=%async_computation.3 | async-start | bytes 5767168 | tf_op jit(solution)/shard_map/all_to_all | solution.py:525
  84.5 55.2 %collective-permute-start.6 = (bf16[512,1024]{1,0:T(8,128)(2,1)}, bf16[512,1024]{1,0:T(8,128)(2,1)}, u32[]{:S(2)}, u32[]{:S(2)}) collective-permute-start(bf16[512,1024]{1,0:T(8,128)(2,1)} %rest_0_.3), channel_id=1, source_target_pairs={{0,1},{1,0},{2,3},{3,2},{4,5},{5,4},{6,7},{7,6},{8,9},{9,8},{10,11... | collective-permute-start | bytes 3145736 | tf_op jit(solution)/shard_map/ppermute | solution.py:30
  86.3 53.3 %collective-permute-start.7 = (bf16[512,1024]{1,0:T(8,128)(2,1)}, bf16[512,1024]{1,0:T(8,128)(2,1)}, u32[]{:S(2)}, u32[]{:S(2)}) collective-permute-start(bf16[512,1024]{1,0:T(8,128)(2,1)} %copy-done.3), channel_id=1, source_target_pairs={{0,1},{1,0},{2,3},{3,2},{4,5},{5,4},{6,7},{7,6},{8,9},{9,8},{10,11... | collective-permute-start | bytes 3145736 | tf_op jit(solution)/shard_map/ppermute | solution.py:30
  122.7 1.6 copy-start
  124.3 34.0 %copy-start.16 = (s32[3]{0:T(128)S(1)}, s32[3]{0:T(128)}, u32[]{:S(2)}) copy-start(s32[3]{0:T(128)} %get-tuple-element.590) | copy-start | bytes 40
  135.5 21.9 %all-to-all-start.4 = ((bf16[32,16,1024]{2,1,0:T(8,128)(2,1)}), bf16[32,16,1024]{2,1,0:T(8,128)(2,1)S(1)}, u32[]{:S(2)}, u32[]{:S(2)}) async-start(bf16[32,16,1024]{2,1,0:T(8,128)(2,1)} %bitcast.65), calls=%async_computation.4 | async-start | bytes 2097152 | tf_op jit(solution)/shard_map/all_to_all | solution.py:539
  157.3 1.0 copy-start.9
  164.5 5.6 %copy-start.15 = (bf16[16,1024]{1,0:T(8,128)(2,1)S(1)}, bf16[16,1024]{1,0:T(8,128)(2,1)}, u32[]{:S(2)}) copy-start(bf16[16,1024]{1,0:T(8,128)(2,1)} %get-tuple-element.217) | copy-start | bytes 98308
  164.5 6.2 %copy-start.14 = (bf16[16,1024]{1,0:T(8,128)(2,1)S(1)}, bf16[16,1024]{1,0:T(8,128)(2,1)}, u32[]{:S(2)}) copy-start(bf16[16,1024]{1,0:T(8,128)(2,1)} %get-tuple-element.218) | copy-start | bytes 98308
  164.5 34.1 %copy-start.1 = (bf16[64,16,1408]{2,1,0:T(8,128)(2,1)S(1)}, bf16[64,16,1408]{2,1,0:T(8,128)(2,1)}, u32[]{:S(2)}) copy-start(bf16[64,16,1408]{2,1,0:T(8,128)(2,1)} %copy-done) | copy-start | bytes 8650756
  164.5 34.1 %all-to-all-start.5 = ((bf16[32,16,2048]{2,1,0:T(8,128)(2,1)}), bf16[32,16,2048]{2,1,0:T(8,128)(2,1)}, u32[]{:S(2)}, u32[]{:S(2)}) async-start(bf16[32,16,2048]{2,1,0:T(8,128)(2,1)} %bitcast.57), calls=%async_computation.5 | async-start | bytes 4194304 | tf_op jit(solution)/shard_map/all_to_all | solution.py:543
